TPU v7x, 32 devices: a whole 2x2x4 slice. The times are simulated.
32 devices in a mesh: grp: 2 (over x), row: 16 (over z, y, core).
Axes of the slice: x: 2, y: 2, z: 4, core: 2. Of those that a mesh axis runs over, the one named last changes fastest.
Arguments:
- cand_embed: bfloat16 [32768, 256], P(('grp', 'row')), parts along dimension 0, may hold values from -8 to 8
- cand_labels: int32 [32768], P(('grp', 'row')), parts along dimension 0, may hold values from 0 to 31
- tgt_embed: bfloat16 [4096, 256], P(('grp', 'row')), parts along dimension 0, may hold values from -8 to 8
- tgt_labels: int32 [4096], P(('grp', 'row')), parts along dimension 0, may hold values from 0 to 31
Outputs:
- cand_potential: float32 [32, 32768], P(None, ('grp', 'row')), parts along dimension 1
- tgt_scaling: float32 [32, 4096], P(None, ('grp', 'row')), parts along dimension 1
- coupling_mass: float32 [32, 32768], P(None, ('grp', 'row')), parts along dimension 1
There are 2 independent parts, one for each index of `grp`. A program takes and returns all parts, laid end to end along the dimension named above; each array names one. Nothing has to cross between parts.
All inputs are finite; a program needn't handle non-finite values.
Results may differ from a plain program's by a relative error of at most 0.0027.
Values may be sent and summed in bfloat16 or wider, within the bound.
No kernel may reach another device: no remote copies, remote signals or barrier semaphores. Data moves between devices by JAX's collectives and lax.ppermute only.
A program may use at most 64 MiB of HBM per device.

v0:
```python
import math

import jax
import jax.numpy as jnp
from jax import lax
from jax.sharding import PartitionSpec as P

CLASSES = 32
ITERS = 3


INVERSE_TEMP = 20.0
ENTROPY_TEMP = 0.05


def unit_rows(values):
    widened = values.astype(jnp.float32)
    meansq = jnp.mean(widened * widened, axis=1, keepdims=True)
    return (widened * lax.rsqrt(meansq + 1e-06) / math.sqrt(values.shape[1])).astype(jnp.bfloat16)


def kernel_tile(left_unit, right_unit):
    affinity_scores = jnp.dot(left_unit, right_unit.T, preferred_element_type=jnp.float32)
    return jnp.exp(INVERSE_TEMP * affinity_scores).astype(jnp.bfloat16)


def class_weights(labels):
    classes = jnp.arange(CLASSES, dtype=jnp.int32)
    return 1.0 + 3.0 * (labels[None, :] == classes[:, None]).astype(jnp.float32)


def row_image(scale_vb, kernel):
    return lax.dot_general(
        scale_vb, kernel, (((1,), (1,)), ((), ())), preferred_element_type=jnp.float32
    )


def shards(cand_embed, cand_labels, tgt_embed, tgt_labels):
    devices = lax.axis_size("row")
    cand_rows = cand_embed.shape[0]
    tgt_rows = tgt_embed.shape[0]
    cand_unit = unit_rows(cand_embed)
    kernel = kernel_tile(cand_unit, unit_rows(lax.all_gather(tgt_embed, "row", axis=0, tiled=True)))
    cand_weight = class_weights(cand_labels)
    tgt_weight = class_weights(tgt_labels)
    totals = lax.psum(jnp.stack([jnp.sum(cand_weight, axis=1), jnp.sum(tgt_weight, axis=1)]), "row")
    cand_marg = cand_weight / totals[0][:, None]
    tgt_marg = tgt_weight / totals[1][:, None]
    tgt_all = lax.all_gather(tgt_marg, "row", axis=1, tiled=True)
    scale_vb = jnp.ones((CLASSES, tgt_rows * devices), jnp.bfloat16)
    candidate_scaling = cand_marg
    target_scaling = tgt_marg
    for step in range(ITERS):
        image = row_image(scale_vb, kernel)
        candidate_scaling = cand_marg / image
        column_part = jnp.dot(
            candidate_scaling.astype(jnp.bfloat16), kernel, preferred_element_type=jnp.float32
        )
        column_vector = lax.psum(column_part, "row")
        complete_scaling = tgt_all / column_vector
        scale_vb = complete_scaling.astype(jnp.bfloat16)
        target_scaling = lax.dynamic_slice_in_dim(
            complete_scaling, lax.axis_index("row") * tgt_rows, tgt_rows, 1
        )
    image = row_image(scale_vb, kernel)
    coupling_mass = cand_rows * devices * candidate_scaling * image
    return (ENTROPY_TEMP * jnp.log(candidate_scaling), target_scaling, coupling_mass)


def solution(mesh):
    return jax.shard_map(
        shards,
        mesh=mesh,
        in_specs=(
            P(("grp", "row"), None),
            P(("grp", "row")),
            P(("grp", "row"), None),
            P(("grp", "row")),
        ),
        out_specs=(P(None, ("grp", "row")), P(None, ("grp", "row")), P(None, ("grp", "row"))),
        check_vma=False,
    )
```

profile of v0, /device:TPU:0, one launch (start us, length us, event | category | flops | bytes accessed | tf_op | source)
XLA Modules:
  0.0 355.1 jit_solution(9393863563888799646)
XLA Ops:
  7.2 0.0 all-gather.2.cloned.1.call-start
  7.2 0.7 all-gather.2.cloned.1.call-update
  7.9 0.0 all-reduce.4.cloned.1.call-start
  7.9 0.8 fusion.36
  8.7 0.8 fusion.20
  9.5 35.0 %psum.28 = f32[2,32]{1,0:T(2,128)S(1)} all-reduce(f32[2,32]{1,0:T(2,128)S(1)} %pad_maximum_fusion), channel_id=1, replica_groups=mesh['grp'=2,'row'=16] {'row'}, use_global_device_ids=true, to_apply=%region_2.0 | all-reduce | flops 64 | bytes 512 | tf_op jit(solution)/shard_map/psum | solution.py:46
  44.6 1.3 fusion.10
  45.9 5.0 %all-gather.2.cloned.1.call-done = bf16[2048,256]{1,0:T(8,128)(2,1)} async-done(((bf16[128,256]{1,0:T(8,128)(2,1)}), bf16[2048,256]{1,0:T(8,128)(2,1)}) %all-gather.2.cloned.1.call-update) | async-done | bytes 1048592 | tf_op jit(solution)/shard_map/all_gather | solution.py:43
  50.9 1.6 fusion
  52.5 4.9 %exponential_convert_fusion = bf16[1024,2048]{1,0:T(8,128)(2,1)} fusion(bf16[2048,256]{1,0:T(8,128)(2,1)} %all-gather.2.cloned.1.call-done, f32[2048]{0:T(1024)S(1)} %add_rsqrt_fusion, bf16[1024,256]{1,0:T(8,128)(2,1)} %param.4, f32[1024]{0:T(1024)S(1)} %add_rsqrt_fusion.1), kind=kOutput, calls=%fused_computation | convolution fusion | flops 1081081856 | bytes 5779456 | tf_op jit(solution)/shard_map/dot_general | solution.py:23
  57.4 6.3 %fusion.9 = f32[32,2048]{1,0:T(8,128)} fusion(bf16[1024,2048]{1,0:T(8,128)(2,1)} %exponential_convert_fusion, f32[32]{0:T(128)S(1)} %get-tuple-element.3, s32[1024]{0:T(1024)S(1)} %copy-done.1), kind=kOutput, calls=%fused_computation.18 | convolution fusion | flops 268632064 | bytes 4460672 | tf_op jit(solution)/shard_map/dot_general | solution.py:56
  63.7 0.0 all-reduce.6.cloned.1.call-start
  63.7 0.1 fusion.35
  63.8 20.3 %all_gather.6 = f32[32,2048]{1,0:T(8,128)S(1)} all-gather(f32[32,128]{1,0:T(8,128)S(1)} %fusion.35), channel_id=1, replica_groups=mesh['grp'=2,'row'=16] {'row'}, dimensions={1}, use_global_device_ids=true | all-gather | bytes 278528 | tf_op jit(solution)/shard_map/all_gather | solution.py:49
  84.1 67.5 %all-reduce.4.cloned.1.call-done = f32[32,2048]{1,0:T(8,128)} async-done(((f32[32,2048]{1,0:T(8,128)}), f32[32,2048]{1,0:T(8,128)}) %all-reduce.4.cloned.1.call-update) | async-done | bytes 262160 | tf_op jit(solution)/shard_map/psum | solution.py:59
  151.6 6.3 %fusion.8 = f32[32,2048]{1,0:T(8,128)} fusion(bf16[1024,2048]{1,0:T(8,128)(2,1)} %exponential_convert_fusion, f32[32,2048]{1,0:T(8,128)S(1)} %all_gather.6, f32[32,2048]{1,0:T(8,128)} %all-reduce.4.cloned.1.call-done, f32[32]{0:T(128)S(1)} %get-tuple-element.3, s32[1024]{0:T(1024)S(1)} %copy-done.1), kind=kOutput, calls=%fused_computation.17 | convolution fusion | flops 268763136 | bytes 4984960 | tf_op jit(solution)/shard_map/dot_general | solution.py:56
  157.9 0.0 all-reduce.8.cloned.1.call-start
  158.0 89.4 %all-reduce.6.cloned.1.call-done = f32[32,2048]{1,0:T(8,128)} async-done(((f32[32,2048]{1,0:T(8,128)}), f32[32,2048]{1,0:T(8,128)}) %all-reduce.6.cloned.1.call-update) | async-done | bytes 262160 | tf_op jit(solution)/shard_map/psum | solution.py:59
  247.3 4.4 %log_multiply_fusion = (f32[32,1024]{1,0:T(8,128)}, f32[32,1024]{1,0:T(8,128)S(1)}) fusion(bf16[1024,2048]{1,0:T(8,128)(2,1)} %exponential_convert_fusion, f32[32,2048]{1,0:T(8,128)S(1)} %all_gather.6, f32[32,2048]{1,0:T(8,128)} %all-reduce.6.cloned.1.call-done, f32[32]{0:T(128)S(1)} %get-tuple-element.3, s32[1024]{0:T(1024)S(1)} %copy-done.1), kind=kOutput, calls=%fused_computation.29 | convolution fusion | flops 134545408 | bytes 4984960 | tf_op jit(solution)/shard_map/dot_general | solution.py:33
  251.8 1.5 fusion.21
  253.3 89.4 %all-reduce.8.cloned.1.call-done = f32[32,2048]{1,0:T(8,128)} async-done(((f32[32,2048]{1,0:T(8,128)}), f32[32,2048]{1,0:T(8,128)}) %all-reduce.8.cloned.1.call-update) | async-done | bytes 262160 | tf_op jit(solution)/shard_map/psum | solution.py:59
  342.8 1.0 div.78
  343.8 4.2 %convolution_multiply_fusion = f32[32,1024]{1,0:T(8,128)} fusion(bf16[1024,2048]{1,0:T(8,128)(2,1)} %exponential_convert_fusion, f32[32,2048]{1,0:T(8,128)S(1)} %div.78, f32[32,1024]{1,0:T(8,128)S(1)} %get-tuple-element.6), kind=kOutput, calls=%fused_computation.8 | convolution fusion | flops 134348800 | bytes 4718592 | tf_op jit(solution)/shard_map/dot_general | solution.py:33
  348.0 0.6 constant_dynamic-slice_fusion
  (13 shorter events, 0.1 us)
Async XLA Ops:
  7.2 43.7 %all-gather.2.cloned.1.call-start = ((), (), s32[]{:S(2)}) async-start(), calls=%async_computation | async-start | bytes 1114112 | tf_op jit(solution)/shard_map/all_gather | solution.py:43
  7.9 143.7 %all-reduce.4.cloned.1.call-start = ((), (), s32[]{:S(2)}) async-start(), calls=%async_computation.1 | async-start | bytes 524288 | tf_op jit(solution)/shard_map/psum | solution.py:59
  52.4 4.9 %copy-start.1 = (s32[1024]{0:T(1024)S(1)}, s32[1024]{0:T(1024)}, u32[]{:S(2)}) copy-start(s32[1024]{0:T(1024)} %param.5) | copy-start | bytes 12292
  57.4 6.3 %copy-start.2 = (s32[128]{0:T(128)S(1)}, s32[128]{0:T(128)}, u32[]{:S(2)}) copy-start(s32[128]{0:T(128)} %param.7) | copy-start | bytes 1540
  63.7 183.7 %all-reduce.6.cloned.1.call-start = ((), (), s32[]{:S(2)}) async-start(), calls=%async_computation.2 | async-start | bytes 524288 | tf_op jit(solution)/shard_map/psum | solution.py:59
  157.9 184.9 %all-reduce.8.cloned.1.call-start = ((), (), s32[]{:S(2)}) async-start(), calls=%async_computation.3 | async-start | bytes 524288 | tf_op jit(solution)/shard_map/psum | solution.py:59
  247.3 4.4 %copy-start = (bf16[1024,2048]{1,0:T(8,128)(2,1)S(1)}, bf16[1024,2048]{1,0:T(8,128)(2,1)}, u32[]{:S(2)}) copy-start(bf16[1024,2048]{1,0:T(8,128)(2,1)} %exponential_convert_fusion) | copy-start | bytes 12582916
Sparse Core Ops, SparseCore 0:
  10.2 40.6 all-gather.1
  63.8 87.7 all-reduce.3
  158.0 89.2 all-reduce.5
  253.5 89.2 all-reduce.7
where the time goes:
time: 356 us; the launch traced here: 355 us
  waiting for transfers between devices  252 us (71%)
  blocking collectives  55.3 us (16%)
  matrix products  27.7 us (8%)
  between operations  13.8 us (4%)
  other arithmetic  5.51 us (2%)
    psum x3, waiting for transfers between devices, shards(): column_vector = lax.psum(column_part, 'row')  246 us
    psum x1, blocking collectives, shards(): lax.psum(jnp.stack([jnp.sum(cand_weight, axis=1), jnp.sum(tgt_weight, axi...  35 us
    all_gather x1, blocking collectives, shards(): tgt_all = lax.all_gather(tgt_marg, 'row', axis=1, tiled=True)  20.3 us
    dot_general x3, matrix products, shards(): jnp.dot(candidate_scaling.astype(jnp.bfloat16), kernel, preferred_element...  14.1 us
    dot_general x2, matrix products, row_image(): lax.dot_general(scale_vb, kernel, (((1,), (1,)), ((), ())), preferred_ele...  8.63 us
  transfers between devices with their start and end apart: 4, of which 4 were waited for; matrix products, arithmetic and copies ran while one was open for 1% of the time, Pallas kernels for 0%

commit v1 on v0

v1 whole, which is shorter than its diff:
```python
import math

import jax
import jax.numpy as jnp
from jax import lax
from jax.sharding import PartitionSpec as P

CLASSES = 32
ITERS = 3
INVERSE_TEMP = 20.0
ENTROPY_TEMP = 0.05
EXTRA = 16


def unit_rows(values):
    widened = values.astype(jnp.float32)
    meansq = jnp.mean(widened * widened, axis=1, keepdims=True)
    return (widened * lax.rsqrt(meansq + 1e-06) / math.sqrt(values.shape[1])).astype(jnp.bfloat16)


def one_hot(labels):
    classes = jnp.arange(CLASSES, dtype=jnp.int32)
    return (labels[None, :] == classes[:, None]).astype(jnp.float32)


def gather_blocks(block):
    devices = lax.axis_size("row")
    return lax.all_to_all(
        jnp.broadcast_to(block[None], (devices,) + block.shape), "row", 0, 0, tiled=False
    )


def scatter_sum(parts):
    got = lax.all_to_all(parts, "row", 0, 0, tiled=False)
    return jnp.sum(got.astype(jnp.float32), axis=0)


def packed_counts(counts, width):
    high = counts.astype(jnp.bfloat16)
    low = (counts - high.astype(jnp.float32)).astype(jnp.bfloat16)
    row = jnp.concatenate([high, low], axis=0)
    return jnp.pad(row, ((0, EXTRA - 4), (0, width - CLASSES)))


def shards(cand_embed, cand_labels, tgt_embed, tgt_labels):
    devices = lax.axis_size("row")
    cand_rows, width = cand_embed.shape
    tgt_rows = tgt_embed.shape[0]
    cand_hot = one_hot(cand_labels)
    tgt_hot = one_hot(tgt_labels)
    counts = jnp.stack([jnp.sum(cand_hot, axis=1), jnp.sum(tgt_hot, axis=1)])
    message = jnp.concatenate([tgt_embed, packed_counts(counts, width)], axis=0)
    gathered = gather_blocks(message)
    tgt_unit = unit_rows(gathered[:, :tgt_rows].reshape(devices * tgt_rows, width))
    parts = gathered[:, tgt_rows : tgt_rows + 4, :CLASSES].astype(jnp.float32)
    sums = jnp.sum(parts, axis=0)
    cand_total = cand_rows * devices + 3.0 * (sums[0] + sums[2])
    tgt_total = tgt_rows * devices + 3.0 * (sums[1] + sums[3])
    cand_marg = (1.0 + 3.0 * cand_hot) / cand_total[:, None]
    tgt_marg = (1.0 + 3.0 * tgt_hot) / tgt_total[:, None]

    scores = jnp.dot(unit_rows(cand_embed), tgt_unit.T, preferred_element_type=jnp.float32)
    kernel = jnp.exp(INVERSE_TEMP * scores).astype(jnp.bfloat16)

    def row_image(scale_vb):
        return jnp.dot(kernel, scale_vb.T, preferred_element_type=jnp.float32).T

    scale_vb = jnp.ones((CLASSES, tgt_rows * devices), jnp.bfloat16)
    for step in range(ITERS):
        scale_u = cand_marg / row_image(scale_vb)
        column_part = jnp.dot(
            scale_u.astype(jnp.bfloat16), kernel, preferred_element_type=jnp.float32
        )
        blocks = column_part.reshape(CLASSES, devices, tgt_rows).transpose(1, 0, 2)
        column = scatter_sum(blocks.astype(jnp.bfloat16))
        scale_v = tgt_marg / column
        got = gather_blocks(scale_v.astype(jnp.bfloat16))
        scale_vb = got.transpose(1, 0, 2).reshape(CLASSES, devices * tgt_rows)
    coupling_mass = cand_rows * devices * scale_u * row_image(scale_vb)
    return (ENTROPY_TEMP * jnp.log(scale_u), scale_v, coupling_mass)


def solution(mesh):
    return jax.shard_map(
        shards,
        mesh=mesh,
        in_specs=(
            P(("grp", "row"), None),
            P(("grp", "row")),
            P(("grp", "row"), None),
            P(("grp", "row")),
        ),
        out_specs=(P(None, ("grp", "row")), P(None, ("grp", "row")), P(None, ("grp", "row"))),
        check_vma=False,
    )
```

time: 356 us -> 129 us (0.36)
  waiting for transfers between devices: 252 us -> 23.8 us
  between operations: 13.8 us -> 0.8 us
  blocking collectives: 55.3 us -> 68.1 us
  starting transfers between devices: 0.16 us -> 7.39 us
  matrix products: 27.7 us -> 21.4 us
    psum x3 -> x0, waiting for transfers between devices: 246 us -> none  [shards(): column_vector = lax.psum(column_part, 'row')]
    all_to_all x0 -> x6, blocking collectives: none -> 68.1 us  [the longest x3 36.5 us: scatter_sum(): got = lax.all_to_all(parts, 'row', 0, 0, tiled=False)]
    psum x1 -> x0, blocking collectives: 35 us -> none  [shards(): lax.psum(jnp.stack([jnp.sum(cand_weight, axis=1), jnp.sum(tgt_weight, axi...]
    all_to_all x0 -> x1, waiting for transfers between devices: none -> 23.8 us  [gather_blocks(): lax.all_to_all(jnp.broadcast_to(block[None], (devices,) + block.shape), '...]
    all_gather x1 -> x0, blocking collectives: 20.3 us -> none  [shards(): tgt_all = lax.all_gather(tgt_marg, 'row', axis=1, tiled=True)]
    all_to_all x0 -> x1, starting transfers between devices: none -> 7.39 us  [gather_blocks(): lax.all_to_all(jnp.broadcast_to(block[None], (devices,) + block.shape), '...]
    dot_general x6, matrix products: 27.7 us -> 21.4 us  [the longest x3 11.9 us: shards(): jnp.dot(scale_u.astype(jnp.bfloat16), kernel, preferred_element_type=jnp....]
    all_gather x1 -> x0, waiting for transfers between devices: 4.99 us -> none  [shards(): lax.all_gather(tgt_embed, 'row', axis=0, tiled=True)]
  transfers between devices with their start and end apart: 4 -> 1, of which waited for: 4 -> 1; matrix products, arithmetic and copies ran while one was open for 1% -> 1% of each run, Pallas kernels for 0% -> 0%
where the time goes in v1:
time: 129 us; the launch traced here: 128 us
  blocking collectives  68.1 us (53%)
  waiting for transfers between devices  23.8 us (18%)
  matrix products  21.4 us (17%)
  starting transfers between devices  7.39 us (6%)
  other arithmetic  5.63 us (4%)
    all_to_all x3, blocking collectives, scatter_sum(): got = lax.all_to_all(parts, 'row', 0, 0, tiled=False)  36.5 us
    all_to_all x3, blocking collectives, gather_blocks(): lax.all_to_all(jnp.broadcast_to(block[None], (devices,) + block.shape), '...  31.6 us
    all_to_all x1, waiting for transfers between devices, gather_blocks(): lax.all_to_all(jnp.broadcast_to(block[None], (devices,) + block.shape), '...  23.8 us
    dot_general x3, matrix products, shards(): jnp.dot(scale_u.astype(jnp.bfloat16), kernel, preferred_element_type=jnp....  11.9 us
    all_to_all x1, starting transfers between devices, gather_blocks(): lax.all_to_all(jnp.broadcast_to(block[None], (devices,) + block.shape), '...  7.39 us
    dot_general x2, matrix products, row_image(): return jnp.dot(kernel, scale_vb.T, preferred_element_type=jnp.float32).T  6.24 us
    dot_general x1, matrix products, shards(): jnp.dot(unit_rows(cand_embed), tgt_unit.T, preferred_element_type=jnp.flo...  3.25 us
  transfers between devices with their start and end apart: 1, of which 1 were waited for; matrix products, arithmetic and copies ran while one was open for 1% of the time, Pallas kernels for 0%

profile of v1, /device:TPU:0, one launch (start us, length us, event | category | flops | bytes accessed | tf_op | source)
XLA Modules:
  0.0 128.4 jit_solution(8545357193645439422)
XLA Ops:
  0.6 0.8 convert_reduce_fusion.3
  1.4 0.8 convert_reduce_fusion.5
  2.3 0.8 pad_maximum_fusion
  3.1 1.1 broadcast_in_dim.8
  4.2 7.4 %all-to-all-start = ((bf16[16,144,256]{2,1,0:T(8,128)(2,1)}), bf16[16,144,256]{2,1,0:T(8,128)(2,1)S(1)}, u32[]{:S(2)}, u32[]{:S(2)}) async-start(bf16[16,144,256]{2,1,0:T(8,128)(2,1)} %broadcast_in_dim.8), calls=%async_computation | async-start | bytes 2359296 | tf_op jit(solution)/shard_map/all_to_all | solution.py:28
  11.6 1.3 %fusion.10 = f32[1024]{0:T(1024)S(1)} fusion(bf16[1024,256]{1,0:T(8,128)(2,1)} %param.4), kind=kLoop, calls=%fused_computation.22 | loop fusion | flops 785408 | bytes 528384 | tf_op jit(solution)/shard_map/reduce_sum | solution.py:17
  12.9 23.8 %all-to-all-done = bf16[16,144,256]{2,1,0:T(8,128)(2,1)S(1)} async-done(((bf16[16,144,256]{2,1,0:T(8,128)(2,1)}), bf16[16,144,256]{2,1,0:T(8,128)(2,1)S(1)}, u32[]{:S(2)}, u32[]{:S(2)}) %all-to-all-start) | async-done | bytes 1179680 | tf_op jit(solution)/shard_map/all_to_all | solution.py:28
  36.7 0.3 multiply_reduce_fusion
  37.1 0.2 slice_convert_fusion
  37.3 0.3 fusion.1
  37.7 3.3 %exponential_convert_fusion = bf16[1024,2048]{1,0:T(8,128)(2,1)} fusion(bf16[2048,256]{1,0:T(8,128)(2,1)S(1)} %fusion.1, bf16[1024,256]{1,0:T(8,128)(2,1)S(1)} %copy-done.1, f32[1024]{0:T(1024)S(1)} %add_rsqrt_fusion), kind=kOutput, calls=%fused_computation | convolution fusion | flops 1078984704 | bytes 5771264 | tf_op jit(solution)/shard_map/dot_general | solution.py:62
  41.0 5.5 %fusion.5 = bf16[4,16,8,128]{3,2,1,0:T(8,128)(2,1)S(1)} fusion(bf16[1024,2048]{1,0:T(8,128)(2,1)} %exponential_convert_fusion, f32[32]{0:T(128)S(1)} %get-tuple-element.6, s32[1024]{0:T(1024)S(1)} %copy-done.2), kind=kOutput, calls=%fused_computation.17 | convolution fusion | flops 268697600 | bytes 4329600 | tf_op jit(solution)/shard_map/dot_general | solution.py:71
  46.6 15.2 %all_to_all.35 = bf16[16,32,128]{2,1,0:T(8,128)(2,1)S(1)} all-to-all(bf16[16,32,128]{2,1,0:T(8,128)(2,1)S(1)} %bitcast.74), channel_id=1, replica_groups=mesh['grp'=2,'row'=16] {'row'}, dimensions={0} | all-to-all | bytes 262144 | tf_op jit(solution)/shard_map/all_to_all | solution.py:34
  61.8 0.1 divide_convert_fusion.1
  61.9 10.5 %all_to_all.36 = bf16[16,32,128]{2,1,0:T(8,128)(2,1)S(1)} all-to-all(bf16[16,32,128]{2,1,0:T(8,128)(2,1)S(1)} %broadcast_in_dim.9), channel_id=1, replica_groups=mesh['grp'=2,'row'=16] {'row'}, dimensions={0} | all-to-all | bytes 262144 | tf_op jit(solution)/shard_map/all_to_all | solution.py:28
  72.4 5.6 %fusion.6 = bf16[4,16,8,128]{3,2,1,0:T(8,128)(2,1)S(1)} fusion(bf16[1024,2048]{1,0:T(8,128)(2,1)} %exponential_convert_fusion, f32[32]{0:T(128)S(1)} %get-tuple-element.6, s32[1024]{0:T(1024)S(1)} %copy-done.2, bf16[16,32,128]{2,1,0:T(8,128)(2,1)S(1)} %all_to_all.36), kind=kOutput, calls=%fused_computation.18 | convolution fusion | flops 268697600 | bytes 4460672 | tf_op jit(solution)/shard_map/dot_general | solution.py:71
  78.0 10.8 %all_to_all.37 = bf16[16,32,128]{2,1,0:T(8,128)(2,1)S(1)} all-to-all(bf16[16,32,128]{2,1,0:T(8,128)(2,1)S(1)} %bitcast.75), channel_id=1, replica_groups=mesh['grp'=2,'row'=16] {'row'}, dimensions={0} | all-to-all | bytes 262144 | tf_op jit(solution)/shard_map/all_to_all | solution.py:34
  89.0 10.5 %all_to_all.38 = bf16[16,32,128]{2,1,0:T(8,128)(2,1)S(1)} all-to-all(bf16[16,32,128]{2,1,0:T(8,128)(2,1)S(1)} %broadcast_in_dim.10), channel_id=1, replica_groups=mesh['grp'=2,'row'=16] {'row'}, dimensions={0} | all-to-all | bytes 262144 | tf_op jit(solution)/shard_map/all_to_all | solution.py:28
  99.5 4.2 %log_multiply_fusion = (f32[32,1024]{1,0:T(8,128)}, f32[32,1024]{1,0:T(8,128)S(1)}) fusion(bf16[1024,2048]{1,0:T(8,128)(2,1)} %exponential_convert_fusion, f32[32]{0:T(128)S(1)} %get-tuple-element.6, s32[1024]{0:T(1024)S(1)} %copy-done.2, bf16[16,32,128]{2,1,0:T(8,128)(2,1)S(1)} %all_to_all.38), kind=kOutput, calls=%fused_computation.41 | convolution fusion | flops 134414336 | bytes 4591744 | tf_op jit(solution)/shard_map/dot_general | solution.py:66
  103.7 0.8 fusion.7
  104.6 10.5 %all_to_all.39 = bf16[16,32,128]{2,1,0:T(8,128)(2,1)S(1)} all-to-all(bf16[16,32,128]{2,1,0:T(8,128)(2,1)S(1)} %bitcast.76), channel_id=1, replica_groups=mesh['grp'=2,'row'=16] {'row'}, dimensions={0} | all-to-all | bytes 262144 | tf_op jit(solution)/shard_map/all_to_all | solution.py:34
  115.1 0.7 fusion.53
  115.8 10.5 %all_to_all.40 = bf16[16,32,128]{2,1,0:T(8,128)(2,1)S(1)} all-to-all(bf16[16,32,128]{2,1,0:T(8,128)(2,1)S(1)} %broadcast_in_dim.11), channel_id=1, replica_groups=mesh['grp'=2,'row'=16] {'row'}, dimensions={0} | all-to-all | bytes 262144 | tf_op jit(solution)/shard_map/all_to_all | solution.py:28
  126.4 2.0 %convolution_multiply_fusion = f32[32,1024]{1,0:T(8,128)} fusion(bf16[1024,2048]{1,0:T(8,128)(2,1)S(1)} %copy-done, f32[32,1024]{1,0:T(8,128)S(1)} %get-tuple-element.8, bf16[16,32,128]{2,1,0:T(8,128)(2,1)S(1)} %all_to_all.40), kind=kOutput, calls=%fused_computation.10 | convolution fusion | flops 134283264 | bytes 4587520 | tf_op jit(solution)/shard_map/dot_general | solution.py:66
  (26 shorter events, 0.4 us)
Async XLA Ops:
  4.2 32.5 %all-to-all-start = ((bf16[16,144,256]{2,1,0:T(8,128)(2,1)}), bf16[16,144,256]{2,1,0:T(8,128)(2,1)S(1)}, u32[]{:S(2)}, u32[]{:S(2)}) async-start(bf16[16,144,256]{2,1,0:T(8,128)(2,1)} %broadcast_in_dim.8), calls=%async_computation | async-start | bytes 2359296 | tf_op jit(solution)/shard_map/all_to_all | solution.py:28
  11.6 26.1 %copy-start.1 = (bf16[1024,256]{1,0:T(8,128)(2,1)S(1)}, bf16[1024,256]{1,0:T(8,128)(2,1)}, u32[]{:S(2)}) copy-start(bf16[1024,256]{1,0:T(8,128)(2,1)} %param.4) | copy-start | bytes 1572868
  37.7 3.3 %copy-start.2 = (s32[1024]{0:T(1024)S(1)}, s32[1024]{0:T(1024)}, u32[]{:S(2)}) copy-start(s32[1024]{0:T(1024)} %param.5) | copy-start | bytes 12292
  41.0 20.8 %copy-start.3 = (s32[128]{0:T(128)S(1)}, s32[128]{0:T(128)}, u32[]{:S(2)}) copy-start(s32[128]{0:T(128)} %param.7) | copy-start | bytes 1540
  78.0 25.7 %copy-start = (bf16[1024,2048]{1,0:T(8,128)(2,1)S(1)}, bf16[1024,2048]{1,0:T(8,128)(2,1)}, u32[]{:S(2)}) copy-start(bf16[1024,2048]{1,0:T(8,128)(2,1)} %exponential_convert_fusion) | copy-start | bytes 12582916

commit v2 on v1

--- a/solution.py
+++ b/solution.py
@@ -23,16 +23,37 @@
     return (labels[None, :] == classes[:, None]).astype(jnp.float32)
 
 
-def gather_blocks(block):
+def exchange(block, flip):
     devices = lax.axis_size("row")
-    return lax.all_to_all(
-        jnp.broadcast_to(block[None], (devices,) + block.shape), "row", 0, 0, tiled=False
-    )
+    return lax.ppermute(block, "row", [(d, d ^ flip) for d in range(devices)])
+
+
+def masks(bits):
+    found = [0]
+    for bit in bits:
+        found += [m | (1 << bit) for m in found]
+    return found
+
+
+def gather_blocks(block, stages):
+    held = {0: block}
+    for bits in stages:
+        keys = sorted(held)
+        stack = jnp.concatenate([held[k] for k in keys]) if len(keys) > 1 else held[keys[0]]
+        rows = block.shape[0]
+        got = {flip: exchange(stack, flip) for flip in masks(bits)[1:]}
+        for flip, found in got.items():
+            for place, k in enumerate(keys):
+                held[k | flip] = found[place * rows : (place + 1) * rows]
+    return [held[s] for s in range(len(held))]
 
 
 def scatter_sum(parts):
-    got = lax.all_to_all(parts, "row", 0, 0, tiled=False)
-    return jnp.sum(got.astype(jnp.float32), axis=0)
+    got = [exchange(parts[s].astype(jnp.bfloat16), s) for s in range(1, len(parts))]
+    total = parts[0]
+    for block in got:
+        total = total + block.astype(jnp.float32)
+    return total
 
 
 def packed_counts(counts, width):
@@ -44,13 +65,15 @@
 
 def shards(cand_embed, cand_labels, tgt_embed, tgt_labels):
     devices = lax.axis_size("row")
+    top = devices.bit_length() - 1
+    pairs = [list(range(low, min(low + 2, top))) for low in range(0, top, 2)]
     cand_rows, width = cand_embed.shape
     tgt_rows = tgt_embed.shape[0]
     cand_hot = one_hot(cand_labels)
     tgt_hot = one_hot(tgt_labels)
     counts = jnp.stack([jnp.sum(cand_hot, axis=1), jnp.sum(tgt_hot, axis=1)])
     message = jnp.concatenate([tgt_embed, packed_counts(counts, width)], axis=0)
-    gathered = gather_blocks(message)
+    gathered = jnp.stack(gather_blocks(message, pairs[1:] + [[1], [0]]))
     tgt_unit = unit_rows(gathered[:, :tgt_rows].reshape(devices * tgt_rows, width))
     parts = gathered[:, tgt_rows : tgt_rows + 4, :CLASSES].astype(jnp.float32)
     sums = jnp.sum(parts, axis=0)
@@ -71,11 +94,9 @@
         column_part = jnp.dot(
             scale_u.astype(jnp.bfloat16), kernel, preferred_element_type=jnp.float32
         )
-        blocks = column_part.reshape(CLASSES, devices, tgt_rows).transpose(1, 0, 2)
-        column = scatter_sum(blocks.astype(jnp.bfloat16))
-        scale_v = tgt_marg / column
-        got = gather_blocks(scale_v.astype(jnp.bfloat16))
-        scale_vb = got.transpose(1, 0, 2).reshape(CLASSES, devices * tgt_rows)
+        blocks = [column_part[:, s * tgt_rows : (s + 1) * tgt_rows] for s in range(devices)]
+        scale_v = tgt_marg / scatter_sum(blocks)
+        scale_vb = jnp.concatenate(gather_blocks(scale_v.astype(jnp.bfloat16), pairs), axis=1)
     coupling_mass = cand_rows * devices * scale_u * row_image(scale_vb)
     return (ENTROPY_TEMP * jnp.log(scale_u), scale_v, coupling_mass)
 

time: 129 us -> 152 us (1.18)
  starting transfers between devices: 7.39 us -> 88.4 us
  blocking collectives: 68.1 us -> 0 us
  waiting for transfers between devices: 23.8 us -> 34.5 us
    ppermute x0 -> x68, starting transfers between devices: none -> 88.4 us  [exchange(): return lax.ppermute(block, 'row', [(d, d ^ flip) for d in range(devices)])]
    all_to_all x6 -> x0, blocking collectives: 68.1 us -> none  [the longest x3 36.5 us: scatter_sum(): got = lax.all_to_all(parts, 'row', 0, 0, tiled=False)]
    ppermute x0 -> x68, waiting for transfers between devices: none -> 34.5 us  [exchange(): return lax.ppermute(block, 'row', [(d, d ^ flip) for d in range(devices)])]
    all_to_all x1 -> x0, waiting for transfers between devices: 23.8 us -> none  [gather_blocks(): lax.all_to_all(jnp.broadcast_to(block[None], (devices,) + block.shape), '...]
    all_to_all x1 -> x0, starting transfers between devices: 7.39 us -> none  [gather_blocks(): lax.all_to_all(jnp.broadcast_to(block[None], (devices,) + block.shape), '...]
  transfers between devices with their start and end apart: 1 -> 68, of which waited for: 1 -> 24; matrix products, arithmetic and copies ran while one was open for 1% -> 0% of each run, Pallas kernels for 0% -> 0%
where the time goes in v2:
time: 152 us
  starting transfers between devices  88.4 us (58%)
  waiting for transfers between devices  34.5 us (23%)
  matrix products  21.7 us (14%)
  other arithmetic  4.54 us (3%)
    ppermute x68, starting transfers between devices, exchange(): return lax.ppermute(block, 'row', [(d, d ^ flip) for d in range(devices)])  88.4 us
    ppermute x68, waiting for transfers between devices, exchange(): return lax.ppermute(block, 'row', [(d, d ^ flip) for d in range(devices)])  34.5 us
    dot_general x3, matrix products, shards(): jnp.dot(scale_u.astype(jnp.bfloat16), kernel, preferred_element_type=jnp....  12 us
    dot_general x2, matrix products, row_image(): return jnp.dot(kernel, scale_vb.T, preferred_element_type=jnp.float32).T  6.37 us
    dot_general x1, matrix products, shards(): jnp.dot(unit_rows(cand_embed), tgt_unit.T, preferred_element_type=jnp.flo...  3.31 us
  transfers between devices with their start and end apart: 68, of which 24 were waited for; matrix products, arithmetic and copies ran while one was open for 0% of the time, Pallas kernels for 0%

profile of v2, /device:TPU:0, one launch (start us, length us, event | category | flops | bytes accessed | tf_op | source)
XLA Modules:
  0.0 151.8 jit_solution(16189455405099622571)
XLA Ops:
  4.0 3.0 %collective-permute-start = (bf16[144,256]{1,0:T(8,128)(2,1)S(1)}, bf16[144,256]{1,0:T(8,128)(2,1)S(1)}, u32[]{:S(2)}, u32[]{:S(2)}) collective-permute-start(bf16[144,256]{1,0:T(8,128)(2,1)S(1)} %pad_maximum_fusion), channel_id=1, source_target_pairs={{0,4},{1,5},{2,6},{3,7},{4,0},{5,1},{6,2},{7,3},{8,12},{9,13},{10,... | collective-permute-start | bytes 221192 | tf_op jit(solution)/shard_map/ppermute | solution.py:28
  7.1 2.6 %collective-permute-start.1 = (bf16[144,256]{1,0:T(8,128)(2,1)S(1)}, bf16[144,256]{1,0:T(8,128)(2,1)S(1)}, u32[]{:S(2)}, u32[]{:S(2)}) collective-permute-start(bf16[144,256]{1,0:T(8,128)(2,1)S(1)} %pad_maximum_fusion), channel_id=1, source_target_pairs={{0,8},{1,9},{2,10},{3,11},{4,12},{5,13},{6,14},{7,15},{8,0},{9,1},... | collective-permute-start | bytes 221192 | tf_op jit(solution)/shard_map/ppermute | solution.py:28
  9.7 5.2 %collective-permute-done.1 = bf16[144,256]{1,0:T(8,128)(2,1)S(1)} collective-permute-done((bf16[144,256]{1,0:T(8,128)(2,1)S(1)}, bf16[144,256]{1,0:T(8,128)(2,1)S(1)}, u32[]{:S(2)}, u32[]{:S(2)}) %collective-permute-start.1) | collective-permute-done | bytes 73760 | tf_op jit(solution)/shard_map/ppermute | solution.py:28
  17.4 5.4 %collective-permute-done.3 = bf16[576,256]{1,0:T(8,128)(2,1)S(1)} collective-permute-done((bf16[576,256]{1,0:T(8,128)(2,1)S(1)}, bf16[576,256]{1,0:T(8,128)(2,1)S(1)}, u32[]{:S(2)}, u32[]{:S(2)}) %collective-permute-start.3) | collective-permute-done | bytes 294944 | tf_op jit(solution)/shard_map/ppermute | solution.py:28
  26.2 3.3 %exponential_convert_fusion = bf16[1024,2048]{1,0:T(8,128)(2,1)} fusion(bf16[2048,256]{1,0:T(8,128)(2,1)S(1)} %fusion.1, bf16[1024,256]{1,0:T(8,128)(2,1)S(1)} %copy-done.2, f32[1024]{0:T(1024)S(1)} %add_rsqrt_fusion), kind=kOutput, calls=%fused_computation | convolution fusion | flops 1078984704 | bytes 5771264 | tf_op jit(solution)/shard_map/dot_general | solution.py:85
  29.5 5.6 %fusion.101 = (bf16[32,2048]{1,0:T(8,128)(2,1)S(1)}, f32[32,2048]{1,0:T(8,128)S(1)}) fusion(bf16[1024,2048]{1,0:T(8,128)(2,1)} %exponential_convert_fusion, f32[32]{0:T(128)S(1)} %get-tuple-element.58, s32[1024]{0:T(1024)S(1)} %copy-done.3), kind=kOutput, calls=%fused_computation.214 | convolution fusion | flops 268697600 | bytes 4591744 | tf_op jit(solution)/shard_map/dot_general | solution.py:94
  35.4 3.0 %collective-permute-start.19 = (bf16[32,128]{1,0:T(8,128)(2,1)S(1)}, bf16[32,128]{1,0:T(8,128)(2,1)S(1)}, u32[]{:S(2)}, u32[]{:S(2)}) collective-permute-start(bf16[32,128]{1,0:T(8,128)(2,1)S(1)} %get-tuple-element.41), channel_id=1, source_target_pairs={{0,15},{1,14},{2,13},{3,12},{4,11},{5,10},{6,9},{7,8},{8,7},{9,6},... | collective-permute-start | bytes 24584 | tf_op jit(solution)/shard_map/ppermute | solution.py:28
  43.4 3.7 %collective-permute-start.14 = (bf16[32,128]{1,0:T(8,128)(2,1)S(1)}, bf16[32,128]{1,0:T(8,128)(2,1)S(1)}, u32[]{:S(2)}, u32[]{:S(2)}) collective-permute-start(bf16[32,128]{1,0:T(8,128)(2,1)S(1)} %get-tuple-element.46), channel_id=1, source_target_pairs={{0,10},{1,11},{2,8},{3,9},{4,14},{5,15},{6,12},{7,13},{8,2},{9,3},... | collective-permute-start | bytes 24584 | tf_op jit(solution)/shard_map/ppermute | solution.py:28
  47.2 2.4 %collective-permute-start.12 = (bf16[32,128]{1,0:T(8,128)(2,1)S(1)}, bf16[32,128]{1,0:T(8,128)(2,1)S(1)}, u32[]{:S(2)}, u32[]{:S(2)}) collective-permute-start(bf16[32,128]{1,0:T(8,128)(2,1)S(1)} %get-tuple-element.48), channel_id=1, source_target_pairs={{0,8},{1,9},{2,10},{3,11},{4,12},{5,13},{6,14},{7,15},{8,0},{9,1},... | collective-permute-start | bytes 24584 | tf_op jit(solution)/shard_map/ppermute | solution.py:28
  65.1 2.3 %collective-permute-start.23 = (bf16[128,128]{1,0:T(8,128)(2,1)S(1)}, bf16[128,128]{1,0:T(8,128)(2,1)S(1)}, u32[]{:S(2)}, u32[]{:S(2)}) collective-permute-start(bf16[128,128]{1,0:T(8,128)(2,1)S(1)} %pad_maximum_fusion.1), channel_id=1, source_target_pairs={{0,4},{1,5},{2,6},{3,7},{4,0},{5,1},{6,2},{7,3},{8,12},{9,13},{10,... | collective-permute-start | bytes 98312 | tf_op jit(solution)/shard_map/ppermute | solution.py:28
  70.0 5.6 %fusion.104 = (bf16[32,2048]{1,0:T(8,128)(2,1)S(1)}, f32[32,2048]{1,0:T(8,128)S(1)}) fusion(bf16[1024,2048]{1,0:T(8,128)(2,1)} %exponential_convert_fusion, bf16[32,2048]{1,0:T(8,128)(2,1)S(1)} %constant_dynamic-update-slice_fusion.30, f32[32]{0:T(128)S(1)} %get-tuple-element.58, s32[1024]{0:T(1024)S(1)} %copy-done.3), kind=kOutput, calls=%fused_computation.215 | convolution fusion | flops 268697600 | bytes 4722816 | tf_op jit(solution)/shard_map/dot_general | solution.py:94
  78.0 2.5 %collective-permute-start.39 = (bf16[32,128]{1,0:T(8,128)(2,1)S(1)}, bf16[32,128]{1,0:T(8,128)(2,1)S(1)}, u32[]{:S(2)}, u32[]{:S(2)}) collective-permute-start(bf16[32,128]{1,0:T(8,128)(2,1)S(1)} %get-tuple-element.27), channel_id=1, source_target_pairs={{0,14},{1,15},{2,12},{3,13},{4,10},{5,11},{6,8},{7,9},{8,6},{9,7},... | collective-permute-start | bytes 24584 | tf_op jit(solution)/shard_map/ppermute | solution.py:28
  83.8 3.9 %collective-permute-start.35 = (bf16[32,128]{1,0:T(8,128)(2,1)S(1)}, bf16[32,128]{1,0:T(8,128)(2,1)S(1)}, u32[]{:S(2)}, u32[]{:S(2)}) collective-permute-start(bf16[32,128]{1,0:T(8,128)(2,1)S(1)} %get-tuple-element.31), channel_id=1, source_target_pairs={{0,10},{1,11},{2,8},{3,9},{4,14},{5,15},{6,12},{7,13},{8,2},{9,3},... | collective-permute-start | bytes 24584 | tf_op jit(solution)/shard_map/ppermute | solution.py:28
  87.7 2.3 %collective-permute-start.33 = (bf16[32,128]{1,0:T(8,128)(2,1)S(1)}, bf16[32,128]{1,0:T(8,128)(2,1)S(1)}, u32[]{:S(2)}, u32[]{:S(2)}) collective-permute-start(bf16[32,128]{1,0:T(8,128)(2,1)S(1)} %get-tuple-element.33), channel_id=1, source_target_pairs={{0,8},{1,9},{2,10},{3,11},{4,12},{5,13},{6,14},{7,15},{8,0},{9,1},... | collective-permute-start | bytes 24584 | tf_op jit(solution)/shard_map/ppermute | solution.py:28
  90.2 2.8 %collective-permute-start.31 = (bf16[32,128]{1,0:T(8,128)(2,1)S(1)}, bf16[32,128]{1,0:T(8,128)(2,1)S(1)}, u32[]{:S(2)}, u32[]{:S(2)}) collective-permute-start(bf16[32,128]{1,0:T(8,128)(2,1)S(1)} %get-tuple-element.35), channel_id=1, source_target_pairs={{0,6},{1,7},{2,4},{3,5},{4,2},{5,3},{6,0},{7,1},{8,14},{9,15},{10,... | collective-permute-start | bytes 24584 | tf_op jit(solution)/shard_map/ppermute | solution.py:28
  104.7 2.3 %collective-permute-start.44 = (bf16[128,128]{1,0:T(8,128)(2,1)S(1)}, bf16[128,128]{1,0:T(8,128)(2,1)S(1)}, u32[]{:S(2)}, u32[]{:S(2)}) collective-permute-start(bf16[128,128]{1,0:T(8,128)(2,1)S(1)} %pad_maximum_fusion.2), channel_id=1, source_target_pairs={{0,4},{1,5},{2,6},{3,7},{4,0},{5,1},{6,2},{7,3},{8,12},{9,13},{10,... | collective-permute-start | bytes 98312 | tf_op jit(solution)/shard_map/ppermute | solution.py:28
  107.1 2.5 %collective-permute-done.44 = bf16[128,128]{1,0:T(8,128)(2,1)S(1)} collective-permute-done((bf16[128,128]{1,0:T(8,128)(2,1)S(1)}, bf16[128,128]{1,0:T(8,128)(2,1)S(1)}, u32[]{:S(2)}, u32[]{:S(2)}) %collective-permute-start.44) | collective-permute-done | bytes 32800 | tf_op jit(solution)/shard_map/ppermute | solution.py:28
  109.8 4.4 %log_multiply_fusion = (f32[32,1024]{1,0:T(8,128)}, f32[32,1024]{1,0:T(8,128)S(1)}) fusion(bf16[32,2048]{1,0:T(8,128)(2,1)S(1)} %constant_dynamic-update-slice_fusion.46, bf16[1024,2048]{1,0:T(8,128)(2,1)} %exponential_convert_fusion, f32[32]{0:T(128)S(1)} %get-tuple-element.58, s32[1024]{0:T(1024)S(1)} %copy-done.3), kind=kOutput, calls=%fused_computation.103 | convolution fusion | flops 134414336 | bytes 4591744 | tf_op jit(solution)/shard_map/dot_general | solution.py:89
  115.1 2.5 %collective-permute-start.61 = (bf16[32,128]{1,0:T(8,128)(2,1)S(1)}, bf16[32,128]{1,0:T(8,128)(2,1)S(1)}, u32[]{:S(2)}, u32[]{:S(2)}) collective-permute-start(bf16[32,128]{1,0:T(8,128)(2,1)S(1)} %get-tuple-element.11), channel_id=1, source_target_pairs={{0,15},{1,14},{2,13},{3,12},{4,11},{5,10},{6,9},{7,8},{8,7},{9,6},... | collective-permute-start | bytes 24584 | tf_op jit(solution)/shard_map/ppermute | solution.py:28
  117.6 2.3 %collective-permute-start.60 = (bf16[32,128]{1,0:T(8,128)(2,1)S(1)}, bf16[32,128]{1,0:T(8,128)(2,1)S(1)}, u32[]{:S(2)}, u32[]{:S(2)}) collective-permute-start(bf16[32,128]{1,0:T(8,128)(2,1)S(1)} %get-tuple-element.12), channel_id=1, source_target_pairs={{0,14},{1,15},{2,12},{3,13},{4,10},{5,11},{6,8},{7,9},{8,6},{9,7},... | collective-permute-start | bytes 24584 | tf_op jit(solution)/shard_map/ppermute | solution.py:28
  123.1 3.9 %collective-permute-start.56 = (bf16[32,128]{1,0:T(8,128)(2,1)S(1)}, bf16[32,128]{1,0:T(8,128)(2,1)S(1)}, u32[]{:S(2)}, u32[]{:S(2)}) collective-permute-start(bf16[32,128]{1,0:T(8,128)(2,1)S(1)} %get-tuple-element.16), channel_id=1, source_target_pairs={{0,10},{1,11},{2,8},{3,9},{4,14},{5,15},{6,12},{7,13},{8,2},{9,3},... | collective-permute-start | bytes 24584 | tf_op jit(solution)/shard_map/ppermute | solution.py:28
  127.0 2.3 %collective-permute-start.54 = (bf16[32,128]{1,0:T(8,128)(2,1)S(1)}, bf16[32,128]{1,0:T(8,128)(2,1)S(1)}, u32[]{:S(2)}, u32[]{:S(2)}) collective-permute-start(bf16[32,128]{1,0:T(8,128)(2,1)S(1)} %get-tuple-element.18), channel_id=1, source_target_pairs={{0,8},{1,9},{2,10},{3,11},{4,12},{5,13},{6,14},{7,15},{8,0},{9,1},... | collective-permute-start | bytes 24584 | tf_op jit(solution)/shard_map/ppermute | solution.py:28
  129.8 2.5 %collective-permute-start.52 = (bf16[32,128]{1,0:T(8,128)(2,1)S(1)}, bf16[32,128]{1,0:T(8,128)(2,1)S(1)}, u32[]{:S(2)}, u32[]{:S(2)}) collective-permute-start(bf16[32,128]{1,0:T(8,128)(2,1)S(1)} %get-tuple-element.20), channel_id=1, source_target_pairs={{0,6},{1,7},{2,4},{3,5},{4,2},{5,3},{6,0},{7,1},{8,14},{9,15},{10,... | collective-permute-start | bytes 24584 | tf_op jit(solution)/shard_map/ppermute | solution.py:28
  144.9 2.4 %collective-permute-start.65 = (bf16[128,128]{1,0:T(8,128)(2,1)S(1)}, bf16[128,128]{1,0:T(8,128)(2,1)S(1)}, u32[]{:S(2)}, u32[]{:S(2)}) collective-permute-start(bf16[128,128]{1,0:T(8,128)(2,1)S(1)} %pad_maximum_fusion.3), channel_id=1, source_target_pairs={{0,4},{1,5},{2,6},{3,7},{4,0},{5,1},{6,2},{7,3},{8,12},{9,13},{10,... | collective-permute-start | bytes 98312 | tf_op jit(solution)/shard_map/ppermute | solution.py:28
  (223 shorter events, 71.8 us)
Async XLA Ops:
  7.1 7.8 %collective-permute-start.1 = (bf16[144,256]{1,0:T(8,128)(2,1)S(1)}, bf16[144,256]{1,0:T(8,128)(2,1)S(1)}, u32[]{:S(2)}, u32[]{:S(2)}) collective-permute-start(bf16[144,256]{1,0:T(8,128)(2,1)S(1)} %pad_maximum_fusion), channel_id=1, source_target_pairs={{0,8},{1,9},{2,10},{3,11},{4,12},{5,13},{6,14},{7,15},{8,0},{9,1},... | collective-permute-start | bytes 221192 | tf_op jit(solution)/shard_map/ppermute | solution.py:28
  15.9 6.9 %collective-permute-start.3 = (bf16[576,256]{1,0:T(8,128)(2,1)S(1)}, bf16[576,256]{1,0:T(8,128)(2,1)S(1)}, u32[]{:S(2)}, u32[]{:S(2)}) collective-permute-start(bf16[576,256]{1,0:T(8,128)(2,1)S(1)} %constant_dynamic-update-slice_fusion), channel_id=1, source_target_pairs={{0,2},{1,3},{2,0},{3,1},{4,6},{5,7},{6,4},{7,5},{8,10},{9,11},{10,... | collective-permute-start | bytes 884744 | tf_op jit(solution)/shard_map/ppermute | solution.py:28
  35.2 8.2 %collective-permute-start.5 = (bf16[32,128]{1,0:T(8,128)(2,1)S(1)}, bf16[32,128]{1,0:T(8,128)(2,1)S(1)}, u32[]{:S(2)}, u32[]{:S(2)}) collective-permute-start(bf16[32,128]{1,0:T(8,128)(2,1)S(1)} %get-tuple-element.40), channel_id=1, source_target_pairs={{0,1},{1,0},{2,3},{3,2},{4,5},{5,4},{6,7},{7,6},{8,9},{9,8},{10,11... | collective-permute-start | bytes 24584 | tf_op jit(solution)/shard_map/ppermute | solution.py:28
  35.4 8.1 %collective-permute-start.19 = (bf16[32,128]{1,0:T(8,128)(2,1)S(1)}, bf16[32,128]{1,0:T(8,128)(2,1)S(1)}, u32[]{:S(2)}, u32[]{:S(2)}) collective-permute-start(bf16[32,128]{1,0:T(8,128)(2,1)S(1)} %get-tuple-element.41), channel_id=1, source_target_pairs={{0,15},{1,14},{2,13},{3,12},{4,11},{5,10},{6,9},{7,8},{8,7},{9,6},... | collective-permute-start | bytes 24584 | tf_op jit(solution)/shard_map/ppermute | solution.py:28
  38.4 8.8 %collective-permute-start.18 = (bf16[32,128]{1,0:T(8,128)(2,1)S(1)}, bf16[32,128]{1,0:T(8,128)(2,1)S(1)}, u32[]{:S(2)}, u32[]{:S(2)}) collective-permute-start(bf16[32,128]{1,0:T(8,128)(2,1)S(1)} %get-tuple-element.42), channel_id=1, source_target_pairs={{0,14},{1,15},{2,12},{3,13},{4,10},{5,11},{6,8},{7,9},{8,6},{9,7},... | collective-permute-start | bytes 24584 | tf_op jit(solution)/shard_map/ppermute | solution.py:28
  40.1 7.1 %collective-permute-start.17 = (bf16[32,128]{1,0:T(8,128)(2,1)S(1)}, bf16[32,128]{1,0:T(8,128)(2,1)S(1)}, u32[]{:S(2)}, u32[]{:S(2)}) collective-permute-start(bf16[32,128]{1,0:T(8,128)(2,1)S(1)} %get-tuple-element.43), channel_id=1, source_target_pairs={{0,13},{1,12},{2,15},{3,14},{4,9},{5,8},{6,11},{7,10},{8,5},{9,4},... | collective-permute-start | bytes 24584 | tf_op jit(solution)/shard_map/ppermute | solution.py:28
  41.6 8.0 %collective-permute-start.16 = (bf16[32,128]{1,0:T(8,128)(2,1)S(1)}, bf16[32,128]{1,0:T(8,128)(2,1)S(1)}, u32[]{:S(2)}, u32[]{:S(2)}) collective-permute-start(bf16[32,128]{1,0:T(8,128)(2,1)S(1)} %get-tuple-element.44), channel_id=1, source_target_pairs={{0,12},{1,13},{2,14},{3,15},{4,8},{5,9},{6,10},{7,11},{8,4},{9,5},... | collective-permute-start | bytes 24584 | tf_op jit(solution)/shard_map/ppermute | solution.py:28
  43.4 7.2 %collective-permute-start.15 = (bf16[32,128]{1,0:T(8,128)(2,1)S(1)}, bf16[32,128]{1,0:T(8,128)(2,1)S(1)}, u32[]{:S(2)}, u32[]{:S(2)}) collective-permute-start(bf16[32,128]{1,0:T(8,128)(2,1)S(1)} %get-tuple-element.45), channel_id=1, source_target_pairs={{0,11},{1,10},{2,9},{3,8},{4,15},{5,14},{6,13},{7,12},{8,3},{9,2},... | collective-permute-start | bytes 24584 | tf_op jit(solution)/shard_map/ppermute | solution.py:28
  43.4 9.0 %collective-permute-start.14 = (bf16[32,128]{1,0:T(8,128)(2,1)S(1)}, bf16[32,128]{1,0:T(8,128)(2,1)S(1)}, u32[]{:S(2)}, u32[]{:S(2)}) collective-permute-start(bf16[32,128]{1,0:T(8,128)(2,1)S(1)} %get-tuple-element.46), channel_id=1, source_target_pairs={{0,10},{1,11},{2,8},{3,9},{4,14},{5,15},{6,12},{7,13},{8,2},{9,3},... | collective-permute-start | bytes 24584 | tf_op jit(solution)/shard_map/ppermute | solution.py:28
  63.0 6.9 %collective-permute-start.25 = (bf16[128,128]{1,0:T(8,128)(2,1)S(1)}, bf16[128,128]{1,0:T(8,128)(2,1)S(1)}, u32[]{:S(2)}, u32[]{:S(2)}) collective-permute-start(bf16[128,128]{1,0:T(8,128)(2,1)S(1)} %pad_maximum_fusion.1), channel_id=1, source_target_pairs={{0,12},{1,13},{2,14},{3,15},{4,8},{5,9},{6,10},{7,11},{8,4},{9,5},... | collective-permute-start | bytes 98312 | tf_op jit(solution)/shard_map/ppermute | solution.py:28
  75.6 8.1 %collective-permute-start.26 = (bf16[32,128]{1,0:T(8,128)(2,1)S(1)}, bf16[32,128]{1,0:T(8,128)(2,1)S(1)}, u32[]{:S(2)}, u32[]{:S(2)}) collective-permute-start(bf16[32,128]{1,0:T(8,128)(2,1)S(1)} %get-tuple-element.25), channel_id=1, source_target_pairs={{0,1},{1,0},{2,3},{3,2},{4,5},{5,4},{6,7},{7,6},{8,9},{9,8},{10,11... | collective-permute-start | bytes 24584 | tf_op jit(solution)/shard_map/ppermute | solution.py:28
  75.7 8.1 %collective-permute-start.40 = (bf16[32,128]{1,0:T(8,128)(2,1)S(1)}, bf16[32,128]{1,0:T(8,128)(2,1)S(1)}, u32[]{:S(2)}, u32[]{:S(2)}) collective-permute-start(bf16[32,128]{1,0:T(8,128)(2,1)S(1)} %get-tuple-element.26), channel_id=1, source_target_pairs={{0,15},{1,14},{2,13},{3,12},{4,11},{5,10},{6,9},{7,8},{8,7},{9,6},... | collective-permute-start | bytes 24584 | tf_op jit(solution)/shard_map/ppermute | solution.py:28
  78.0 9.6 %collective-permute-start.39 = (bf16[32,128]{1,0:T(8,128)(2,1)S(1)}, bf16[32,128]{1,0:T(8,128)(2,1)S(1)}, u32[]{:S(2)}, u32[]{:S(2)}) collective-permute-start(bf16[32,128]{1,0:T(8,128)(2,1)S(1)} %get-tuple-element.27), channel_id=1, source_target_pairs={{0,14},{1,15},{2,12},{3,13},{4,10},{5,11},{6,8},{7,9},{8,6},{9,7},... | collective-permute-start | bytes 24584 | tf_op jit(solution)/shard_map/ppermute | solution.py:28
  80.6 7.1 %collective-permute-start.38 = (bf16[32,128]{1,0:T(8,128)(2,1)S(1)}, bf16[32,128]{1,0:T(8,128)(2,1)S(1)}, u32[]{:S(2)}, u32[]{:S(2)}) collective-permute-start(bf16[32,128]{1,0:T(8,128)(2,1)S(1)} %get-tuple-element.28), channel_id=1, source_target_pairs={{0,13},{1,12},{2,15},{3,14},{4,9},{5,8},{6,11},{7,10},{8,5},{9,4},... | collective-permute-start | bytes 24584 | tf_op jit(solution)/shard_map/ppermute | solution.py:28
  81.9 8.1 %collective-permute-start.37 = (bf16[32,128]{1,0:T(8,128)(2,1)S(1)}, bf16[32,128]{1,0:T(8,128)(2,1)S(1)}, u32[]{:S(2)}, u32[]{:S(2)}) collective-permute-start(bf16[32,128]{1,0:T(8,128)(2,1)S(1)} %get-tuple-element.29), channel_id=1, source_target_pairs={{0,12},{1,13},{2,14},{3,15},{4,8},{5,9},{6,10},{7,11},{8,4},{9,5},... | collective-permute-start | bytes 24584 | tf_op jit(solution)/shard_map/ppermute | solution.py:28
  83.8 9.2 %collective-permute-start.35 = (bf16[32,128]{1,0:T(8,128)(2,1)S(1)}, bf16[32,128]{1,0:T(8,128)(2,1)S(1)}, u32[]{:S(2)}, u32[]{:S(2)}) collective-permute-start(bf16[32,128]{1,0:T(8,128)(2,1)S(1)} %get-tuple-element.31), channel_id=1, source_target_pairs={{0,10},{1,11},{2,8},{3,9},{4,14},{5,15},{6,12},{7,13},{8,2},{9,3},... | collective-permute-start | bytes 24584 | tf_op jit(solution)/shard_map/ppermute | solution.py:28
  102.7 7.0 %collective-permute-start.46 = (bf16[128,128]{1,0:T(8,128)(2,1)S(1)}, bf16[128,128]{1,0:T(8,128)(2,1)S(1)}, u32[]{:S(2)}, u32[]{:S(2)}) collective-permute-start(bf16[128,128]{1,0:T(8,128)(2,1)S(1)} %pad_maximum_fusion.2), channel_id=1, source_target_pairs={{0,12},{1,13},{2,14},{3,15},{4,8},{5,9},{6,10},{7,11},{8,4},{9,5},... | collective-permute-start | bytes 98312 | tf_op jit(solution)/shard_map/ppermute | solution.py:28
  115.0 8.1 %collective-permute-start.47 = (bf16[32,128]{1,0:T(8,128)(2,1)S(1)}, bf16[32,128]{1,0:T(8,128)(2,1)S(1)}, u32[]{:S(2)}, u32[]{:S(2)}) collective-permute-start(bf16[32,128]{1,0:T(8,128)(2,1)S(1)} %get-tuple-element.10), channel_id=1, source_target_pairs={{0,1},{1,0},{2,3},{3,2},{4,5},{5,4},{6,7},{7,6},{8,9},{9,8},{10,11... | collective-permute-start | bytes 24584 | tf_op jit(solution)/shard_map/ppermute | solution.py:28
  115.1 8.1 %collective-permute-start.61 = (bf16[32,128]{1,0:T(8,128)(2,1)S(1)}, bf16[32,128]{1,0:T(8,128)(2,1)S(1)}, u32[]{:S(2)}, u32[]{:S(2)}) collective-permute-start(bf16[32,128]{1,0:T(8,128)(2,1)S(1)} %get-tuple-element.11), channel_id=1, source_target_pairs={{0,15},{1,14},{2,13},{3,12},{4,11},{5,10},{6,9},{7,8},{8,7},{9,6},... | collective-permute-start | bytes 24584 | tf_op jit(solution)/shard_map/ppermute | solution.py:28
  117.6 9.4 %collective-permute-start.60 = (bf16[32,128]{1,0:T(8,128)(2,1)S(1)}, bf16[32,128]{1,0:T(8,128)(2,1)S(1)}, u32[]{:S(2)}, u32[]{:S(2)}) collective-permute-start(bf16[32,128]{1,0:T(8,128)(2,1)S(1)} %get-tuple-element.12), channel_id=1, source_target_pairs={{0,14},{1,15},{2,12},{3,13},{4,10},{5,11},{6,8},{7,9},{8,6},{9,7},... | collective-permute-start | bytes 24584 | tf_op jit(solution)/shard_map/ppermute | solution.py:28
  119.9 7.1 %collective-permute-start.59 = (bf16[32,128]{1,0:T(8,128)(2,1)S(1)}, bf16[32,128]{1,0:T(8,128)(2,1)S(1)}, u32[]{:S(2)}, u32[]{:S(2)}) collective-permute-start(bf16[32,128]{1,0:T(8,128)(2,1)S(1)} %get-tuple-element.13), channel_id=1, source_target_pairs={{0,13},{1,12},{2,15},{3,14},{4,9},{5,8},{6,11},{7,10},{8,5},{9,4},... | collective-permute-start | bytes 24584 | tf_op jit(solution)/shard_map/ppermute | solution.py:28
  121.1 8.2 %collective-permute-start.58 = (bf16[32,128]{1,0:T(8,128)(2,1)S(1)}, bf16[32,128]{1,0:T(8,128)(2,1)S(1)}, u32[]{:S(2)}, u32[]{:S(2)}) collective-permute-start(bf16[32,128]{1,0:T(8,128)(2,1)S(1)} %get-tuple-element.14), channel_id=1, source_target_pairs={{0,12},{1,13},{2,14},{3,15},{4,8},{5,9},{6,10},{7,11},{8,4},{9,5},... | collective-permute-start | bytes 24584 | tf_op jit(solution)/shard_map/ppermute | solution.py:28
  123.1 9.2 %collective-permute-start.56 = (bf16[32,128]{1,0:T(8,128)(2,1)S(1)}, bf16[32,128]{1,0:T(8,128)(2,1)S(1)}, u32[]{:S(2)}, u32[]{:S(2)}) collective-permute-start(bf16[32,128]{1,0:T(8,128)(2,1)S(1)} %get-tuple-element.16), channel_id=1, source_target_pairs={{0,10},{1,11},{2,8},{3,9},{4,14},{5,15},{6,12},{7,13},{8,2},{9,3},... | collective-permute-start | bytes 24584 | tf_op jit(solution)/shard_map/ppermute | solution.py:28
  142.9 6.9 %collective-permute-start.67 = (bf16[128,128]{1,0:T(8,128)(2,1)S(1)}, bf16[128,128]{1,0:T(8,128)(2,1)S(1)}, u32[]{:S(2)}, u32[]{:S(2)}) collective-permute-start(bf16[128,128]{1,0:T(8,128)(2,1)S(1)} %pad_maximum_fusion.3), channel_id=1, source_target_pairs={{0,12},{1,13},{2,14},{3,15},{4,8},{5,9},{6,10},{7,11},{8,4},{9,5},... | collective-permute-start | bytes 98312 | tf_op jit(solution)/shard_map/ppermute | solution.py:28
  (49 other events, 278.3 us)

commit v3 on v0

v3 whole, which is shorter than its diff:
```python
import functools
import math

import jax
import jax.numpy as jnp
from jax import lax
from jax.experimental import pallas as pl
from jax.experimental.pallas import tpu as pltpu
from jax.sharding import PartitionSpec as P

CLASSES = 32
ITERS = 3
INVERSE_TEMP = 20.0
ENTROPY_TEMP = 0.05
LANES = 128
EXTRA = 16
TILE = 256
F32 = jnp.float32
BF16 = jnp.bfloat16


def exchange(block, bit):
    devices = lax.axis_size("row")
    return lax.ppermute(block, "row", [(d, d ^ (1 << bit)) for d in range(devices)])


def call(body, outs, *args, flops=0):
    space = pl.BlockSpec(memory_space=pltpu.VMEM)
    moved = sum(a.size * a.dtype.itemsize for a in args)
    return pl.pallas_call(
        body,
        out_shape=[pltpu.VMEM(shape, dtype) for shape, dtype in outs],
        in_specs=[space] * len(args),
        out_specs=[space] * len(outs),
        compiler_params=pltpu.CompilerParams(vmem_limit_bytes=24 * 1024 * 1024),
        cost_estimate=pl.CostEstimate(flops=flops, bytes_accessed=moved, transcendentals=0),
    )(*[pltpu.with_memory_space_constraint(a, pltpu.VMEM) for a in args])


def unit_rows(values):
    widened = values.astype(F32)
    meansq = jnp.mean(widened * widened, axis=1, keepdims=True)
    return (widened * lax.rsqrt(meansq + 1e-06) / math.sqrt(values.shape[1])).astype(BF16)


def hot(labels, classes=CLASSES):
    rows = lax.broadcasted_iota(jnp.int32, (classes, labels.shape[1]), 0)
    return (labels == rows).astype(F32)


def pack_body(embed_ref, tgt_ref, cand_ref, out_ref):
    rows = embed_ref.shape[0]
    out_ref[:rows, :] = embed_ref[...]
    out_ref[rows:, :LANES] = jnp.broadcast_to(
        tgt_ref[...].astype(F32), (EXTRA, LANES)
    ).astype(BF16)
    counts = lax.dot_general(
        jnp.ones((EXTRA, cand_ref.shape[1]), BF16),
        hot(cand_ref[...], LANES).astype(BF16),
        (((1,), (1,)), ((), ())),
        preferred_element_type=F32,
    )
    high = counts.astype(BF16).astype(F32)
    even = lax.broadcasted_iota(jnp.int32, (EXTRA, LANES), 0) % 2 == 0
    out_ref[rows:, LANES:] = jnp.where(even, high, counts - high).astype(BF16)


def fill_kernel(unit_ref, held_ref, kernel_ref, tgt_rows):
    rows = tgt_rows + EXTRA
    cand_rows = unit_ref.shape[0]
    per = TILE // tgt_rows
    for col in range(0, kernel_ref.shape[1], TILE):
        first = col // tgt_rows
        block = jnp.concatenate(
            [held_ref[pl.ds((first + s) * rows, tgt_rows), :] for s in range(per)]
        )
        tgt_unit = unit_rows(block)
        for row in range(0, cand_rows, TILE):
            scores = lax.dot_general(
                unit_ref[row : row + TILE, :],
                tgt_unit,
                (((1,), (1,)), ((), ())),
                preferred_element_type=F32,
            )
            kernel_ref[row : row + TILE, col : col + TILE] = jnp.exp(
                INVERSE_TEMP * scores
            ).astype(BF16)


def image_of(kernel_ref, scale_v):
    image = lax.dot_general(
        kernel_ref[...], scale_v, (((1,), (1,)), ((), ())), preferred_element_type=F32
    )
    return image.T


def side_by_side(ref):
    return jnp.concatenate([ref[s] for s in range(ref.shape[0])], axis=1)


def put_column(scale_ub, kernel_ref, out_ref):
    part = jnp.dot(scale_ub, kernel_ref[...], preferred_element_type=F32)
    width = out_ref.shape[2]
    for s in range(out_ref.shape[0]):
        out_ref[s] = part[:, s * width : (s + 1) * width].astype(out_ref.dtype)


def near_body(unit_ref, held_ref, kernel_ref, image_ref, *, tgt_rows):
    fill_kernel(unit_ref, held_ref, kernel_ref, tgt_rows)
    image_ref[...] = image_of(kernel_ref, jnp.ones((CLASSES, kernel_ref.shape[1]), BF16))


def far_body(
    unit_ref, near_ref, far_ref, image_ref, label_ref,
    kernel_ref, marg_ref, tgt_marg_ref, scale_ref, column_ref, *, tgt_rows,
):
    rows = tgt_rows + EXTRA
    slots = tgt_marg_ref.shape[0]
    fill_kernel(unit_ref, far_ref, kernel_ref, tgt_rows)
    counts = jnp.zeros((EXTRA, LANES), F32)
    tgt_total = jnp.zeros((CLASSES, 1), F32)
    for ref in (near_ref, far_ref):
        for s in range(slots):
            extra = ref[pl.ds(s * rows + tgt_rows, EXTRA), :].astype(F32)
            counts += extra[:, LANES:]
            weight = 1.0 + 3.0 * hot(extra[:1, :LANES].astype(jnp.int32))
            tgt_total += jnp.sum(weight, axis=1, keepdims=True)
            if ref is near_ref:
                tgt_marg_ref[s] = weight
    for s in range(slots):
        tgt_marg_ref[s] = tgt_marg_ref[s] / tgt_total
    count = jnp.broadcast_to(counts[:1] + counts[1:2], (LANES, LANES)).T[:CLASSES, :1]
    devices = 2 * slots
    cand_total = unit_ref.shape[0] * devices + 3.0 * count
    marg = (1.0 + 3.0 * hot(label_ref[...])) / cand_total
    marg_ref[...] = marg
    ones = jnp.ones((CLASSES, kernel_ref.shape[1]), BF16)
    scale_ub = (marg / (image_ref[...] + image_of(kernel_ref, ones))).astype(BF16)
    scale_ref[...] = scale_ub
    put_column(scale_ub, kernel_ref, column_ref)


def column_body(scale_ref, kernel_ref, column_ref):
    put_column(scale_ref[...], kernel_ref, column_ref)


def image_body(kernel_ref, scale_ref, image_ref):
    image_ref[...] = image_of(kernel_ref, side_by_side(scale_ref))


def step_body(kernel_ref, scale_ref, image_ref, marg_ref, out_ref, rounded_ref, column_ref):
    image = image_ref[...] + image_of(kernel_ref, side_by_side(scale_ref))
    scale_u = marg_ref[...] / image
    out_ref[...] = scale_u
    rounded_ref[...] = scale_u.astype(BF16)
    put_column(scale_u.astype(BF16), kernel_ref, column_ref)


def last_body(kernel_ref, scale_ref, image_ref, u_ref, mass_ref, potential_ref, *, candidates):
    image = image_ref[...] + image_of(kernel_ref, side_by_side(scale_ref))
    scale_u = u_ref[...]
    mass_ref[...] = candidates * scale_u * image
    potential_ref[...] = ENTROPY_TEMP * jnp.log(scale_u)


def shards(cand_embed, cand_labels, tgt_embed, tgt_labels):
    devices = lax.axis_size("row")
    top = devices.bit_length() - 1
    slots = devices // 2
    cand_rows, width = cand_embed.shape
    tgt_rows = tgt_embed.shape[0]
    half = slots * tgt_rows
    cand_labels = cand_labels.reshape(1, cand_rows)
    block = (slots, CLASSES, tgt_rows)
    image_type = ((CLASSES, cand_rows), F32)
    pass_flops = 2 * cand_rows * half * 128

    (held,) = call(
        pack_body,
        [((tgt_rows + EXTRA, width), BF16)],
        tgt_embed, tgt_labels.reshape(1, tgt_rows), cand_labels,
    )
    cand_unit = unit_rows(cand_embed)
    for bit in range(top - 1, 0, -1):
        held = jnp.concatenate([held, exchange(held, bit)])
    far = exchange(held, 0)
    near_kernel, image = call(
        functools.partial(near_body, tgt_rows=tgt_rows),
        [((cand_rows, half), BF16), image_type],
        cand_unit, held, flops=4 * pass_flops,
    )
    far_kernel, cand_marg, tgt_marg, scale_ub, far_column = call(
        functools.partial(far_body, tgt_rows=tgt_rows),
        [
            ((cand_rows, half), BF16), image_type, (block, F32),
            ((CLASSES, cand_rows), BF16), (block, BF16),
        ],
        cand_unit, held, far, image, cand_labels, flops=5 * pass_flops,
    )
    scale_u = None
    for step in range(ITERS):
        if step:
            scale_u, scale_ub, far_column = call(
                step_body,
                [image_type, ((CLASSES, cand_rows), BF16), (block, BF16)],
                far_kernel, far_vb, image, cand_marg, flops=2 * pass_flops,
            )
        got = exchange(far_column, 0)
        (column,) = call(column_body, [(block, F32)], scale_ub, near_kernel, flops=pass_flops)
        column = column + got.astype(F32)
        for bit in range(1, top):
            got = exchange(column.astype(BF16), bit).astype(F32)
            pair = got.reshape((-1, 2, 1 << (top - 1 - bit)) + block[1:])
            column = column + pair[:, ::-1].reshape(block)
        scale_v = tgt_marg / column
        scale_vb = scale_v.astype(BF16)
        far_vb = exchange(scale_vb, 0)
        (image,) = call(image_body, [image_type], near_kernel, scale_vb, flops=pass_flops)
    mass, potential = call(
        functools.partial(last_body, candidates=float(cand_rows * devices)),
        [image_type, image_type],
        far_kernel, far_vb, image, scale_u, flops=pass_flops,
    )
    return (potential, scale_v[0], mass)


def solution(mesh):
    return jax.shard_map(
        shards,
        mesh=mesh,
        in_specs=(
            P(("grp", "row"), None),
            P(("grp", "row")),
            P(("grp", "row"), None),
            P(("grp", "row")),
        ),
        out_specs=(P(None, ("grp", "row")), P(None, ("grp", "row")), P(None, ("grp", "row"))),
        check_vma=False,
    )
```

time: 356 us -> 86.8 us (0.24)
  waiting for transfers between devices: 252 us -> 38.4 us
  blocking collectives: 55.3 us -> 0 us
  starting transfers between devices: 0.16 us -> 28.6 us
  matrix products: 27.7 us -> 0 us
  between operations: 13.8 us -> 0.89 us
  Pallas kernels: 0 us -> 11.6 us
  local copies, waits for them, and re-layouts: 0.63 us -> 6.27 us
  other arithmetic: 5.51 us -> 0.8 us
    psum x3 -> x0, waiting for transfers between devices: 246 us -> none  [shards(): column_vector = lax.psum(column_part, 'row')]
    ppermute x0 -> x19, waiting for transfers between devices: none -> 38.4 us  [exchange(): lax.ppermute(block, 'row', [(d, d ^ 1 << bit) for d in range(devices)])]
    psum x1 -> x0, blocking collectives: 35 us -> none  [shards(): lax.psum(jnp.stack([jnp.sum(cand_weight, axis=1), jnp.sum(tgt_weight, axi...]
    ppermute x0 -> x19, starting transfers between devices: none -> 28.6 us  [exchange(): lax.ppermute(block, 'row', [(d, d ^ 1 << bit) for d in range(devices)])]
    dot_general x6 -> x0, matrix products: 27.7 us -> none  [the longest x3 14.1 us: shards(): jnp.dot(candidate_scaling.astype(jnp.bfloat16), kernel, preferred_element...]
    all_gather x1 -> x0, blocking collectives: 20.3 us -> none  [shards(): tgt_all = lax.all_gather(tgt_marg, 'row', axis=1, tiled=True)]
    pallas_call x0 -> x12, Pallas kernels: none -> 11.6 us  [call(): pl.pallas_call(body, out_shape=[pltpu.VMEM(shape, dtype) for shape, dtype...]
    unnamed x6 -> x18, local copies, waits for them, and re-layouts: 0.01 us -> 5.57 us
  transfers between devices with their start and end apart: 4 -> 19, of which waited for: 4 -> 17; matrix products, arithmetic and copies ran while one was open for 1% -> 1% of each run, Pallas kernels for 0% -> 6%
where the time goes in v3:
time: 86.8 us; the launch traced here: 86.5 us
  waiting for transfers between devices  38.4 us (44%)
  starting transfers between devices  28.6 us (33%)
  Pallas kernels  11.6 us (13%)
  local copies, waits for them, and re-layouts  6.27 us (7%)
  between operations  0.89 us (1%)
    ppermute x19, waiting for transfers between devices, exchange(): lax.ppermute(block, 'row', [(d, d ^ 1 << bit) for d in range(devices)])  38.4 us
    ppermute x19, starting transfers between devices, exchange(): lax.ppermute(block, 'row', [(d, d ^ 1 << bit) for d in range(devices)])  28.6 us
    pallas_call x12, Pallas kernels, call(): pl.pallas_call(body, out_shape=[pltpu.VMEM(shape, dtype) for shape, dtype...  11.6 us
    unnamed x18, local copies, waits for them, and re-layouts  5.57 us
  transfers between devices with their start and end apart: 19, of which 17 were waited for; matrix products, arithmetic and copies ran while one was open for 1% of the time, Pallas kernels for 6%

profile of v3, /device:TPU:0, one launch (start us, length us, event | category | flops | bytes accessed | tf_op | source)
XLA Modules:
  0.0 86.5 jit_solution(1950649505604419524)
XLA Ops:
  3.0 4.0 %collective-permute-start = (bf16[144,256]{1,0:T(8,128)(2,1)S(1)}, bf16[144,256]{1,0:T(8,128)(2,1)S(1)}, u32[]{:S(2)}, u32[]{:S(2)}) collective-permute-start(bf16[144,256]{1,0:T(8,128)(2,1)S(1)} %shard_map.67), channel_id=1, source_target_pairs={{0,8},{1,9},{2,10},{3,11},{4,12},{5,13},{6,14},{7,15},{8,0},{9,1},... | collective-permute-start | bytes 221192 | tf_op jit(solution)/shard_map/ppermute | solution.py:24
  7.1 3.9 %collective-permute-done = bf16[144,256]{1,0:T(8,128)(2,1)S(1)} collective-permute-done((bf16[144,256]{1,0:T(8,128)(2,1)S(1)}, bf16[144,256]{1,0:T(8,128)(2,1)S(1)}, u32[]{:S(2)}, u32[]{:S(2)}) %collective-permute-start) | collective-permute-done | bytes 73760 | tf_op jit(solution)/shard_map/ppermute | solution.py:24
  11.7 4.5 %collective-permute-done.1 = bf16[288,256]{1,0:T(8,128)(2,1)S(1)} collective-permute-done((bf16[288,256]{1,0:T(8,128)(2,1)S(1)}, bf16[288,256]{1,0:T(8,128)(2,1)S(1)}, u32[]{:S(2)}, u32[]{:S(2)}) %collective-permute-start.1) | collective-permute-done | bytes 147488 | tf_op jit(solution)/shard_map/ppermute | solution.py:24
  16.2 1.8 %collective-permute-start.2 = (bf16[576,256]{1,0:T(8,128)(2,1)S(1)}, bf16[576,256]{1,0:T(8,128)(2,1)S(1)}, u32[]{:S(2)}, u32[]{:S(2)}) collective-permute-start(bf16[576,256]{1,0:T(8,128)(2,1)S(1)} %pad_maximum_fusion.1), channel_id=1, source_target_pairs={{0,2},{1,3},{2,0},{3,1},{4,6},{5,7},{6,4},{7,5},{8,10},{9,11},{10,... | collective-permute-start | bytes 884744 | tf_op jit(solution)/shard_map/ppermute | solution.py:24
  18.0 5.0 %collective-permute-done.2 = bf16[576,256]{1,0:T(8,128)(2,1)S(1)} collective-permute-done((bf16[576,256]{1,0:T(8,128)(2,1)S(1)}, bf16[576,256]{1,0:T(8,128)(2,1)S(1)}, u32[]{:S(2)}, u32[]{:S(2)}) %collective-permute-start.2) | collective-permute-done | bytes 294944 | tf_op jit(solution)/shard_map/ppermute | solution.py:24
  23.6 1.6 %shard_map.68 = (bf16[1024,1024]{1,0:T(8,128)(2,1)S(1)}, f32[32,1024]{1,0:T(8,128)S(1)}) custom-call(bf16[1024,256]{1,0:T(8,128)(2,1)S(1)} %fusion.2.unit_ref, bf16[1152,256]{1,0:T(8,128)(2,1)S(1)} %pad_maximum_fusion.held_ref.near_ref), custom_call_target="tpu_custom_call" | custom-call | flops 1073741824 | bytes 1114112 | tf_op jit(solution)/shard_map/pallas_call | solution.py:30
  25.2 2.4 %shard_map.69 = (bf16[1024,1024]{1,0:T(8,128)(2,1)S(1)}, f32[32,1024]{1,0:T(8,128)S(1)}, f32[8,32,128]{2,1,0:T(8,128)S(1)}, bf16[32,1024]{1,0:T(8,128)(2,1)S(1)}, bf16[8,32,128]{2,1,0:T(8,128)(2,1)S(1)}) custom-call(bf16[1024,256]{1,0:T(8,128)(2,1)S(1)} %fusion.2.unit_ref, bf16[1152,256]{1,0:T(8,128)(2,1)S(1)} %pad_maximum_fusion.held_ref.near_ref, ...), custom_call_target="tpu_custom_call" | custom-call | flops 1342177280 | bytes 1839104 | tf_op jit(solution)/shard_map/pallas_call | solution.py:30
  30.3 1.8 %collective-permute-start.5 = (bf16[8,32,128]{2,1,0:T(8,128)(2,1)S(1)}, bf16[8,32,128]{2,1,0:T(8,128)(2,1)S(1)}, u32[]{:S(2)}, u32[]{:S(2)}) collective-permute-start(bf16[8,32,128]{2,1,0:T(8,128)(2,1)S(1)} %fusion.8), channel_id=1, source_target_pairs={{0,2},{1,3},{2,0},{3,1},{4,6},{5,7},{6,4},{7,5},{8,10},{9,11},{10,... | collective-permute-start | bytes 196616 | tf_op jit(solution)/shard_map/ppermute | solution.py:24
  32.1 2.6 %collective-permute-done.5 = bf16[8,32,128]{2,1,0:T(8,128)(2,1)S(1)} collective-permute-done((bf16[8,32,128]{2,1,0:T(8,128)(2,1)S(1)}, bf16[8,32,128]{2,1,0:T(8,128)(2,1)S(1)}, u32[]{:S(2)}, u32[]{:S(2)}) %collective-permute-start.5) | collective-permute-done | bytes 65568 | tf_op jit(solution)/shard_map/ppermute | solution.py:24
  34.8 2.2 %collective-permute-start.6 = (bf16[8,32,128]{2,1,0:T(8,128)(2,1)S(1)}, bf16[8,32,128]{2,1,0:T(8,128)(2,1)S(1)}, u32[]{:S(2)}, u32[]{:S(2)}) collective-permute-start(bf16[8,32,128]{2,1,0:T(8,128)(2,1)S(1)} %get-tuple-element.37), channel_id=1, source_target_pairs={{0,4},{1,5},{2,6},{3,7},{4,0},{5,1},{6,2},{7,3},{8,12},{9,13},{10,... | collective-permute-start | bytes 196616 | tf_op jit(solution)/shard_map/ppermute | solution.py:24
  36.9 2.2 %collective-permute-done.6 = bf16[8,32,128]{2,1,0:T(8,128)(2,1)S(1)} collective-permute-done((bf16[8,32,128]{2,1,0:T(8,128)(2,1)S(1)}, bf16[8,32,128]{2,1,0:T(8,128)(2,1)S(1)}, u32[]{:S(2)}, u32[]{:S(2)}) %collective-permute-start.6) | collective-permute-done | bytes 65568 | tf_op jit(solution)/shard_map/ppermute | solution.py:24
  39.2 4.1 %collective-permute-start.7 = (bf16[8,32,128]{2,1,0:T(8,128)(2,1)S(1)}, bf16[8,32,128]{2,1,0:T(8,128)(2,1)S(1)}, u32[]{:S(2)}, u32[]{:S(2)}) collective-permute-start(bf16[8,32,128]{2,1,0:T(8,128)(2,1)S(1)} %fusion.11), channel_id=1, source_target_pairs={{0,8},{1,9},{2,10},{3,11},{4,12},{5,13},{6,14},{7,15},{8,0},{9,1},... | collective-permute-start | bytes 196616 | tf_op jit(solution)/shard_map/ppermute | solution.py:24
  43.3 2.2 %collective-permute-done.7 = bf16[8,32,128]{2,1,0:T(8,128)(2,1)S(1)} collective-permute-done((bf16[8,32,128]{2,1,0:T(8,128)(2,1)S(1)}, bf16[8,32,128]{2,1,0:T(8,128)(2,1)S(1)}, u32[]{:S(2)}, u32[]{:S(2)}) %collective-permute-start.7) | collective-permute-done | bytes 65568 | tf_op jit(solution)/shard_map/ppermute | solution.py:24
  47.2 1.7 %shard_map.72 = (f32[32,1024]{1,0:T(8,128)}, bf16[32,1024]{1,0:T(8,128)(2,1)S(1)}, bf16[8,32,128]{2,1,0:T(8,128)(2,1)S(1)}) custom-call(bf16[1024,1024]{1,0:T(8,128)(2,1)S(1)} %copy-done.1, bf16[8,32,128]{2,1,0:T(8,128)(2,1)S(1)} %collective-permute-done.8.scale_ref, f32[32,1024]{1,0:T(8,128)S(1)} %shard_map.71.image_ref, ...), custom_call_target="tpu_custom_call" | custom-call | flops 536870912 | bytes 2424832 | tf_op jit(solution)/shard_map/pallas_call | solution.py:30
  51.7 2.8 %collective-permute-done.10 = bf16[8,32,128]{2,1,0:T(8,128)(2,1)S(1)} collective-permute-done((bf16[8,32,128]{2,1,0:T(8,128)(2,1)S(1)}, bf16[8,32,128]{2,1,0:T(8,128)(2,1)S(1)}, u32[]{:S(2)}, u32[]{:S(2)}) %collective-permute-start.10) | collective-permute-done | bytes 65568 | tf_op jit(solution)/shard_map/ppermute | solution.py:24
  54.5 1.8 %collective-permute-start.11 = (bf16[8,32,128]{2,1,0:T(8,128)(2,1)S(1)}, bf16[8,32,128]{2,1,0:T(8,128)(2,1)S(1)}, u32[]{:S(2)}, u32[]{:S(2)}) collective-permute-start(bf16[8,32,128]{2,1,0:T(8,128)(2,1)S(1)} %get-tuple-element.35), channel_id=1, source_target_pairs={{0,4},{1,5},{2,6},{3,7},{4,0},{5,1},{6,2},{7,3},{8,12},{9,13},{10,... | collective-permute-start | bytes 196616 | tf_op jit(solution)/shard_map/ppermute | solution.py:24
  56.3 2.6 %collective-permute-done.11 = bf16[8,32,128]{2,1,0:T(8,128)(2,1)S(1)} collective-permute-done((bf16[8,32,128]{2,1,0:T(8,128)(2,1)S(1)}, bf16[8,32,128]{2,1,0:T(8,128)(2,1)S(1)}, u32[]{:S(2)}, u32[]{:S(2)}) %collective-permute-start.11) | collective-permute-done | bytes 65568 | tf_op jit(solution)/shard_map/ppermute | solution.py:24
  58.9 3.1 %collective-permute-start.12 = (bf16[8,32,128]{2,1,0:T(8,128)(2,1)S(1)}, bf16[8,32,128]{2,1,0:T(8,128)(2,1)S(1)}, u32[]{:S(2)}, u32[]{:S(2)}) collective-permute-start(bf16[8,32,128]{2,1,0:T(8,128)(2,1)S(1)} %fusion.12), channel_id=1, source_target_pairs={{0,8},{1,9},{2,10},{3,11},{4,12},{5,13},{6,14},{7,15},{8,0},{9,1},... | collective-permute-start | bytes 196616 | tf_op jit(solution)/shard_map/ppermute | solution.py:24
  62.0 2.2 %collective-permute-done.12 = bf16[8,32,128]{2,1,0:T(8,128)(2,1)S(1)} collective-permute-done((bf16[8,32,128]{2,1,0:T(8,128)(2,1)S(1)}, bf16[8,32,128]{2,1,0:T(8,128)(2,1)S(1)}, u32[]{:S(2)}, u32[]{:S(2)}) %collective-permute-start.12) | collective-permute-done | bytes 65568 | tf_op jit(solution)/shard_map/ppermute | solution.py:24
  70.2 2.8 %collective-permute-done.15 = bf16[8,32,128]{2,1,0:T(8,128)(2,1)S(1)} collective-permute-done((bf16[8,32,128]{2,1,0:T(8,128)(2,1)S(1)}, bf16[8,32,128]{2,1,0:T(8,128)(2,1)S(1)}, u32[]{:S(2)}, u32[]{:S(2)}) %collective-permute-start.15) | collective-permute-done | bytes 65568 | tf_op jit(solution)/shard_map/ppermute | solution.py:24
  73.0 2.1 %collective-permute-start.16 = (bf16[8,32,128]{2,1,0:T(8,128)(2,1)S(1)}, bf16[8,32,128]{2,1,0:T(8,128)(2,1)S(1)}, u32[]{:S(2)}, u32[]{:S(2)}) collective-permute-start(bf16[8,32,128]{2,1,0:T(8,128)(2,1)S(1)} %get-tuple-element.33), channel_id=1, source_target_pairs={{0,4},{1,5},{2,6},{3,7},{4,0},{5,1},{6,2},{7,3},{8,12},{9,13},{10,... | collective-permute-start | bytes 196616 | tf_op jit(solution)/shard_map/ppermute | solution.py:24
  75.1 2.2 %collective-permute-done.16 = bf16[8,32,128]{2,1,0:T(8,128)(2,1)S(1)} collective-permute-done((bf16[8,32,128]{2,1,0:T(8,128)(2,1)S(1)}, bf16[8,32,128]{2,1,0:T(8,128)(2,1)S(1)}, u32[]{:S(2)}, u32[]{:S(2)}) %collective-permute-start.16) | collective-permute-done | bytes 65568 | tf_op jit(solution)/shard_map/ppermute | solution.py:24
  77.4 3.1 %collective-permute-start.17 = (bf16[8,32,128]{2,1,0:T(8,128)(2,1)S(1)}, bf16[8,32,128]{2,1,0:T(8,128)(2,1)S(1)}, u32[]{:S(2)}, u32[]{:S(2)}) collective-permute-start(bf16[8,32,128]{2,1,0:T(8,128)(2,1)S(1)} %fusion.13), channel_id=1, source_target_pairs={{0,8},{1,9},{2,10},{3,11},{4,12},{5,13},{6,14},{7,15},{8,0},{9,1},... | collective-permute-start | bytes 196616 | tf_op jit(solution)/shard_map/ppermute | solution.py:24
  80.5 2.2 %collective-permute-done.17 = bf16[8,32,128]{2,1,0:T(8,128)(2,1)S(1)} collective-permute-done((bf16[8,32,128]{2,1,0:T(8,128)(2,1)S(1)}, bf16[8,32,128]{2,1,0:T(8,128)(2,1)S(1)}, u32[]{:S(2)}, u32[]{:S(2)}) %collective-permute-start.17) | collective-permute-done | bytes 65568 | tf_op jit(solution)/shard_map/ppermute | solution.py:24
  (72 shorter events, 20.7 us)
Async XLA Ops:
  2.8 20.3 %copy-start.7 = (bf16[1024,256]{1,0:T(8,128)(2,1)S(1)}, bf16[1024,256]{1,0:T(8,128)(2,1)}, u32[]{:S(2)}) copy-start(bf16[1024,256]{1,0:T(8,128)(2,1)} %param.4) | copy-start | bytes 1572868
  3.0 8.0 %collective-permute-start = (bf16[144,256]{1,0:T(8,128)(2,1)S(1)}, bf16[144,256]{1,0:T(8,128)(2,1)S(1)}, u32[]{:S(2)}, u32[]{:S(2)}) collective-permute-start(bf16[144,256]{1,0:T(8,128)(2,1)S(1)} %shard_map.67), channel_id=1, source_target_pairs={{0,8},{1,9},{2,10},{3,11},{4,12},{5,13},{6,14},{7,15},{8,0},{9,1},... | collective-permute-start | bytes 221192 | tf_op jit(solution)/shard_map/ppermute | solution.py:24
  11.0 5.2 %collective-permute-start.1 = (bf16[288,256]{1,0:T(8,128)(2,1)S(1)}, bf16[288,256]{1,0:T(8,128)(2,1)S(1)}, u32[]{:S(2)}, u32[]{:S(2)}) collective-permute-start(bf16[288,256]{1,0:T(8,128)(2,1)S(1)} %pad_maximum_fusion.2), channel_id=1, source_target_pairs={{0,4},{1,5},{2,6},{3,7},{4,0},{5,1},{6,2},{7,3},{8,12},{9,13},{10,... | collective-permute-start | bytes 442376 | tf_op jit(solution)/shard_map/ppermute | solution.py:24
  16.2 6.8 %collective-permute-start.2 = (bf16[576,256]{1,0:T(8,128)(2,1)S(1)}, bf16[576,256]{1,0:T(8,128)(2,1)S(1)}, u32[]{:S(2)}, u32[]{:S(2)}) collective-permute-start(bf16[576,256]{1,0:T(8,128)(2,1)S(1)} %pad_maximum_fusion.1), channel_id=1, source_target_pairs={{0,2},{1,3},{2,0},{3,1},{4,6},{5,7},{6,4},{7,5},{8,10},{9,11},{10,... | collective-permute-start | bytes 884744 | tf_op jit(solution)/shard_map/ppermute | solution.py:24
  23.1 2.1 %collective-permute-start.3 = (bf16[1152,256]{1,0:T(8,128)(2,1)S(1)}, bf16[1152,256]{1,0:T(8,128)(2,1)S(1)}, u32[]{:S(2)}, u32[]{:S(2)}) collective-permute-start(bf16[1152,256]{1,0:T(8,128)(2,1)S(1)} %pad_maximum_fusion.held_ref.near_ref), channel_id=1, source_target_pairs={{0,1},{1,0},{2,3},{3,2},{4,5},{5,4},{6,7},{7,6},{8,9},{9,8},{10,11... | collective-permute-start | bytes 1769480 | tf_op jit(solution)/shard_map/ppermute | solution.py:24
  27.5 1.4 %copy-start = (bf16[1024,1024]{1,0:T(8,128)(2,1)}, bf16[1024,1024]{1,0:T(8,128)(2,1)S(1)}, u32[]{:S(2)}) copy-start(bf16[1024,1024]{1,0:T(8,128)(2,1)S(1)} %get-tuple-element.18.kernel_ref) | copy-start | bytes 6291460
  28.9 1.4 %collective-permute-start.4 = (bf16[8,32,128]{2,1,0:T(8,128)(2,1)S(1)}, bf16[8,32,128]{2,1,0:T(8,128)(2,1)S(1)}, u32[]{:S(2)}, u32[]{:S(2)}) collective-permute-start(bf16[8,32,128]{2,1,0:T(8,128)(2,1)S(1)} %get-tuple-element.22), channel_id=1, source_target_pairs={{0,1},{1,0},{2,3},{3,2},{4,5},{5,4},{6,7},{7,6},{8,9},{9,8},{10,11... | collective-permute-start | bytes 196616 | tf_op jit(solution)/shard_map/ppermute | solution.py:24
  30.3 4.4 %collective-permute-start.5 = (bf16[8,32,128]{2,1,0:T(8,128)(2,1)S(1)}, bf16[8,32,128]{2,1,0:T(8,128)(2,1)S(1)}, u32[]{:S(2)}, u32[]{:S(2)}) collective-permute-start(bf16[8,32,128]{2,1,0:T(8,128)(2,1)S(1)} %fusion.8), channel_id=1, source_target_pairs={{0,2},{1,3},{2,0},{3,1},{4,6},{5,7},{6,4},{7,5},{8,10},{9,11},{10,... | collective-permute-start | bytes 196616 | tf_op jit(solution)/shard_map/ppermute | solution.py:24
  34.8 4.4 %collective-permute-start.6 = (bf16[8,32,128]{2,1,0:T(8,128)(2,1)S(1)}, bf16[8,32,128]{2,1,0:T(8,128)(2,1)S(1)}, u32[]{:S(2)}, u32[]{:S(2)}) collective-permute-start(bf16[8,32,128]{2,1,0:T(8,128)(2,1)S(1)} %get-tuple-element.37), channel_id=1, source_target_pairs={{0,4},{1,5},{2,6},{3,7},{4,0},{5,1},{6,2},{7,3},{8,12},{9,13},{10,... | collective-permute-start | bytes 196616 | tf_op jit(solution)/shard_map/ppermute | solution.py:24
  39.2 6.3 %collective-permute-start.7 = (bf16[8,32,128]{2,1,0:T(8,128)(2,1)S(1)}, bf16[8,32,128]{2,1,0:T(8,128)(2,1)S(1)}, u32[]{:S(2)}, u32[]{:S(2)}) collective-permute-start(bf16[8,32,128]{2,1,0:T(8,128)(2,1)S(1)} %fusion.11), channel_id=1, source_target_pairs={{0,8},{1,9},{2,10},{3,11},{4,12},{5,13},{6,14},{7,15},{8,0},{9,1},... | collective-permute-start | bytes 196616 | tf_op jit(solution)/shard_map/ppermute | solution.py:24
  45.6 1.6 %copy-start.1 = (bf16[1024,1024]{1,0:T(8,128)(2,1)S(1)}, bf16[1024,1024]{1,0:T(8,128)(2,1)}, u32[]{:S(2)}) copy-start(bf16[1024,1024]{1,0:T(8,128)(2,1)} %copy-done) | copy-start | bytes 6291460
  45.6 1.3 %collective-permute-start.8 = (bf16[8,32,128]{2,1,0:T(8,128)(2,1)S(1)}, bf16[8,32,128]{2,1,0:T(8,128)(2,1)S(1)}, u32[]{:S(2)}, u32[]{:S(2)}) collective-permute-start(bf16[8,32,128]{2,1,0:T(8,128)(2,1)S(1)} %fusion.7.scale_ref), channel_id=1, source_target_pairs={{0,1},{1,0},{2,3},{3,2},{4,5},{5,4},{6,7},{7,6},{8,9},{9,8},{10,11... | collective-permute-start | bytes 196616 | tf_op jit(solution)/shard_map/ppermute | solution.py:24
  48.8 1.3 %collective-permute-start.9 = (bf16[8,32,128]{2,1,0:T(8,128)(2,1)S(1)}, bf16[8,32,128]{2,1,0:T(8,128)(2,1)S(1)}, u32[]{:S(2)}, u32[]{:S(2)}) collective-permute-start(bf16[8,32,128]{2,1,0:T(8,128)(2,1)S(1)} %get-tuple-element.25), channel_id=1, source_target_pairs={{0,1},{1,0},{2,3},{3,2},{4,5},{5,4},{6,7},{7,6},{8,9},{9,8},{10,11... | collective-permute-start | bytes 196616 | tf_op jit(solution)/shard_map/ppermute | solution.py:24
  50.1 4.3 %collective-permute-start.10 = (bf16[8,32,128]{2,1,0:T(8,128)(2,1)S(1)}, bf16[8,32,128]{2,1,0:T(8,128)(2,1)S(1)}, u32[]{:S(2)}, u32[]{:S(2)}) collective-permute-start(bf16[8,32,128]{2,1,0:T(8,128)(2,1)S(1)} %fusion.9), channel_id=1, source_target_pairs={{0,2},{1,3},{2,0},{3,1},{4,6},{5,7},{6,4},{7,5},{8,10},{9,11},{10,... | collective-permute-start | bytes 196616 | tf_op jit(solution)/shard_map/ppermute | solution.py:24
  54.5 4.3 %collective-permute-start.11 = (bf16[8,32,128]{2,1,0:T(8,128)(2,1)S(1)}, bf16[8,32,128]{2,1,0:T(8,128)(2,1)S(1)}, u32[]{:S(2)}, u32[]{:S(2)}) collective-permute-start(bf16[8,32,128]{2,1,0:T(8,128)(2,1)S(1)} %get-tuple-element.35), channel_id=1, source_target_pairs={{0,4},{1,5},{2,6},{3,7},{4,0},{5,1},{6,2},{7,3},{8,12},{9,13},{10,... | collective-permute-start | bytes 196616 | tf_op jit(solution)/shard_map/ppermute | solution.py:24
  58.9 5.3 %collective-permute-start.12 = (bf16[8,32,128]{2,1,0:T(8,128)(2,1)S(1)}, bf16[8,32,128]{2,1,0:T(8,128)(2,1)S(1)}, u32[]{:S(2)}, u32[]{:S(2)}) collective-permute-start(bf16[8,32,128]{2,1,0:T(8,128)(2,1)S(1)} %fusion.12), channel_id=1, source_target_pairs={{0,8},{1,9},{2,10},{3,11},{4,12},{5,13},{6,14},{7,15},{8,0},{9,1},... | collective-permute-start | bytes 196616 | tf_op jit(solution)/shard_map/ppermute | solution.py:24
  64.3 1.6 %copy-start.2 = (bf16[1024,1024]{1,0:T(8,128)(2,1)S(1)}, bf16[1024,1024]{1,0:T(8,128)(2,1)}, u32[]{:S(2)}) copy-start(bf16[1024,1024]{1,0:T(8,128)(2,1)} %copy-done) | copy-start | bytes 6291460
  64.3 1.3 %collective-permute-start.13 = (bf16[8,32,128]{2,1,0:T(8,128)(2,1)S(1)}, bf16[8,32,128]{2,1,0:T(8,128)(2,1)S(1)}, u32[]{:S(2)}, u32[]{:S(2)}) collective-permute-start(bf16[8,32,128]{2,1,0:T(8,128)(2,1)S(1)} %fusion.5.scale_ref), channel_id=1, source_target_pairs={{0,1},{1,0},{2,3},{3,2},{4,5},{5,4},{6,7},{7,6},{8,9},{9,8},{10,11... | collective-permute-start | bytes 196616 | tf_op jit(solution)/shard_map/ppermute | solution.py:24
  67.4 1.3 %collective-permute-start.14 = (bf16[8,32,128]{2,1,0:T(8,128)(2,1)S(1)}, bf16[8,32,128]{2,1,0:T(8,128)(2,1)S(1)}, u32[]{:S(2)}, u32[]{:S(2)}) collective-permute-start(bf16[8,32,128]{2,1,0:T(8,128)(2,1)S(1)} %get-tuple-element.27), channel_id=1, source_target_pairs={{0,1},{1,0},{2,3},{3,2},{4,5},{5,4},{6,7},{7,6},{8,9},{9,8},{10,11... | collective-permute-start | bytes 196616 | tf_op jit(solution)/shard_map/ppermute | solution.py:24
  68.7 4.3 %collective-permute-start.15 = (bf16[8,32,128]{2,1,0:T(8,128)(2,1)S(1)}, bf16[8,32,128]{2,1,0:T(8,128)(2,1)S(1)}, u32[]{:S(2)}, u32[]{:S(2)}) collective-permute-start(bf16[8,32,128]{2,1,0:T(8,128)(2,1)S(1)} %fusion.10), channel_id=1, source_target_pairs={{0,2},{1,3},{2,0},{3,1},{4,6},{5,7},{6,4},{7,5},{8,10},{9,11},{10,... | collective-permute-start | bytes 196616 | tf_op jit(solution)/shard_map/ppermute | solution.py:24
  73.0 4.3 %collective-permute-start.16 = (bf16[8,32,128]{2,1,0:T(8,128)(2,1)S(1)}, bf16[8,32,128]{2,1,0:T(8,128)(2,1)S(1)}, u32[]{:S(2)}, u32[]{:S(2)}) collective-permute-start(bf16[8,32,128]{2,1,0:T(8,128)(2,1)S(1)} %get-tuple-element.33), channel_id=1, source_target_pairs={{0,4},{1,5},{2,6},{3,7},{4,0},{5,1},{6,2},{7,3},{8,12},{9,13},{10,... | collective-permute-start | bytes 196616 | tf_op jit(solution)/shard_map/ppermute | solution.py:24
  77.4 5.4 %collective-permute-start.17 = (bf16[8,32,128]{2,1,0:T(8,128)(2,1)S(1)}, bf16[8,32,128]{2,1,0:T(8,128)(2,1)S(1)}, u32[]{:S(2)}, u32[]{:S(2)}) collective-permute-start(bf16[8,32,128]{2,1,0:T(8,128)(2,1)S(1)} %fusion.13), channel_id=1, source_target_pairs={{0,8},{1,9},{2,10},{3,11},{4,12},{5,13},{6,14},{7,15},{8,0},{9,1},... | collective-permute-start | bytes 196616 | tf_op jit(solution)/shard_map/ppermute | solution.py:24
  82.8 1.6 %copy-start.3 = (bf16[1024,1024]{1,0:T(8,128)(2,1)S(1)}, bf16[1024,1024]{1,0:T(8,128)(2,1)}, u32[]{:S(2)}) copy-start(bf16[1024,1024]{1,0:T(8,128)(2,1)} %copy-done) | copy-start | bytes 6291460
  82.9 1.4 %collective-permute-start.18 = (bf16[8,32,128]{2,1,0:T(8,128)(2,1)S(1)}, bf16[8,32,128]{2,1,0:T(8,128)(2,1)S(1)}, u32[]{:S(2)}, u32[]{:S(2)}) collective-permute-start(bf16[8,32,128]{2,1,0:T(8,128)(2,1)S(1)} %get-tuple-element.31.scale_ref), channel_id=1, source_target_pairs={{0,1},{1,0},{2,3},{3,2},{4,5},{5,4},{6,7},{7,6},{8,9},{9,8},{10,11... | collective-permute-start | bytes 196616 | tf_op jit(solution)/shard_map/ppermute | solution.py:24
  (3 other events, 2.2 us)

commit v4 on v3

v4 whole, which is shorter than its diff:
```python
import functools
import math

import jax
import jax.numpy as jnp
from jax import lax
from jax.experimental import pallas as pl
from jax.experimental.pallas import tpu as pltpu
from jax.sharding import PartitionSpec as P

CLASSES = 32
ITERS = 3
INVERSE_TEMP = 20.0
ENTROPY_TEMP = 0.05
LANES = 128
EXTRA = 16
TILE = 256
F32 = jnp.float32
BF16 = jnp.bfloat16


def exchange(block, flip):
    devices = lax.axis_size("row")
    return lax.ppermute(block, "row", [(d, d ^ flip) for d in range(devices)])


def call(body, outs, *args, flops=0):
    space = pl.BlockSpec(memory_space=pltpu.VMEM)
    moved = sum(a.size * a.dtype.itemsize for a in args)
    return pl.pallas_call(
        body,
        out_shape=[pltpu.VMEM(shape, dtype) for shape, dtype in outs],
        in_specs=[space] * len(args),
        out_specs=[space] * len(outs),
        compiler_params=pltpu.CompilerParams(vmem_limit_bytes=12 * 1024 * 1024),
        cost_estimate=pl.CostEstimate(flops=flops, bytes_accessed=moved, transcendentals=0),
    )(*[pltpu.with_memory_space_constraint(a, pltpu.VMEM) for a in args])


def unit_rows(values):
    widened = values.astype(F32)
    meansq = jnp.mean(widened * widened, axis=1, keepdims=True)
    return (widened * lax.rsqrt(meansq + 1e-06) / math.sqrt(values.shape[1])).astype(BF16)


def hot(labels, classes=CLASSES):
    rows = lax.broadcasted_iota(jnp.int32, (classes, labels.shape[1]), 0)
    return (labels == rows).astype(F32)


def pack_body(embed_hbm, tgt_hbm, cand_hbm, out_ref, tgt_ref, cand_ref, sems):
    rows = embed_hbm.shape[0]
    copies = [
        pltpu.make_async_copy(cand_hbm, cand_ref, sems.at[0]),
        pltpu.make_async_copy(tgt_hbm, tgt_ref, sems.at[1]),
        pltpu.make_async_copy(embed_hbm, out_ref.at[pl.ds(0, rows)], sems.at[2]),
    ]
    for copy in copies:
        copy.start()
    copies[0].wait()
    counts = lax.dot_general(
        jnp.ones((EXTRA, cand_ref.shape[1]), BF16),
        hot(cand_ref[...], LANES).astype(BF16),
        (((1,), (1,)), ((), ())),
        preferred_element_type=F32,
    )
    high = counts.astype(BF16).astype(F32)
    even = lax.broadcasted_iota(jnp.int32, (EXTRA, LANES), 0) % 2 == 0
    out_ref[rows:, LANES:] = jnp.where(even, high, counts - high).astype(BF16)
    copies[1].wait()
    out_ref[rows:, :LANES] = jnp.broadcast_to(
        tgt_ref[...].astype(F32), (EXTRA, LANES)
    ).astype(BF16)
    copies[2].wait()


def pack(tgt_embed, tgt_labels, cand_labels):
    rows, width = tgt_embed.shape
    anywhere = pl.BlockSpec(memory_space=pl.ANY)
    return pl.pallas_call(
        pack_body,
        out_shape=pltpu.VMEM((rows + EXTRA, width), BF16),
        in_specs=[anywhere] * 3,
        out_specs=pl.BlockSpec(memory_space=pltpu.VMEM),
        scratch_shapes=[
            pltpu.VMEM(tgt_labels.shape, jnp.int32),
            pltpu.VMEM(cand_labels.shape, jnp.int32),
            pltpu.SemaphoreType.DMA((3,)),
        ],
        compiler_params=pltpu.CompilerParams(vmem_limit_bytes=12 * 1024 * 1024),
    )(*[
        pltpu.with_memory_space_constraint(a, pltpu.HBM)
        for a in (tgt_embed, tgt_labels, cand_labels)
    ])


def fill_body(unit_ref, held_ref, kernel_ref, sums_ref, *, tgt_rows):
    rows = tgt_rows + EXTRA
    cand_rows = unit_ref.shape[0]
    per = TILE // tgt_rows
    for col in range(0, kernel_ref.shape[1], TILE):
        first = col // tgt_rows
        block = jnp.concatenate(
            [held_ref[pl.ds((first + s) * rows, tgt_rows), :] for s in range(per)]
        )
        tgt_unit = unit_rows(block)
        for row in range(0, cand_rows, TILE):
            scores = lax.dot_general(
                unit_ref[row : row + TILE, :],
                tgt_unit,
                (((1,), (1,)), ((), ())),
                preferred_element_type=F32,
            )
            tile = jnp.exp(INVERSE_TEMP * scores)
            kernel_ref[row : row + TILE, col : col + TILE] = tile.astype(BF16)
            sums = tile[:, :LANES]
            for lane in range(LANES, TILE, LANES):
                sums += tile[:, lane : lane + LANES]
            if col:
                sums += sums_ref[row : row + TILE, :]
            sums_ref[row : row + TILE, :] = sums


def image_of(kernels, scale_ref):
    image = 0.0
    first = 0
    for kernel_ref in kernels:
        slots = kernel_ref.shape[1] // scale_ref.shape[2]
        scale_v = jnp.concatenate([scale_ref[s] for s in range(first, first + slots)], axis=1)
        image += lax.dot_general(
            kernel_ref[...], scale_v, (((1,), (1,)), ((), ())), preferred_element_type=F32
        )
        first += slots
    return image.T


def put_column(scale_ub, kernels, out_ref):
    width = out_ref.shape[2]
    first = 0
    for kernel_ref in kernels:
        part = jnp.dot(scale_ub, kernel_ref[...], preferred_element_type=F32)
        slots = kernel_ref.shape[1] // width
        for s in range(slots):
            out_ref[first + s] = part[:, s * width : (s + 1) * width].astype(out_ref.dtype)
        first += slots


def extras(refs, tgt_rows):
    rows = tgt_rows + EXTRA
    for ref in refs:
        for s in range(ref.shape[0] // rows):
            yield ref[pl.ds(s * rows + tgt_rows, EXTRA), :].astype(F32)


def target_body(near0, near1, far0, far1, marg_ref):
    slots, _, tgt_rows = marg_ref.shape
    total = jnp.zeros((CLASSES, tgt_rows), F32)
    for s, extra in enumerate(extras((near0, near1, far0, far1), tgt_rows)):
        weight = 1.0 + 3.0 * hot(extra[:1, :LANES].astype(jnp.int32))
        total += weight
        if s < slots:
            marg_ref[s] = weight
    total = jnp.sum(total, axis=1, keepdims=True)
    for s in range(slots):
        marg_ref[s] = marg_ref[s] / total


def first_body(
    far0_ref, far1_ref, sums0, sums1, sums2, sums3, near0, near1, held0, held1, weight_ref,
    marg_ref, scale_ref, column_ref,
):
    tgt_rows = column_ref.shape[2]
    counts = jnp.zeros((EXTRA, LANES), F32)
    for extra in extras((near0, near1, held0, held1), tgt_rows):
        counts += extra[:, LANES:]
    count = jnp.broadcast_to(counts[:1] + counts[1:2], (LANES, LANES)).T[:CLASSES, :1]
    candidates = weight_ref.shape[1] * 2 * column_ref.shape[0]
    marg = weight_ref[...] / (candidates + 3.0 * count)
    marg_ref[...] = marg
    sums = sums0[...] + sums1[...] + sums2[...] + sums3[...]
    image = jnp.sum(sums.T, axis=0, keepdims=True)
    scale_ub = (marg / image).astype(BF16)
    scale_ref[...] = scale_ub
    put_column(scale_ub, (far0_ref, far1_ref), column_ref)


def column_body(scale_ref, kernel0, kernel1, column_ref):
    put_column(scale_ref[...], (kernel0, kernel1), column_ref)


def image_body(kernel0, kernel1, scale_ref, image_ref):
    image_ref[...] = image_of((kernel0, kernel1), scale_ref)


def step_body(
    kernel0, kernel1, scale_ref, image_ref, marg_ref, out_ref, rounded_ref, column_ref
):
    image = image_ref[...] + image_of((kernel0, kernel1), scale_ref)
    scale_u = marg_ref[...] / image
    out_ref[...] = scale_u
    rounded_ref[...] = scale_u.astype(BF16)
    put_column(scale_u.astype(BF16), (kernel0, kernel1), column_ref)


def last_body(kernel0, kernel1, scale_ref, image_ref, u_ref, mass_ref, *, candidates):
    image = image_ref[...] + image_of((kernel0, kernel1), scale_ref)
    mass_ref[...] = candidates * u_ref[...] * image


def other_order(blocks, flip):
    slots = blocks.shape[0]
    bits = slots.bit_length() - 1
    cube = blocks.reshape((2,) * bits + blocks.shape[1:])
    turned = [bit - 1 for bit in range(1, bits + 1) if flip >> bit & 1]
    return jnp.flip(cube, turned).reshape(blocks.shape)


def shards(cand_embed, cand_labels, tgt_embed, tgt_labels):
    devices = lax.axis_size("row")
    top = devices.bit_length() - 1
    slots = devices // 2
    cand_rows, width = cand_embed.shape
    tgt_rows = tgt_embed.shape[0]
    quarter = slots // 2 * tgt_rows
    cand_labels = cand_labels.reshape(1, cand_rows)
    block = (slots, CLASSES, tgt_rows)
    image_type = ((CLASSES, cand_rows), F32)
    rounded_type = ((CLASSES, cand_rows), BF16)
    pass_flops = 2 * cand_rows * quarter * 128

    def fill(held):
        return call(
            functools.partial(fill_body, tgt_rows=tgt_rows),
            [((cand_rows, quarter), BF16), ((cand_rows, LANES), F32)],
            cand_unit, held, flops=4 * pass_flops,
        )

    near = [pack(tgt_embed, tgt_labels.reshape(1, tgt_rows), cand_labels)]
    cand_unit = unit_rows(cand_embed)
    weight = 1.0 + 3.0 * hot(cand_labels)
    for bit in range(top - 1, 1, -1):
        near[0] = jnp.concatenate([near[0], exchange(near[0], 1 << bit)])
        near[0], cand_unit, weight = lax.optimization_barrier((near[0], cand_unit, weight))
    near.append(exchange(near[0], 2))
    far = [exchange(near[0], 1)]
    filled = [fill(near[0]), fill(far[0])]
    near[1], filled = lax.optimization_barrier((near[1], filled))
    far.append(exchange(near[1], 1))
    filled += [fill(near[1]), fill(far[1])]
    kernels, sums = zip(*filled)
    near_kernels, far_kernels = kernels[::2], kernels[1::2]

    cand_marg, scale_ub, far_column = call(
        first_body,
        [image_type, rounded_type, (block, BF16)],
        *far_kernels, *sums, *near, *far, weight, flops=2 * pass_flops,
    )
    (tgt_marg,) = call(target_body, [(block, F32)], *near, *far, flops=pass_flops)
    scale_u = None
    for step in range(ITERS):
        if step:
            scale_u, scale_ub, far_column = call(
                step_body,
                [image_type, rounded_type, (block, BF16)],
                *far_kernels, far_vb, image, cand_marg, flops=4 * pass_flops,
            )
        got = exchange(far_column, 1)
        (column,) = call(
            column_body, [(block, F32)], scale_ub, *near_kernels, flops=2 * pass_flops
        )
        column = column + got.astype(F32)
        for low in range(1, top, 2):
            bits = [1 << bit for bit in range(low, min(low + 2, top))]
            flips = bits + [sum(bits)] if len(bits) > 1 else bits
            sent = column.astype(BF16)
            found = [(flip, exchange(sent, flip)) for flip in flips]
            for flip, got in found:
                column = column + other_order(got, flip).astype(F32)
        scale_v = tgt_marg / column
        scale_vb = scale_v.astype(BF16)
        far_vb = exchange(scale_vb, 1)
        (image,) = call(image_body, [image_type], *near_kernels, scale_vb, flops=2 * pass_flops)
    space = pl.BlockSpec(memory_space=pltpu.VMEM)
    last = [*far_kernels, far_vb, image, scale_u]
    mass = pl.pallas_call(
        functools.partial(last_body, candidates=float(cand_rows * devices)),
        out_shape=jax.ShapeDtypeStruct(*image_type),
        in_specs=[space] * len(last),
        out_specs=space,
        compiler_params=pltpu.CompilerParams(vmem_limit_bytes=12 * 1024 * 1024),
    )(*[pltpu.with_memory_space_constraint(a, pltpu.VMEM) for a in last])
    return (ENTROPY_TEMP * jnp.log(scale_u), scale_v[0], mass)


def solution(mesh):
    return jax.shard_map(
        shards,
        mesh=mesh,
        in_specs=(
            P(("grp", "row"), None),
            P(("grp", "row")),
            P(("grp", "row"), None),
            P(("grp", "row")),
        ),
        out_specs=(P(None, ("grp", "row")), P(None, ("grp", "row")), P(None, ("grp", "row"))),
        check_vma=False,
    )
```

time: 86.8 us -> 101 us (1.16); the launches traced: 86.5 us -> 99.5 us
  local copies, waits for them, and re-layouts: 6.27 us -> 22.4 us
  waiting for transfers between devices: 38.4 us -> 26.3 us
  other arithmetic: 0.8 us -> 10.2 us
  starting transfers between devices: 28.6 us -> 27.5 us
    rev x9 -> x12, local copies, waits for them, and re-layouts: 0.09 us -> 13.4 us  [other_order(): return jnp.flip(cube, turned).reshape(blocks.shape)]
    ppermute x19 -> x23, waiting for transfers between devices: 38.4 us -> 26.3 us  [exchange(): return lax.ppermute(block, 'row', [(d, d ^ flip) for d in range(devices)])]
    convert_element_type x9 -> x6, other arithmetic: 0.19 us -> 4.94 us  [shards(): sent = column.astype(BF16)]
    convert_element_type x3, other arithmetic: 0.12 us -> 3.1 us  [shards(): scale_vb = scale_v.astype(BF16)]
    unnamed x18 -> x62, local copies, waits for them, and re-layouts: 5.57 us -> 8.42 us
    pallas_call x0 -> x2, Pallas kernels: none -> 2.36 us  [the longest x1 1.38 us: shards(): pl.pallas_call(functools.partial(last_body, candidates=float(cand_rows *...]
    pallas_call x12 -> x14, Pallas kernels: 11.6 us -> 9.8 us  [call(): pl.pallas_call(body, out_shape=[pltpu.VMEM(shape, dtype) for shape, dtype...]
    ppermute x19 -> x23, starting transfers between devices: 28.6 us -> 27.5 us  [exchange(): return lax.ppermute(block, 'row', [(d, d ^ flip) for d in range(devices)])]
  transfers between devices with their start and end apart: 19 -> 23, of which waited for: 17 -> 17; matrix products, arithmetic and copies ran while one was open for 1% -> 9% of each run, Pallas kernels for 6% -> 5%
where the time goes in v4:
time: 101 us; the launch traced here: 99.5 us
  starting transfers between devices  27.5 us (27%)
  waiting for transfers between devices  26.3 us (26%)
  local copies, waits for them, and re-layouts  22.4 us (22%)
  Pallas kernels  12.2 us (12%)
  other arithmetic  10.2 us (10%)
    ppermute x23, starting transfers between devices, exchange(): return lax.ppermute(block, 'row', [(d, d ^ flip) for d in range(devices)])  27.5 us
    ppermute x23, waiting for transfers between devices, exchange(): return lax.ppermute(block, 'row', [(d, d ^ flip) for d in range(devices)])  26.3 us
    rev x12, local copies, waits for them, and re-layouts, other_order(): return jnp.flip(cube, turned).reshape(blocks.shape)  13.4 us
    pallas_call x14, Pallas kernels, call(): pl.pallas_call(body, out_shape=[pltpu.VMEM(shape, dtype) for shape, dtype...  9.8 us
    unnamed x62, local copies, waits for them, and re-layouts  8.42 us
    convert_element_type x6, other arithmetic, shards(): sent = column.astype(BF16)  4.94 us
    convert_element_type x3, other arithmetic, shards(): scale_vb = scale_v.astype(BF16)  3.1 us
  transfers between devices with their start and end apart: 23, of which 17 were waited for; matrix products, arithmetic and copies ran while one was open for 9% of the time, Pallas kernels for 5%

profile of v4, /device:TPU:0, one launch (start us, length us, event | category | flops | bytes accessed | tf_op | source)
XLA Modules:
  0.0 99.5 jit_solution(1473940380997336383)
XLA Ops:
  1.6 4.1 %collective-permute-start = (bf16[144,256]{1,0:T(8,128)(2,1)S(1)}, bf16[144,256]{1,0:T(8,128)(2,1)S(1)}, u32[]{:S(2)}, u32[]{:S(2)}) collective-permute-start(bf16[144,256]{1,0:T(8,128)(2,1)S(1)} %shard_map.67), channel_id=1, source_target_pairs={{0,8},{1,9},{2,10},{3,11},{4,12},{5,13},{6,14},{7,15},{8,0},{9,1},... | collective-permute-start | bytes 221192 | tf_op jit(solution)/shard_map/ppermute | solution.py:24
  5.7 1.3 %fusion = f32[1024]{0:T(1024)S(1)} fusion(bf16[1024,256]{1,0:T(8,128)(2,1)} %param.4), kind=kLoop, calls=%fused_computation.2 | loop fusion | flops 785408 | bytes 528384 | tf_op jit(solution)/shard_map/reduce_sum | solution.py:42
  7.7 1.9 %collective-permute-done = bf16[144,256]{1,0:T(8,128)(2,1)S(1)} collective-permute-done((bf16[144,256]{1,0:T(8,128)(2,1)S(1)}, bf16[144,256]{1,0:T(8,128)(2,1)S(1)}, u32[]{:S(2)}, u32[]{:S(2)}) %collective-permute-start) | collective-permute-done | bytes 73760 | tf_op jit(solution)/shard_map/ppermute | solution.py:24
  10.4 4.5 %collective-permute-done.1 = bf16[288,256]{1,0:T(8,128)(2,1)S(1)} collective-permute-done((bf16[288,256]{1,0:T(8,128)(2,1)S(1)}, bf16[288,256]{1,0:T(8,128)(2,1)S(1)}, u32[]{:S(2)}, u32[]{:S(2)}) %collective-permute-start.1) | collective-permute-done | bytes 147488 | tf_op jit(solution)/shard_map/ppermute | solution.py:24
  15.0 1.8 %collective-permute-start.2 = (bf16[576,256]{1,0:T(8,128)(2,1)S(1)}, bf16[576,256]{1,0:T(8,128)(2,1)S(1)}, u32[]{:S(2)}, u32[]{:S(2)}) collective-permute-start(bf16[576,256]{1,0:T(8,128)(2,1)S(1)} %pad_maximum_fusion.held_ref.near0), channel_id=1, source_target_pairs={{0,2},{1,3},{2,0},{3,1},{4,6},{5,7},{6,4},{7,5},{8,10},{9,11},{10,... | collective-permute-start | bytes 884744 | tf_op jit(solution)/shard_map/ppermute | solution.py:24
  18.0 6.4 %collective-permute-done.2.near1.held_ref = bf16[576,256]{1,0:T(8,128)(2,1)S(1)} collective-permute-done((bf16[576,256]{1,0:T(8,128)(2,1)S(1)}, bf16[576,256]{1,0:T(8,128)(2,1)S(1)}, u32[]{:S(2)}, u32[]{:S(2)}) %collective-permute-start.2) | collective-permute-done | bytes 294944 | tf_op jit(solution)/shard_map/ppermute | solution.py:24
  29.5 1.7 %collective-permute-start.6 = (bf16[8,32,128]{2,1,0:T(8,128)(2,1)}, bf16[8,32,128]{2,1,0:T(8,128)(2,1)S(1)}, u32[]{:S(2)}, u32[]{:S(2)}) collective-permute-start(bf16[8,32,128]{2,1,0:T(8,128)(2,1)} %fusion.8), channel_id=1, source_target_pairs={{0,2},{1,3},{2,0},{3,1},{4,6},{5,7},{6,4},{7,5},{8,10},{9,11},{10,... | collective-permute-start | bytes 196616 | tf_op jit(solution)/shard_map/ppermute | solution.py:24
  36.1 1.5 %rev.41 = bf16[2,2,2,32,128]{4,3,2,1,0:T(8,128)(2,1)} reverse(bf16[2,2,2,32,128]{4,3,2,1,0:T(8,128)(2,1)} %bitcast.4), dimensions={1} | reverse | bytes 131072 | tf_op jit(solution)/shard_map/jit(_flip)/rev | solution.py:215
  37.6 1.5 %rev.42 = bf16[2,2,2,32,128]{4,3,2,1,0:T(8,128)(2,1)} reverse(bf16[2,2,2,32,128]{4,3,2,1,0:T(8,128)(2,1)} %bitcast.6), dimensions={0,1} | reverse | bytes 131072 | tf_op jit(solution)/shard_map/jit(_flip)/rev | solution.py:215
  40.1 3.4 %collective-permute-start.9 = (bf16[8,32,128]{2,1,0:T(8,128)(2,1)S(1)}, bf16[8,32,128]{2,1,0:T(8,128)(2,1)S(1)}, u32[]{:S(2)}, u32[]{:S(2)}) collective-permute-start(bf16[8,32,128]{2,1,0:T(8,128)(2,1)S(1)} %fusion.11), channel_id=1, source_target_pairs={{0,8},{1,9},{2,10},{3,11},{4,12},{5,13},{6,14},{7,15},{8,0},{9,1},... | collective-permute-start | bytes 196616 | tf_op jit(solution)/shard_map/ppermute | solution.py:24
  50.3 1.6 %shard_map.76 = (f32[32,1024]{1,0:T(8,128)}, bf16[32,1024]{1,0:T(8,128)(2,1)S(1)}, bf16[8,32,128]{2,1,0:T(8,128)(2,1)S(1)}) custom-call(bf16[1024,512]{1,0:T(8,128)(2,1)S(1)} %get-tuple-element.39.far0_ref.kernel0, bf16[1024,512]{1,0:T(8,128)(2,1)S(1)} %copy-done.1, bf16[8,32,128]{2,1,0:T(8,128)(2,1)S(1)} %collective-permute-done.10.scale_ref, ...), custom_call_target="tpu_custom_call" | custom-call | flops 536870912 | bytes 2424832 | tf_op jit(solution)/shard_map/pallas_call | solution.py:30
  54.2 1.4 %collective-permute-start.13 = (bf16[8,32,128]{2,1,0:T(8,128)(2,1)}, bf16[8,32,128]{2,1,0:T(8,128)(2,1)S(1)}, u32[]{:S(2)}, u32[]{:S(2)}) collective-permute-start(bf16[8,32,128]{2,1,0:T(8,128)(2,1)} %fusion.9), channel_id=1, source_target_pairs={{0,4},{1,5},{2,6},{3,7},{4,0},{5,1},{6,2},{7,3},{8,12},{9,13},{10,... | collective-permute-start | bytes 196616 | tf_op jit(solution)/shard_map/ppermute | solution.py:24
  55.6 1.8 %collective-permute-start.14 = (bf16[8,32,128]{2,1,0:T(8,128)(2,1)}, bf16[8,32,128]{2,1,0:T(8,128)(2,1)}, u32[]{:S(2)}, u32[]{:S(2)}) collective-permute-start(bf16[8,32,128]{2,1,0:T(8,128)(2,1)} %fusion.9), channel_id=1, source_target_pairs={{0,6},{1,7},{2,4},{3,5},{4,2},{5,3},{6,0},{7,1},{8,14},{9,15},{10,... | collective-permute-start | bytes 196616 | tf_op jit(solution)/shard_map/ppermute | solution.py:24
  61.3 1.5 %rev.46 = bf16[2,2,2,32,128]{4,3,2,1,0:T(8,128)(2,1)} reverse(bf16[2,2,2,32,128]{4,3,2,1,0:T(8,128)(2,1)} %bitcast.14), dimensions={0,1} | reverse | bytes 131072 | tf_op jit(solution)/shard_map/jit(_flip)/rev | solution.py:215
  63.8 2.9 %collective-permute-start.15 = (bf16[8,32,128]{2,1,0:T(8,128)(2,1)S(1)}, bf16[8,32,128]{2,1,0:T(8,128)(2,1)S(1)}, u32[]{:S(2)}, u32[]{:S(2)}) collective-permute-start(bf16[8,32,128]{2,1,0:T(8,128)(2,1)S(1)} %fusion.12), channel_id=1, source_target_pairs={{0,8},{1,9},{2,10},{3,11},{4,12},{5,13},{6,14},{7,15},{8,0},{9,1},... | collective-permute-start | bytes 196616 | tf_op jit(solution)/shard_map/ppermute | solution.py:24
  66.7 3.0 %collective-permute-done.15 = bf16[8,32,128]{2,1,0:T(8,128)(2,1)S(1)} collective-permute-done((bf16[8,32,128]{2,1,0:T(8,128)(2,1)S(1)}, bf16[8,32,128]{2,1,0:T(8,128)(2,1)S(1)}, u32[]{:S(2)}, u32[]{:S(2)}) %collective-permute-start.15) | collective-permute-done | bytes 65568 | tf_op jit(solution)/shard_map/ppermute | solution.py:24
  70.3 1.5 %rev.47 = bf16[2,2,2,32,128]{4,3,2,1,0:T(8,128)(2,1)} reverse(bf16[2,2,2,32,128]{4,3,2,1,0:T(8,128)(2,1)} %bitcast.99), dimensions={2} | reverse | bytes 131072 | tf_op jit(solution)/shard_map/jit(_flip)/rev | solution.py:215
  74.1 1.5 %shard_map.79 = (f32[32,1024]{1,0:T(8,128)S(1)}, bf16[32,1024]{1,0:T(8,128)(2,1)S(1)}, bf16[8,32,128]{2,1,0:T(8,128)(2,1)S(1)}) custom-call(bf16[1024,512]{1,0:T(8,128)(2,1)S(1)} %get-tuple-element.39.far0_ref.kernel0, bf16[1024,512]{1,0:T(8,128)(2,1)S(1)} %copy-done.2, bf16[8,32,128]{2,1,0:T(8,128)(2,1)S(1)} %collective-permute-done.16.scale_ref, ...), custom_call_target="tpu_custom_call" | custom-call | flops 536870912 | bytes 2424832 | tf_op jit(solution)/shard_map/pallas_call | solution.py:30
  79.7 2.0 %collective-permute-start.20 = (bf16[8,32,128]{2,1,0:T(8,128)(2,1)}, bf16[8,32,128]{2,1,0:T(8,128)(2,1)S(1)}, u32[]{:S(2)}, u32[]{:S(2)}) collective-permute-start(bf16[8,32,128]{2,1,0:T(8,128)(2,1)} %fusion.10), channel_id=1, source_target_pairs={{0,6},{1,7},{2,4},{3,5},{4,2},{5,3},{6,0},{7,1},{8,14},{9,15},{10,... | collective-permute-start | bytes 196616 | tf_op jit(solution)/shard_map/ppermute | solution.py:24
  82.8 1.5 %rev.48 = bf16[2,2,2,32,128]{4,3,2,1,0:T(8,128)(2,1)} reverse(bf16[2,2,2,32,128]{4,3,2,1,0:T(8,128)(2,1)} %bitcast.18), dimensions={0} | reverse | bytes 131072 | tf_op jit(solution)/shard_map/jit(_flip)/rev | solution.py:215
  86.8 3.3 %collective-permute-start.21 = (bf16[8,32,128]{2,1,0:T(8,128)(2,1)S(1)}, bf16[8,32,128]{2,1,0:T(8,128)(2,1)S(1)}, u32[]{:S(2)}, u32[]{:S(2)}) collective-permute-start(bf16[8,32,128]{2,1,0:T(8,128)(2,1)S(1)} %fusion.13), channel_id=1, source_target_pairs={{0,8},{1,9},{2,10},{3,11},{4,12},{5,13},{6,14},{7,15},{8,0},{9,1},... | collective-permute-start | bytes 196616 | tf_op jit(solution)/shard_map/ppermute | solution.py:24
  90.8 2.3 %collective-permute-done.21 = bf16[8,32,128]{2,1,0:T(8,128)(2,1)S(1)} collective-permute-done((bf16[8,32,128]{2,1,0:T(8,128)(2,1)S(1)}, bf16[8,32,128]{2,1,0:T(8,128)(2,1)S(1)}, u32[]{:S(2)}, u32[]{:S(2)}) %collective-permute-start.21) | collective-permute-done | bytes 65568 | tf_op jit(solution)/shard_map/ppermute | solution.py:24
  93.7 1.5 %rev.51 = bf16[2,2,2,32,128]{4,3,2,1,0:T(8,128)(2,1)} reverse(bf16[2,2,2,32,128]{4,3,2,1,0:T(8,128)(2,1)} %bitcast.98), dimensions={2} | reverse | bytes 131072 | tf_op jit(solution)/shard_map/jit(_flip)/rev | solution.py:215
  98.1 1.4 %shard_map.82 = f32[32,1024]{1,0:T(8,128)} custom-call(bf16[1024,512]{1,0:T(8,128)(2,1)S(1)} %get-tuple-element.39.far0_ref.kernel0, bf16[1024,512]{1,0:T(8,128)(2,1)S(1)} %copy-done.3, bf16[8,32,128]{2,1,0:T(8,128)(2,1)S(1)} %collective-permute-done.22.scale_ref, f32[32,1024]{1,0:T(8,128)S(1)} %shard_map.81.image_ref, f32[32,1024]{1,0:T(8,128)S(1)} %copy-done.17), custom_call_target="tpu_custom_call" | custom-call | tf_op jit(solution)/shard_map/pallas_call | solution.py:285
  (129 shorter events, 43.4 us)
Async XLA Ops:
  1.6 8.0 %collective-permute-start = (bf16[144,256]{1,0:T(8,128)(2,1)S(1)}, bf16[144,256]{1,0:T(8,128)(2,1)S(1)}, u32[]{:S(2)}, u32[]{:S(2)}) collective-permute-start(bf16[144,256]{1,0:T(8,128)(2,1)S(1)} %shard_map.67), channel_id=1, source_target_pairs={{0,8},{1,9},{2,10},{3,11},{4,12},{5,13},{6,14},{7,15},{8,0},{9,1},... | collective-permute-start | bytes 221192 | tf_op jit(solution)/shard_map/ppermute | solution.py:24
  9.7 5.2 %collective-permute-start.1 = (bf16[288,256]{1,0:T(8,128)(2,1)S(1)}, bf16[288,256]{1,0:T(8,128)(2,1)S(1)}, u32[]{:S(2)}, u32[]{:S(2)}) collective-permute-start(bf16[288,256]{1,0:T(8,128)(2,1)S(1)} %pad_maximum_fusion.1), channel_id=1, source_target_pairs={{0,4},{1,5},{2,6},{3,7},{4,0},{5,1},{6,2},{7,3},{8,12},{9,13},{10,... | collective-permute-start | bytes 442376 | tf_op jit(solution)/shard_map/ppermute | solution.py:24
  14.9 2.5 %collective-permute-start.3 = (bf16[576,256]{1,0:T(8,128)(2,1)S(1)}, bf16[576,256]{1,0:T(8,128)(2,1)S(1)}, u32[]{:S(2)}, u32[]{:S(2)}) collective-permute-start(bf16[576,256]{1,0:T(8,128)(2,1)S(1)} %pad_maximum_fusion.held_ref.near0), channel_id=1, source_target_pairs={{0,1},{1,0},{2,3},{3,2},{4,5},{5,4},{6,7},{7,6},{8,9},{9,8},{10,11... | collective-permute-start | bytes 884744 | tf_op jit(solution)/shard_map/ppermute | solution.py:24
  15.0 9.4 %collective-permute-start.2 = (bf16[576,256]{1,0:T(8,128)(2,1)S(1)}, bf16[576,256]{1,0:T(8,128)(2,1)S(1)}, u32[]{:S(2)}, u32[]{:S(2)}) collective-permute-start(bf16[576,256]{1,0:T(8,128)(2,1)S(1)} %pad_maximum_fusion.held_ref.near0), channel_id=1, source_target_pairs={{0,2},{1,3},{2,0},{3,1},{4,6},{5,7},{6,4},{7,5},{8,10},{9,11},{10,... | collective-permute-start | bytes 884744 | tf_op jit(solution)/shard_map/ppermute | solution.py:24
  17.4 9.2 %copy-start.8 = (bf16[576,256]{1,0:T(8,128)(2,1)}, bf16[576,256]{1,0:T(8,128)(2,1)S(1)}, u32[]{:S(2)}) copy-start(bf16[576,256]{1,0:T(8,128)(2,1)S(1)} %collective-permute-done.3.held_ref.far0.held0) | copy-start | bytes 884740
  24.4 1.6 %collective-permute-start.4 = (bf16[576,256]{1,0:T(8,128)(2,1)S(1)}, bf16[576,256]{1,0:T(8,128)(2,1)S(1)}, u32[]{:S(2)}, u32[]{:S(2)}) collective-permute-start(bf16[576,256]{1,0:T(8,128)(2,1)S(1)} %collective-permute-done.2.near1.held_ref), channel_id=1, source_target_pairs={{0,1},{1,0},{2,3},{3,2},{4,5},{5,4},{6,7},{7,6},{8,9},{9,8},{10,11... | collective-permute-start | bytes 884744 | tf_op jit(solution)/shard_map/ppermute | solution.py:24
  27.6 1.3 %collective-permute-start.5 = (bf16[8,32,128]{2,1,0:T(8,128)(2,1)S(1)}, bf16[8,32,128]{2,1,0:T(8,128)(2,1)S(1)}, u32[]{:S(2)}, u32[]{:S(2)}) collective-permute-start(bf16[8,32,128]{2,1,0:T(8,128)(2,1)S(1)} %get-tuple-element.50), channel_id=1, source_target_pairs={{0,1},{1,0},{2,3},{3,2},{4,5},{5,4},{6,7},{7,6},{8,9},{9,8},{10,11... | collective-permute-start | bytes 196616 | tf_op jit(solution)/shard_map/ppermute | solution.py:24
  29.5 4.5 %collective-permute-start.6 = (bf16[8,32,128]{2,1,0:T(8,128)(2,1)}, bf16[8,32,128]{2,1,0:T(8,128)(2,1)S(1)}, u32[]{:S(2)}, u32[]{:S(2)}) collective-permute-start(bf16[8,32,128]{2,1,0:T(8,128)(2,1)} %fusion.8), channel_id=1, source_target_pairs={{0,2},{1,3},{2,0},{3,1},{4,6},{5,7},{6,4},{7,5},{8,10},{9,11},{10,... | collective-permute-start | bytes 196616 | tf_op jit(solution)/shard_map/ppermute | solution.py:24
  31.3 4.9 %collective-permute-start.7 = (bf16[8,32,128]{2,1,0:T(8,128)(2,1)}, bf16[8,32,128]{2,1,0:T(8,128)(2,1)}, u32[]{:S(2)}, u32[]{:S(2)}) collective-permute-start(bf16[8,32,128]{2,1,0:T(8,128)(2,1)} %fusion.8), channel_id=1, source_target_pairs={{0,4},{1,5},{2,6},{3,7},{4,0},{5,1},{6,2},{7,3},{8,12},{9,13},{10,... | collective-permute-start | bytes 196616 | tf_op jit(solution)/shard_map/ppermute | solution.py:24
  32.1 5.5 %collective-permute-start.8 = (bf16[8,32,128]{2,1,0:T(8,128)(2,1)}, bf16[8,32,128]{2,1,0:T(8,128)(2,1)}, u32[]{:S(2)}, u32[]{:S(2)}) collective-permute-start(bf16[8,32,128]{2,1,0:T(8,128)(2,1)} %fusion.8), channel_id=1, source_target_pairs={{0,6},{1,7},{2,4},{3,5},{4,2},{5,3},{6,0},{7,1},{8,14},{9,15},{10,... | collective-permute-start | bytes 196616 | tf_op jit(solution)/shard_map/ppermute | solution.py:24
  40.1 6.3 %collective-permute-start.9 = (bf16[8,32,128]{2,1,0:T(8,128)(2,1)S(1)}, bf16[8,32,128]{2,1,0:T(8,128)(2,1)S(1)}, u32[]{:S(2)}, u32[]{:S(2)}) collective-permute-start(bf16[8,32,128]{2,1,0:T(8,128)(2,1)S(1)} %fusion.11), channel_id=1, source_target_pairs={{0,8},{1,9},{2,10},{3,11},{4,12},{5,13},{6,14},{7,15},{8,0},{9,1},... | collective-permute-start | bytes 196616 | tf_op jit(solution)/shard_map/ppermute | solution.py:24
  49.0 1.3 %collective-permute-start.10 = (bf16[8,32,128]{2,1,0:T(8,128)(2,1)S(1)}, bf16[8,32,128]{2,1,0:T(8,128)(2,1)S(1)}, u32[]{:S(2)}, u32[]{:S(2)}) collective-permute-start(bf16[8,32,128]{2,1,0:T(8,128)(2,1)S(1)} %fusion.7.scale_ref), channel_id=1, source_target_pairs={{0,1},{1,0},{2,3},{3,2},{4,5},{5,4},{6,7},{7,6},{8,9},{9,8},{10,11... | collective-permute-start | bytes 196616 | tf_op jit(solution)/shard_map/ppermute | solution.py:24
  52.0 1.3 %collective-permute-start.11 = (bf16[8,32,128]{2,1,0:T(8,128)(2,1)S(1)}, bf16[8,32,128]{2,1,0:T(8,128)(2,1)S(1)}, u32[]{:S(2)}, u32[]{:S(2)}) collective-permute-start(bf16[8,32,128]{2,1,0:T(8,128)(2,1)S(1)} %get-tuple-element.53), channel_id=1, source_target_pairs={{0,1},{1,0},{2,3},{3,2},{4,5},{5,4},{6,7},{7,6},{8,9},{9,8},{10,11... | collective-permute-start | bytes 196616 | tf_op jit(solution)/shard_map/ppermute | solution.py:24
  53.9 4.5 %collective-permute-start.12 = (bf16[8,32,128]{2,1,0:T(8,128)(2,1)}, bf16[8,32,128]{2,1,0:T(8,128)(2,1)S(1)}, u32[]{:S(2)}, u32[]{:S(2)}) collective-permute-start(bf16[8,32,128]{2,1,0:T(8,128)(2,1)} %fusion.9), channel_id=1, source_target_pairs={{0,2},{1,3},{2,0},{3,1},{4,6},{5,7},{6,4},{7,5},{8,10},{9,11},{10,... | collective-permute-start | bytes 196616 | tf_op jit(solution)/shard_map/ppermute | solution.py:24
  54.2 5.7 %collective-permute-start.13 = (bf16[8,32,128]{2,1,0:T(8,128)(2,1)}, bf16[8,32,128]{2,1,0:T(8,128)(2,1)S(1)}, u32[]{:S(2)}, u32[]{:S(2)}) collective-permute-start(bf16[8,32,128]{2,1,0:T(8,128)(2,1)} %fusion.9), channel_id=1, source_target_pairs={{0,4},{1,5},{2,6},{3,7},{4,0},{5,1},{6,2},{7,3},{8,12},{9,13},{10,... | collective-permute-start | bytes 196616 | tf_op jit(solution)/shard_map/ppermute | solution.py:24
  55.6 5.7 %collective-permute-start.14 = (bf16[8,32,128]{2,1,0:T(8,128)(2,1)}, bf16[8,32,128]{2,1,0:T(8,128)(2,1)}, u32[]{:S(2)}, u32[]{:S(2)}) collective-permute-start(bf16[8,32,128]{2,1,0:T(8,128)(2,1)} %fusion.9), channel_id=1, source_target_pairs={{0,6},{1,7},{2,4},{3,5},{4,2},{5,3},{6,0},{7,1},{8,14},{9,15},{10,... | collective-permute-start | bytes 196616 | tf_op jit(solution)/shard_map/ppermute | solution.py:24
  63.8 5.9 %collective-permute-start.15 = (bf16[8,32,128]{2,1,0:T(8,128)(2,1)S(1)}, bf16[8,32,128]{2,1,0:T(8,128)(2,1)S(1)}, u32[]{:S(2)}, u32[]{:S(2)}) collective-permute-start(bf16[8,32,128]{2,1,0:T(8,128)(2,1)S(1)} %fusion.12), channel_id=1, source_target_pairs={{0,8},{1,9},{2,10},{3,11},{4,12},{5,13},{6,14},{7,15},{8,0},{9,1},... | collective-permute-start | bytes 196616 | tf_op jit(solution)/shard_map/ppermute | solution.py:24
  72.8 1.3 %collective-permute-start.16 = (bf16[8,32,128]{2,1,0:T(8,128)(2,1)S(1)}, bf16[8,32,128]{2,1,0:T(8,128)(2,1)S(1)}, u32[]{:S(2)}, u32[]{:S(2)}) collective-permute-start(bf16[8,32,128]{2,1,0:T(8,128)(2,1)S(1)} %fusion.5.scale_ref), channel_id=1, source_target_pairs={{0,1},{1,0},{2,3},{3,2},{4,5},{5,4},{6,7},{7,6},{8,9},{9,8},{10,11... | collective-permute-start | bytes 196616 | tf_op jit(solution)/shard_map/ppermute | solution.py:24
  76.3 1.3 %collective-permute-start.17 = (bf16[8,32,128]{2,1,0:T(8,128)(2,1)S(1)}, bf16[8,32,128]{2,1,0:T(8,128)(2,1)S(1)}, u32[]{:S(2)}, u32[]{:S(2)}) collective-permute-start(bf16[8,32,128]{2,1,0:T(8,128)(2,1)S(1)} %get-tuple-element.56), channel_id=1, source_target_pairs={{0,1},{1,0},{2,3},{3,2},{4,5},{5,4},{6,7},{7,6},{8,9},{9,8},{10,11... | collective-permute-start | bytes 196616 | tf_op jit(solution)/shard_map/ppermute | solution.py:24
  78.2 4.6 %collective-permute-start.18 = (bf16[8,32,128]{2,1,0:T(8,128)(2,1)}, bf16[8,32,128]{2,1,0:T(8,128)(2,1)}, u32[]{:S(2)}, u32[]{:S(2)}) collective-permute-start(bf16[8,32,128]{2,1,0:T(8,128)(2,1)} %fusion.10), channel_id=1, source_target_pairs={{0,2},{1,3},{2,0},{3,1},{4,6},{5,7},{6,4},{7,5},{8,10},{9,11},{10,... | collective-permute-start | bytes 196616 | tf_op jit(solution)/shard_map/ppermute | solution.py:24
  79.2 5.0 %collective-permute-start.19 = (bf16[8,32,128]{2,1,0:T(8,128)(2,1)}, bf16[8,32,128]{2,1,0:T(8,128)(2,1)S(1)}, u32[]{:S(2)}, u32[]{:S(2)}) collective-permute-start(bf16[8,32,128]{2,1,0:T(8,128)(2,1)} %fusion.10), channel_id=1, source_target_pairs={{0,4},{1,5},{2,6},{3,7},{4,0},{5,1},{6,2},{7,3},{8,12},{9,13},{10,... | collective-permute-start | bytes 196616 | tf_op jit(solution)/shard_map/ppermute | solution.py:24
  79.7 5.5 %collective-permute-start.20 = (bf16[8,32,128]{2,1,0:T(8,128)(2,1)}, bf16[8,32,128]{2,1,0:T(8,128)(2,1)S(1)}, u32[]{:S(2)}, u32[]{:S(2)}) collective-permute-start(bf16[8,32,128]{2,1,0:T(8,128)(2,1)} %fusion.10), channel_id=1, source_target_pairs={{0,6},{1,7},{2,4},{3,5},{4,2},{5,3},{6,0},{7,1},{8,14},{9,15},{10,... | collective-permute-start | bytes 196616 | tf_op jit(solution)/shard_map/ppermute | solution.py:24
  86.8 6.3 %collective-permute-start.21 = (bf16[8,32,128]{2,1,0:T(8,128)(2,1)S(1)}, bf16[8,32,128]{2,1,0:T(8,128)(2,1)S(1)}, u32[]{:S(2)}, u32[]{:S(2)}) collective-permute-start(bf16[8,32,128]{2,1,0:T(8,128)(2,1)S(1)} %fusion.13), channel_id=1, source_target_pairs={{0,8},{1,9},{2,10},{3,11},{4,12},{5,13},{6,14},{7,15},{8,0},{9,1},... | collective-permute-start | bytes 196616 | tf_op jit(solution)/shard_map/ppermute | solution.py:24
  96.2 1.4 %collective-permute-start.22 = (bf16[8,32,128]{2,1,0:T(8,128)(2,1)S(1)}, bf16[8,32,128]{2,1,0:T(8,128)(2,1)S(1)}, u32[]{:S(2)}, u32[]{:S(2)}) collective-permute-start(bf16[8,32,128]{2,1,0:T(8,128)(2,1)S(1)} %get-tuple-element.57.scale_ref), channel_id=1, source_target_pairs={{0,1},{1,0},{2,3},{3,2},{4,5},{5,4},{6,7},{7,6},{8,9},{9,8},{10,11... | collective-permute-start | bytes 196616 | tf_op jit(solution)/shard_map/ppermute | solution.py:24
  (30 other events, 50.2 us)

commit v5 on v4

--- a/solution.py
+++ b/solution.py
@@ -207,12 +207,32 @@
     mass_ref[...] = candidates * u_ref[...] * image
 
 
-def other_order(blocks, flip):
-    slots = blocks.shape[0]
-    bits = slots.bit_length() - 1
-    cube = blocks.reshape((2,) * bits + blocks.shape[1:])
-    turned = [bit - 1 for bit in range(1, bits + 1) if flip >> bit & 1]
-    return jnp.flip(cube, turned).reshape(blocks.shape)
+def slot_of(slot, flip, slots):
+    top = slots.bit_length()
+    return slot ^ sum(1 << (top - 1 - bit) for bit in range(1, top) if flip >> bit & 1)
+
+
+def total_of(slot, own_ref, got_refs, flips):
+    total = own_ref[slot]
+    for flip, got_ref in zip(flips, got_refs):
+        total += got_ref[slot_of(slot, flip, own_ref.shape[0])].astype(F32)
+    return total
+
+
+def sum_body(own_ref, *refs, flips):
+    *got_refs, total_ref, sent_ref = refs
+    for slot in range(own_ref.shape[0]):
+        total = total_of(slot, own_ref, got_refs, flips)
+        total_ref[slot] = total
+        sent_ref[slot] = total.astype(BF16)
+
+
+def scale_body(own_ref, marg_ref, *refs, flips):
+    *got_refs, scale_ref, rounded_ref = refs
+    for slot in range(own_ref.shape[0]):
+        scale_v = marg_ref[slot] / total_of(slot, own_ref, got_refs, flips)
+        scale_ref[slot] = scale_v
+        rounded_ref[slot] = scale_v.astype(BF16)
 
 
 def shards(cand_embed, cand_labels, tgt_embed, tgt_labels):
@@ -269,15 +289,17 @@
             column_body, [(block, F32)], scale_ub, *near_kernels, flops=2 * pass_flops
         )
         column = column + got.astype(F32)
+        sent = column.astype(BF16)
+        both = [(block, F32), (block, BF16)]
         for low in range(1, top, 2):
             bits = [1 << bit for bit in range(low, min(low + 2, top))]
             flips = bits + [sum(bits)] if len(bits) > 1 else bits
-            sent = column.astype(BF16)
-            found = [(flip, exchange(sent, flip)) for flip in flips]
-            for flip, got in found:
-                column = column + other_order(got, flip).astype(F32)
-        scale_v = tgt_marg / column
-        scale_vb = scale_v.astype(BF16)
+            found = [exchange(sent, flip) for flip in flips]
+            if low + 2 < top:
+                column, sent = call(functools.partial(sum_body, flips=flips), both, column, *found)
+        scale_v, scale_vb = call(
+            functools.partial(scale_body, flips=flips), both, column, tgt_marg, *found
+        )
         far_vb = exchange(scale_vb, 1)
         (image,) = call(image_body, [image_type], *near_kernels, scale_vb, flops=2 * pass_flops)
     space = pl.BlockSpec(memory_space=pltpu.VMEM)

time: 101 us -> 81.1 us (0.80); the launches traced: 99.5 us -> 80.9 us
  local copies, waits for them, and re-layouts: 22.4 us -> 1.08 us
  waiting for transfers between devices: 26.3 us -> 35.8 us
  other arithmetic: 10.2 us -> 2.25 us
  Pallas kernels: 12.2 us -> 13.6 us
    rev x12 -> x0, local copies, waits for them, and re-layouts: 13.4 us -> none  [other_order(): return jnp.flip(cube, turned).reshape(blocks.shape)]
    ppermute x23, waiting for transfers between devices: 26.3 us -> 35.8 us  [exchange(): return lax.ppermute(block, 'row', [(d, d ^ flip) for d in range(devices)])]
    unnamed x62 -> x4, local copies, waits for them, and re-layouts: 8.42 us -> 0.48 us
    convert_element_type x6 -> x3, other arithmetic: 4.94 us -> 0.06 us  [shards(): sent = column.astype(BF16)]
    convert_element_type x3 -> x0, other arithmetic: 3.1 us -> none  [shards(): scale_vb = scale_v.astype(BF16)]
    pallas_call x14 -> x20, Pallas kernels: 9.8 us -> 11.3 us  [call(): pl.pallas_call(body, out_shape=[pltpu.VMEM(shape, dtype) for shape, dtype...]
  transfers between devices with their start and end apart: 23 -> 23, of which waited for: 17 -> 21; matrix products, arithmetic and copies ran while one was open for 9% -> 3% of each run, Pallas kernels for 5% -> 7%
where the time goes in v5:
time: 81.1 us; the launch traced here: 80.9 us
  waiting for transfers between devices  35.8 us (44%)
  starting transfers between devices  27.3 us (34%)
  Pallas kernels  13.6 us (17%)
  other arithmetic  2.25 us (3%)
  local copies, waits for them, and re-layouts  1.08 us (1%)
    ppermute x23, waiting for transfers between devices, exchange(): return lax.ppermute(block, 'row', [(d, d ^ flip) for d in range(devices)])  35.8 us
    ppermute x23, starting transfers between devices, exchange(): return lax.ppermute(block, 'row', [(d, d ^ flip) for d in range(devices)])  27.3 us
    pallas_call x20, Pallas kernels, call(): pl.pallas_call(body, out_shape=[pltpu.VMEM(shape, dtype) for shape, dtype...  11.3 us
  transfers between devices with their start and end apart: 23, of which 21 were waited for; matrix products, arithmetic and copies ran while one was open for 3% of the time, Pallas kernels for 7%

profile of v5, /device:TPU:0, one launch (start us, length us, event | category | flops | bytes accessed | tf_op | source)
XLA Modules:
  0.0 80.9 jit_solution(3345551248475609952)
XLA Ops:
  1.6 4.1 %collective-permute-start = (bf16[144,256]{1,0:T(8,128)(2,1)S(1)}, bf16[144,256]{1,0:T(8,128)(2,1)S(1)}, u32[]{:S(2)}, u32[]{:S(2)}) collective-permute-start(bf16[144,256]{1,0:T(8,128)(2,1)S(1)} %shard_map.67), channel_id=1, source_target_pairs={{0,8},{1,9},{2,10},{3,11},{4,12},{5,13},{6,14},{7,15},{8,0},{9,1},... | collective-permute-start | bytes 221192 | tf_op jit(solution)/shard_map/ppermute | solution.py:24
  5.7 1.3 %fusion = f32[1024]{0:T(1024)S(1)} fusion(bf16[1024,256]{1,0:T(8,128)(2,1)} %param.4), kind=kLoop, calls=%fused_computation.2 | loop fusion | flops 785408 | bytes 528384 | tf_op jit(solution)/shard_map/reduce_sum | solution.py:42
  7.7 1.9 %collective-permute-done = bf16[144,256]{1,0:T(8,128)(2,1)S(1)} collective-permute-done((bf16[144,256]{1,0:T(8,128)(2,1)S(1)}, bf16[144,256]{1,0:T(8,128)(2,1)S(1)}, u32[]{:S(2)}, u32[]{:S(2)}) %collective-permute-start) | collective-permute-done | bytes 73760 | tf_op jit(solution)/shard_map/ppermute | solution.py:24
  10.4 4.5 %collective-permute-done.1 = bf16[288,256]{1,0:T(8,128)(2,1)S(1)} collective-permute-done((bf16[288,256]{1,0:T(8,128)(2,1)S(1)}, bf16[288,256]{1,0:T(8,128)(2,1)S(1)}, u32[]{:S(2)}, u32[]{:S(2)}) %collective-permute-start.1) | collective-permute-done | bytes 147488 | tf_op jit(solution)/shard_map/ppermute | solution.py:24
  15.0 1.8 %collective-permute-start.2 = (bf16[576,256]{1,0:T(8,128)(2,1)S(1)}, bf16[576,256]{1,0:T(8,128)(2,1)S(1)}, u32[]{:S(2)}, u32[]{:S(2)}) collective-permute-start(bf16[576,256]{1,0:T(8,128)(2,1)S(1)} %pad_maximum_fusion.held_ref.near0), channel_id=1, source_target_pairs={{0,2},{1,3},{2,0},{3,1},{4,6},{5,7},{6,4},{7,5},{8,10},{9,11},{10,... | collective-permute-start | bytes 884744 | tf_op jit(solution)/shard_map/ppermute | solution.py:24
  18.0 6.4 %collective-permute-done.2.held_ref.near1 = bf16[576,256]{1,0:T(8,128)(2,1)S(1)} collective-permute-done((bf16[576,256]{1,0:T(8,128)(2,1)S(1)}, bf16[576,256]{1,0:T(8,128)(2,1)S(1)}, u32[]{:S(2)}, u32[]{:S(2)}) %collective-permute-start.2) | collective-permute-done | bytes 294944 | tf_op jit(solution)/shard_map/ppermute | solution.py:24
  28.5 1.8 %collective-permute-start.6 = (bf16[8,32,128]{2,1,0:T(8,128)(2,1)S(1)}, bf16[8,32,128]{2,1,0:T(8,128)(2,1)S(1)}, u32[]{:S(2)}, u32[]{:S(2)}) collective-permute-start(bf16[8,32,128]{2,1,0:T(8,128)(2,1)S(1)} %get-tuple-element.81), channel_id=1, source_target_pairs={{0,2},{1,3},{2,0},{3,1},{4,6},{5,7},{6,4},{7,5},{8,10},{9,11},{10,... | collective-permute-start | bytes 196616 | tf_op jit(solution)/shard_map/ppermute | solution.py:24
  32.8 2.0 %collective-permute-done.7.refs_1_ = bf16[8,32,128]{2,1,0:T(8,128)(2,1)S(1)} collective-permute-done((bf16[8,32,128]{2,1,0:T(8,128)(2,1)S(1)}, bf16[8,32,128]{2,1,0:T(8,128)(2,1)S(1)}, u32[]{:S(2)}, u32[]{:S(2)}) %collective-permute-start.7) | collective-permute-done | bytes 65568 | tf_op jit(solution)/shard_map/ppermute | solution.py:24
  34.9 1.4 %collective-permute-done.8.refs_2_ = bf16[8,32,128]{2,1,0:T(8,128)(2,1)S(1)} collective-permute-done((bf16[8,32,128]{2,1,0:T(8,128)(2,1)S(1)}, bf16[8,32,128]{2,1,0:T(8,128)(2,1)S(1)}, u32[]{:S(2)}, u32[]{:S(2)}) %collective-permute-start.8) | collective-permute-done | bytes 65568 | tf_op jit(solution)/shard_map/ppermute | solution.py:24
  36.3 3.5 %collective-permute-start.9 = (bf16[8,32,128]{2,1,0:T(8,128)(2,1)S(1)}, bf16[8,32,128]{2,1,0:T(8,128)(2,1)S(1)}, u32[]{:S(2)}, u32[]{:S(2)}) collective-permute-start(bf16[8,32,128]{2,1,0:T(8,128)(2,1)S(1)} %get-tuple-element.62), channel_id=1, source_target_pairs={{0,8},{1,9},{2,10},{3,11},{4,12},{5,13},{6,14},{7,15},{8,0},{9,1},... | collective-permute-start | bytes 196616 | tf_op jit(solution)/shard_map/ppermute | solution.py:24
  39.9 2.8 %collective-permute-done.9.refs_0_ = bf16[8,32,128]{2,1,0:T(8,128)(2,1)S(1)} collective-permute-done((bf16[8,32,128]{2,1,0:T(8,128)(2,1)S(1)}, bf16[8,32,128]{2,1,0:T(8,128)(2,1)S(1)}, u32[]{:S(2)}, u32[]{:S(2)}) %collective-permute-start.9) | collective-permute-done | bytes 65568 | tf_op jit(solution)/shard_map/ppermute | solution.py:24
  44.7 1.6 %shard_map.78 = (f32[32,1024]{1,0:T(8,128)}, bf16[32,1024]{1,0:T(8,128)(2,1)S(1)}, bf16[8,32,128]{2,1,0:T(8,128)(2,1)S(1)}) custom-call(bf16[1024,512]{1,0:T(8,128)(2,1)S(1)} %get-tuple-element.49.far0_ref.kernel0, bf16[1024,512]{1,0:T(8,128)(2,1)S(1)} %get-tuple-element.51.far1_ref.kernel1, bf16[8,32,128]{2,1,0:T(8,128)(2,1)S(1)} %collective-permute-done.10.scale_ref, ...), custom_call_target="tpu_custom_call" | custom-call | flops 536870912 | bytes 2424832 | tf_op jit(solution)/shard_map/pallas_call | solution.py:30
  48.8 2.3 %collective-permute-start.14 = (bf16[8,32,128]{2,1,0:T(8,128)(2,1)S(1)}, bf16[8,32,128]{2,1,0:T(8,128)(2,1)S(1)}, u32[]{:S(2)}, u32[]{:S(2)}) collective-permute-start(bf16[8,32,128]{2,1,0:T(8,128)(2,1)S(1)} %get-tuple-element.79), channel_id=1, source_target_pairs={{0,6},{1,7},{2,4},{3,5},{4,2},{5,3},{6,0},{7,1},{8,14},{9,15},{10,... | collective-permute-start | bytes 196616 | tf_op jit(solution)/shard_map/ppermute | solution.py:24
  51.9 1.1 %collective-permute-done.13.refs_1_ = bf16[8,32,128]{2,1,0:T(8,128)(2,1)S(1)} collective-permute-done((bf16[8,32,128]{2,1,0:T(8,128)(2,1)S(1)}, bf16[8,32,128]{2,1,0:T(8,128)(2,1)S(1)}, u32[]{:S(2)}, u32[]{:S(2)}) %collective-permute-start.13) | collective-permute-done | bytes 65568 | tf_op jit(solution)/shard_map/ppermute | solution.py:24
  53.0 1.4 %collective-permute-done.14.refs_2_ = bf16[8,32,128]{2,1,0:T(8,128)(2,1)S(1)} collective-permute-done((bf16[8,32,128]{2,1,0:T(8,128)(2,1)S(1)}, bf16[8,32,128]{2,1,0:T(8,128)(2,1)S(1)}, u32[]{:S(2)}, u32[]{:S(2)}) %collective-permute-start.14) | collective-permute-done | bytes 65568 | tf_op jit(solution)/shard_map/ppermute | solution.py:24
  54.4 3.0 %collective-permute-start.15 = (bf16[8,32,128]{2,1,0:T(8,128)(2,1)S(1)}, bf16[8,32,128]{2,1,0:T(8,128)(2,1)S(1)}, u32[]{:S(2)}, u32[]{:S(2)}) collective-permute-start(bf16[8,32,128]{2,1,0:T(8,128)(2,1)S(1)} %get-tuple-element.68), channel_id=1, source_target_pairs={{0,8},{1,9},{2,10},{3,11},{4,12},{5,13},{6,14},{7,15},{8,0},{9,1},... | collective-permute-start | bytes 196616 | tf_op jit(solution)/shard_map/ppermute | solution.py:24
  57.4 3.0 %collective-permute-done.15.refs_0_ = bf16[8,32,128]{2,1,0:T(8,128)(2,1)S(1)} collective-permute-done((bf16[8,32,128]{2,1,0:T(8,128)(2,1)S(1)}, bf16[8,32,128]{2,1,0:T(8,128)(2,1)S(1)}, u32[]{:S(2)}, u32[]{:S(2)}) %collective-permute-start.15) | collective-permute-done | bytes 65568 | tf_op jit(solution)/shard_map/ppermute | solution.py:24
  62.3 1.5 %shard_map.83 = (f32[32,1024]{1,0:T(8,128)S(1)}, bf16[32,1024]{1,0:T(8,128)(2,1)S(1)}, bf16[8,32,128]{2,1,0:T(8,128)(2,1)S(1)}) custom-call(bf16[1024,512]{1,0:T(8,128)(2,1)S(1)} %get-tuple-element.49.far0_ref.kernel0, bf16[1024,512]{1,0:T(8,128)(2,1)S(1)} %get-tuple-element.51.far1_ref.kernel1, bf16[8,32,128]{2,1,0:T(8,128)(2,1)S(1)} %collective-permute-done.16.scale_ref, ...), custom_call_target="tpu_custom_call" | custom-call | flops 536870912 | bytes 2424832 | tf_op jit(solution)/shard_map/pallas_call | solution.py:30
  65.2 1.7 %collective-permute-start.19 = (bf16[8,32,128]{2,1,0:T(8,128)(2,1)S(1)}, bf16[8,32,128]{2,1,0:T(8,128)(2,1)S(1)}, u32[]{:S(2)}, u32[]{:S(2)}) collective-permute-start(bf16[8,32,128]{2,1,0:T(8,128)(2,1)S(1)} %get-tuple-element.77), channel_id=1, source_target_pairs={{0,4},{1,5},{2,6},{3,7},{4,0},{5,1},{6,2},{7,3},{8,12},{9,13},{10,... | collective-permute-start | bytes 196616 | tf_op jit(solution)/shard_map/ppermute | solution.py:24
  66.9 1.7 %collective-permute-start.20 = (bf16[8,32,128]{2,1,0:T(8,128)(2,1)S(1)}, bf16[8,32,128]{2,1,0:T(8,128)(2,1)S(1)}, u32[]{:S(2)}, u32[]{:S(2)}) collective-permute-start(bf16[8,32,128]{2,1,0:T(8,128)(2,1)S(1)} %get-tuple-element.77), channel_id=1, source_target_pairs={{0,6},{1,7},{2,4},{3,5},{4,2},{5,3},{6,0},{7,1},{8,14},{9,15},{10,... | collective-permute-start | bytes 196616 | tf_op jit(solution)/shard_map/ppermute | solution.py:24
  69.9 2.2 %collective-permute-done.20.refs_2_ = bf16[8,32,128]{2,1,0:T(8,128)(2,1)S(1)} collective-permute-done((bf16[8,32,128]{2,1,0:T(8,128)(2,1)S(1)}, bf16[8,32,128]{2,1,0:T(8,128)(2,1)S(1)}, u32[]{:S(2)}, u32[]{:S(2)}) %collective-permute-start.20) | collective-permute-done | bytes 65568 | tf_op jit(solution)/shard_map/ppermute | solution.py:24
  72.2 2.9 %collective-permute-start.21 = (bf16[8,32,128]{2,1,0:T(8,128)(2,1)S(1)}, bf16[8,32,128]{2,1,0:T(8,128)(2,1)S(1)}, u32[]{:S(2)}, u32[]{:S(2)}) collective-permute-start(bf16[8,32,128]{2,1,0:T(8,128)(2,1)S(1)} %get-tuple-element.74), channel_id=1, source_target_pairs={{0,8},{1,9},{2,10},{3,11},{4,12},{5,13},{6,14},{7,15},{8,0},{9,1},... | collective-permute-start | bytes 196616 | tf_op jit(solution)/shard_map/ppermute | solution.py:24
  75.8 2.3 %collective-permute-done.21.refs_0_ = bf16[8,32,128]{2,1,0:T(8,128)(2,1)S(1)} collective-permute-done((bf16[8,32,128]{2,1,0:T(8,128)(2,1)S(1)}, bf16[8,32,128]{2,1,0:T(8,128)(2,1)S(1)}, u32[]{:S(2)}, u32[]{:S(2)}) %collective-permute-start.21) | collective-permute-done | bytes 65568 | tf_op jit(solution)/shard_map/ppermute | solution.py:24
  79.5 1.4 %shard_map.88 = f32[32,1024]{1,0:T(8,128)} custom-call(bf16[1024,512]{1,0:T(8,128)(2,1)S(1)} %get-tuple-element.49.far0_ref.kernel0, bf16[1024,512]{1,0:T(8,128)(2,1)S(1)} %get-tuple-element.51.far1_ref.kernel1, bf16[8,32,128]{2,1,0:T(8,128)(2,1)S(1)} %collective-permute-done.22.scale_ref, f32[32,1024]{1,0:T(8,128)S(1)} %shard_map.87.image_ref, ...), custom_call_target="tpu_custom_call" | custom-call | tf_op jit(solution)/shard_map/pallas_call | solution.py:307
  (59 shorter events, 22.5 us)
Async XLA Ops:
  0.6 6.4 %copy-start = (bf16[1024,256]{1,0:T(8,128)(2,1)S(1)}, bf16[1024,256]{1,0:T(8,128)(2,1)}, u32[]{:S(2)}) copy-start(bf16[1024,256]{1,0:T(8,128)(2,1)} %param.4) | copy-start | bytes 1572868
  1.6 8.0 %collective-permute-start = (bf16[144,256]{1,0:T(8,128)(2,1)S(1)}, bf16[144,256]{1,0:T(8,128)(2,1)S(1)}, u32[]{:S(2)}, u32[]{:S(2)}) collective-permute-start(bf16[144,256]{1,0:T(8,128)(2,1)S(1)} %shard_map.67), channel_id=1, source_target_pairs={{0,8},{1,9},{2,10},{3,11},{4,12},{5,13},{6,14},{7,15},{8,0},{9,1},... | collective-permute-start | bytes 221192 | tf_op jit(solution)/shard_map/ppermute | solution.py:24
  9.7 5.2 %collective-permute-start.1 = (bf16[288,256]{1,0:T(8,128)(2,1)S(1)}, bf16[288,256]{1,0:T(8,128)(2,1)S(1)}, u32[]{:S(2)}, u32[]{:S(2)}) collective-permute-start(bf16[288,256]{1,0:T(8,128)(2,1)S(1)} %pad_maximum_fusion.1), channel_id=1, source_target_pairs={{0,4},{1,5},{2,6},{3,7},{4,0},{5,1},{6,2},{7,3},{8,12},{9,13},{10,... | collective-permute-start | bytes 442376 | tf_op jit(solution)/shard_map/ppermute | solution.py:24
  14.9 2.5 %collective-permute-start.3 = (bf16[576,256]{1,0:T(8,128)(2,1)S(1)}, bf16[576,256]{1,0:T(8,128)(2,1)S(1)}, u32[]{:S(2)}, u32[]{:S(2)}) collective-permute-start(bf16[576,256]{1,0:T(8,128)(2,1)S(1)} %pad_maximum_fusion.held_ref.near0), channel_id=1, source_target_pairs={{0,1},{1,0},{2,3},{3,2},{4,5},{5,4},{6,7},{7,6},{8,9},{9,8},{10,11... | collective-permute-start | bytes 884744 | tf_op jit(solution)/shard_map/ppermute | solution.py:24
  15.0 9.4 %collective-permute-start.2 = (bf16[576,256]{1,0:T(8,128)(2,1)S(1)}, bf16[576,256]{1,0:T(8,128)(2,1)S(1)}, u32[]{:S(2)}, u32[]{:S(2)}) collective-permute-start(bf16[576,256]{1,0:T(8,128)(2,1)S(1)} %pad_maximum_fusion.held_ref.near0), channel_id=1, source_target_pairs={{0,2},{1,3},{2,0},{3,1},{4,6},{5,7},{6,4},{7,5},{8,10},{9,11},{10,... | collective-permute-start | bytes 884744 | tf_op jit(solution)/shard_map/ppermute | solution.py:24
  24.4 1.6 %collective-permute-start.4 = (bf16[576,256]{1,0:T(8,128)(2,1)S(1)}, bf16[576,256]{1,0:T(8,128)(2,1)S(1)}, u32[]{:S(2)}, u32[]{:S(2)}) collective-permute-start(bf16[576,256]{1,0:T(8,128)(2,1)S(1)} %collective-permute-done.2.held_ref.near1), channel_id=1, source_target_pairs={{0,1},{1,0},{2,3},{3,2},{4,5},{5,4},{6,7},{7,6},{8,9},{9,8},{10,11... | collective-permute-start | bytes 884744 | tf_op jit(solution)/shard_map/ppermute | solution.py:24
  27.2 1.3 %collective-permute-start.5 = (bf16[8,32,128]{2,1,0:T(8,128)(2,1)S(1)}, bf16[8,32,128]{2,1,0:T(8,128)(2,1)S(1)}, u32[]{:S(2)}, u32[]{:S(2)}) collective-permute-start(bf16[8,32,128]{2,1,0:T(8,128)(2,1)S(1)} %get-tuple-element.60), channel_id=1, source_target_pairs={{0,1},{1,0},{2,3},{3,2},{4,5},{5,4},{6,7},{7,6},{8,9},{9,8},{10,11... | collective-permute-start | bytes 196616 | tf_op jit(solution)/shard_map/ppermute | solution.py:24
  28.5 4.3 %collective-permute-start.6 = (bf16[8,32,128]{2,1,0:T(8,128)(2,1)S(1)}, bf16[8,32,128]{2,1,0:T(8,128)(2,1)S(1)}, u32[]{:S(2)}, u32[]{:S(2)}) collective-permute-start(bf16[8,32,128]{2,1,0:T(8,128)(2,1)S(1)} %get-tuple-element.81), channel_id=1, source_target_pairs={{0,2},{1,3},{2,0},{3,1},{4,6},{5,7},{6,4},{7,5},{8,10},{9,11},{10,... | collective-permute-start | bytes 196616 | tf_op jit(solution)/shard_map/ppermute | solution.py:24
  30.3 4.6 %collective-permute-start.7 = (bf16[8,32,128]{2,1,0:T(8,128)(2,1)S(1)}, bf16[8,32,128]{2,1,0:T(8,128)(2,1)S(1)}, u32[]{:S(2)}, u32[]{:S(2)}) collective-permute-start(bf16[8,32,128]{2,1,0:T(8,128)(2,1)S(1)} %get-tuple-element.81), channel_id=1, source_target_pairs={{0,4},{1,5},{2,6},{3,7},{4,0},{5,1},{6,2},{7,3},{8,12},{9,13},{10,... | collective-permute-start | bytes 196616 | tf_op jit(solution)/shard_map/ppermute | solution.py:24
  31.1 5.2 %collective-permute-start.8 = (bf16[8,32,128]{2,1,0:T(8,128)(2,1)S(1)}, bf16[8,32,128]{2,1,0:T(8,128)(2,1)S(1)}, u32[]{:S(2)}, u32[]{:S(2)}) collective-permute-start(bf16[8,32,128]{2,1,0:T(8,128)(2,1)S(1)} %get-tuple-element.81), channel_id=1, source_target_pairs={{0,6},{1,7},{2,4},{3,5},{4,2},{5,3},{6,0},{7,1},{8,14},{9,15},{10,... | collective-permute-start | bytes 196616 | tf_op jit(solution)/shard_map/ppermute | solution.py:24
  36.3 6.4 %collective-permute-start.9 = (bf16[8,32,128]{2,1,0:T(8,128)(2,1)S(1)}, bf16[8,32,128]{2,1,0:T(8,128)(2,1)S(1)}, u32[]{:S(2)}, u32[]{:S(2)}) collective-permute-start(bf16[8,32,128]{2,1,0:T(8,128)(2,1)S(1)} %get-tuple-element.62), channel_id=1, source_target_pairs={{0,8},{1,9},{2,10},{3,11},{4,12},{5,13},{6,14},{7,15},{8,0},{9,1},... | collective-permute-start | bytes 196616 | tf_op jit(solution)/shard_map/ppermute | solution.py:24
  43.4 1.3 %collective-permute-start.10 = (bf16[8,32,128]{2,1,0:T(8,128)(2,1)S(1)}, bf16[8,32,128]{2,1,0:T(8,128)(2,1)S(1)}, u32[]{:S(2)}, u32[]{:S(2)}) collective-permute-start(bf16[8,32,128]{2,1,0:T(8,128)(2,1)S(1)} %get-tuple-element.63.scale_ref), channel_id=1, source_target_pairs={{0,1},{1,0},{2,3},{3,2},{4,5},{5,4},{6,7},{7,6},{8,9},{9,8},{10,11... | collective-permute-start | bytes 196616 | tf_op jit(solution)/shard_map/ppermute | solution.py:24
  46.3 1.3 %collective-permute-start.11 = (bf16[8,32,128]{2,1,0:T(8,128)(2,1)S(1)}, bf16[8,32,128]{2,1,0:T(8,128)(2,1)S(1)}, u32[]{:S(2)}, u32[]{:S(2)}) collective-permute-start(bf16[8,32,128]{2,1,0:T(8,128)(2,1)S(1)} %get-tuple-element.66), channel_id=1, source_target_pairs={{0,1},{1,0},{2,3},{3,2},{4,5},{5,4},{6,7},{7,6},{8,9},{9,8},{10,11... | collective-permute-start | bytes 196616 | tf_op jit(solution)/shard_map/ppermute | solution.py:24
  47.6 4.3 %collective-permute-start.12 = (bf16[8,32,128]{2,1,0:T(8,128)(2,1)S(1)}, bf16[8,32,128]{2,1,0:T(8,128)(2,1)S(1)}, u32[]{:S(2)}, u32[]{:S(2)}) collective-permute-start(bf16[8,32,128]{2,1,0:T(8,128)(2,1)S(1)} %get-tuple-element.79), channel_id=1, source_target_pairs={{0,2},{1,3},{2,0},{3,1},{4,6},{5,7},{6,4},{7,5},{8,10},{9,11},{10,... | collective-permute-start | bytes 196616 | tf_op jit(solution)/shard_map/ppermute | solution.py:24
  48.2 4.8 %collective-permute-start.13 = (bf16[8,32,128]{2,1,0:T(8,128)(2,1)S(1)}, bf16[8,32,128]{2,1,0:T(8,128)(2,1)S(1)}, u32[]{:S(2)}, u32[]{:S(2)}) collective-permute-start(bf16[8,32,128]{2,1,0:T(8,128)(2,1)S(1)} %get-tuple-element.79), channel_id=1, source_target_pairs={{0,4},{1,5},{2,6},{3,7},{4,0},{5,1},{6,2},{7,3},{8,12},{9,13},{10,... | collective-permute-start | bytes 196616 | tf_op jit(solution)/shard_map/ppermute | solution.py:24
  48.8 5.6 %collective-permute-start.14 = (bf16[8,32,128]{2,1,0:T(8,128)(2,1)S(1)}, bf16[8,32,128]{2,1,0:T(8,128)(2,1)S(1)}, u32[]{:S(2)}, u32[]{:S(2)}) collective-permute-start(bf16[8,32,128]{2,1,0:T(8,128)(2,1)S(1)} %get-tuple-element.79), channel_id=1, source_target_pairs={{0,6},{1,7},{2,4},{3,5},{4,2},{5,3},{6,0},{7,1},{8,14},{9,15},{10,... | collective-permute-start | bytes 196616 | tf_op jit(solution)/shard_map/ppermute | solution.py:24
  54.4 5.9 %collective-permute-start.15 = (bf16[8,32,128]{2,1,0:T(8,128)(2,1)S(1)}, bf16[8,32,128]{2,1,0:T(8,128)(2,1)S(1)}, u32[]{:S(2)}, u32[]{:S(2)}) collective-permute-start(bf16[8,32,128]{2,1,0:T(8,128)(2,1)S(1)} %get-tuple-element.68), channel_id=1, source_target_pairs={{0,8},{1,9},{2,10},{3,11},{4,12},{5,13},{6,14},{7,15},{8,0},{9,1},... | collective-permute-start | bytes 196616 | tf_op jit(solution)/shard_map/ppermute | solution.py:24
  61.0 1.3 %collective-permute-start.16 = (bf16[8,32,128]{2,1,0:T(8,128)(2,1)S(1)}, bf16[8,32,128]{2,1,0:T(8,128)(2,1)S(1)}, u32[]{:S(2)}, u32[]{:S(2)}) collective-permute-start(bf16[8,32,128]{2,1,0:T(8,128)(2,1)S(1)} %get-tuple-element.69.scale_ref), channel_id=1, source_target_pairs={{0,1},{1,0},{2,3},{3,2},{4,5},{5,4},{6,7},{7,6},{8,9},{9,8},{10,11... | collective-permute-start | bytes 196616 | tf_op jit(solution)/shard_map/ppermute | solution.py:24
  63.8 1.3 %collective-permute-start.17 = (bf16[8,32,128]{2,1,0:T(8,128)(2,1)S(1)}, bf16[8,32,128]{2,1,0:T(8,128)(2,1)S(1)}, u32[]{:S(2)}, u32[]{:S(2)}) collective-permute-start(bf16[8,32,128]{2,1,0:T(8,128)(2,1)S(1)} %get-tuple-element.72), channel_id=1, source_target_pairs={{0,1},{1,0},{2,3},{3,2},{4,5},{5,4},{6,7},{7,6},{8,9},{9,8},{10,11... | collective-permute-start | bytes 196616 | tf_op jit(solution)/shard_map/ppermute | solution.py:24
  65.1 4.3 %collective-permute-start.18 = (bf16[8,32,128]{2,1,0:T(8,128)(2,1)S(1)}, bf16[8,32,128]{2,1,0:T(8,128)(2,1)S(1)}, u32[]{:S(2)}, u32[]{:S(2)}) collective-permute-start(bf16[8,32,128]{2,1,0:T(8,128)(2,1)S(1)} %get-tuple-element.77), channel_id=1, source_target_pairs={{0,2},{1,3},{2,0},{3,1},{4,6},{5,7},{6,4},{7,5},{8,10},{9,11},{10,... | collective-permute-start | bytes 196616 | tf_op jit(solution)/shard_map/ppermute | solution.py:24
  65.2 4.7 %collective-permute-start.19 = (bf16[8,32,128]{2,1,0:T(8,128)(2,1)S(1)}, bf16[8,32,128]{2,1,0:T(8,128)(2,1)S(1)}, u32[]{:S(2)}, u32[]{:S(2)}) collective-permute-start(bf16[8,32,128]{2,1,0:T(8,128)(2,1)S(1)} %get-tuple-element.77), channel_id=1, source_target_pairs={{0,4},{1,5},{2,6},{3,7},{4,0},{5,1},{6,2},{7,3},{8,12},{9,13},{10,... | collective-permute-start | bytes 196616 | tf_op jit(solution)/shard_map/ppermute | solution.py:24
  66.9 5.2 %collective-permute-start.20 = (bf16[8,32,128]{2,1,0:T(8,128)(2,1)S(1)}, bf16[8,32,128]{2,1,0:T(8,128)(2,1)S(1)}, u32[]{:S(2)}, u32[]{:S(2)}) collective-permute-start(bf16[8,32,128]{2,1,0:T(8,128)(2,1)S(1)} %get-tuple-element.77), channel_id=1, source_target_pairs={{0,6},{1,7},{2,4},{3,5},{4,2},{5,3},{6,0},{7,1},{8,14},{9,15},{10,... | collective-permute-start | bytes 196616 | tf_op jit(solution)/shard_map/ppermute | solution.py:24
  72.2 5.9 %collective-permute-start.21 = (bf16[8,32,128]{2,1,0:T(8,128)(2,1)S(1)}, bf16[8,32,128]{2,1,0:T(8,128)(2,1)S(1)}, u32[]{:S(2)}, u32[]{:S(2)}) collective-permute-start(bf16[8,32,128]{2,1,0:T(8,128)(2,1)S(1)} %get-tuple-element.74), channel_id=1, source_target_pairs={{0,8},{1,9},{2,10},{3,11},{4,12},{5,13},{6,14},{7,15},{8,0},{9,1},... | collective-permute-start | bytes 196616 | tf_op jit(solution)/shard_map/ppermute | solution.py:24
  78.1 1.4 %collective-permute-start.22 = (bf16[8,32,128]{2,1,0:T(8,128)(2,1)S(1)}, bf16[8,32,128]{2,1,0:T(8,128)(2,1)S(1)}, u32[]{:S(2)}, u32[]{:S(2)}) collective-permute-start(bf16[8,32,128]{2,1,0:T(8,128)(2,1)S(1)} %get-tuple-element.76.scale_ref), channel_id=1, source_target_pairs={{0,1},{1,0},{2,3},{3,2},{4,5},{5,4},{6,7},{7,6},{8,9},{9,8},{10,11... | collective-permute-start | bytes 196616 | tf_op jit(solution)/shard_map/ppermute | solution.py:24
  (1 other events, 0.7 us)

commit v6 on v5

--- a/solution.py
+++ b/solution.py
@@ -152,10 +152,11 @@
             yield ref[pl.ds(s * rows + tgt_rows, EXTRA), :].astype(F32)
 
 
-def target_body(near0, near1, far0, far1, marg_ref):
+def target_body(*refs):
+    *held_refs, marg_ref = refs
     slots, _, tgt_rows = marg_ref.shape
     total = jnp.zeros((CLASSES, tgt_rows), F32)
-    for s, extra in enumerate(extras((near0, near1, far0, far1), tgt_rows)):
+    for s, extra in enumerate(extras(held_refs, tgt_rows)):
         weight = 1.0 + 3.0 * hot(extra[:1, :LANES].astype(jnp.int32))
         total += weight
         if s < slots:
@@ -165,51 +166,66 @@
         marg_ref[s] = marg_ref[s] / total
 
 
-def first_body(
-    far0_ref, far1_ref, sums0, sums1, sums2, sums3, near0, near1, held0, held1, weight_ref,
-    marg_ref, scale_ref, column_ref,
-):
-    tgt_rows = column_ref.shape[2]
+def first_body(weight_ref, *refs, parts):
+    refs, (marg_ref, scale_ref, column_ref) = refs[:-3], refs[-3:]
+    kernels, sums_refs, held_refs = refs[:parts], refs[parts : 3 * parts], refs[3 * parts :]
     counts = jnp.zeros((EXTRA, LANES), F32)
-    for extra in extras((near0, near1, held0, held1), tgt_rows):
+    for extra in extras(held_refs, column_ref.shape[2]):
         counts += extra[:, LANES:]
     count = jnp.broadcast_to(counts[:1] + counts[1:2], (LANES, LANES)).T[:CLASSES, :1]
     candidates = weight_ref.shape[1] * 2 * column_ref.shape[0]
     marg = weight_ref[...] / (candidates + 3.0 * count)
     marg_ref[...] = marg
-    sums = sums0[...] + sums1[...] + sums2[...] + sums3[...]
+    sums = sum(ref[...] for ref in sums_refs)
     image = jnp.sum(sums.T, axis=0, keepdims=True)
     scale_ub = (marg / image).astype(BF16)
     scale_ref[...] = scale_ub
-    put_column(scale_ub, (far0_ref, far1_ref), column_ref)
-
-
-def column_body(scale_ref, kernel0, kernel1, column_ref):
-    put_column(scale_ref[...], (kernel0, kernel1), column_ref)
-
-
-def image_body(kernel0, kernel1, scale_ref, image_ref):
-    image_ref[...] = image_of((kernel0, kernel1), scale_ref)
-
-
-def step_body(
-    kernel0, kernel1, scale_ref, image_ref, marg_ref, out_ref, rounded_ref, column_ref
-):
-    image = image_ref[...] + image_of((kernel0, kernel1), scale_ref)
+    put_column(scale_ub, kernels, column_ref)
+
+
+def column_body(scale_ref, *refs):
+    put_column(scale_ref[...], refs[:-1], refs[-1])
+
+
+def image_body(scale_ref, *refs):
+    refs[-1][...] = image_of(refs[:-1], scale_ref)
+
+
+def step_body(scale_ref, image_ref, marg_ref, *refs):
+    kernels, (out_ref, rounded_ref, column_ref) = refs[:-3], refs[-3:]
+    image = image_ref[...] + image_of(kernels, scale_ref)
     scale_u = marg_ref[...] / image
     out_ref[...] = scale_u
     rounded_ref[...] = scale_u.astype(BF16)
-    put_column(scale_u.astype(BF16), (kernel0, kernel1), column_ref)
-
-
-def last_body(kernel0, kernel1, scale_ref, image_ref, u_ref, mass_ref, *, candidates):
-    image = image_ref[...] + image_of((kernel0, kernel1), scale_ref)
+    put_column(scale_u.astype(BF16), kernels, column_ref)
+
+
+def last_body(scale_ref, image_ref, u_ref, scale_v_ref, *refs, candidates):
+    kernels, (mass_ref, own_ref) = refs[:-2], refs[-2:]
+    own_ref[...] = scale_v_ref[0]
+    image = image_ref[...] + image_of(kernels, scale_ref)
     mass_ref[...] = candidates * u_ref[...] * image
 
 
 def slot_of(slot, flip, slots):
     top = slots.bit_length()
     return slot ^ sum(1 << (top - 1 - bit) for bit in range(1, top) if flip >> bit & 1)
+
+
+def group_body(got_ref, total_ref, sent_ref, *, members):
+    me = lax.axis_index("row") // 2 % members
+    slots = total_ref.shape[0]
+    for slot in range(slots):
+        total = 0.0
+        for place in range(members):
+            turned = sum(
+                ((me // (1 << bit) + place // (1 << bit)) % 2) * (slots >> (bit + 1))
+                * (1 - 2 * (slot // (slots >> (bit + 1)) % 2))
+                for bit in range(members.bit_length() - 1)
+            )
+            total += got_ref[place, slot + turned].astype(F32)
+        total_ref[slot] = total
+        sent_ref[slot] = total.astype(BF16)
 
 
 def total_of(slot, own_ref, got_refs, flips):
@@ -228,11 +244,11 @@
 
 
 def scale_body(own_ref, marg_ref, *refs, flips):
-    *got_refs, scale_ref, rounded_ref = refs
+    got_refs, outs = refs[: len(flips)], refs[len(flips) :]
     for slot in range(own_ref.shape[0]):
         scale_v = marg_ref[slot] / total_of(slot, own_ref, got_refs, flips)
-        scale_ref[slot] = scale_v
-        rounded_ref[slot] = scale_v.astype(BF16)
+        for out_ref in outs:
+            out_ref[slot] = scale_v.astype(out_ref.dtype)
 
 
 def shards(cand_embed, cand_labels, tgt_embed, tgt_labels):
@@ -241,77 +257,97 @@
     slots = devices // 2
     cand_rows, width = cand_embed.shape
     tgt_rows = tgt_embed.shape[0]
-    quarter = slots // 2 * tgt_rows
     cand_labels = cand_labels.reshape(1, cand_rows)
     block = (slots, CLASSES, tgt_rows)
     image_type = ((CLASSES, cand_rows), F32)
     rounded_type = ((CLASSES, cand_rows), BF16)
-    pass_flops = 2 * cand_rows * quarter * 128
+    half_flops = 2 * cand_rows * slots * tgt_rows * 128
 
     def fill(held):
+        columns = held.shape[0] // (tgt_rows + EXTRA) * tgt_rows
         return call(
             functools.partial(fill_body, tgt_rows=tgt_rows),
-            [((cand_rows, quarter), BF16), ((cand_rows, LANES), F32)],
-            cand_unit, held, flops=4 * pass_flops,
-        )
-
-    near = [pack(tgt_embed, tgt_labels.reshape(1, tgt_rows), cand_labels)]
+            [((cand_rows, columns), BF16), ((cand_rows, LANES), F32)],
+            cand_unit, held, flops=4 * 2 * cand_rows * columns * 128,
+        )
+
+    held = piece = pack(tgt_embed, tgt_labels.reshape(1, tgt_rows), cand_labels)
     cand_unit = unit_rows(cand_embed)
     weight = 1.0 + 3.0 * hot(cand_labels)
+    across = []
     for bit in range(top - 1, 1, -1):
-        near[0] = jnp.concatenate([near[0], exchange(near[0], 1 << bit)])
-        near[0], cand_unit, weight = lax.optimization_barrier((near[0], cand_unit, weight))
-    near.append(exchange(near[0], 2))
-    far = [exchange(near[0], 1)]
-    filled = [fill(near[0]), fill(far[0])]
-    near[1], filled = lax.optimization_barrier((near[1], filled))
-    far.append(exchange(near[1], 1))
-    filled += [fill(near[1]), fill(far[1])]
-    kernels, sums = zip(*filled)
-    near_kernels, far_kernels = kernels[::2], kernels[1::2]
+        turned = exchange(held, 1 << bit)
+        across.append(exchange(piece, 2))
+        piece, across, cand_unit, weight = lax.optimization_barrier(
+            (turned, across, cand_unit, weight)
+        )
+        held = jnp.concatenate([held, piece])
+    later = exchange(piece, 2)
+    near = [held, jnp.concatenate(across)]
+    far = [exchange(part, 1) for part in near]
+    filled = [[fill(part) for part in side] for side in (near, far)]
+    later, filled = lax.optimization_barrier((later, filled))
+    near.append(later)
+    far.append(exchange(later, 1))
+    for side, parts in zip((near, far), filled):
+        parts.append(fill(side[-1]))
+    near_kernels, near_sums = zip(*filled[0])
+    far_kernels, far_sums = zip(*filled[1])
 
     cand_marg, scale_ub, far_column = call(
-        first_body,
+        functools.partial(first_body, parts=len(near)),
         [image_type, rounded_type, (block, BF16)],
-        *far_kernels, *sums, *near, *far, weight, flops=2 * pass_flops,
+        weight, *far_kernels, *near_sums, *far_sums, *near, *far, flops=half_flops,
     )
-    (tgt_marg,) = call(target_body, [(block, F32)], *near, *far, flops=pass_flops)
-    scale_u = None
+    (tgt_marg,) = call(target_body, [(block, F32)], *near, *far, flops=half_flops)
     for step in range(ITERS):
         if step:
             scale_u, scale_ub, far_column = call(
                 step_body,
                 [image_type, rounded_type, (block, BF16)],
-                *far_kernels, far_vb, image, cand_marg, flops=4 * pass_flops,
+                far_vb, image, cand_marg, *far_kernels, flops=2 * half_flops,
             )
         got = exchange(far_column, 1)
         (column,) = call(
-            column_body, [(block, F32)], scale_ub, *near_kernels, flops=2 * pass_flops
-        )
-        column = column + got.astype(F32)
-        sent = column.astype(BF16)
+            column_body, [(block, F32)], scale_ub, *near_kernels, flops=half_flops
+        )
+        sent = (column + got.astype(F32)).astype(BF16)
+        groups = [
+            [base + core + 2 * place for place in range(4)]
+            for base in range(0, devices, 8) for core in range(2)
+        ]
+        got = lax.all_to_all(
+            jnp.broadcast_to(sent[None], (4,) + sent.shape), "row", 0, 0,
+            axis_index_groups=groups,
+        )
         both = [(block, F32), (block, BF16)]
-        for low in range(1, top, 2):
+        column, sent = call(functools.partial(group_body, members=4), both, got)
+        for low in range(3, top, 2):
             bits = [1 << bit for bit in range(low, min(low + 2, top))]
             flips = bits + [sum(bits)] if len(bits) > 1 else bits
             found = [exchange(sent, flip) for flip in flips]
             if low + 2 < top:
                 column, sent = call(functools.partial(sum_body, flips=flips), both, column, *found)
-        scale_v, scale_vb = call(
-            functools.partial(scale_body, flips=flips), both, column, tgt_marg, *found
+        last = step == ITERS - 1
+        scale_vb, *scale_v = call(
+            functools.partial(scale_body, flips=flips),
+            [(block, BF16)] + [(block, F32)] * last,
+            column, tgt_marg, *found,
         )
         far_vb = exchange(scale_vb, 1)
-        (image,) = call(image_body, [image_type], *near_kernels, scale_vb, flops=2 * pass_flops)
+        (image,) = call(image_body, [image_type], scale_vb, *near_kernels, flops=half_flops)
     space = pl.BlockSpec(memory_space=pltpu.VMEM)
-    last = [*far_kernels, far_vb, image, scale_u]
-    mass = pl.pallas_call(
+    args = [far_vb, image, scale_u, *scale_v, *far_kernels]
+    mass, tgt_scaling = pl.pallas_call(
         functools.partial(last_body, candidates=float(cand_rows * devices)),
-        out_shape=jax.ShapeDtypeStruct(*image_type),
-        in_specs=[space] * len(last),
-        out_specs=space,
+        out_shape=[
+            jax.ShapeDtypeStruct(*image_type), jax.ShapeDtypeStruct((CLASSES, tgt_rows), F32)
+        ],
+        in_specs=[space] * len(args),
+        out_specs=[space] * 2,
         compiler_params=pltpu.CompilerParams(vmem_limit_bytes=12 * 1024 * 1024),
-    )(*[pltpu.with_memory_space_constraint(a, pltpu.VMEM) for a in last])
-    return (ENTROPY_TEMP * jnp.log(scale_u), scale_v[0], mass)
+    )(*[pltpu.with_memory_space_constraint(a, pltpu.VMEM) for a in args])
+    return (ENTROPY_TEMP * jnp.log(scale_u), tgt_scaling, mass)
 
 
 def solution(mesh):

time: 81.1 us -> 82.4 us (1.016)
  blocking collectives: 0 us -> 26.3 us
  waiting for transfers between devices: 35.8 us -> 21.9 us
  starting transfers between devices: 27.3 us -> 17.2 us
    all_to_all x0 -> x3, blocking collectives: none -> 26.3 us  [shards(): lax.all_to_all(jnp.broadcast_to(sent[None], (4,) + sent.shape), 'row', 0,...]
    ppermute x23 -> x17, waiting for transfers between devices: 35.8 us -> 21.9 us  [exchange(): return lax.ppermute(block, 'row', [(d, d ^ flip) for d in range(devices)])]
    ppermute x23 -> x17, starting transfers between devices: 27.3 us -> 17.2 us  [exchange(): return lax.ppermute(block, 'row', [(d, d ^ flip) for d in range(devices)])]
    pallas_call x20 -> x22, Pallas kernels: 11.3 us -> 10.7 us  [call(): pl.pallas_call(body, out_shape=[pltpu.VMEM(shape, dtype) for shape, dtype...]
  transfers between devices with their start and end apart: 23 -> 17, of which waited for: 21 -> 13; matrix products, arithmetic and copies ran while one was open for 3% -> 3% of each run, Pallas kernels for 7% -> 7%
where the time goes in v6:
time: 82.4 us; the launch traced here: 82.1 us
  blocking collectives  26.3 us (32%)
  waiting for transfers between devices  21.9 us (27%)
  starting transfers between devices  17.2 us (21%)
  Pallas kernels  13 us (16%)
  other arithmetic  2.24 us (3%)
  between operations  0.89 us (1%)
    all_to_all x3, blocking collectives, shards(): lax.all_to_all(jnp.broadcast_to(sent[None], (4,) + sent.shape), 'row', 0,...  26.3 us
    ppermute x17, waiting for transfers between devices, exchange(): return lax.ppermute(block, 'row', [(d, d ^ flip) for d in range(devices)])  21.9 us
    ppermute x17, starting transfers between devices, exchange(): return lax.ppermute(block, 'row', [(d, d ^ flip) for d in range(devices)])  17.2 us
    pallas_call x22, Pallas kernels, call(): pl.pallas_call(body, out_shape=[pltpu.VMEM(shape, dtype) for shape, dtype...  10.7 us
  transfers between devices with their start and end apart: 17, of which 13 were waited for; matrix products, arithmetic and copies ran while one was open for 3% of the time, Pallas kernels for 7%

profile of v6, /device:TPU:0, one launch (start us, length us, event | category | flops | bytes accessed | tf_op | source)
XLA Modules:
  0.0 82.1 jit_solution(5756359736032360028)
XLA Ops:
  0.6 1.0 %shard_map.67 = bf16[144,256]{1,0:T(8,128)(2,1)S(1)} custom-call(bf16[128,256]{1,0:T(8,128)(2,1)} %embed_hbm.1, s32[1,128]{1,0:T(1,128)} %bitcast.3, s32[1,1024]{1,0:T(1,128)} %bitcast.2), custom_call_target="tpu_custom_call" | custom-call | tf_op jit(solution)/shard_map/pallas_call | solution.py:80
  1.6 4.1 %collective-permute-start = (bf16[144,256]{1,0:T(8,128)(2,1)S(1)}, bf16[144,256]{1,0:T(8,128)(2,1)S(1)}, u32[]{:S(2)}, u32[]{:S(2)}) collective-permute-start(bf16[144,256]{1,0:T(8,128)(2,1)S(1)} %shard_map.67), channel_id=1, source_target_pairs={{0,8},{1,9},{2,10},{3,11},{4,12},{5,13},{6,14},{7,15},{8,0},{9,1},... | collective-permute-start | bytes 221192 | tf_op jit(solution)/shard_map/ppermute | solution.py:24
  5.7 1.5 %collective-permute-start.1 = (bf16[144,256]{1,0:T(8,128)(2,1)S(1)}, bf16[144,256]{1,0:T(8,128)(2,1)S(1)}, u32[]{:S(2)}, u32[]{:S(2)}) collective-permute-start(bf16[144,256]{1,0:T(8,128)(2,1)S(1)} %shard_map.67), channel_id=1, source_target_pairs={{0,2},{1,3},{2,0},{3,1},{4,6},{5,7},{6,4},{7,5},{8,10},{9,11},{10,... | collective-permute-start | bytes 221192 | tf_op jit(solution)/shard_map/ppermute | solution.py:24
  7.3 1.3 %fusion = f32[1024]{0:T(1024)S(1)} fusion(bf16[1024,256]{1,0:T(8,128)(2,1)} %param.4), kind=kLoop, calls=%fused_computation.2 | loop fusion | flops 785408 | bytes 528384 | tf_op jit(solution)/shard_map/reduce_sum | solution.py:42
  10.1 1.6 %collective-permute-start.2 = (bf16[288,256]{1,0:T(8,128)(2,1)S(1)}, bf16[288,256]{1,0:T(8,128)(2,1)S(1)}, u32[]{:S(2)}, u32[]{:S(2)}) collective-permute-start(bf16[288,256]{1,0:T(8,128)(2,1)S(1)} %pad_maximum_fusion.1), channel_id=1, source_target_pairs={{0,4},{1,5},{2,6},{3,7},{4,0},{5,1},{6,2},{7,3},{8,12},{9,13},{10,... | collective-permute-start | bytes 442376 | tf_op jit(solution)/shard_map/ppermute | solution.py:24
  11.7 1.5 %collective-permute-start.3 = (bf16[144,256]{1,0:T(8,128)(2,1)S(1)}, bf16[144,256]{1,0:T(8,128)(2,1)S(1)}, u32[]{:S(2)}, u32[]{:S(2)}) collective-permute-start(bf16[144,256]{1,0:T(8,128)(2,1)S(1)} %collective-permute-done), channel_id=1, source_target_pairs={{0,2},{1,3},{2,0},{3,1},{4,6},{5,7},{6,4},{7,5},{8,10},{9,11},{10,... | collective-permute-start | bytes 221192 | tf_op jit(solution)/shard_map/ppermute | solution.py:24
  13.3 2.8 %collective-permute-done.3 = bf16[144,256]{1,0:T(8,128)(2,1)S(1)} collective-permute-done((bf16[144,256]{1,0:T(8,128)(2,1)S(1)}, bf16[144,256]{1,0:T(8,128)(2,1)S(1)}, u32[]{:S(2)}, u32[]{:S(2)}) %collective-permute-start.3) | collective-permute-done | bytes 73760 | tf_op jit(solution)/shard_map/ppermute | solution.py:24
  16.8 1.5 %collective-permute-start.4 = (bf16[288,256]{1,0:T(8,128)(2,1)S(1)}, bf16[288,256]{1,0:T(8,128)(2,1)S(1)}, u32[]{:S(2)}, u32[]{:S(2)}) collective-permute-start(bf16[288,256]{1,0:T(8,128)(2,1)S(1)} %collective-permute-done.2), channel_id=1, source_target_pairs={{0,2},{1,3},{2,0},{3,1},{4,6},{5,7},{6,4},{7,5},{8,10},{9,11},{10,... | collective-permute-start | bytes 442376 | tf_op jit(solution)/shard_map/ppermute | solution.py:24
  20.4 2.2 %collective-permute-done.4.held_ref.refs_11_.refs_2_ = bf16[288,256]{1,0:T(8,128)(2,1)S(1)} collective-permute-done((bf16[288,256]{1,0:T(8,128)(2,1)S(1)}, bf16[288,256]{1,0:T(8,128)(2,1)S(1)}, u32[]{:S(2)}, u32[]{:S(2)}) %collective-permute-start.4) | collective-permute-done | bytes 147488 | tf_op jit(solution)/shard_map/ppermute | solution.py:24
  23.1 0.9 %collective-permute-done.7.held_ref.refs_14_.refs_5_ = bf16[288,256]{1,0:T(8,128)(2,1)S(1)} collective-permute-done((bf16[288,256]{1,0:T(8,128)(2,1)S(1)}, bf16[288,256]{1,0:T(8,128)(2,1)S(1)}, u32[]{:S(2)}, u32[]{:S(2)}) %collective-permute-start.7) | collective-permute-done | bytes 147488 | tf_op jit(solution)/shard_map/ppermute | solution.py:24
  26.4 8.8 %all_to_all.15.got_ref = bf16[4,8,32,128]{3,2,1,0:T(8,128)(2,1)S(1)} all-to-all(bf16[4,8,32,128]{3,2,1,0:T(8,128)(2,1)S(1)} %broadcast_in_dim.6), channel_id=1, replica_groups={{0,2,4,6},{1,3,5,7},{8,10,12,14},{9,11,13,15},{16,18,20,22},{17,19,21,2..., dimensions={0} | all-to-all | bytes 524288 | tf_op jit(solution)/shard_map/all_to_all | solution.py:319
  35.3 2.5 %collective-permute-start.9 = (bf16[8,32,128]{2,1,0:T(8,128)(2,1)S(1)}, bf16[8,32,128]{2,1,0:T(8,128)(2,1)S(1)}, u32[]{:S(2)}, u32[]{:S(2)}) collective-permute-start(bf16[8,32,128]{2,1,0:T(8,128)(2,1)S(1)} %get-tuple-element.84), channel_id=1, source_target_pairs={{0,8},{1,9},{2,10},{3,11},{4,12},{5,13},{6,14},{7,15},{8,0},{9,1},... | collective-permute-start | bytes 196616 | tf_op jit(solution)/shard_map/ppermute | solution.py:24
  37.9 3.3 %collective-permute-done.9.refs_0_ = bf16[8,32,128]{2,1,0:T(8,128)(2,1)S(1)} collective-permute-done((bf16[8,32,128]{2,1,0:T(8,128)(2,1)S(1)}, bf16[8,32,128]{2,1,0:T(8,128)(2,1)S(1)}, u32[]{:S(2)}, u32[]{:S(2)}) %collective-permute-start.9) | collective-permute-done | bytes 65568 | tf_op jit(solution)/shard_map/ppermute | solution.py:24
  41.3 0.7 shard_map.79.image_ref
  42.6 1.7 %shard_map.80 = (f32[32,1024]{1,0:T(8,128)}, bf16[32,1024]{1,0:T(8,128)(2,1)S(1)}, bf16[8,32,128]{2,1,0:T(8,128)(2,1)S(1)}) custom-call(bf16[8,32,128]{2,1,0:T(8,128)(2,1)S(1)} %collective-permute-done.10.scale_ref, f32[32,1024]{1,0:T(8,128)S(1)} %shard_map.79.image_ref, f32[32,1024]{1,0:T(8,128)S(1)} %get-tuple-element.85.marg_ref, ...), custom_call_target="tpu_custom_call" | custom-call | flops 536870912 | bytes 2424832 | tf_op jit(solution)/shard_map/pallas_call | solution.py:30
  45.6 8.7 %all_to_all.16.got_ref = bf16[4,8,32,128]{3,2,1,0:T(8,128)(2,1)S(1)} all-to-all(bf16[4,8,32,128]{3,2,1,0:T(8,128)(2,1)S(1)} %broadcast_in_dim.7), channel_id=1, replica_groups={{0,2,4,6},{1,3,5,7},{8,10,12,14},{9,11,13,15},{16,18,20,22},{17,19,21,2..., dimensions={0} | all-to-all | bytes 524288 | tf_op jit(solution)/shard_map/all_to_all | solution.py:319
  54.4 1.9 %collective-permute-start.12 = (bf16[8,32,128]{2,1,0:T(8,128)(2,1)S(1)}, bf16[8,32,128]{2,1,0:T(8,128)(2,1)S(1)}, u32[]{:S(2)}, u32[]{:S(2)}) collective-permute-start(bf16[8,32,128]{2,1,0:T(8,128)(2,1)S(1)} %get-tuple-element.89), channel_id=1, source_target_pairs={{0,8},{1,9},{2,10},{3,11},{4,12},{5,13},{6,14},{7,15},{8,0},{9,1},... | collective-permute-start | bytes 196616 | tf_op jit(solution)/shard_map/ppermute | solution.py:24
  56.2 4.1 %collective-permute-done.12.refs_0_ = bf16[8,32,128]{2,1,0:T(8,128)(2,1)S(1)} collective-permute-done((bf16[8,32,128]{2,1,0:T(8,128)(2,1)S(1)}, bf16[8,32,128]{2,1,0:T(8,128)(2,1)S(1)}, u32[]{:S(2)}, u32[]{:S(2)}) %collective-permute-start.12) | collective-permute-done | bytes 65568 | tf_op jit(solution)/shard_map/ppermute | solution.py:24
  60.4 0.7 shard_map.84.image_ref
  61.7 1.5 %shard_map.85 = (f32[32,1024]{1,0:T(8,128)S(1)}, bf16[32,1024]{1,0:T(8,128)(2,1)S(1)}, bf16[8,32,128]{2,1,0:T(8,128)(2,1)S(1)}) custom-call(bf16[8,32,128]{2,1,0:T(8,128)(2,1)S(1)} %collective-permute-done.13.scale_ref, f32[32,1024]{1,0:T(8,128)S(1)} %shard_map.84.image_ref, f32[32,1024]{1,0:T(8,128)S(1)} %get-tuple-element.85.marg_ref, ...), custom_call_target="tpu_custom_call" | custom-call | flops 536870912 | bytes 2424832 | tf_op jit(solution)/shard_map/pallas_call | solution.py:30
  64.5 8.7 %all_to_all.17.got_ref = bf16[4,8,32,128]{3,2,1,0:T(8,128)(2,1)S(1)} all-to-all(bf16[4,8,32,128]{3,2,1,0:T(8,128)(2,1)S(1)} %broadcast_in_dim.8), channel_id=1, replica_groups={{0,2,4,6},{1,3,5,7},{8,10,12,14},{9,11,13,15},{16,18,20,22},{17,19,21,2..., dimensions={0} | all-to-all | bytes 524288 | tf_op jit(solution)/shard_map/all_to_all | solution.py:319
  73.3 1.3 %collective-permute-start.15 = (bf16[8,32,128]{2,1,0:T(8,128)(2,1)S(1)}, bf16[8,32,128]{2,1,0:T(8,128)(2,1)S(1)}, u32[]{:S(2)}, u32[]{:S(2)}) collective-permute-start(bf16[8,32,128]{2,1,0:T(8,128)(2,1)S(1)} %get-tuple-element.94), channel_id=1, source_target_pairs={{0,8},{1,9},{2,10},{3,11},{4,12},{5,13},{6,14},{7,15},{8,0},{9,1},... | collective-permute-start | bytes 196616 | tf_op jit(solution)/shard_map/ppermute | solution.py:24
  74.5 4.7 %collective-permute-done.15.refs_0_ = bf16[8,32,128]{2,1,0:T(8,128)(2,1)S(1)} collective-permute-done((bf16[8,32,128]{2,1,0:T(8,128)(2,1)S(1)}, bf16[8,32,128]{2,1,0:T(8,128)(2,1)S(1)}, u32[]{:S(2)}, u32[]{:S(2)}) %collective-permute-start.15) | collective-permute-done | bytes 65568 | tf_op jit(solution)/shard_map/ppermute | solution.py:24
  80.7 1.4 %shard_map.90 = (f32[32,1024]{1,0:T(8,128)}, f32[32,128]{1,0:T(8,128)}) custom-call(bf16[8,32,128]{2,1,0:T(8,128)(2,1)S(1)} %collective-permute-done.16.scale_ref, f32[32,1024]{1,0:T(8,128)S(1)} %shard_map.89.image_ref, f32[32,1024]{1,0:T(8,128)S(1)} %get-tuple-element.90.u_ref, f32[8,32,128]{2,1,0:T(8,128)S(1)} %get-tuple-element.96.scale_v_ref, ...), custom_call_target="tpu_custom_call" | custom-call | tf_op jit(solution)/shard_map/pallas_call | solution.py:341
  (56 shorter events, 12.8 us)
Async XLA Ops:
  0.6 7.9 %copy-start = (bf16[1024,256]{1,0:T(8,128)(2,1)S(1)}, bf16[1024,256]{1,0:T(8,128)(2,1)}, u32[]{:S(2)}) copy-start(bf16[1024,256]{1,0:T(8,128)(2,1)} %param.4) | copy-start | bytes 1572868
  1.6 8.0 %collective-permute-start = (bf16[144,256]{1,0:T(8,128)(2,1)S(1)}, bf16[144,256]{1,0:T(8,128)(2,1)S(1)}, u32[]{:S(2)}, u32[]{:S(2)}) collective-permute-start(bf16[144,256]{1,0:T(8,128)(2,1)S(1)} %shard_map.67), channel_id=1, source_target_pairs={{0,8},{1,9},{2,10},{3,11},{4,12},{5,13},{6,14},{7,15},{8,0},{9,1},... | collective-permute-start | bytes 221192 | tf_op jit(solution)/shard_map/ppermute | solution.py:24
  5.7 4.4 %collective-permute-start.1 = (bf16[144,256]{1,0:T(8,128)(2,1)S(1)}, bf16[144,256]{1,0:T(8,128)(2,1)S(1)}, u32[]{:S(2)}, u32[]{:S(2)}) collective-permute-start(bf16[144,256]{1,0:T(8,128)(2,1)S(1)} %shard_map.67), channel_id=1, source_target_pairs={{0,2},{1,3},{2,0},{3,1},{4,6},{5,7},{6,4},{7,5},{8,10},{9,11},{10,... | collective-permute-start | bytes 221192 | tf_op jit(solution)/shard_map/ppermute | solution.py:24
  8.5 0.7 copy-start.1
  10.1 6.0 %collective-permute-start.2 = (bf16[288,256]{1,0:T(8,128)(2,1)S(1)}, bf16[288,256]{1,0:T(8,128)(2,1)S(1)}, u32[]{:S(2)}, u32[]{:S(2)}) collective-permute-start(bf16[288,256]{1,0:T(8,128)(2,1)S(1)} %pad_maximum_fusion.1), channel_id=1, source_target_pairs={{0,4},{1,5},{2,6},{3,7},{4,0},{5,1},{6,2},{7,3},{8,12},{9,13},{10,... | collective-permute-start | bytes 442376 | tf_op jit(solution)/shard_map/ppermute | solution.py:24
  11.7 4.4 %collective-permute-start.3 = (bf16[144,256]{1,0:T(8,128)(2,1)S(1)}, bf16[144,256]{1,0:T(8,128)(2,1)S(1)}, u32[]{:S(2)}, u32[]{:S(2)}) collective-permute-start(bf16[144,256]{1,0:T(8,128)(2,1)S(1)} %collective-permute-done), channel_id=1, source_target_pairs={{0,2},{1,3},{2,0},{3,1},{4,6},{5,7},{6,4},{7,5},{8,10},{9,11},{10,... | collective-permute-start | bytes 221192 | tf_op jit(solution)/shard_map/ppermute | solution.py:24
  16.1 3.7 %collective-permute-start.5 = (bf16[576,256]{1,0:T(8,128)(2,1)S(1)}, bf16[576,256]{1,0:T(8,128)(2,1)S(1)}, u32[]{:S(2)}, u32[]{:S(2)}) collective-permute-start(bf16[576,256]{1,0:T(8,128)(2,1)S(1)} %pad_maximum_fusion.held_ref.refs_9_.refs_0_), channel_id=1, source_target_pairs={{0,1},{1,0},{2,3},{3,2},{4,5},{5,4},{6,7},{7,6},{8,9},{9,8},{10,11... | collective-permute-start | bytes 884744 | tf_op jit(solution)/shard_map/ppermute | solution.py:24
  16.2 3.1 %collective-permute-start.6 = (bf16[288,256]{1,0:T(8,128)(2,1)S(1)}, bf16[288,256]{1,0:T(8,128)(2,1)S(1)}, u32[]{:S(2)}, u32[]{:S(2)}) collective-permute-start(bf16[288,256]{1,0:T(8,128)(2,1)S(1)} %constant_dynamic-update-slice_fusion.held_ref.refs_10_.refs_1_), channel_id=1, source_target_pairs={{0,1},{1,0},{2,3},{3,2},{4,5},{5,4},{6,7},{7,6},{8,9},{9,8},{10,11... | collective-permute-start | bytes 442376 | tf_op jit(solution)/shard_map/ppermute | solution.py:24
  16.8 5.8 %collective-permute-start.4 = (bf16[288,256]{1,0:T(8,128)(2,1)S(1)}, bf16[288,256]{1,0:T(8,128)(2,1)S(1)}, u32[]{:S(2)}, u32[]{:S(2)}) collective-permute-start(bf16[288,256]{1,0:T(8,128)(2,1)S(1)} %collective-permute-done.2), channel_id=1, source_target_pairs={{0,2},{1,3},{2,0},{3,1},{4,6},{5,7},{6,4},{7,5},{8,10},{9,11},{10,... | collective-permute-start | bytes 442376 | tf_op jit(solution)/shard_map/ppermute | solution.py:24
  22.6 1.4 %collective-permute-start.7 = (bf16[288,256]{1,0:T(8,128)(2,1)S(1)}, bf16[288,256]{1,0:T(8,128)(2,1)S(1)}, u32[]{:S(2)}, u32[]{:S(2)}) collective-permute-start(bf16[288,256]{1,0:T(8,128)(2,1)S(1)} %collective-permute-done.4.held_ref.refs_11_.refs_2_), channel_id=1, source_target_pairs={{0,1},{1,0},{2,3},{3,2},{4,5},{5,4},{6,7},{7,6},{8,9},{9,8},{10,11... | collective-permute-start | bytes 442376 | tf_op jit(solution)/shard_map/ppermute | solution.py:24
  25.1 1.3 %collective-permute-start.8 = (bf16[8,32,128]{2,1,0:T(8,128)(2,1)S(1)}, bf16[8,32,128]{2,1,0:T(8,128)(2,1)S(1)}, u32[]{:S(2)}, u32[]{:S(2)}) collective-permute-start(bf16[8,32,128]{2,1,0:T(8,128)(2,1)S(1)} %get-tuple-element.82), channel_id=1, source_target_pairs={{0,1},{1,0},{2,3},{3,2},{4,5},{5,4},{6,7},{7,6},{8,9},{9,8},{10,11... | collective-permute-start | bytes 196616 | tf_op jit(solution)/shard_map/ppermute | solution.py:24
  35.3 5.9 %collective-permute-start.9 = (bf16[8,32,128]{2,1,0:T(8,128)(2,1)S(1)}, bf16[8,32,128]{2,1,0:T(8,128)(2,1)S(1)}, u32[]{:S(2)}, u32[]{:S(2)}) collective-permute-start(bf16[8,32,128]{2,1,0:T(8,128)(2,1)S(1)} %get-tuple-element.84), channel_id=1, source_target_pairs={{0,8},{1,9},{2,10},{3,11},{4,12},{5,13},{6,14},{7,15},{8,0},{9,1},... | collective-permute-start | bytes 196616 | tf_op jit(solution)/shard_map/ppermute | solution.py:24
  41.3 1.3 %collective-permute-start.10 = (bf16[8,32,128]{2,1,0:T(8,128)(2,1)S(1)}, bf16[8,32,128]{2,1,0:T(8,128)(2,1)S(1)}, u32[]{:S(2)}, u32[]{:S(2)}) collective-permute-start(bf16[8,32,128]{2,1,0:T(8,128)(2,1)S(1)} %shard_map.78.scale_ref), channel_id=1, source_target_pairs={{0,1},{1,0},{2,3},{3,2},{4,5},{5,4},{6,7},{7,6},{8,9},{9,8},{10,11... | collective-permute-start | bytes 196616 | tf_op jit(solution)/shard_map/ppermute | solution.py:24
  44.3 1.3 %collective-permute-start.11 = (bf16[8,32,128]{2,1,0:T(8,128)(2,1)S(1)}, bf16[8,32,128]{2,1,0:T(8,128)(2,1)S(1)}, u32[]{:S(2)}, u32[]{:S(2)}) collective-permute-start(bf16[8,32,128]{2,1,0:T(8,128)(2,1)S(1)} %get-tuple-element.87), channel_id=1, source_target_pairs={{0,1},{1,0},{2,3},{3,2},{4,5},{5,4},{6,7},{7,6},{8,9},{9,8},{10,11... | collective-permute-start | bytes 196616 | tf_op jit(solution)/shard_map/ppermute | solution.py:24
  54.4 5.9 %collective-permute-start.12 = (bf16[8,32,128]{2,1,0:T(8,128)(2,1)S(1)}, bf16[8,32,128]{2,1,0:T(8,128)(2,1)S(1)}, u32[]{:S(2)}, u32[]{:S(2)}) collective-permute-start(bf16[8,32,128]{2,1,0:T(8,128)(2,1)S(1)} %get-tuple-element.89), channel_id=1, source_target_pairs={{0,8},{1,9},{2,10},{3,11},{4,12},{5,13},{6,14},{7,15},{8,0},{9,1},... | collective-permute-start | bytes 196616 | tf_op jit(solution)/shard_map/ppermute | solution.py:24
  60.3 1.3 %collective-permute-start.13 = (bf16[8,32,128]{2,1,0:T(8,128)(2,1)S(1)}, bf16[8,32,128]{2,1,0:T(8,128)(2,1)S(1)}, u32[]{:S(2)}, u32[]{:S(2)}) collective-permute-start(bf16[8,32,128]{2,1,0:T(8,128)(2,1)S(1)} %shard_map.83.scale_ref), channel_id=1, source_target_pairs={{0,1},{1,0},{2,3},{3,2},{4,5},{5,4},{6,7},{7,6},{8,9},{9,8},{10,11... | collective-permute-start | bytes 196616 | tf_op jit(solution)/shard_map/ppermute | solution.py:24
  63.2 1.3 %collective-permute-start.14 = (bf16[8,32,128]{2,1,0:T(8,128)(2,1)S(1)}, bf16[8,32,128]{2,1,0:T(8,128)(2,1)S(1)}, u32[]{:S(2)}, u32[]{:S(2)}) collective-permute-start(bf16[8,32,128]{2,1,0:T(8,128)(2,1)S(1)} %get-tuple-element.92), channel_id=1, source_target_pairs={{0,1},{1,0},{2,3},{3,2},{4,5},{5,4},{6,7},{7,6},{8,9},{9,8},{10,11... | collective-permute-start | bytes 196616 | tf_op jit(solution)/shard_map/ppermute | solution.py:24
  73.3 5.9 %collective-permute-start.15 = (bf16[8,32,128]{2,1,0:T(8,128)(2,1)S(1)}, bf16[8,32,128]{2,1,0:T(8,128)(2,1)S(1)}, u32[]{:S(2)}, u32[]{:S(2)}) collective-permute-start(bf16[8,32,128]{2,1,0:T(8,128)(2,1)S(1)} %get-tuple-element.94), channel_id=1, source_target_pairs={{0,8},{1,9},{2,10},{3,11},{4,12},{5,13},{6,14},{7,15},{8,0},{9,1},... | collective-permute-start | bytes 196616 | tf_op jit(solution)/shard_map/ppermute | solution.py:24
  79.2 1.5 %collective-permute-start.16 = (bf16[8,32,128]{2,1,0:T(8,128)(2,1)S(1)}, bf16[8,32,128]{2,1,0:T(8,128)(2,1)S(1)}, u32[]{:S(2)}, u32[]{:S(2)}) collective-permute-start(bf16[8,32,128]{2,1,0:T(8,128)(2,1)S(1)} %get-tuple-element.95.scale_ref), channel_id=1, source_target_pairs={{0,1},{1,0},{2,3},{3,2},{4,5},{5,4},{6,7},{7,6},{8,9},{9,8},{10,11... | collective-permute-start | bytes 196616 | tf_op jit(solution)/shard_map/ppermute | solution.py:24

commit v7 on v6

--- a/solution.py
+++ b/solution.py
@@ -1,4 +1,5 @@
 import functools
+import itertools
 import math
 
 import jax
@@ -19,9 +20,27 @@
 BF16 = jnp.bfloat16
 
 
-def exchange(block, flip):
+def slot_bits(core, top):
+    layer = list(range(2, top))
+    return (layer if core else layer[::-1]) + [1]
+
+
+def rounds(core, top):
+    groups = [list(range(low, min(low + 2, top))) for low in range(1, top, 2)]
+    return groups[::-1] if core else groups
+
+
+def flips_of(bits):
+    flips = [0]
+    for bit in bits:
+        flips += [flip | 1 << bit for flip in flips]
+    return flips[1:]
+
+
+def exchange(block, *flips):
     devices = lax.axis_size("row")
-    return lax.ppermute(block, "row", [(d, d ^ flip) for d in range(devices)])
+    pairs = [(d, d ^ flips[d % len(flips)]) for d in range(devices) if flips[d % len(flips)]]
+    return lax.ppermute(block, "row", pairs)
 
 
 def call(body, outs, *args, flops=0):
@@ -207,31 +226,21 @@
     mass_ref[...] = candidates * u_ref[...] * image
 
 
-def slot_of(slot, flip, slots):
+def slot_of(slot, flips, slots):
     top = slots.bit_length()
-    return slot ^ sum(1 << (top - 1 - bit) for bit in range(1, top) if flip >> bit & 1)
-
-
-def group_body(got_ref, total_ref, sent_ref, *, members):
-    me = lax.axis_index("row") // 2 % members
-    slots = total_ref.shape[0]
-    for slot in range(slots):
-        total = 0.0
-        for place in range(members):
-            turned = sum(
-                ((me // (1 << bit) + place // (1 << bit)) % 2) * (slots >> (bit + 1))
-                * (1 - 2 * (slot // (slots >> (bit + 1)) % 2))
-                for bit in range(members.bit_length() - 1)
-            )
-            total += got_ref[place, slot + turned].astype(F32)
-        total_ref[slot] = total
-        sent_ref[slot] = total.astype(BF16)
+    found = []
+    for core, flip in enumerate(flips):
+        turned = sum(1 << i for i, bit in enumerate(slot_bits(core, top)) if flip >> bit & 1)
+        found.append(slot ^ turned)
+    if found[0] == found[1]:
+        return found[0]
+    return found[0] + lax.axis_index("row") % 2 * (found[1] - found[0])
 
 
 def total_of(slot, own_ref, got_refs, flips):
     total = own_ref[slot]
-    for flip, got_ref in zip(flips, got_refs):
-        total += got_ref[slot_of(slot, flip, own_ref.shape[0])].astype(F32)
+    for pair, got_ref in zip(flips, got_refs):
+        total += got_ref[slot_of(slot, pair, own_ref.shape[0])].astype(F32)
     return total
 
 
@@ -275,8 +284,8 @@
     cand_unit = unit_rows(cand_embed)
     weight = 1.0 + 3.0 * hot(cand_labels)
     across = []
-    for bit in range(top - 1, 1, -1):
-        turned = exchange(held, 1 << bit)
+    for bits in list(zip(slot_bits(0, top), slot_bits(1, top)))[:-1]:
+        turned = exchange(held, *[1 << bit for bit in bits])
         across.append(exchange(piece, 2))
         piece, across, cand_unit, weight = lax.optimization_barrier(
             (turned, across, cand_unit, weight)
@@ -311,24 +320,21 @@
         (column,) = call(
             column_body, [(block, F32)], scale_ub, *near_kernels, flops=half_flops
         )
-        sent = (column + got.astype(F32)).astype(BF16)
-        groups = [
-            [base + core + 2 * place for place in range(4)]
-            for base in range(0, devices, 8) for core in range(2)
-        ]
-        got = lax.all_to_all(
-            jnp.broadcast_to(sent[None], (4,) + sent.shape), "row", 0, 0,
-            axis_index_groups=groups,
-        )
-        both = [(block, F32), (block, BF16)]
-        column, sent = call(functools.partial(group_body, members=4), both, got)
-        for low in range(3, top, 2):
-            bits = [1 << bit for bit in range(low, min(low + 2, top))]
-            flips = bits + [sum(bits)] if len(bits) > 1 else bits
-            found = [exchange(sent, flip) for flip in flips]
-            if low + 2 < top:
-                column, sent = call(functools.partial(sum_body, flips=flips), both, column, *found)
+        column = column + got.astype(F32)
+        sent = column.astype(BF16)
+        order = list(zip(rounds(0, top), rounds(1, top)))
+        for place, pair in enumerate(order):
+            flips = list(itertools.zip_longest(*[flips_of(bits) for bits in pair], fillvalue=0))
+            found = [exchange(sent, *turn) for turn in flips]
+            if place < len(order) - 1:
+                column, sent = call(
+                    functools.partial(sum_body, flips=flips),
+                    [(block, F32), (block, BF16)], column, *found,
+                )
         last = step == ITERS - 1
+        if last:
+            potential = ENTROPY_TEMP * jnp.log(scale_u)
+            found, potential = lax.optimization_barrier((found, potential))
         scale_vb, *scale_v = call(
             functools.partial(scale_body, flips=flips),
             [(block, BF16)] + [(block, F32)] * last,
@@ -347,7 +353,7 @@
         out_specs=[space] * 2,
         compiler_params=pltpu.CompilerParams(vmem_limit_bytes=12 * 1024 * 1024),
     )(*[pltpu.with_memory_space_constraint(a, pltpu.VMEM) for a in args])
-    return (ENTROPY_TEMP * jnp.log(scale_u), tgt_scaling, mass)
+    return (potential, tgt_scaling, mass)
 
 
 def solution(mesh):

time: 82.4 us -> 89.4 us (1.085)
  blocking collectives: 26.3 us -> 0 us
  starting transfers between devices: 17.2 us -> 42.5 us
  waiting for transfers between devices: 21.9 us -> 29.7 us
    all_to_all x3 -> x0, blocking collectives: 26.3 us -> none  [shards(): lax.all_to_all(jnp.broadcast_to(sent[None], (4,) + sent.shape), 'row', 0,...]
    ppermute x17 -> x32, starting transfers between devices: 17.2 us -> 42.5 us  [exchange(): return lax.ppermute(block, 'row', pairs)]
    ppermute x17 -> x32, waiting for transfers between devices: 21.9 us -> 29.7 us  [exchange(): return lax.ppermute(block, 'row', pairs)]
  transfers between devices with their start and end apart: 17 -> 32, of which waited for: 13 -> 18; matrix products, arithmetic and copies ran while one was open for 3% -> 2% of each run, Pallas kernels for 7% -> 7%
where the time goes in v7:
time: 89.4 us; the launch traced here: 89 us
  starting transfers between devices  42.5 us (48%)
  waiting for transfers between devices  29.7 us (33%)
  Pallas kernels  13.1 us (15%)
  other arithmetic  2.25 us (3%)
  between operations  1.01 us (1%)
    ppermute x32, starting transfers between devices, exchange(): return lax.ppermute(block, 'row', pairs)  42.5 us
    ppermute x32, waiting for transfers between devices, exchange(): return lax.ppermute(block, 'row', pairs)  29.7 us
    pallas_call x22, Pallas kernels, call(): pl.pallas_call(body, out_shape=[pltpu.VMEM(shape, dtype) for shape, dtype...  10.7 us
  transfers between devices with their start and end apart: 32, of which 18 were waited for; matrix products, arithmetic and copies ran while one was open for 2% of the time, Pallas kernels for 7%

profile of v7, /device:TPU:0, one launch (start us, length us, event | category | flops | bytes accessed | tf_op | source)
XLA Modules:
  0.0 89.0 jit_solution(3279607156521209161)
XLA Ops:
  1.6 4.1 %collective-permute-start = (bf16[144,256]{1,0:T(8,128)(2,1)S(1)}, bf16[144,256]{1,0:T(8,128)(2,1)S(1)}, u32[]{:S(2)}, u32[]{:S(2)}) collective-permute-start(bf16[144,256]{1,0:T(8,128)(2,1)S(1)} %shard_map.67), channel_id=1, source_target_pairs={{0,8},{1,5},{2,10},{3,7},{4,12},{5,1},{6,14},{7,3},{8,0},{9,13},{1... | collective-permute-start | bytes 221192 | tf_op jit(solution)/shard_map/ppermute | solution.py:43
  5.7 1.5 %collective-permute-start.1 = (bf16[144,256]{1,0:T(8,128)(2,1)S(1)}, bf16[144,256]{1,0:T(8,128)(2,1)S(1)}, u32[]{:S(2)}, u32[]{:S(2)}) collective-permute-start(bf16[144,256]{1,0:T(8,128)(2,1)S(1)} %shard_map.67), channel_id=1, source_target_pairs={{0,2},{1,3},{2,0},{3,1},{4,6},{5,7},{6,4},{7,5},{8,10},{9,11},{10,... | collective-permute-start | bytes 221192 | tf_op jit(solution)/shard_map/ppermute | solution.py:43
  10.1 1.6 %collective-permute-start.2 = (bf16[288,256]{1,0:T(8,128)(2,1)S(1)}, bf16[288,256]{1,0:T(8,128)(2,1)S(1)}, u32[]{:S(2)}, u32[]{:S(2)}) collective-permute-start(bf16[288,256]{1,0:T(8,128)(2,1)S(1)} %pad_maximum_fusion.1), channel_id=1, source_target_pairs={{0,4},{1,9},{2,6},{3,11},{4,0},{5,13},{6,2},{7,15},{8,12},{9,1},{1... | collective-permute-start | bytes 442376 | tf_op jit(solution)/shard_map/ppermute | solution.py:43
  11.7 1.5 %collective-permute-start.3 = (bf16[144,256]{1,0:T(8,128)(2,1)S(1)}, bf16[144,256]{1,0:T(8,128)(2,1)S(1)}, u32[]{:S(2)}, u32[]{:S(2)}) collective-permute-start(bf16[144,256]{1,0:T(8,128)(2,1)S(1)} %collective-permute-done), channel_id=1, source_target_pairs={{0,2},{1,3},{2,0},{3,1},{4,6},{5,7},{6,4},{7,5},{8,10},{9,11},{10,... | collective-permute-start | bytes 221192 | tf_op jit(solution)/shard_map/ppermute | solution.py:43
  13.3 2.8 %collective-permute-done.3 = bf16[144,256]{1,0:T(8,128)(2,1)S(1)} collective-permute-done((bf16[144,256]{1,0:T(8,128)(2,1)S(1)}, bf16[144,256]{1,0:T(8,128)(2,1)S(1)}, u32[]{:S(2)}, u32[]{:S(2)}) %collective-permute-start.3) | collective-permute-done | bytes 73760 | tf_op jit(solution)/shard_map/ppermute | solution.py:43
  16.8 1.5 %collective-permute-start.4 = (bf16[288,256]{1,0:T(8,128)(2,1)S(1)}, bf16[288,256]{1,0:T(8,128)(2,1)S(1)}, u32[]{:S(2)}, u32[]{:S(2)}) collective-permute-start(bf16[288,256]{1,0:T(8,128)(2,1)S(1)} %collective-permute-done.2), channel_id=1, source_target_pairs={{0,2},{1,3},{2,0},{3,1},{4,6},{5,7},{6,4},{7,5},{8,10},{9,11},{10,... | collective-permute-start | bytes 442376 | tf_op jit(solution)/shard_map/ppermute | solution.py:43
  20.4 2.2 %collective-permute-done.4.held_ref.refs_11_.refs_2_ = bf16[288,256]{1,0:T(8,128)(2,1)S(1)} collective-permute-done((bf16[288,256]{1,0:T(8,128)(2,1)S(1)}, bf16[288,256]{1,0:T(8,128)(2,1)S(1)}, u32[]{:S(2)}, u32[]{:S(2)}) %collective-permute-start.4) | collective-permute-done | bytes 147488 | tf_op jit(solution)/shard_map/ppermute | solution.py:43
  26.4 1.6 %collective-permute-start.9 = (bf16[8,32,128]{2,1,0:T(8,128)(2,1)S(1)}, bf16[8,32,128]{2,1,0:T(8,128)(2,1)S(1)}, u32[]{:S(2)}, u32[]{:S(2)}) collective-permute-start(bf16[8,32,128]{2,1,0:T(8,128)(2,1)S(1)} %get-tuple-element.111), channel_id=1, source_target_pairs={{0,2},{1,9},{2,0},{3,11},{4,6},{5,13},{6,4},{7,15},{8,10},{9,1},{1... | collective-permute-start | bytes 196616 | tf_op jit(solution)/shard_map/ppermute | solution.py:43
  28.0 2.7 %collective-permute-start.10 = (bf16[8,32,128]{2,1,0:T(8,128)(2,1)S(1)}, bf16[8,32,128]{2,1,0:T(8,128)(2,1)S(1)}, u32[]{:S(2)}, u32[]{:S(2)}) collective-permute-start(bf16[8,32,128]{2,1,0:T(8,128)(2,1)S(1)} %get-tuple-element.111), channel_id=1, source_target_pairs={{0,4},{2,6},{4,0},{6,2},{8,12},{10,14},{12,8},{14,10},{16,20},{18,... | collective-permute-start | bytes 196616 | tf_op jit(solution)/shard_map/ppermute | solution.py:43
  30.6 3.1 %collective-permute-start.11 = (bf16[8,32,128]{2,1,0:T(8,128)(2,1)S(1)}, bf16[8,32,128]{2,1,0:T(8,128)(2,1)S(1)}, u32[]{:S(2)}, u32[]{:S(2)}) collective-permute-start(bf16[8,32,128]{2,1,0:T(8,128)(2,1)S(1)} %get-tuple-element.111), channel_id=1, source_target_pairs={{0,6},{2,4},{4,2},{6,0},{8,14},{10,12},{12,10},{14,8},{16,22},{18,... | collective-permute-start | bytes 196616 | tf_op jit(solution)/shard_map/ppermute | solution.py:43
  34.1 4.2 %collective-permute-done.11.refs_2_ = bf16[8,32,128]{2,1,0:T(8,128)(2,1)S(1)} collective-permute-done((bf16[8,32,128]{2,1,0:T(8,128)(2,1)S(1)}, bf16[8,32,128]{2,1,0:T(8,128)(2,1)S(1)}, u32[]{:S(2)}, u32[]{:S(2)}) %collective-permute-start.11) | collective-permute-done | bytes 65568 | tf_op jit(solution)/shard_map/ppermute | solution.py:43
  41.0 3.3 %collective-permute-done.12.refs_0_ = bf16[8,32,128]{2,1,0:T(8,128)(2,1)S(1)} collective-permute-done((bf16[8,32,128]{2,1,0:T(8,128)(2,1)S(1)}, bf16[8,32,128]{2,1,0:T(8,128)(2,1)S(1)}, u32[]{:S(2)}, u32[]{:S(2)}) %collective-permute-start.12) | collective-permute-done | bytes 65568 | tf_op jit(solution)/shard_map/ppermute | solution.py:43
  45.7 1.7 %shard_map.80 = (f32[32,1024]{1,0:T(8,128)}, bf16[32,1024]{1,0:T(8,128)(2,1)S(1)}, bf16[8,32,128]{2,1,0:T(8,128)(2,1)S(1)}) custom-call(bf16[8,32,128]{2,1,0:T(8,128)(2,1)S(1)} %collective-permute-done.15.scale_ref, f32[32,1024]{1,0:T(8,128)S(1)} %shard_map.79.image_ref, f32[32,1024]{1,0:T(8,128)S(1)} %get-tuple-element.89.marg_ref, ...), custom_call_target="tpu_custom_call" | custom-call | flops 536870912 | bytes 2424832 | tf_op jit(solution)/shard_map/pallas_call | solution.py:49
  48.8 2.9 %collective-permute-start.18 = (bf16[8,32,128]{2,1,0:T(8,128)(2,1)S(1)}, bf16[8,32,128]{2,1,0:T(8,128)(2,1)S(1)}, u32[]{:S(2)}, u32[]{:S(2)}) collective-permute-start(bf16[8,32,128]{2,1,0:T(8,128)(2,1)S(1)} %get-tuple-element.109), channel_id=1, source_target_pairs={{0,4},{2,6},{4,0},{6,2},{8,12},{10,14},{12,8},{14,10},{16,20},{18,... | collective-permute-start | bytes 196616 | tf_op jit(solution)/shard_map/ppermute | solution.py:43
  51.6 4.4 %collective-permute-start.19 = (bf16[8,32,128]{2,1,0:T(8,128)(2,1)S(1)}, bf16[8,32,128]{2,1,0:T(8,128)(2,1)S(1)}, u32[]{:S(2)}, u32[]{:S(2)}) collective-permute-start(bf16[8,32,128]{2,1,0:T(8,128)(2,1)S(1)} %get-tuple-element.109), channel_id=1, source_target_pairs={{0,6},{2,4},{4,2},{6,0},{8,14},{10,12},{12,10},{14,8},{16,22},{18,... | collective-permute-start | bytes 196616 | tf_op jit(solution)/shard_map/ppermute | solution.py:43
  56.1 2.6 %collective-permute-done.19.refs_2_ = bf16[8,32,128]{2,1,0:T(8,128)(2,1)S(1)} collective-permute-done((bf16[8,32,128]{2,1,0:T(8,128)(2,1)S(1)}, bf16[8,32,128]{2,1,0:T(8,128)(2,1)S(1)}, u32[]{:S(2)}, u32[]{:S(2)}) %collective-permute-start.19) | collective-permute-done | bytes 65568 | tf_op jit(solution)/shard_map/ppermute | solution.py:43
  58.7 2.4 %collective-permute-start.20 = (bf16[8,32,128]{2,1,0:T(8,128)(2,1)S(1)}, bf16[8,32,128]{2,1,0:T(8,128)(2,1)S(1)}, u32[]{:S(2)}, u32[]{:S(2)}) collective-permute-start(bf16[8,32,128]{2,1,0:T(8,128)(2,1)S(1)} %get-tuple-element.93), channel_id=1, source_target_pairs={{0,8},{1,3},{2,10},{3,1},{4,12},{5,7},{6,14},{7,5},{8,0},{9,11},{1... | collective-permute-start | bytes 196616 | tf_op jit(solution)/shard_map/ppermute | solution.py:43
  62.5 1.5 %collective-permute-done.20.refs_0_ = bf16[8,32,128]{2,1,0:T(8,128)(2,1)S(1)} collective-permute-done((bf16[8,32,128]{2,1,0:T(8,128)(2,1)S(1)}, bf16[8,32,128]{2,1,0:T(8,128)(2,1)S(1)}, u32[]{:S(2)}, u32[]{:S(2)}) %collective-permute-start.20) | collective-permute-done | bytes 65568 | tf_op jit(solution)/shard_map/ppermute | solution.py:43
  65.3 1.5 %shard_map.85 = (f32[32,1024]{1,0:T(8,128)S(1)}, bf16[32,1024]{1,0:T(8,128)(2,1)S(1)}, bf16[8,32,128]{2,1,0:T(8,128)(2,1)S(1)}) custom-call(bf16[8,32,128]{2,1,0:T(8,128)(2,1)S(1)} %collective-permute-done.23.scale_ref, f32[32,1024]{1,0:T(8,128)S(1)} %shard_map.84.image_ref, f32[32,1024]{1,0:T(8,128)S(1)} %get-tuple-element.89.marg_ref, ...), custom_call_target="tpu_custom_call" | custom-call | flops 536870912 | bytes 2424832 | tf_op jit(solution)/shard_map/pallas_call | solution.py:49
  68.1 1.7 %collective-permute-start.25 = (bf16[8,32,128]{2,1,0:T(8,128)(2,1)S(1)}, bf16[8,32,128]{2,1,0:T(8,128)(2,1)S(1)}, u32[]{:S(2)}, u32[]{:S(2)}) collective-permute-start(bf16[8,32,128]{2,1,0:T(8,128)(2,1)S(1)} %get-tuple-element.107), channel_id=1, source_target_pairs={{0,2},{1,9},{2,0},{3,11},{4,6},{5,13},{6,4},{7,15},{8,10},{9,1},{1... | collective-permute-start | bytes 196616 | tf_op jit(solution)/shard_map/ppermute | solution.py:43
  69.9 3.3 %collective-permute-start.26 = (bf16[8,32,128]{2,1,0:T(8,128)(2,1)S(1)}, bf16[8,32,128]{2,1,0:T(8,128)(2,1)S(1)}, u32[]{:S(2)}, u32[]{:S(2)}) collective-permute-start(bf16[8,32,128]{2,1,0:T(8,128)(2,1)S(1)} %get-tuple-element.107), channel_id=1, source_target_pairs={{0,4},{2,6},{4,0},{6,2},{8,12},{10,14},{12,8},{14,10},{16,20},{18,... | collective-permute-start | bytes 196616 | tf_op jit(solution)/shard_map/ppermute | solution.py:43
  73.2 2.3 %collective-permute-start.27 = (bf16[8,32,128]{2,1,0:T(8,128)(2,1)S(1)}, bf16[8,32,128]{2,1,0:T(8,128)(2,1)S(1)}, u32[]{:S(2)}, u32[]{:S(2)}) collective-permute-start(bf16[8,32,128]{2,1,0:T(8,128)(2,1)S(1)} %get-tuple-element.107), channel_id=1, source_target_pairs={{0,6},{2,4},{4,2},{6,0},{8,14},{10,12},{12,10},{14,8},{16,22},{18,... | collective-permute-start | bytes 196616 | tf_op jit(solution)/shard_map/ppermute | solution.py:43
  76.0 4.2 %collective-permute-done.27.refs_2_ = bf16[8,32,128]{2,1,0:T(8,128)(2,1)S(1)} collective-permute-done((bf16[8,32,128]{2,1,0:T(8,128)(2,1)S(1)}, bf16[8,32,128]{2,1,0:T(8,128)(2,1)S(1)}, u32[]{:S(2)}, u32[]{:S(2)}) %collective-permute-start.27) | collective-permute-done | bytes 65568 | tf_op jit(solution)/shard_map/ppermute | solution.py:43
  83.6 2.6 %collective-permute-done.28.refs_0_ = bf16[8,32,128]{2,1,0:T(8,128)(2,1)S(1)} collective-permute-done((bf16[8,32,128]{2,1,0:T(8,128)(2,1)S(1)}, bf16[8,32,128]{2,1,0:T(8,128)(2,1)S(1)}, u32[]{:S(2)}, u32[]{:S(2)}) %collective-permute-start.28) | collective-permute-done | bytes 65568 | tf_op jit(solution)/shard_map/ppermute | solution.py:43
  (80 shorter events, 26.5 us)
Async XLA Ops:
  1.6 7.6 %collective-permute-start = (bf16[144,256]{1,0:T(8,128)(2,1)S(1)}, bf16[144,256]{1,0:T(8,128)(2,1)S(1)}, u32[]{:S(2)}, u32[]{:S(2)}) collective-permute-start(bf16[144,256]{1,0:T(8,128)(2,1)S(1)} %shard_map.67), channel_id=1, source_target_pairs={{0,8},{1,5},{2,10},{3,7},{4,12},{5,1},{6,14},{7,3},{8,0},{9,13},{1... | collective-permute-start | bytes 221192 | tf_op jit(solution)/shard_map/ppermute | solution.py:43
  5.7 4.4 %collective-permute-start.1 = (bf16[144,256]{1,0:T(8,128)(2,1)S(1)}, bf16[144,256]{1,0:T(8,128)(2,1)S(1)}, u32[]{:S(2)}, u32[]{:S(2)}) collective-permute-start(bf16[144,256]{1,0:T(8,128)(2,1)S(1)} %shard_map.67), channel_id=1, source_target_pairs={{0,2},{1,3},{2,0},{3,1},{4,6},{5,7},{6,4},{7,5},{8,10},{9,11},{10,... | collective-permute-start | bytes 221192 | tf_op jit(solution)/shard_map/ppermute | solution.py:43
  10.1 6.0 %collective-permute-start.2 = (bf16[288,256]{1,0:T(8,128)(2,1)S(1)}, bf16[288,256]{1,0:T(8,128)(2,1)S(1)}, u32[]{:S(2)}, u32[]{:S(2)}) collective-permute-start(bf16[288,256]{1,0:T(8,128)(2,1)S(1)} %pad_maximum_fusion.1), channel_id=1, source_target_pairs={{0,4},{1,9},{2,6},{3,11},{4,0},{5,13},{6,2},{7,15},{8,12},{9,1},{1... | collective-permute-start | bytes 442376 | tf_op jit(solution)/shard_map/ppermute | solution.py:43
  11.7 4.4 %collective-permute-start.3 = (bf16[144,256]{1,0:T(8,128)(2,1)S(1)}, bf16[144,256]{1,0:T(8,128)(2,1)S(1)}, u32[]{:S(2)}, u32[]{:S(2)}) collective-permute-start(bf16[144,256]{1,0:T(8,128)(2,1)S(1)} %collective-permute-done), channel_id=1, source_target_pairs={{0,2},{1,3},{2,0},{3,1},{4,6},{5,7},{6,4},{7,5},{8,10},{9,11},{10,... | collective-permute-start | bytes 221192 | tf_op jit(solution)/shard_map/ppermute | solution.py:43
  16.1 3.7 %collective-permute-start.5 = (bf16[576,256]{1,0:T(8,128)(2,1)S(1)}, bf16[576,256]{1,0:T(8,128)(2,1)S(1)}, u32[]{:S(2)}, u32[]{:S(2)}) collective-permute-start(bf16[576,256]{1,0:T(8,128)(2,1)S(1)} %pad_maximum_fusion.held_ref.refs_9_.refs_0_), channel_id=1, source_target_pairs={{0,1},{1,0},{2,3},{3,2},{4,5},{5,4},{6,7},{7,6},{8,9},{9,8},{10,11... | collective-permute-start | bytes 884744 | tf_op jit(solution)/shard_map/ppermute | solution.py:43
  16.2 3.1 %collective-permute-start.6 = (bf16[288,256]{1,0:T(8,128)(2,1)S(1)}, bf16[288,256]{1,0:T(8,128)(2,1)S(1)}, u32[]{:S(2)}, u32[]{:S(2)}) collective-permute-start(bf16[288,256]{1,0:T(8,128)(2,1)S(1)} %constant_dynamic-update-slice_fusion.held_ref.refs_10_.refs_1_), channel_id=1, source_target_pairs={{0,1},{1,0},{2,3},{3,2},{4,5},{5,4},{6,7},{7,6},{8,9},{9,8},{10,11... | collective-permute-start | bytes 442376 | tf_op jit(solution)/shard_map/ppermute | solution.py:43
  16.8 5.8 %collective-permute-start.4 = (bf16[288,256]{1,0:T(8,128)(2,1)S(1)}, bf16[288,256]{1,0:T(8,128)(2,1)S(1)}, u32[]{:S(2)}, u32[]{:S(2)}) collective-permute-start(bf16[288,256]{1,0:T(8,128)(2,1)S(1)} %collective-permute-done.2), channel_id=1, source_target_pairs={{0,2},{1,3},{2,0},{3,1},{4,6},{5,7},{6,4},{7,5},{8,10},{9,11},{10,... | collective-permute-start | bytes 442376 | tf_op jit(solution)/shard_map/ppermute | solution.py:43
  26.4 7.4 %collective-permute-start.9 = (bf16[8,32,128]{2,1,0:T(8,128)(2,1)S(1)}, bf16[8,32,128]{2,1,0:T(8,128)(2,1)S(1)}, u32[]{:S(2)}, u32[]{:S(2)}) collective-permute-start(bf16[8,32,128]{2,1,0:T(8,128)(2,1)S(1)} %get-tuple-element.111), channel_id=1, source_target_pairs={{0,2},{1,9},{2,0},{3,11},{4,6},{5,13},{6,4},{7,15},{8,10},{9,1},{1... | collective-permute-start | bytes 196616 | tf_op jit(solution)/shard_map/ppermute | solution.py:43
  28.0 6.1 %collective-permute-start.10 = (bf16[8,32,128]{2,1,0:T(8,128)(2,1)S(1)}, bf16[8,32,128]{2,1,0:T(8,128)(2,1)S(1)}, u32[]{:S(2)}, u32[]{:S(2)}) collective-permute-start(bf16[8,32,128]{2,1,0:T(8,128)(2,1)S(1)} %get-tuple-element.111), channel_id=1, source_target_pairs={{0,4},{2,6},{4,0},{6,2},{8,12},{10,14},{12,8},{14,10},{16,20},{18,... | collective-permute-start | bytes 196616 | tf_op jit(solution)/shard_map/ppermute | solution.py:43
  30.6 7.7 %collective-permute-start.11 = (bf16[8,32,128]{2,1,0:T(8,128)(2,1)S(1)}, bf16[8,32,128]{2,1,0:T(8,128)(2,1)S(1)}, u32[]{:S(2)}, u32[]{:S(2)}) collective-permute-start(bf16[8,32,128]{2,1,0:T(8,128)(2,1)S(1)} %get-tuple-element.111), channel_id=1, source_target_pairs={{0,6},{2,4},{4,2},{6,0},{8,14},{10,12},{12,10},{14,8},{16,22},{18,... | collective-permute-start | bytes 196616 | tf_op jit(solution)/shard_map/ppermute | solution.py:43
  38.4 5.9 %collective-permute-start.12 = (bf16[8,32,128]{2,1,0:T(8,128)(2,1)S(1)}, bf16[8,32,128]{2,1,0:T(8,128)(2,1)S(1)}, u32[]{:S(2)}, u32[]{:S(2)}) collective-permute-start(bf16[8,32,128]{2,1,0:T(8,128)(2,1)S(1)} %get-tuple-element.88), channel_id=1, source_target_pairs={{0,8},{1,3},{2,10},{3,1},{4,12},{5,7},{6,14},{7,5},{8,0},{9,11},{1... | collective-permute-start | bytes 196616 | tf_op jit(solution)/shard_map/ppermute | solution.py:43
  39.5 4.8 %collective-permute-start.13 = (bf16[8,32,128]{2,1,0:T(8,128)(2,1)S(1)}, bf16[8,32,128]{2,1,0:T(8,128)(2,1)S(1)}, u32[]{:S(2)}, u32[]{:S(2)}) collective-permute-start(bf16[8,32,128]{2,1,0:T(8,128)(2,1)S(1)} %get-tuple-element.88), channel_id=1, source_target_pairs={{1,5},{3,7},{5,1},{7,3},{9,13},{11,15},{13,9},{15,11},{17,21},{19,... | collective-permute-start | bytes 196616 | tf_op jit(solution)/shard_map/ppermute | solution.py:43
  40.2 4.1 %collective-permute-start.14 = (bf16[8,32,128]{2,1,0:T(8,128)(2,1)S(1)}, bf16[8,32,128]{2,1,0:T(8,128)(2,1)S(1)}, u32[]{:S(2)}, u32[]{:S(2)}) collective-permute-start(bf16[8,32,128]{2,1,0:T(8,128)(2,1)S(1)} %get-tuple-element.88), channel_id=1, source_target_pairs={{1,7},{3,5},{5,3},{7,1},{9,15},{11,13},{13,11},{15,9},{17,23},{19,... | collective-permute-start | bytes 196616 | tf_op jit(solution)/shard_map/ppermute | solution.py:43
  48.7 7.4 %collective-permute-start.17 = (bf16[8,32,128]{2,1,0:T(8,128)(2,1)S(1)}, bf16[8,32,128]{2,1,0:T(8,128)(2,1)S(1)}, u32[]{:S(2)}, u32[]{:S(2)}) collective-permute-start(bf16[8,32,128]{2,1,0:T(8,128)(2,1)S(1)} %get-tuple-element.109), channel_id=1, source_target_pairs={{0,2},{1,9},{2,0},{3,11},{4,6},{5,13},{6,4},{7,15},{8,10},{9,1},{1... | collective-permute-start | bytes 196616 | tf_op jit(solution)/shard_map/ppermute | solution.py:43
  48.8 7.3 %collective-permute-start.18 = (bf16[8,32,128]{2,1,0:T(8,128)(2,1)S(1)}, bf16[8,32,128]{2,1,0:T(8,128)(2,1)S(1)}, u32[]{:S(2)}, u32[]{:S(2)}) collective-permute-start(bf16[8,32,128]{2,1,0:T(8,128)(2,1)S(1)} %get-tuple-element.109), channel_id=1, source_target_pairs={{0,4},{2,6},{4,0},{6,2},{8,12},{10,14},{12,8},{14,10},{16,20},{18,... | collective-permute-start | bytes 196616 | tf_op jit(solution)/shard_map/ppermute | solution.py:43
  51.6 7.1 %collective-permute-start.19 = (bf16[8,32,128]{2,1,0:T(8,128)(2,1)S(1)}, bf16[8,32,128]{2,1,0:T(8,128)(2,1)S(1)}, u32[]{:S(2)}, u32[]{:S(2)}) collective-permute-start(bf16[8,32,128]{2,1,0:T(8,128)(2,1)S(1)} %get-tuple-element.109), channel_id=1, source_target_pairs={{0,6},{2,4},{4,2},{6,0},{8,14},{10,12},{12,10},{14,8},{16,22},{18,... | collective-permute-start | bytes 196616 | tf_op jit(solution)/shard_map/ppermute | solution.py:43
  58.7 5.2 %collective-permute-start.20 = (bf16[8,32,128]{2,1,0:T(8,128)(2,1)S(1)}, bf16[8,32,128]{2,1,0:T(8,128)(2,1)S(1)}, u32[]{:S(2)}, u32[]{:S(2)}) collective-permute-start(bf16[8,32,128]{2,1,0:T(8,128)(2,1)S(1)} %get-tuple-element.93), channel_id=1, source_target_pairs={{0,8},{1,3},{2,10},{3,1},{4,12},{5,7},{6,14},{7,5},{8,0},{9,11},{1... | collective-permute-start | bytes 196616 | tf_op jit(solution)/shard_map/ppermute | solution.py:43
  61.1 2.8 %collective-permute-start.21 = (bf16[8,32,128]{2,1,0:T(8,128)(2,1)S(1)}, bf16[8,32,128]{2,1,0:T(8,128)(2,1)S(1)}, u32[]{:S(2)}, u32[]{:S(2)}) collective-permute-start(bf16[8,32,128]{2,1,0:T(8,128)(2,1)S(1)} %get-tuple-element.93), channel_id=1, source_target_pairs={{1,5},{3,7},{5,1},{7,3},{9,13},{11,15},{13,9},{15,11},{17,21},{19,... | collective-permute-start | bytes 196616 | tf_op jit(solution)/shard_map/ppermute | solution.py:43
  68.1 7.4 %collective-permute-start.25 = (bf16[8,32,128]{2,1,0:T(8,128)(2,1)S(1)}, bf16[8,32,128]{2,1,0:T(8,128)(2,1)S(1)}, u32[]{:S(2)}, u32[]{:S(2)}) collective-permute-start(bf16[8,32,128]{2,1,0:T(8,128)(2,1)S(1)} %get-tuple-element.107), channel_id=1, source_target_pairs={{0,2},{1,9},{2,0},{3,11},{4,6},{5,13},{6,4},{7,15},{8,10},{9,1},{1... | collective-permute-start | bytes 196616 | tf_op jit(solution)/shard_map/ppermute | solution.py:43
  69.9 6.1 %collective-permute-start.26 = (bf16[8,32,128]{2,1,0:T(8,128)(2,1)S(1)}, bf16[8,32,128]{2,1,0:T(8,128)(2,1)S(1)}, u32[]{:S(2)}, u32[]{:S(2)}) collective-permute-start(bf16[8,32,128]{2,1,0:T(8,128)(2,1)S(1)} %get-tuple-element.107), channel_id=1, source_target_pairs={{0,4},{2,6},{4,0},{6,2},{8,12},{10,14},{12,8},{14,10},{16,20},{18,... | collective-permute-start | bytes 196616 | tf_op jit(solution)/shard_map/ppermute | solution.py:43
  73.2 7.1 %collective-permute-start.27 = (bf16[8,32,128]{2,1,0:T(8,128)(2,1)S(1)}, bf16[8,32,128]{2,1,0:T(8,128)(2,1)S(1)}, u32[]{:S(2)}, u32[]{:S(2)}) collective-permute-start(bf16[8,32,128]{2,1,0:T(8,128)(2,1)S(1)} %get-tuple-element.107), channel_id=1, source_target_pairs={{0,6},{2,4},{4,2},{6,0},{8,14},{10,12},{12,10},{14,8},{16,22},{18,... | collective-permute-start | bytes 196616 | tf_op jit(solution)/shard_map/ppermute | solution.py:43
  80.3 5.9 %collective-permute-start.28 = (bf16[8,32,128]{2,1,0:T(8,128)(2,1)S(1)}, bf16[8,32,128]{2,1,0:T(8,128)(2,1)S(1)}, u32[]{:S(2)}, u32[]{:S(2)}) collective-permute-start(bf16[8,32,128]{2,1,0:T(8,128)(2,1)S(1)} %get-tuple-element.96), channel_id=1, source_target_pairs={{0,8},{1,3},{2,10},{3,1},{4,12},{5,7},{6,14},{7,5},{8,0},{9,11},{1... | collective-permute-start | bytes 196616 | tf_op jit(solution)/shard_map/ppermute | solution.py:43
  81.6 4.7 %collective-permute-start.29 = (bf16[8,32,128]{2,1,0:T(8,128)(2,1)S(1)}, bf16[8,32,128]{2,1,0:T(8,128)(2,1)S(1)}, u32[]{:S(2)}, u32[]{:S(2)}) collective-permute-start(bf16[8,32,128]{2,1,0:T(8,128)(2,1)S(1)} %get-tuple-element.96), channel_id=1, source_target_pairs={{1,5},{3,7},{5,1},{7,3},{9,13},{11,15},{13,9},{15,11},{17,21},{19,... | collective-permute-start | bytes 196616 | tf_op jit(solution)/shard_map/ppermute | solution.py:43
  82.2 4.0 %collective-permute-start.30 = (bf16[8,32,128]{2,1,0:T(8,128)(2,1)S(1)}, bf16[8,32,128]{2,1,0:T(8,128)(2,1)S(1)}, u32[]{:S(2)}, u32[]{:S(2)}) collective-permute-start(bf16[8,32,128]{2,1,0:T(8,128)(2,1)S(1)} %get-tuple-element.96), channel_id=1, source_target_pairs={{1,7},{3,5},{5,3},{7,1},{9,15},{11,13},{13,11},{15,9},{17,23},{19,... | collective-permute-start | bytes 196616 | tf_op jit(solution)/shard_map/ppermute | solution.py:43
  (10 other events, 19.9 us)

commit v8 on v7

--- a/solution.py
+++ b/solution.py
@@ -1,5 +1,4 @@
 import functools
-import itertools
 import math
 
 import jax
@@ -26,8 +25,9 @@
 
 
 def rounds(core, top):
-    groups = [list(range(low, min(low + 2, top))) for low in range(1, top, 2)]
-    return groups[::-1] if core else groups
+    bits = list(range(1, top))
+    bits = bits[core:] + bits[:core]
+    return [bits[low : low + 2] for low in range(0, len(bits), 2)]
 
 
 def flips_of(bits):
@@ -39,8 +39,7 @@
 
 def exchange(block, *flips):
     devices = lax.axis_size("row")
-    pairs = [(d, d ^ flips[d % len(flips)]) for d in range(devices) if flips[d % len(flips)]]
-    return lax.ppermute(block, "row", pairs)
+    return lax.ppermute(block, "row", [(d, d ^ flips[d % len(flips)]) for d in range(devices)])
 
 
 def call(body, outs, *args, flops=0):
@@ -79,13 +78,14 @@
     copies[0].wait()
     counts = lax.dot_general(
         jnp.ones((EXTRA, cand_ref.shape[1]), BF16),
-        hot(cand_ref[...], LANES).astype(BF16),
+        hot(cand_ref[...]).astype(BF16),
         (((1,), (1,)), ((), ())),
         preferred_element_type=F32,
     )
     high = counts.astype(BF16).astype(F32)
-    even = lax.broadcasted_iota(jnp.int32, (EXTRA, LANES), 0) % 2 == 0
-    out_ref[rows:, LANES:] = jnp.where(even, high, counts - high).astype(BF16)
+    even = lax.broadcasted_iota(jnp.int32, counts.shape, 0) % 2 == 0
+    out_ref[rows:, LANES:] = jnp.zeros((EXTRA, LANES), BF16)
+    out_ref[rows:, LANES : LANES + CLASSES] = jnp.where(even, high, counts - high).astype(BF16)
     copies[1].wait()
     out_ref[rows:, :LANES] = jnp.broadcast_to(
         tgt_ref[...].astype(F32), (EXTRA, LANES)
@@ -324,7 +324,7 @@
         sent = column.astype(BF16)
         order = list(zip(rounds(0, top), rounds(1, top)))
         for place, pair in enumerate(order):
-            flips = list(itertools.zip_longest(*[flips_of(bits) for bits in pair], fillvalue=0))
+            flips = list(zip(*[flips_of(bits) for bits in pair]))
             found = [exchange(sent, *turn) for turn in flips]
             if place < len(order) - 1:
                 column, sent = call(

time: 89.4 us -> 77.9 us (0.87)
  starting transfers between devices: 42.5 us -> 26.9 us
  waiting for transfers between devices: 29.7 us -> 34.2 us
    ppermute x32 -> x26, starting transfers between devices: 42.5 us -> 26.9 us  [exchange(): lax.ppermute(block, 'row', [(d, d ^ flips[d % len(flips)]) for d in range...]
    ppermute x32 -> x26, waiting for transfers between devices: 29.7 us -> 34.2 us  [exchange(): lax.ppermute(block, 'row', [(d, d ^ flips[d % len(flips)]) for d in range...]
  transfers between devices with their start and end apart: 32 -> 26, of which waited for: 18 -> 22; matrix products, arithmetic and copies ran while one was open for 2% -> 3% of each run, Pallas kernels for 7% -> 8%
where the time goes in v8:
time: 77.9 us; the launch traced here: 77.7 us
  waiting for transfers between devices  34.2 us (44%)
  starting transfers between devices  26.9 us (35%)
  Pallas kernels  13 us (17%)
  other arithmetic  2.25 us (3%)
  between operations  0.89 us (1%)
    ppermute x26, waiting for transfers between devices, exchange(): lax.ppermute(block, 'row', [(d, d ^ flips[d % len(flips)]) for d in range...  34.2 us
    ppermute x26, starting transfers between devices, exchange(): lax.ppermute(block, 'row', [(d, d ^ flips[d % len(flips)]) for d in range...  26.9 us
    pallas_call x22, Pallas kernels, call(): pl.pallas_call(body, out_shape=[pltpu.VMEM(shape, dtype) for shape, dtype...  10.7 us
  transfers between devices with their start and end apart: 26, of which 22 were waited for; matrix products, arithmetic and copies ran while one was open for 3% of the time, Pallas kernels for 8%

profile of v8, /device:TPU:0, one launch (start us, length us, event | category | flops | bytes accessed | tf_op | source)
XLA Modules:
  0.0 77.7 jit_solution(3699074967875990706)
XLA Ops:
  1.6 4.1 %collective-permute-start = (bf16[144,256]{1,0:T(8,128)(2,1)S(1)}, bf16[144,256]{1,0:T(8,128)(2,1)S(1)}, u32[]{:S(2)}, u32[]{:S(2)}) collective-permute-start(bf16[144,256]{1,0:T(8,128)(2,1)S(1)} %shard_map.67), channel_id=1, source_target_pairs={{0,8},{1,5},{2,10},{3,7},{4,12},{5,1},{6,14},{7,3},{8,0},{9,13},{1... | collective-permute-start | bytes 221192 | tf_op jit(solution)/shard_map/ppermute | solution.py:42
  5.7 1.5 %collective-permute-start.1 = (bf16[144,256]{1,0:T(8,128)(2,1)S(1)}, bf16[144,256]{1,0:T(8,128)(2,1)S(1)}, u32[]{:S(2)}, u32[]{:S(2)}) collective-permute-start(bf16[144,256]{1,0:T(8,128)(2,1)S(1)} %shard_map.67), channel_id=1, source_target_pairs={{0,2},{1,3},{2,0},{3,1},{4,6},{5,7},{6,4},{7,5},{8,10},{9,11},{10,... | collective-permute-start | bytes 221192 | tf_op jit(solution)/shard_map/ppermute | solution.py:42
  7.2 1.3 %fusion = f32[1024]{0:T(1024)S(1)} fusion(bf16[1024,256]{1,0:T(8,128)(2,1)} %param.4), kind=kLoop, calls=%fused_computation.2 | loop fusion | flops 785408 | bytes 528384 | tf_op jit(solution)/shard_map/reduce_sum | solution.py:60
  10.1 1.6 %collective-permute-start.2 = (bf16[288,256]{1,0:T(8,128)(2,1)S(1)}, bf16[288,256]{1,0:T(8,128)(2,1)S(1)}, u32[]{:S(2)}, u32[]{:S(2)}) collective-permute-start(bf16[288,256]{1,0:T(8,128)(2,1)S(1)} %pad_maximum_fusion.1), channel_id=1, source_target_pairs={{0,4},{1,9},{2,6},{3,11},{4,0},{5,13},{6,2},{7,15},{8,12},{9,1},{1... | collective-permute-start | bytes 442376 | tf_op jit(solution)/shard_map/ppermute | solution.py:42
  11.7 1.5 %collective-permute-start.3 = (bf16[144,256]{1,0:T(8,128)(2,1)S(1)}, bf16[144,256]{1,0:T(8,128)(2,1)S(1)}, u32[]{:S(2)}, u32[]{:S(2)}) collective-permute-start(bf16[144,256]{1,0:T(8,128)(2,1)S(1)} %collective-permute-done), channel_id=1, source_target_pairs={{0,2},{1,3},{2,0},{3,1},{4,6},{5,7},{6,4},{7,5},{8,10},{9,11},{10,... | collective-permute-start | bytes 221192 | tf_op jit(solution)/shard_map/ppermute | solution.py:42
  13.2 2.8 %collective-permute-done.3 = bf16[144,256]{1,0:T(8,128)(2,1)S(1)} collective-permute-done((bf16[144,256]{1,0:T(8,128)(2,1)S(1)}, bf16[144,256]{1,0:T(8,128)(2,1)S(1)}, u32[]{:S(2)}, u32[]{:S(2)}) %collective-permute-start.3) | collective-permute-done | bytes 73760 | tf_op jit(solution)/shard_map/ppermute | solution.py:42
  16.8 1.5 %collective-permute-start.4 = (bf16[288,256]{1,0:T(8,128)(2,1)S(1)}, bf16[288,256]{1,0:T(8,128)(2,1)S(1)}, u32[]{:S(2)}, u32[]{:S(2)}) collective-permute-start(bf16[288,256]{1,0:T(8,128)(2,1)S(1)} %collective-permute-done.2), channel_id=1, source_target_pairs={{0,2},{1,3},{2,0},{3,1},{4,6},{5,7},{6,4},{7,5},{8,10},{9,11},{10,... | collective-permute-start | bytes 442376 | tf_op jit(solution)/shard_map/ppermute | solution.py:42
  20.4 2.2 %collective-permute-done.4.held_ref.refs_11_.refs_2_ = bf16[288,256]{1,0:T(8,128)(2,1)S(1)} collective-permute-done((bf16[288,256]{1,0:T(8,128)(2,1)S(1)}, bf16[288,256]{1,0:T(8,128)(2,1)S(1)}, u32[]{:S(2)}, u32[]{:S(2)}) %collective-permute-start.4) | collective-permute-done | bytes 147488 | tf_op jit(solution)/shard_map/ppermute | solution.py:42
  26.4 1.6 %collective-permute-start.9 = (bf16[8,32,128]{2,1,0:T(8,128)(2,1)S(1)}, bf16[8,32,128]{2,1,0:T(8,128)(2,1)S(1)}, u32[]{:S(2)}, u32[]{:S(2)}) collective-permute-start(bf16[8,32,128]{2,1,0:T(8,128)(2,1)S(1)} %get-tuple-element.107), channel_id=1, source_target_pairs={{0,2},{1,5},{2,0},{3,7},{4,6},{5,1},{6,4},{7,3},{8,10},{9,13},{10,... | collective-permute-start | bytes 196616 | tf_op jit(solution)/shard_map/ppermute | solution.py:42
  30.7 1.5 %collective-permute-done.10.refs_1_ = bf16[8,32,128]{2,1,0:T(8,128)(2,1)S(1)} collective-permute-done((bf16[8,32,128]{2,1,0:T(8,128)(2,1)S(1)}, bf16[8,32,128]{2,1,0:T(8,128)(2,1)S(1)}, u32[]{:S(2)}, u32[]{:S(2)}) %collective-permute-start.10) | collective-permute-done | bytes 65568 | tf_op jit(solution)/shard_map/ppermute | solution.py:42
  32.2 2.2 %collective-permute-done.11.refs_2_ = bf16[8,32,128]{2,1,0:T(8,128)(2,1)S(1)} collective-permute-done((bf16[8,32,128]{2,1,0:T(8,128)(2,1)S(1)}, bf16[8,32,128]{2,1,0:T(8,128)(2,1)S(1)}, u32[]{:S(2)}, u32[]{:S(2)}) %collective-permute-start.11) | collective-permute-done | bytes 65568 | tf_op jit(solution)/shard_map/ppermute | solution.py:42
  34.5 1.3 %collective-permute-start.12 = (bf16[8,32,128]{2,1,0:T(8,128)(2,1)S(1)}, bf16[8,32,128]{2,1,0:T(8,128)(2,1)S(1)}, u32[]{:S(2)}, u32[]{:S(2)}) collective-permute-start(bf16[8,32,128]{2,1,0:T(8,128)(2,1)S(1)} %get-tuple-element.86), channel_id=1, source_target_pairs={{0,8},{1,3},{2,10},{3,1},{4,12},{5,7},{6,14},{7,5},{8,0},{9,11},{1... | collective-permute-start | bytes 196616 | tf_op jit(solution)/shard_map/ppermute | solution.py:42
  35.9 4.5 %collective-permute-done.12.refs_0_ = bf16[8,32,128]{2,1,0:T(8,128)(2,1)S(1)} collective-permute-done((bf16[8,32,128]{2,1,0:T(8,128)(2,1)S(1)}, bf16[8,32,128]{2,1,0:T(8,128)(2,1)S(1)}, u32[]{:S(2)}, u32[]{:S(2)}) %collective-permute-start.12) | collective-permute-done | bytes 65568 | tf_op jit(solution)/shard_map/ppermute | solution.py:42
  41.8 1.7 %shard_map.80 = (f32[32,1024]{1,0:T(8,128)}, bf16[32,1024]{1,0:T(8,128)(2,1)S(1)}, bf16[8,32,128]{2,1,0:T(8,128)(2,1)S(1)}) custom-call(bf16[8,32,128]{2,1,0:T(8,128)(2,1)S(1)} %collective-permute-done.13.scale_ref, f32[32,1024]{1,0:T(8,128)S(1)} %shard_map.79.image_ref, f32[32,1024]{1,0:T(8,128)S(1)} %get-tuple-element.87.marg_ref, ...), custom_call_target="tpu_custom_call" | custom-call | flops 536870912 | bytes 2424832 | tf_op jit(solution)/shard_map/pallas_call | solution.py:48
  45.6 2.8 %collective-permute-start.17 = (bf16[8,32,128]{2,1,0:T(8,128)(2,1)S(1)}, bf16[8,32,128]{2,1,0:T(8,128)(2,1)S(1)}, u32[]{:S(2)}, u32[]{:S(2)}) collective-permute-start(bf16[8,32,128]{2,1,0:T(8,128)(2,1)S(1)} %get-tuple-element.105), channel_id=1, source_target_pairs={{0,6},{1,13},{2,4},{3,15},{4,2},{5,9},{6,0},{7,11},{8,14},{9,5},{1... | collective-permute-start | bytes 196616 | tf_op jit(solution)/shard_map/ppermute | solution.py:42
  49.9 1.4 %collective-permute-done.17.refs_2_ = bf16[8,32,128]{2,1,0:T(8,128)(2,1)S(1)} collective-permute-done((bf16[8,32,128]{2,1,0:T(8,128)(2,1)S(1)}, bf16[8,32,128]{2,1,0:T(8,128)(2,1)S(1)}, u32[]{:S(2)}, u32[]{:S(2)}) %collective-permute-start.17) | collective-permute-done | bytes 65568 | tf_op jit(solution)/shard_map/ppermute | solution.py:42
  51.3 2.5 %collective-permute-start.18 = (bf16[8,32,128]{2,1,0:T(8,128)(2,1)S(1)}, bf16[8,32,128]{2,1,0:T(8,128)(2,1)S(1)}, u32[]{:S(2)}, u32[]{:S(2)}) collective-permute-start(bf16[8,32,128]{2,1,0:T(8,128)(2,1)S(1)} %get-tuple-element.91), channel_id=1, source_target_pairs={{0,8},{1,3},{2,10},{3,1},{4,12},{5,7},{6,14},{7,5},{8,0},{9,11},{1... | collective-permute-start | bytes 196616 | tf_op jit(solution)/shard_map/ppermute | solution.py:42
  53.8 2.7 %collective-permute-done.18.refs_0_ = bf16[8,32,128]{2,1,0:T(8,128)(2,1)S(1)} collective-permute-done((bf16[8,32,128]{2,1,0:T(8,128)(2,1)S(1)}, bf16[8,32,128]{2,1,0:T(8,128)(2,1)S(1)}, u32[]{:S(2)}, u32[]{:S(2)}) %collective-permute-start.18) | collective-permute-done | bytes 65568 | tf_op jit(solution)/shard_map/ppermute | solution.py:42
  57.9 1.5 %shard_map.85 = (f32[32,1024]{1,0:T(8,128)S(1)}, bf16[32,1024]{1,0:T(8,128)(2,1)S(1)}, bf16[8,32,128]{2,1,0:T(8,128)(2,1)S(1)}) custom-call(bf16[8,32,128]{2,1,0:T(8,128)(2,1)S(1)} %collective-permute-done.19.scale_ref, f32[32,1024]{1,0:T(8,128)S(1)} %shard_map.84.image_ref, f32[32,1024]{1,0:T(8,128)S(1)} %get-tuple-element.87.marg_ref, ...), custom_call_target="tpu_custom_call" | custom-call | flops 536870912 | bytes 2424832 | tf_op jit(solution)/shard_map/pallas_call | solution.py:48
  61.8 1.9 %collective-permute-start.22 = (bf16[8,32,128]{2,1,0:T(8,128)(2,1)S(1)}, bf16[8,32,128]{2,1,0:T(8,128)(2,1)S(1)}, u32[]{:S(2)}, u32[]{:S(2)}) collective-permute-start(bf16[8,32,128]{2,1,0:T(8,128)(2,1)S(1)} %get-tuple-element.103), channel_id=1, source_target_pairs={{0,4},{1,9},{2,6},{3,11},{4,0},{5,13},{6,2},{7,15},{8,12},{9,1},{1... | collective-permute-start | bytes 196616 | tf_op jit(solution)/shard_map/ppermute | solution.py:42
  65.1 1.4 %collective-permute-done.22.refs_1_ = bf16[8,32,128]{2,1,0:T(8,128)(2,1)S(1)} collective-permute-done((bf16[8,32,128]{2,1,0:T(8,128)(2,1)S(1)}, bf16[8,32,128]{2,1,0:T(8,128)(2,1)S(1)}, u32[]{:S(2)}, u32[]{:S(2)}) %collective-permute-start.22) | collective-permute-done | bytes 65568 | tf_op jit(solution)/shard_map/ppermute | solution.py:42
  66.5 3.1 %collective-permute-done.23.refs_2_ = bf16[8,32,128]{2,1,0:T(8,128)(2,1)S(1)} collective-permute-done((bf16[8,32,128]{2,1,0:T(8,128)(2,1)S(1)}, bf16[8,32,128]{2,1,0:T(8,128)(2,1)S(1)}, u32[]{:S(2)}, u32[]{:S(2)}) %collective-permute-start.23) | collective-permute-done | bytes 65568 | tf_op jit(solution)/shard_map/ppermute | solution.py:42
  71.1 3.9 %collective-permute-done.24.refs_0_ = bf16[8,32,128]{2,1,0:T(8,128)(2,1)S(1)} collective-permute-done((bf16[8,32,128]{2,1,0:T(8,128)(2,1)S(1)}, bf16[8,32,128]{2,1,0:T(8,128)(2,1)S(1)}, u32[]{:S(2)}, u32[]{:S(2)}) %collective-permute-start.24) | collective-permute-done | bytes 65568 | tf_op jit(solution)/shard_map/ppermute | solution.py:42
  76.3 1.4 %shard_map.90 = (f32[32,1024]{1,0:T(8,128)}, f32[32,128]{1,0:T(8,128)}) custom-call(bf16[8,32,128]{2,1,0:T(8,128)(2,1)S(1)} %collective-permute-done.25.scale_ref, f32[32,1024]{1,0:T(8,128)S(1)} %shard_map.89.image_ref, f32[32,1024]{1,0:T(8,128)S(1)} %get-tuple-element.95.u_ref, f32[8,32,128]{2,1,0:T(8,128)S(1)} %get-tuple-element.100.scale_v_ref, ...), custom_call_target="tpu_custom_call" | custom-call | tf_op jit(solution)/shard_map/pallas_call | solution.py:347
  (68 shorter events, 24.7 us)
Async XLA Ops:
  1.6 7.6 %collective-permute-start = (bf16[144,256]{1,0:T(8,128)(2,1)S(1)}, bf16[144,256]{1,0:T(8,128)(2,1)S(1)}, u32[]{:S(2)}, u32[]{:S(2)}) collective-permute-start(bf16[144,256]{1,0:T(8,128)(2,1)S(1)} %shard_map.67), channel_id=1, source_target_pairs={{0,8},{1,5},{2,10},{3,7},{4,12},{5,1},{6,14},{7,3},{8,0},{9,13},{1... | collective-permute-start | bytes 221192 | tf_op jit(solution)/shard_map/ppermute | solution.py:42
  5.7 4.4 %collective-permute-start.1 = (bf16[144,256]{1,0:T(8,128)(2,1)S(1)}, bf16[144,256]{1,0:T(8,128)(2,1)S(1)}, u32[]{:S(2)}, u32[]{:S(2)}) collective-permute-start(bf16[144,256]{1,0:T(8,128)(2,1)S(1)} %shard_map.67), channel_id=1, source_target_pairs={{0,2},{1,3},{2,0},{3,1},{4,6},{5,7},{6,4},{7,5},{8,10},{9,11},{10,... | collective-permute-start | bytes 221192 | tf_op jit(solution)/shard_map/ppermute | solution.py:42
  10.1 6.0 %collective-permute-start.2 = (bf16[288,256]{1,0:T(8,128)(2,1)S(1)}, bf16[288,256]{1,0:T(8,128)(2,1)S(1)}, u32[]{:S(2)}, u32[]{:S(2)}) collective-permute-start(bf16[288,256]{1,0:T(8,128)(2,1)S(1)} %pad_maximum_fusion.1), channel_id=1, source_target_pairs={{0,4},{1,9},{2,6},{3,11},{4,0},{5,13},{6,2},{7,15},{8,12},{9,1},{1... | collective-permute-start | bytes 442376 | tf_op jit(solution)/shard_map/ppermute | solution.py:42
  11.7 4.4 %collective-permute-start.3 = (bf16[144,256]{1,0:T(8,128)(2,1)S(1)}, bf16[144,256]{1,0:T(8,128)(2,1)S(1)}, u32[]{:S(2)}, u32[]{:S(2)}) collective-permute-start(bf16[144,256]{1,0:T(8,128)(2,1)S(1)} %collective-permute-done), channel_id=1, source_target_pairs={{0,2},{1,3},{2,0},{3,1},{4,6},{5,7},{6,4},{7,5},{8,10},{9,11},{10,... | collective-permute-start | bytes 221192 | tf_op jit(solution)/shard_map/ppermute | solution.py:42
  16.1 3.7 %collective-permute-start.5 = (bf16[576,256]{1,0:T(8,128)(2,1)S(1)}, bf16[576,256]{1,0:T(8,128)(2,1)S(1)}, u32[]{:S(2)}, u32[]{:S(2)}) collective-permute-start(bf16[576,256]{1,0:T(8,128)(2,1)S(1)} %pad_maximum_fusion.held_ref.refs_9_.refs_0_), channel_id=1, source_target_pairs={{0,1},{1,0},{2,3},{3,2},{4,5},{5,4},{6,7},{7,6},{8,9},{9,8},{10,11... | collective-permute-start | bytes 884744 | tf_op jit(solution)/shard_map/ppermute | solution.py:42
  16.2 3.1 %collective-permute-start.6 = (bf16[288,256]{1,0:T(8,128)(2,1)S(1)}, bf16[288,256]{1,0:T(8,128)(2,1)S(1)}, u32[]{:S(2)}, u32[]{:S(2)}) collective-permute-start(bf16[288,256]{1,0:T(8,128)(2,1)S(1)} %constant_dynamic-update-slice_fusion.held_ref.refs_10_.refs_1_), channel_id=1, source_target_pairs={{0,1},{1,0},{2,3},{3,2},{4,5},{5,4},{6,7},{7,6},{8,9},{9,8},{10,11... | collective-permute-start | bytes 442376 | tf_op jit(solution)/shard_map/ppermute | solution.py:42
  16.8 5.8 %collective-permute-start.4 = (bf16[288,256]{1,0:T(8,128)(2,1)S(1)}, bf16[288,256]{1,0:T(8,128)(2,1)S(1)}, u32[]{:S(2)}, u32[]{:S(2)}) collective-permute-start(bf16[288,256]{1,0:T(8,128)(2,1)S(1)} %collective-permute-done.2), channel_id=1, source_target_pairs={{0,2},{1,3},{2,0},{3,1},{4,6},{5,7},{6,4},{7,5},{8,10},{9,11},{10,... | collective-permute-start | bytes 442376 | tf_op jit(solution)/shard_map/ppermute | solution.py:42
  22.6 1.4 %collective-permute-start.7 = (bf16[288,256]{1,0:T(8,128)(2,1)S(1)}, bf16[288,256]{1,0:T(8,128)(2,1)S(1)}, u32[]{:S(2)}, u32[]{:S(2)}) collective-permute-start(bf16[288,256]{1,0:T(8,128)(2,1)S(1)} %collective-permute-done.4.held_ref.refs_11_.refs_2_), channel_id=1, source_target_pairs={{0,1},{1,0},{2,3},{3,2},{4,5},{5,4},{6,7},{7,6},{8,9},{9,8},{10,11... | collective-permute-start | bytes 442376 | tf_op jit(solution)/shard_map/ppermute | solution.py:42
  25.1 1.3 %collective-permute-start.8 = (bf16[8,32,128]{2,1,0:T(8,128)(2,1)S(1)}, bf16[8,32,128]{2,1,0:T(8,128)(2,1)S(1)}, u32[]{:S(2)}, u32[]{:S(2)}) collective-permute-start(bf16[8,32,128]{2,1,0:T(8,128)(2,1)S(1)} %get-tuple-element.84), channel_id=1, source_target_pairs={{0,1},{1,0},{2,3},{3,2},{4,5},{5,4},{6,7},{7,6},{8,9},{9,8},{10,11... | collective-permute-start | bytes 196616 | tf_op jit(solution)/shard_map/ppermute | solution.py:42
  26.4 4.3 %collective-permute-start.9 = (bf16[8,32,128]{2,1,0:T(8,128)(2,1)S(1)}, bf16[8,32,128]{2,1,0:T(8,128)(2,1)S(1)}, u32[]{:S(2)}, u32[]{:S(2)}) collective-permute-start(bf16[8,32,128]{2,1,0:T(8,128)(2,1)S(1)} %get-tuple-element.107), channel_id=1, source_target_pairs={{0,2},{1,5},{2,0},{3,7},{4,6},{5,1},{6,4},{7,3},{8,10},{9,13},{10,... | collective-permute-start | bytes 196616 | tf_op jit(solution)/shard_map/ppermute | solution.py:42
  27.9 4.3 %collective-permute-start.10 = (bf16[8,32,128]{2,1,0:T(8,128)(2,1)S(1)}, bf16[8,32,128]{2,1,0:T(8,128)(2,1)S(1)}, u32[]{:S(2)}, u32[]{:S(2)}) collective-permute-start(bf16[8,32,128]{2,1,0:T(8,128)(2,1)S(1)} %get-tuple-element.107), channel_id=1, source_target_pairs={{0,4},{1,9},{2,6},{3,11},{4,0},{5,13},{6,2},{7,15},{8,12},{9,1},{1... | collective-permute-start | bytes 196616 | tf_op jit(solution)/shard_map/ppermute | solution.py:42
  28.7 5.7 %collective-permute-start.11 = (bf16[8,32,128]{2,1,0:T(8,128)(2,1)S(1)}, bf16[8,32,128]{2,1,0:T(8,128)(2,1)S(1)}, u32[]{:S(2)}, u32[]{:S(2)}) collective-permute-start(bf16[8,32,128]{2,1,0:T(8,128)(2,1)S(1)} %get-tuple-element.107), channel_id=1, source_target_pairs={{0,6},{1,13},{2,4},{3,15},{4,2},{5,9},{6,0},{7,11},{8,14},{9,5},{1... | collective-permute-start | bytes 196616 | tf_op jit(solution)/shard_map/ppermute | solution.py:42
  34.5 5.9 %collective-permute-start.12 = (bf16[8,32,128]{2,1,0:T(8,128)(2,1)S(1)}, bf16[8,32,128]{2,1,0:T(8,128)(2,1)S(1)}, u32[]{:S(2)}, u32[]{:S(2)}) collective-permute-start(bf16[8,32,128]{2,1,0:T(8,128)(2,1)S(1)} %get-tuple-element.86), channel_id=1, source_target_pairs={{0,8},{1,3},{2,10},{3,1},{4,12},{5,7},{6,14},{7,5},{8,0},{9,11},{1... | collective-permute-start | bytes 196616 | tf_op jit(solution)/shard_map/ppermute | solution.py:42
  40.4 1.3 %collective-permute-start.13 = (bf16[8,32,128]{2,1,0:T(8,128)(2,1)S(1)}, bf16[8,32,128]{2,1,0:T(8,128)(2,1)S(1)}, u32[]{:S(2)}, u32[]{:S(2)}) collective-permute-start(bf16[8,32,128]{2,1,0:T(8,128)(2,1)S(1)} %shard_map.78.scale_ref), channel_id=1, source_target_pairs={{0,1},{1,0},{2,3},{3,2},{4,5},{5,4},{6,7},{7,6},{8,9},{9,8},{10,11... | collective-permute-start | bytes 196616 | tf_op jit(solution)/shard_map/ppermute | solution.py:42
  44.8 4.3 %collective-permute-start.15 = (bf16[8,32,128]{2,1,0:T(8,128)(2,1)S(1)}, bf16[8,32,128]{2,1,0:T(8,128)(2,1)S(1)}, u32[]{:S(2)}, u32[]{:S(2)}) collective-permute-start(bf16[8,32,128]{2,1,0:T(8,128)(2,1)S(1)} %get-tuple-element.105), channel_id=1, source_target_pairs={{0,2},{1,5},{2,0},{3,7},{4,6},{5,1},{6,4},{7,3},{8,10},{9,13},{10,... | collective-permute-start | bytes 196616 | tf_op jit(solution)/shard_map/ppermute | solution.py:42
  44.9 5.0 %collective-permute-start.16 = (bf16[8,32,128]{2,1,0:T(8,128)(2,1)S(1)}, bf16[8,32,128]{2,1,0:T(8,128)(2,1)S(1)}, u32[]{:S(2)}, u32[]{:S(2)}) collective-permute-start(bf16[8,32,128]{2,1,0:T(8,128)(2,1)S(1)} %get-tuple-element.105), channel_id=1, source_target_pairs={{0,4},{1,9},{2,6},{3,11},{4,0},{5,13},{6,2},{7,15},{8,12},{9,1},{1... | collective-permute-start | bytes 196616 | tf_op jit(solution)/shard_map/ppermute | solution.py:42
  45.6 5.7 %collective-permute-start.17 = (bf16[8,32,128]{2,1,0:T(8,128)(2,1)S(1)}, bf16[8,32,128]{2,1,0:T(8,128)(2,1)S(1)}, u32[]{:S(2)}, u32[]{:S(2)}) collective-permute-start(bf16[8,32,128]{2,1,0:T(8,128)(2,1)S(1)} %get-tuple-element.105), channel_id=1, source_target_pairs={{0,6},{1,13},{2,4},{3,15},{4,2},{5,9},{6,0},{7,11},{8,14},{9,5},{1... | collective-permute-start | bytes 196616 | tf_op jit(solution)/shard_map/ppermute | solution.py:42
  51.3 5.2 %collective-permute-start.18 = (bf16[8,32,128]{2,1,0:T(8,128)(2,1)S(1)}, bf16[8,32,128]{2,1,0:T(8,128)(2,1)S(1)}, u32[]{:S(2)}, u32[]{:S(2)}) collective-permute-start(bf16[8,32,128]{2,1,0:T(8,128)(2,1)S(1)} %get-tuple-element.91), channel_id=1, source_target_pairs={{0,8},{1,3},{2,10},{3,1},{4,12},{5,7},{6,14},{7,5},{8,0},{9,11},{1... | collective-permute-start | bytes 196616 | tf_op jit(solution)/shard_map/ppermute | solution.py:42
  56.6 1.3 %collective-permute-start.19 = (bf16[8,32,128]{2,1,0:T(8,128)(2,1)S(1)}, bf16[8,32,128]{2,1,0:T(8,128)(2,1)S(1)}, u32[]{:S(2)}, u32[]{:S(2)}) collective-permute-start(bf16[8,32,128]{2,1,0:T(8,128)(2,1)S(1)} %shard_map.83.scale_ref), channel_id=1, source_target_pairs={{0,1},{1,0},{2,3},{3,2},{4,5},{5,4},{6,7},{7,6},{8,9},{9,8},{10,11... | collective-permute-start | bytes 196616 | tf_op jit(solution)/shard_map/ppermute | solution.py:42
  60.7 4.3 %collective-permute-start.21 = (bf16[8,32,128]{2,1,0:T(8,128)(2,1)S(1)}, bf16[8,32,128]{2,1,0:T(8,128)(2,1)S(1)}, u32[]{:S(2)}, u32[]{:S(2)}) collective-permute-start(bf16[8,32,128]{2,1,0:T(8,128)(2,1)S(1)} %get-tuple-element.103), channel_id=1, source_target_pairs={{0,2},{1,5},{2,0},{3,7},{4,6},{5,1},{6,4},{7,3},{8,10},{9,13},{10,... | collective-permute-start | bytes 196616 | tf_op jit(solution)/shard_map/ppermute | solution.py:42
  61.8 4.6 %collective-permute-start.22 = (bf16[8,32,128]{2,1,0:T(8,128)(2,1)S(1)}, bf16[8,32,128]{2,1,0:T(8,128)(2,1)S(1)}, u32[]{:S(2)}, u32[]{:S(2)}) collective-permute-start(bf16[8,32,128]{2,1,0:T(8,128)(2,1)S(1)} %get-tuple-element.103), channel_id=1, source_target_pairs={{0,4},{1,9},{2,6},{3,11},{4,0},{5,13},{6,2},{7,15},{8,12},{9,1},{1... | collective-permute-start | bytes 196616 | tf_op jit(solution)/shard_map/ppermute | solution.py:42
  63.8 5.9 %collective-permute-start.23 = (bf16[8,32,128]{2,1,0:T(8,128)(2,1)S(1)}, bf16[8,32,128]{2,1,0:T(8,128)(2,1)S(1)}, u32[]{:S(2)}, u32[]{:S(2)}) collective-permute-start(bf16[8,32,128]{2,1,0:T(8,128)(2,1)S(1)} %get-tuple-element.103), channel_id=1, source_target_pairs={{0,6},{1,13},{2,4},{3,15},{4,2},{5,9},{6,0},{7,11},{8,14},{9,5},{1... | collective-permute-start | bytes 196616 | tf_op jit(solution)/shard_map/ppermute | solution.py:42
  69.7 5.3 %collective-permute-start.24 = (bf16[8,32,128]{2,1,0:T(8,128)(2,1)S(1)}, bf16[8,32,128]{2,1,0:T(8,128)(2,1)S(1)}, u32[]{:S(2)}, u32[]{:S(2)}) collective-permute-start(bf16[8,32,128]{2,1,0:T(8,128)(2,1)S(1)} %get-tuple-element.94), channel_id=1, source_target_pairs={{0,8},{1,3},{2,10},{3,1},{4,12},{5,7},{6,14},{7,5},{8,0},{9,11},{1... | collective-permute-start | bytes 196616 | tf_op jit(solution)/shard_map/ppermute | solution.py:42
  75.0 1.3 %collective-permute-start.25 = (bf16[8,32,128]{2,1,0:T(8,128)(2,1)S(1)}, bf16[8,32,128]{2,1,0:T(8,128)(2,1)S(1)}, u32[]{:S(2)}, u32[]{:S(2)}) collective-permute-start(bf16[8,32,128]{2,1,0:T(8,128)(2,1)S(1)} %get-tuple-element.99.scale_ref), channel_id=1, source_target_pairs={{0,1},{1,0},{2,3},{3,2},{4,5},{5,4},{6,7},{7,6},{8,9},{9,8},{10,11... | collective-permute-start | bytes 196616 | tf_op jit(solution)/shard_map/ppermute | solution.py:42
  (4 other events, 11.1 us)

commit v9 on v8

--- a/solution.py
+++ b/solution.py
@@ -24,17 +24,21 @@
     return (layer if core else layer[::-1]) + [1]
 
 
-def rounds(core, top):
-    bits = list(range(1, top))
-    bits = bits[core:] + bits[:core]
-    return [bits[low : low + 2] for low in range(0, len(bits), 2)]
-
-
 def flips_of(bits):
     flips = [0]
     for bit in bits:
         flips += [flip | 1 << bit for flip in flips]
     return flips[1:]
+
+
+def rounds(top):
+    layers = [list(range(low, min(low + 2, top))) for low in range(2, top, 2)]
+    order = [flips_of(bits) for bits in [[1]] + layers]
+    found = []
+    for pair in zip(order, order[1:] + order[:1]):
+        longest = max(len(flips) for flips in pair)
+        found.append(list(zip(*[flips + [0] * (longest - len(flips)) for flips in pair])))
+    return found
 
 
 def exchange(block, *flips):
@@ -240,7 +244,10 @@
 def total_of(slot, own_ref, got_refs, flips):
     total = own_ref[slot]
     for pair, got_ref in zip(flips, got_refs):
-        total += got_ref[slot_of(slot, pair, own_ref.shape[0])].astype(F32)
+        got = got_ref[slot_of(slot, pair, own_ref.shape[0])].astype(F32)
+        if not all(pair):
+            got = jnp.where(lax.axis_index("row") % 2 == (pair[0] == 0), got, 0.0)
+        total += got
     return total
 
 
@@ -322,9 +329,8 @@
         )
         column = column + got.astype(F32)
         sent = column.astype(BF16)
-        order = list(zip(rounds(0, top), rounds(1, top)))
-        for place, pair in enumerate(order):
-            flips = list(zip(*[flips_of(bits) for bits in pair]))
+        order = rounds(top)
+        for place, flips in enumerate(order):
             found = [exchange(sent, *turn) for turn in flips]
             if place < len(order) - 1:
                 column, sent = call(

time: 77.9 us -> 88.4 us (1.13)
  starting transfers between devices: 26.9 us -> 45.1 us
  waiting for transfers between devices: 34.2 us -> 26 us
    ppermute x26 -> x32, starting transfers between devices: 26.9 us -> 45.1 us  [exchange(): lax.ppermute(block, 'row', [(d, d ^ flips[d % len(flips)]) for d in range...]
    ppermute x26 -> x32, waiting for transfers between devices: 34.2 us -> 26 us  [exchange(): lax.ppermute(block, 'row', [(d, d ^ flips[d % len(flips)]) for d in range...]
  transfers between devices with their start and end apart: 26 -> 32, of which waited for: 22 -> 16; matrix products, arithmetic and copies ran while one was open for 3% -> 2% of each run, Pallas kernels for 8% -> 7%
where the time goes in v9:
time: 88.4 us; the launch traced here: 88 us
  starting transfers between devices  45.1 us (51%)
  waiting for transfers between devices  26 us (29%)
  Pallas kernels  13.1 us (15%)
  other arithmetic  2.25 us (3%)
  between operations  1.03 us (1%)
    ppermute x32, starting transfers between devices, exchange(): lax.ppermute(block, 'row', [(d, d ^ flips[d % len(flips)]) for d in range...  45.1 us
    ppermute x32, waiting for transfers between devices, exchange(): lax.ppermute(block, 'row', [(d, d ^ flips[d % len(flips)]) for d in range...  26 us
    pallas_call x22, Pallas kernels, call(): pl.pallas_call(body, out_shape=[pltpu.VMEM(shape, dtype) for shape, dtype...  10.8 us
  transfers between devices with their start and end apart: 32, of which 16 were waited for; matrix products, arithmetic and copies ran while one was open for 2% of the time, Pallas kernels for 7%

profile of v9, /device:TPU:0, one launch (start us, length us, event | category | flops | bytes accessed | tf_op | source)
XLA Modules:
  0.0 88.0 jit_solution(11381911759084049943)
XLA Ops:
  1.6 4.1 %collective-permute-start = (bf16[144,256]{1,0:T(8,128)(2,1)S(1)}, bf16[144,256]{1,0:T(8,128)(2,1)S(1)}, u32[]{:S(2)}, u32[]{:S(2)}) collective-permute-start(bf16[144,256]{1,0:T(8,128)(2,1)S(1)} %shard_map.67), channel_id=1, source_target_pairs={{0,8},{1,5},{2,10},{3,7},{4,12},{5,1},{6,14},{7,3},{8,0},{9,13},{1... | collective-permute-start | bytes 221192 | tf_op jit(solution)/shard_map/ppermute | solution.py:46
  5.7 1.5 %collective-permute-start.1 = (bf16[144,256]{1,0:T(8,128)(2,1)S(1)}, bf16[144,256]{1,0:T(8,128)(2,1)S(1)}, u32[]{:S(2)}, u32[]{:S(2)}) collective-permute-start(bf16[144,256]{1,0:T(8,128)(2,1)S(1)} %shard_map.67), channel_id=1, source_target_pairs={{0,2},{1,3},{2,0},{3,1},{4,6},{5,7},{6,4},{7,5},{8,10},{9,11},{10,... | collective-permute-start | bytes 221192 | tf_op jit(solution)/shard_map/ppermute | solution.py:46
  10.1 1.6 %collective-permute-start.2 = (bf16[288,256]{1,0:T(8,128)(2,1)S(1)}, bf16[288,256]{1,0:T(8,128)(2,1)S(1)}, u32[]{:S(2)}, u32[]{:S(2)}) collective-permute-start(bf16[288,256]{1,0:T(8,128)(2,1)S(1)} %pad_maximum_fusion.1), channel_id=1, source_target_pairs={{0,4},{1,9},{2,6},{3,11},{4,0},{5,13},{6,2},{7,15},{8,12},{9,1},{1... | collective-permute-start | bytes 442376 | tf_op jit(solution)/shard_map/ppermute | solution.py:46
  11.7 1.5 %collective-permute-start.3 = (bf16[144,256]{1,0:T(8,128)(2,1)S(1)}, bf16[144,256]{1,0:T(8,128)(2,1)S(1)}, u32[]{:S(2)}, u32[]{:S(2)}) collective-permute-start(bf16[144,256]{1,0:T(8,128)(2,1)S(1)} %collective-permute-done), channel_id=1, source_target_pairs={{0,2},{1,3},{2,0},{3,1},{4,6},{5,7},{6,4},{7,5},{8,10},{9,11},{10,... | collective-permute-start | bytes 221192 | tf_op jit(solution)/shard_map/ppermute | solution.py:46
  13.2 2.8 %collective-permute-done.3 = bf16[144,256]{1,0:T(8,128)(2,1)S(1)} collective-permute-done((bf16[144,256]{1,0:T(8,128)(2,1)S(1)}, bf16[144,256]{1,0:T(8,128)(2,1)S(1)}, u32[]{:S(2)}, u32[]{:S(2)}) %collective-permute-start.3) | collective-permute-done | bytes 73760 | tf_op jit(solution)/shard_map/ppermute | solution.py:46
  16.8 1.5 %collective-permute-start.4 = (bf16[288,256]{1,0:T(8,128)(2,1)S(1)}, bf16[288,256]{1,0:T(8,128)(2,1)S(1)}, u32[]{:S(2)}, u32[]{:S(2)}) collective-permute-start(bf16[288,256]{1,0:T(8,128)(2,1)S(1)} %collective-permute-done.2), channel_id=1, source_target_pairs={{0,2},{1,3},{2,0},{3,1},{4,6},{5,7},{6,4},{7,5},{8,10},{9,11},{10,... | collective-permute-start | bytes 442376 | tf_op jit(solution)/shard_map/ppermute | solution.py:46
  20.4 2.2 %collective-permute-done.4.held_ref.refs_11_.refs_2_ = bf16[288,256]{1,0:T(8,128)(2,1)S(1)} collective-permute-done((bf16[288,256]{1,0:T(8,128)(2,1)S(1)}, bf16[288,256]{1,0:T(8,128)(2,1)S(1)}, u32[]{:S(2)}, u32[]{:S(2)}) %collective-permute-start.4) | collective-permute-done | bytes 147488 | tf_op jit(solution)/shard_map/ppermute | solution.py:46
  26.4 1.6 %collective-permute-start.9 = (bf16[8,32,128]{2,1,0:T(8,128)(2,1)S(1)}, bf16[8,32,128]{2,1,0:T(8,128)(2,1)S(1)}, u32[]{:S(2)}, u32[]{:S(2)}) collective-permute-start(bf16[8,32,128]{2,1,0:T(8,128)(2,1)S(1)} %get-tuple-element.111), channel_id=1, source_target_pairs={{0,2},{1,5},{2,0},{3,7},{4,6},{5,1},{6,4},{7,3},{8,10},{9,13},{10,... | collective-permute-start | bytes 196616 | tf_op jit(solution)/shard_map/ppermute | solution.py:46
  29.3 1.4 %collective-permute-done.9.refs_0_ = bf16[8,32,128]{2,1,0:T(8,128)(2,1)S(1)} collective-permute-done((bf16[8,32,128]{2,1,0:T(8,128)(2,1)S(1)}, bf16[8,32,128]{2,1,0:T(8,128)(2,1)S(1)}, u32[]{:S(2)}, u32[]{:S(2)}) %collective-permute-start.9) | collective-permute-done | bytes 65568 | tf_op jit(solution)/shard_map/ppermute | solution.py:46
  31.6 3.5 %collective-permute-start.13 = (bf16[8,32,128]{2,1,0:T(8,128)(2,1)S(1)}, bf16[8,32,128]{2,1,0:T(8,128)(2,1)S(1)}, u32[]{:S(2)}, u32[]{:S(2)}) collective-permute-start(bf16[8,32,128]{2,1,0:T(8,128)(2,1)S(1)} %get-tuple-element.88), channel_id=1, source_target_pairs={{0,8},{1,1},{2,10},{3,3},{4,12},{5,5},{6,14},{7,7},{8,0},{9,9},{10... | collective-permute-start | bytes 196616 | tf_op jit(solution)/shard_map/ppermute | solution.py:46
  35.1 3.9 %collective-permute-start.14 = (bf16[8,32,128]{2,1,0:T(8,128)(2,1)S(1)}, bf16[8,32,128]{2,1,0:T(8,128)(2,1)S(1)}, u32[]{:S(2)}, u32[]{:S(2)}) collective-permute-start(bf16[8,32,128]{2,1,0:T(8,128)(2,1)S(1)} %get-tuple-element.88), channel_id=1, source_target_pairs={{0,12},{1,1},{2,14},{3,3},{4,8},{5,5},{6,10},{7,7},{8,4},{9,9},{10... | collective-permute-start | bytes 196616 | tf_op jit(solution)/shard_map/ppermute | solution.py:46
  39.2 3.9 %collective-permute-done.14.refs_2_ = bf16[8,32,128]{2,1,0:T(8,128)(2,1)S(1)} collective-permute-done((bf16[8,32,128]{2,1,0:T(8,128)(2,1)S(1)}, bf16[8,32,128]{2,1,0:T(8,128)(2,1)S(1)}, u32[]{:S(2)}, u32[]{:S(2)}) %collective-permute-start.14) | collective-permute-done | bytes 65568 | tf_op jit(solution)/shard_map/ppermute | solution.py:46
  44.4 1.7 %shard_map.80 = (f32[32,1024]{1,0:T(8,128)}, bf16[32,1024]{1,0:T(8,128)(2,1)S(1)}, bf16[8,32,128]{2,1,0:T(8,128)(2,1)S(1)}) custom-call(bf16[8,32,128]{2,1,0:T(8,128)(2,1)S(1)} %collective-permute-done.15.scale_ref, f32[32,1024]{1,0:T(8,128)S(1)} %shard_map.79.image_ref, f32[32,1024]{1,0:T(8,128)S(1)} %get-tuple-element.89.marg_ref, ...), custom_call_target="tpu_custom_call" | custom-call | flops 536870912 | bytes 2424832 | tf_op jit(solution)/shard_map/pallas_call | solution.py:52
  47.4 1.6 %collective-permute-start.17 = (bf16[8,32,128]{2,1,0:T(8,128)(2,1)S(1)}, bf16[8,32,128]{2,1,0:T(8,128)(2,1)S(1)}, u32[]{:S(2)}, u32[]{:S(2)}) collective-permute-start(bf16[8,32,128]{2,1,0:T(8,128)(2,1)S(1)} %get-tuple-element.109), channel_id=1, source_target_pairs={{0,2},{1,5},{2,0},{3,7},{4,6},{5,1},{6,4},{7,3},{8,10},{9,13},{10,... | collective-permute-start | bytes 196616 | tf_op jit(solution)/shard_map/ppermute | solution.py:46
  50.4 1.4 %collective-permute-done.17.refs_0_ = bf16[8,32,128]{2,1,0:T(8,128)(2,1)S(1)} collective-permute-done((bf16[8,32,128]{2,1,0:T(8,128)(2,1)S(1)}, bf16[8,32,128]{2,1,0:T(8,128)(2,1)S(1)}, u32[]{:S(2)}, u32[]{:S(2)}) %collective-permute-start.17) | collective-permute-done | bytes 65568 | tf_op jit(solution)/shard_map/ppermute | solution.py:46
  51.9 4.5 %collective-permute-start.21 = (bf16[8,32,128]{2,1,0:T(8,128)(2,1)S(1)}, bf16[8,32,128]{2,1,0:T(8,128)(2,1)S(1)}, u32[]{:S(2)}, u32[]{:S(2)}) collective-permute-start(bf16[8,32,128]{2,1,0:T(8,128)(2,1)S(1)} %get-tuple-element.93), channel_id=1, source_target_pairs={{0,8},{1,1},{2,10},{3,3},{4,12},{5,5},{6,14},{7,7},{8,0},{9,9},{10... | collective-permute-start | bytes 196616 | tf_op jit(solution)/shard_map/ppermute | solution.py:46
  56.4 3.7 %collective-permute-start.22 = (bf16[8,32,128]{2,1,0:T(8,128)(2,1)S(1)}, bf16[8,32,128]{2,1,0:T(8,128)(2,1)S(1)}, u32[]{:S(2)}, u32[]{:S(2)}) collective-permute-start(bf16[8,32,128]{2,1,0:T(8,128)(2,1)S(1)} %get-tuple-element.93), channel_id=1, source_target_pairs={{0,12},{1,1},{2,14},{3,3},{4,8},{5,5},{6,10},{7,7},{8,4},{9,9},{10... | collective-permute-start | bytes 196616 | tf_op jit(solution)/shard_map/ppermute | solution.py:46
  60.1 4.2 %collective-permute-done.22.refs_2_ = bf16[8,32,128]{2,1,0:T(8,128)(2,1)S(1)} collective-permute-done((bf16[8,32,128]{2,1,0:T(8,128)(2,1)S(1)}, bf16[8,32,128]{2,1,0:T(8,128)(2,1)S(1)}, u32[]{:S(2)}, u32[]{:S(2)}) %collective-permute-start.22) | collective-permute-done | bytes 65568 | tf_op jit(solution)/shard_map/ppermute | solution.py:46
  65.7 1.5 %shard_map.85 = (f32[32,1024]{1,0:T(8,128)S(1)}, bf16[32,1024]{1,0:T(8,128)(2,1)S(1)}, bf16[8,32,128]{2,1,0:T(8,128)(2,1)S(1)}) custom-call(bf16[8,32,128]{2,1,0:T(8,128)(2,1)S(1)} %collective-permute-done.23.scale_ref, f32[32,1024]{1,0:T(8,128)S(1)} %shard_map.84.image_ref, f32[32,1024]{1,0:T(8,128)S(1)} %get-tuple-element.89.marg_ref, ...), custom_call_target="tpu_custom_call" | custom-call | flops 536870912 | bytes 2424832 | tf_op jit(solution)/shard_map/pallas_call | solution.py:52
  68.5 1.6 %collective-permute-start.25 = (bf16[8,32,128]{2,1,0:T(8,128)(2,1)S(1)}, bf16[8,32,128]{2,1,0:T(8,128)(2,1)S(1)}, u32[]{:S(2)}, u32[]{:S(2)}) collective-permute-start(bf16[8,32,128]{2,1,0:T(8,128)(2,1)S(1)} %get-tuple-element.107), channel_id=1, source_target_pairs={{0,2},{1,5},{2,0},{3,7},{4,6},{5,1},{6,4},{7,3},{8,10},{9,13},{10,... | collective-permute-start | bytes 196616 | tf_op jit(solution)/shard_map/ppermute | solution.py:46
  71.4 1.4 %collective-permute-done.25.refs_0_ = bf16[8,32,128]{2,1,0:T(8,128)(2,1)S(1)} collective-permute-done((bf16[8,32,128]{2,1,0:T(8,128)(2,1)S(1)}, bf16[8,32,128]{2,1,0:T(8,128)(2,1)S(1)}, u32[]{:S(2)}, u32[]{:S(2)}) %collective-permute-start.25) | collective-permute-done | bytes 65568 | tf_op jit(solution)/shard_map/ppermute | solution.py:46
  73.0 4.2 %collective-permute-start.29 = (bf16[8,32,128]{2,1,0:T(8,128)(2,1)S(1)}, bf16[8,32,128]{2,1,0:T(8,128)(2,1)S(1)}, u32[]{:S(2)}, u32[]{:S(2)}) collective-permute-start(bf16[8,32,128]{2,1,0:T(8,128)(2,1)S(1)} %get-tuple-element.96), channel_id=1, source_target_pairs={{0,8},{1,1},{2,10},{3,3},{4,12},{5,5},{6,14},{7,7},{8,0},{9,9},{10... | collective-permute-start | bytes 196616 | tf_op jit(solution)/shard_map/ppermute | solution.py:46
  77.2 3.9 %collective-permute-start.30 = (bf16[8,32,128]{2,1,0:T(8,128)(2,1)S(1)}, bf16[8,32,128]{2,1,0:T(8,128)(2,1)S(1)}, u32[]{:S(2)}, u32[]{:S(2)}) collective-permute-start(bf16[8,32,128]{2,1,0:T(8,128)(2,1)S(1)} %get-tuple-element.96), channel_id=1, source_target_pairs={{0,12},{1,1},{2,14},{3,3},{4,8},{5,5},{6,10},{7,7},{8,4},{9,9},{10... | collective-permute-start | bytes 196616 | tf_op jit(solution)/shard_map/ppermute | solution.py:46
  81.9 3.3 %collective-permute-done.30.refs_2_ = bf16[8,32,128]{2,1,0:T(8,128)(2,1)S(1)} collective-permute-done((bf16[8,32,128]{2,1,0:T(8,128)(2,1)S(1)}, bf16[8,32,128]{2,1,0:T(8,128)(2,1)S(1)}, u32[]{:S(2)}, u32[]{:S(2)}) %collective-permute-start.30) | collective-permute-done | bytes 65568 | tf_op jit(solution)/shard_map/ppermute | solution.py:46
  (80 shorter events, 24.2 us)
Async XLA Ops:
  1.6 7.6 %collective-permute-start = (bf16[144,256]{1,0:T(8,128)(2,1)S(1)}, bf16[144,256]{1,0:T(8,128)(2,1)S(1)}, u32[]{:S(2)}, u32[]{:S(2)}) collective-permute-start(bf16[144,256]{1,0:T(8,128)(2,1)S(1)} %shard_map.67), channel_id=1, source_target_pairs={{0,8},{1,5},{2,10},{3,7},{4,12},{5,1},{6,14},{7,3},{8,0},{9,13},{1... | collective-permute-start | bytes 221192 | tf_op jit(solution)/shard_map/ppermute | solution.py:46
  5.7 4.4 %collective-permute-start.1 = (bf16[144,256]{1,0:T(8,128)(2,1)S(1)}, bf16[144,256]{1,0:T(8,128)(2,1)S(1)}, u32[]{:S(2)}, u32[]{:S(2)}) collective-permute-start(bf16[144,256]{1,0:T(8,128)(2,1)S(1)} %shard_map.67), channel_id=1, source_target_pairs={{0,2},{1,3},{2,0},{3,1},{4,6},{5,7},{6,4},{7,5},{8,10},{9,11},{10,... | collective-permute-start | bytes 221192 | tf_op jit(solution)/shard_map/ppermute | solution.py:46
  10.1 6.0 %collective-permute-start.2 = (bf16[288,256]{1,0:T(8,128)(2,1)S(1)}, bf16[288,256]{1,0:T(8,128)(2,1)S(1)}, u32[]{:S(2)}, u32[]{:S(2)}) collective-permute-start(bf16[288,256]{1,0:T(8,128)(2,1)S(1)} %pad_maximum_fusion.1), channel_id=1, source_target_pairs={{0,4},{1,9},{2,6},{3,11},{4,0},{5,13},{6,2},{7,15},{8,12},{9,1},{1... | collective-permute-start | bytes 442376 | tf_op jit(solution)/shard_map/ppermute | solution.py:46
  11.7 4.4 %collective-permute-start.3 = (bf16[144,256]{1,0:T(8,128)(2,1)S(1)}, bf16[144,256]{1,0:T(8,128)(2,1)S(1)}, u32[]{:S(2)}, u32[]{:S(2)}) collective-permute-start(bf16[144,256]{1,0:T(8,128)(2,1)S(1)} %collective-permute-done), channel_id=1, source_target_pairs={{0,2},{1,3},{2,0},{3,1},{4,6},{5,7},{6,4},{7,5},{8,10},{9,11},{10,... | collective-permute-start | bytes 221192 | tf_op jit(solution)/shard_map/ppermute | solution.py:46
  16.1 3.7 %collective-permute-start.5 = (bf16[576,256]{1,0:T(8,128)(2,1)S(1)}, bf16[576,256]{1,0:T(8,128)(2,1)S(1)}, u32[]{:S(2)}, u32[]{:S(2)}) collective-permute-start(bf16[576,256]{1,0:T(8,128)(2,1)S(1)} %pad_maximum_fusion.held_ref.refs_9_.refs_0_), channel_id=1, source_target_pairs={{0,1},{1,0},{2,3},{3,2},{4,5},{5,4},{6,7},{7,6},{8,9},{9,8},{10,11... | collective-permute-start | bytes 884744 | tf_op jit(solution)/shard_map/ppermute | solution.py:46
  16.2 3.1 %collective-permute-start.6 = (bf16[288,256]{1,0:T(8,128)(2,1)S(1)}, bf16[288,256]{1,0:T(8,128)(2,1)S(1)}, u32[]{:S(2)}, u32[]{:S(2)}) collective-permute-start(bf16[288,256]{1,0:T(8,128)(2,1)S(1)} %constant_dynamic-update-slice_fusion.held_ref.refs_10_.refs_1_), channel_id=1, source_target_pairs={{0,1},{1,0},{2,3},{3,2},{4,5},{5,4},{6,7},{7,6},{8,9},{9,8},{10,11... | collective-permute-start | bytes 442376 | tf_op jit(solution)/shard_map/ppermute | solution.py:46
  16.8 5.8 %collective-permute-start.4 = (bf16[288,256]{1,0:T(8,128)(2,1)S(1)}, bf16[288,256]{1,0:T(8,128)(2,1)S(1)}, u32[]{:S(2)}, u32[]{:S(2)}) collective-permute-start(bf16[288,256]{1,0:T(8,128)(2,1)S(1)} %collective-permute-done.2), channel_id=1, source_target_pairs={{0,2},{1,3},{2,0},{3,1},{4,6},{5,7},{6,4},{7,5},{8,10},{9,11},{10,... | collective-permute-start | bytes 442376 | tf_op jit(solution)/shard_map/ppermute | solution.py:46
  26.4 4.3 %collective-permute-start.9 = (bf16[8,32,128]{2,1,0:T(8,128)(2,1)S(1)}, bf16[8,32,128]{2,1,0:T(8,128)(2,1)S(1)}, u32[]{:S(2)}, u32[]{:S(2)}) collective-permute-start(bf16[8,32,128]{2,1,0:T(8,128)(2,1)S(1)} %get-tuple-element.111), channel_id=1, source_target_pairs={{0,2},{1,5},{2,0},{3,7},{4,6},{5,1},{6,4},{7,3},{8,10},{9,13},{10,... | collective-permute-start | bytes 196616 | tf_op jit(solution)/shard_map/ppermute | solution.py:46
  27.9 2.8 %collective-permute-start.10 = (bf16[8,32,128]{2,1,0:T(8,128)(2,1)S(1)}, bf16[8,32,128]{2,1,0:T(8,128)(2,1)S(1)}, u32[]{:S(2)}, u32[]{:S(2)}) collective-permute-start(bf16[8,32,128]{2,1,0:T(8,128)(2,1)S(1)} %get-tuple-element.111), channel_id=1, source_target_pairs={{0,0},{1,9},{2,2},{3,11},{4,4},{5,13},{6,6},{7,15},{8,8},{9,1},{10... | collective-permute-start | bytes 196616 | tf_op jit(solution)/shard_map/ppermute | solution.py:46
  28.6 2.1 %collective-permute-start.11 = (bf16[8,32,128]{2,1,0:T(8,128)(2,1)S(1)}, bf16[8,32,128]{2,1,0:T(8,128)(2,1)S(1)}, u32[]{:S(2)}, u32[]{:S(2)}) collective-permute-start(bf16[8,32,128]{2,1,0:T(8,128)(2,1)S(1)} %get-tuple-element.111), channel_id=1, source_target_pairs={{0,0},{1,13},{2,2},{3,15},{4,4},{5,9},{6,6},{7,11},{8,8},{9,5},{10... | collective-permute-start | bytes 196616 | tf_op jit(solution)/shard_map/ppermute | solution.py:46
  30.7 8.4 %collective-permute-start.12 = (bf16[8,32,128]{2,1,0:T(8,128)(2,1)S(1)}, bf16[8,32,128]{2,1,0:T(8,128)(2,1)S(1)}, u32[]{:S(2)}, u32[]{:S(2)}) collective-permute-start(bf16[8,32,128]{2,1,0:T(8,128)(2,1)S(1)} %get-tuple-element.88), channel_id=1, source_target_pairs={{0,4},{1,3},{2,6},{3,1},{4,0},{5,7},{6,2},{7,5},{8,12},{9,11},{10,... | collective-permute-start | bytes 196616 | tf_op jit(solution)/shard_map/ppermute | solution.py:46
  31.6 7.6 %collective-permute-start.13 = (bf16[8,32,128]{2,1,0:T(8,128)(2,1)S(1)}, bf16[8,32,128]{2,1,0:T(8,128)(2,1)S(1)}, u32[]{:S(2)}, u32[]{:S(2)}) collective-permute-start(bf16[8,32,128]{2,1,0:T(8,128)(2,1)S(1)} %get-tuple-element.88), channel_id=1, source_target_pairs={{0,8},{1,1},{2,10},{3,3},{4,12},{5,5},{6,14},{7,7},{8,0},{9,9},{10... | collective-permute-start | bytes 196616 | tf_op jit(solution)/shard_map/ppermute | solution.py:46
  35.1 8.0 %collective-permute-start.14 = (bf16[8,32,128]{2,1,0:T(8,128)(2,1)S(1)}, bf16[8,32,128]{2,1,0:T(8,128)(2,1)S(1)}, u32[]{:S(2)}, u32[]{:S(2)}) collective-permute-start(bf16[8,32,128]{2,1,0:T(8,128)(2,1)S(1)} %get-tuple-element.88), channel_id=1, source_target_pairs={{0,12},{1,1},{2,14},{3,3},{4,8},{5,5},{6,10},{7,7},{8,4},{9,9},{10... | collective-permute-start | bytes 196616 | tf_op jit(solution)/shard_map/ppermute | solution.py:46
  47.4 4.3 %collective-permute-start.17 = (bf16[8,32,128]{2,1,0:T(8,128)(2,1)S(1)}, bf16[8,32,128]{2,1,0:T(8,128)(2,1)S(1)}, u32[]{:S(2)}, u32[]{:S(2)}) collective-permute-start(bf16[8,32,128]{2,1,0:T(8,128)(2,1)S(1)} %get-tuple-element.109), channel_id=1, source_target_pairs={{0,2},{1,5},{2,0},{3,7},{4,6},{5,1},{6,4},{7,3},{8,10},{9,13},{10,... | collective-permute-start | bytes 196616 | tf_op jit(solution)/shard_map/ppermute | solution.py:46
  49.0 2.7 %collective-permute-start.18 = (bf16[8,32,128]{2,1,0:T(8,128)(2,1)S(1)}, bf16[8,32,128]{2,1,0:T(8,128)(2,1)S(1)}, u32[]{:S(2)}, u32[]{:S(2)}) collective-permute-start(bf16[8,32,128]{2,1,0:T(8,128)(2,1)S(1)} %get-tuple-element.109), channel_id=1, source_target_pairs={{0,0},{1,9},{2,2},{3,11},{4,4},{5,13},{6,6},{7,15},{8,8},{9,1},{10... | collective-permute-start | bytes 196616 | tf_op jit(solution)/shard_map/ppermute | solution.py:46
  51.8 8.3 %collective-permute-start.20 = (bf16[8,32,128]{2,1,0:T(8,128)(2,1)S(1)}, bf16[8,32,128]{2,1,0:T(8,128)(2,1)S(1)}, u32[]{:S(2)}, u32[]{:S(2)}) collective-permute-start(bf16[8,32,128]{2,1,0:T(8,128)(2,1)S(1)} %get-tuple-element.93), channel_id=1, source_target_pairs={{0,4},{1,3},{2,6},{3,1},{4,0},{5,7},{6,2},{7,5},{8,12},{9,11},{10,... | collective-permute-start | bytes 196616 | tf_op jit(solution)/shard_map/ppermute | solution.py:46
  51.9 8.2 %collective-permute-start.21 = (bf16[8,32,128]{2,1,0:T(8,128)(2,1)S(1)}, bf16[8,32,128]{2,1,0:T(8,128)(2,1)S(1)}, u32[]{:S(2)}, u32[]{:S(2)}) collective-permute-start(bf16[8,32,128]{2,1,0:T(8,128)(2,1)S(1)} %get-tuple-element.93), channel_id=1, source_target_pairs={{0,8},{1,1},{2,10},{3,3},{4,12},{5,5},{6,14},{7,7},{8,0},{9,9},{10... | collective-permute-start | bytes 196616 | tf_op jit(solution)/shard_map/ppermute | solution.py:46
  56.4 8.0 %collective-permute-start.22 = (bf16[8,32,128]{2,1,0:T(8,128)(2,1)S(1)}, bf16[8,32,128]{2,1,0:T(8,128)(2,1)S(1)}, u32[]{:S(2)}, u32[]{:S(2)}) collective-permute-start(bf16[8,32,128]{2,1,0:T(8,128)(2,1)S(1)} %get-tuple-element.93), channel_id=1, source_target_pairs={{0,12},{1,1},{2,14},{3,3},{4,8},{5,5},{6,10},{7,7},{8,4},{9,9},{10... | collective-permute-start | bytes 196616 | tf_op jit(solution)/shard_map/ppermute | solution.py:46
  68.5 4.3 %collective-permute-start.25 = (bf16[8,32,128]{2,1,0:T(8,128)(2,1)S(1)}, bf16[8,32,128]{2,1,0:T(8,128)(2,1)S(1)}, u32[]{:S(2)}, u32[]{:S(2)}) collective-permute-start(bf16[8,32,128]{2,1,0:T(8,128)(2,1)S(1)} %get-tuple-element.107), channel_id=1, source_target_pairs={{0,2},{1,5},{2,0},{3,7},{4,6},{5,1},{6,4},{7,3},{8,10},{9,13},{10,... | collective-permute-start | bytes 196616 | tf_op jit(solution)/shard_map/ppermute | solution.py:46
  70.1 2.8 %collective-permute-start.26 = (bf16[8,32,128]{2,1,0:T(8,128)(2,1)S(1)}, bf16[8,32,128]{2,1,0:T(8,128)(2,1)S(1)}, u32[]{:S(2)}, u32[]{:S(2)}) collective-permute-start(bf16[8,32,128]{2,1,0:T(8,128)(2,1)S(1)} %get-tuple-element.107), channel_id=1, source_target_pairs={{0,0},{1,9},{2,2},{3,11},{4,4},{5,13},{6,6},{7,15},{8,8},{9,1},{10... | collective-permute-start | bytes 196616 | tf_op jit(solution)/shard_map/ppermute | solution.py:46
  70.8 2.1 %collective-permute-start.27 = (bf16[8,32,128]{2,1,0:T(8,128)(2,1)S(1)}, bf16[8,32,128]{2,1,0:T(8,128)(2,1)S(1)}, u32[]{:S(2)}, u32[]{:S(2)}) collective-permute-start(bf16[8,32,128]{2,1,0:T(8,128)(2,1)S(1)} %get-tuple-element.107), channel_id=1, source_target_pairs={{0,0},{1,13},{2,2},{3,15},{4,4},{5,9},{6,6},{7,11},{8,8},{9,5},{10... | collective-permute-start | bytes 196616 | tf_op jit(solution)/shard_map/ppermute | solution.py:46
  72.9 9.0 %collective-permute-start.28 = (bf16[8,32,128]{2,1,0:T(8,128)(2,1)S(1)}, bf16[8,32,128]{2,1,0:T(8,128)(2,1)S(1)}, u32[]{:S(2)}, u32[]{:S(2)}) collective-permute-start(bf16[8,32,128]{2,1,0:T(8,128)(2,1)S(1)} %get-tuple-element.96), channel_id=1, source_target_pairs={{0,4},{1,3},{2,6},{3,1},{4,0},{5,7},{6,2},{7,5},{8,12},{9,11},{10,... | collective-permute-start | bytes 196616 | tf_op jit(solution)/shard_map/ppermute | solution.py:46
  73.0 8.9 %collective-permute-start.29 = (bf16[8,32,128]{2,1,0:T(8,128)(2,1)S(1)}, bf16[8,32,128]{2,1,0:T(8,128)(2,1)S(1)}, u32[]{:S(2)}, u32[]{:S(2)}) collective-permute-start(bf16[8,32,128]{2,1,0:T(8,128)(2,1)S(1)} %get-tuple-element.96), channel_id=1, source_target_pairs={{0,8},{1,1},{2,10},{3,3},{4,12},{5,5},{6,14},{7,7},{8,0},{9,9},{10... | collective-permute-start | bytes 196616 | tf_op jit(solution)/shard_map/ppermute | solution.py:46
  77.2 8.0 %collective-permute-start.30 = (bf16[8,32,128]{2,1,0:T(8,128)(2,1)S(1)}, bf16[8,32,128]{2,1,0:T(8,128)(2,1)S(1)}, u32[]{:S(2)}, u32[]{:S(2)}) collective-permute-start(bf16[8,32,128]{2,1,0:T(8,128)(2,1)S(1)} %get-tuple-element.96), channel_id=1, source_target_pairs={{0,12},{1,1},{2,14},{3,3},{4,8},{5,5},{6,10},{7,7},{8,4},{9,9},{10... | collective-permute-start | bytes 196616 | tf_op jit(solution)/shard_map/ppermute | solution.py:46
  (10 other events, 19.8 us)

commit v10 on v8

--- a/solution.py
+++ b/solution.py
@@ -27,7 +27,7 @@
 def rounds(core, top):
     bits = list(range(1, top))
     bits = bits[core:] + bits[:core]
-    return [bits[low : low + 2] for low in range(0, len(bits), 2)]
+    return [[bit] for bit in bits]
 
 
 def flips_of(bits):

time: 77.9 us -> 81.3 us (1.044)
  waiting for transfers between devices: 34.2 us -> 45.3 us
  starting transfers between devices: 26.9 us -> 19.1 us
    ppermute x26 -> x23, waiting for transfers between devices: 34.2 us -> 45.3 us  [exchange(): lax.ppermute(block, 'row', [(d, d ^ flips[d % len(flips)]) for d in range...]
    ppermute x26 -> x23, starting transfers between devices: 26.9 us -> 19.1 us  [exchange(): lax.ppermute(block, 'row', [(d, d ^ flips[d % len(flips)]) for d in range...]
    pallas_call x22 -> x25, Pallas kernels: 10.7 us -> 10.6 us  [call(): pl.pallas_call(body, out_shape=[pltpu.VMEM(shape, dtype) for shape, dtype...]
  transfers between devices with their start and end apart: 26 -> 23, of which waited for: 22 -> 19; matrix products, arithmetic and copies ran while one was open for 3% -> 3% of each run, Pallas kernels for 8% -> 8%
where the time goes in v10:
time: 81.3 us; the launch traced here: 81.1 us
  waiting for transfers between devices  45.3 us (56%)
  starting transfers between devices  19.1 us (23%)
  Pallas kernels  13 us (16%)
  other arithmetic  2.25 us (3%)
  between operations  0.91 us (1%)
    ppermute x23, waiting for transfers between devices, exchange(): lax.ppermute(block, 'row', [(d, d ^ flips[d % len(flips)]) for d in range...  45.3 us
    ppermute x23, starting transfers between devices, exchange(): lax.ppermute(block, 'row', [(d, d ^ flips[d % len(flips)]) for d in range...  19.1 us
    pallas_call x25, Pallas kernels, call(): pl.pallas_call(body, out_shape=[pltpu.VMEM(shape, dtype) for shape, dtype...  10.6 us
  transfers between devices with their start and end apart: 23, of which 19 were waited for; matrix products, arithmetic and copies ran while one was open for 3% of the time, Pallas kernels for 8%

profile of v10, /device:TPU:0, one launch (start us, length us, event | category | flops | bytes accessed | tf_op | source)
XLA Modules:
  0.0 81.1 jit_solution(1446725550392521647)
XLA Ops:
  1.6 4.1 %collective-permute-start = (bf16[144,256]{1,0:T(8,128)(2,1)S(1)}, bf16[144,256]{1,0:T(8,128)(2,1)S(1)}, u32[]{:S(2)}, u32[]{:S(2)}) collective-permute-start(bf16[144,256]{1,0:T(8,128)(2,1)S(1)} %shard_map.67), channel_id=1, source_target_pairs={{0,8},{1,5},{2,10},{3,7},{4,12},{5,1},{6,14},{7,3},{8,0},{9,13},{1... | collective-permute-start | bytes 221192 | tf_op jit(solution)/shard_map/ppermute | solution.py:42
  5.7 1.5 %collective-permute-start.1 = (bf16[144,256]{1,0:T(8,128)(2,1)S(1)}, bf16[144,256]{1,0:T(8,128)(2,1)S(1)}, u32[]{:S(2)}, u32[]{:S(2)}) collective-permute-start(bf16[144,256]{1,0:T(8,128)(2,1)S(1)} %shard_map.67), channel_id=1, source_target_pairs={{0,2},{1,3},{2,0},{3,1},{4,6},{5,7},{6,4},{7,5},{8,10},{9,11},{10,... | collective-permute-start | bytes 221192 | tf_op jit(solution)/shard_map/ppermute | solution.py:42
  7.2 1.3 %fusion = f32[1024]{0:T(1024)S(1)} fusion(bf16[1024,256]{1,0:T(8,128)(2,1)} %param.4), kind=kLoop, calls=%fused_computation.2 | loop fusion | flops 785408 | bytes 528384 | tf_op jit(solution)/shard_map/reduce_sum | solution.py:60
  10.1 1.6 %collective-permute-start.2 = (bf16[288,256]{1,0:T(8,128)(2,1)S(1)}, bf16[288,256]{1,0:T(8,128)(2,1)S(1)}, u32[]{:S(2)}, u32[]{:S(2)}) collective-permute-start(bf16[288,256]{1,0:T(8,128)(2,1)S(1)} %pad_maximum_fusion.1), channel_id=1, source_target_pairs={{0,4},{1,9},{2,6},{3,11},{4,0},{5,13},{6,2},{7,15},{8,12},{9,1},{1... | collective-permute-start | bytes 442376 | tf_op jit(solution)/shard_map/ppermute | solution.py:42
  11.7 1.5 %collective-permute-start.3 = (bf16[144,256]{1,0:T(8,128)(2,1)S(1)}, bf16[144,256]{1,0:T(8,128)(2,1)S(1)}, u32[]{:S(2)}, u32[]{:S(2)}) collective-permute-start(bf16[144,256]{1,0:T(8,128)(2,1)S(1)} %collective-permute-done), channel_id=1, source_target_pairs={{0,2},{1,3},{2,0},{3,1},{4,6},{5,7},{6,4},{7,5},{8,10},{9,11},{10,... | collective-permute-start | bytes 221192 | tf_op jit(solution)/shard_map/ppermute | solution.py:42
  13.2 2.8 %collective-permute-done.3 = bf16[144,256]{1,0:T(8,128)(2,1)S(1)} collective-permute-done((bf16[144,256]{1,0:T(8,128)(2,1)S(1)}, bf16[144,256]{1,0:T(8,128)(2,1)S(1)}, u32[]{:S(2)}, u32[]{:S(2)}) %collective-permute-start.3) | collective-permute-done | bytes 73760 | tf_op jit(solution)/shard_map/ppermute | solution.py:42
  16.8 1.5 %collective-permute-start.4 = (bf16[288,256]{1,0:T(8,128)(2,1)S(1)}, bf16[288,256]{1,0:T(8,128)(2,1)S(1)}, u32[]{:S(2)}, u32[]{:S(2)}) collective-permute-start(bf16[288,256]{1,0:T(8,128)(2,1)S(1)} %collective-permute-done.2), channel_id=1, source_target_pairs={{0,2},{1,3},{2,0},{3,1},{4,6},{5,7},{6,4},{7,5},{8,10},{9,11},{10,... | collective-permute-start | bytes 442376 | tf_op jit(solution)/shard_map/ppermute | solution.py:42
  20.4 2.2 %collective-permute-done.4.held_ref.refs_11_.refs_2_ = bf16[288,256]{1,0:T(8,128)(2,1)S(1)} collective-permute-done((bf16[288,256]{1,0:T(8,128)(2,1)S(1)}, bf16[288,256]{1,0:T(8,128)(2,1)S(1)}, u32[]{:S(2)}, u32[]{:S(2)}) %collective-permute-start.4) | collective-permute-done | bytes 147488 | tf_op jit(solution)/shard_map/ppermute | solution.py:42
  26.4 1.6 %collective-permute-start.9 = (bf16[8,32,128]{2,1,0:T(8,128)(2,1)S(1)}, bf16[8,32,128]{2,1,0:T(8,128)(2,1)S(1)}, u32[]{:S(2)}, u32[]{:S(2)}) collective-permute-start(bf16[8,32,128]{2,1,0:T(8,128)(2,1)S(1)} %get-tuple-element.119), channel_id=1, source_target_pairs={{0,2},{1,5},{2,0},{3,7},{4,6},{5,1},{6,4},{7,3},{8,10},{9,13},{10,... | collective-permute-start | bytes 196616 | tf_op jit(solution)/shard_map/ppermute | solution.py:42
  27.9 2.7 %collective-permute-done.9.refs_0_ = bf16[8,32,128]{2,1,0:T(8,128)(2,1)S(1)} collective-permute-done((bf16[8,32,128]{2,1,0:T(8,128)(2,1)S(1)}, bf16[8,32,128]{2,1,0:T(8,128)(2,1)S(1)}, u32[]{:S(2)}, u32[]{:S(2)}) %collective-permute-start.9) | collective-permute-done | bytes 65568 | tf_op jit(solution)/shard_map/ppermute | solution.py:42
  31.6 3.8 %collective-permute-done.10.refs_0_ = bf16[8,32,128]{2,1,0:T(8,128)(2,1)S(1)} collective-permute-done((bf16[8,32,128]{2,1,0:T(8,128)(2,1)S(1)}, bf16[8,32,128]{2,1,0:T(8,128)(2,1)S(1)}, u32[]{:S(2)}, u32[]{:S(2)}) %collective-permute-start.10) | collective-permute-done | bytes 65568 | tf_op jit(solution)/shard_map/ppermute | solution.py:42
  35.4 1.3 %collective-permute-start.11 = (bf16[8,32,128]{2,1,0:T(8,128)(2,1)S(1)}, bf16[8,32,128]{2,1,0:T(8,128)(2,1)S(1)}, u32[]{:S(2)}, u32[]{:S(2)}) collective-permute-start(bf16[8,32,128]{2,1,0:T(8,128)(2,1)S(1)} %get-tuple-element.94), channel_id=1, source_target_pairs={{0,8},{1,3},{2,10},{3,1},{4,12},{5,7},{6,14},{7,5},{8,0},{9,11},{1... | collective-permute-start | bytes 196616 | tf_op jit(solution)/shard_map/ppermute | solution.py:42
  36.8 4.4 %collective-permute-done.11.refs_0_ = bf16[8,32,128]{2,1,0:T(8,128)(2,1)S(1)} collective-permute-done((bf16[8,32,128]{2,1,0:T(8,128)(2,1)S(1)}, bf16[8,32,128]{2,1,0:T(8,128)(2,1)S(1)}, u32[]{:S(2)}, u32[]{:S(2)}) %collective-permute-start.11) | collective-permute-done | bytes 65568 | tf_op jit(solution)/shard_map/ppermute | solution.py:42
  42.6 1.7 %shard_map.81 = (f32[32,1024]{1,0:T(8,128)}, bf16[32,1024]{1,0:T(8,128)(2,1)S(1)}, bf16[8,32,128]{2,1,0:T(8,128)(2,1)S(1)}) custom-call(bf16[8,32,128]{2,1,0:T(8,128)(2,1)S(1)} %collective-permute-done.12.scale_ref, f32[32,1024]{1,0:T(8,128)S(1)} %shard_map.80.image_ref, f32[32,1024]{1,0:T(8,128)S(1)} %get-tuple-element.95.marg_ref, ...), custom_call_target="tpu_custom_call" | custom-call | flops 536870912 | bytes 2424832 | tf_op jit(solution)/shard_map/pallas_call | solution.py:48
  45.6 1.6 %collective-permute-start.14 = (bf16[8,32,128]{2,1,0:T(8,128)(2,1)S(1)}, bf16[8,32,128]{2,1,0:T(8,128)(2,1)S(1)}, u32[]{:S(2)}, u32[]{:S(2)}) collective-permute-start(bf16[8,32,128]{2,1,0:T(8,128)(2,1)S(1)} %get-tuple-element.117), channel_id=1, source_target_pairs={{0,2},{1,5},{2,0},{3,7},{4,6},{5,1},{6,4},{7,3},{8,10},{9,13},{10,... | collective-permute-start | bytes 196616 | tf_op jit(solution)/shard_map/ppermute | solution.py:42
  47.2 2.8 %collective-permute-done.14.refs_0_ = bf16[8,32,128]{2,1,0:T(8,128)(2,1)S(1)} collective-permute-done((bf16[8,32,128]{2,1,0:T(8,128)(2,1)S(1)}, bf16[8,32,128]{2,1,0:T(8,128)(2,1)S(1)}, u32[]{:S(2)}, u32[]{:S(2)}) %collective-permute-start.14) | collective-permute-done | bytes 65568 | tf_op jit(solution)/shard_map/ppermute | solution.py:42
  50.0 4.6 %collective-permute-done.15.refs_0_ = bf16[8,32,128]{2,1,0:T(8,128)(2,1)S(1)} collective-permute-done((bf16[8,32,128]{2,1,0:T(8,128)(2,1)S(1)}, bf16[8,32,128]{2,1,0:T(8,128)(2,1)S(1)}, u32[]{:S(2)}, u32[]{:S(2)}) %collective-permute-start.15) | collective-permute-done | bytes 65568 | tf_op jit(solution)/shard_map/ppermute | solution.py:42
  55.0 4.8 %collective-permute-done.16.refs_0_ = bf16[8,32,128]{2,1,0:T(8,128)(2,1)S(1)} collective-permute-done((bf16[8,32,128]{2,1,0:T(8,128)(2,1)S(1)}, bf16[8,32,128]{2,1,0:T(8,128)(2,1)S(1)}, u32[]{:S(2)}, u32[]{:S(2)}) %collective-permute-start.16) | collective-permute-done | bytes 65568 | tf_op jit(solution)/shard_map/ppermute | solution.py:42
  61.2 1.5 %shard_map.87 = (f32[32,1024]{1,0:T(8,128)S(1)}, bf16[32,1024]{1,0:T(8,128)(2,1)S(1)}, bf16[8,32,128]{2,1,0:T(8,128)(2,1)S(1)}) custom-call(bf16[8,32,128]{2,1,0:T(8,128)(2,1)S(1)} %collective-permute-done.17.scale_ref, f32[32,1024]{1,0:T(8,128)S(1)} %shard_map.86.image_ref, f32[32,1024]{1,0:T(8,128)S(1)} %get-tuple-element.95.marg_ref, ...), custom_call_target="tpu_custom_call" | custom-call | flops 536870912 | bytes 2424832 | tf_op jit(solution)/shard_map/pallas_call | solution.py:48
  64.0 1.6 %collective-permute-start.19 = (bf16[8,32,128]{2,1,0:T(8,128)(2,1)S(1)}, bf16[8,32,128]{2,1,0:T(8,128)(2,1)S(1)}, u32[]{:S(2)}, u32[]{:S(2)}) collective-permute-start(bf16[8,32,128]{2,1,0:T(8,128)(2,1)S(1)} %get-tuple-element.115), channel_id=1, source_target_pairs={{0,2},{1,5},{2,0},{3,7},{4,6},{5,1},{6,4},{7,3},{8,10},{9,13},{10,... | collective-permute-start | bytes 196616 | tf_op jit(solution)/shard_map/ppermute | solution.py:42
  65.6 2.8 %collective-permute-done.19.refs_0_ = bf16[8,32,128]{2,1,0:T(8,128)(2,1)S(1)} collective-permute-done((bf16[8,32,128]{2,1,0:T(8,128)(2,1)S(1)}, bf16[8,32,128]{2,1,0:T(8,128)(2,1)S(1)}, u32[]{:S(2)}, u32[]{:S(2)}) %collective-permute-start.19) | collective-permute-done | bytes 65568 | tf_op jit(solution)/shard_map/ppermute | solution.py:42
  68.5 4.6 %collective-permute-done.20.refs_0_ = bf16[8,32,128]{2,1,0:T(8,128)(2,1)S(1)} collective-permute-done((bf16[8,32,128]{2,1,0:T(8,128)(2,1)S(1)}, bf16[8,32,128]{2,1,0:T(8,128)(2,1)S(1)}, u32[]{:S(2)}, u32[]{:S(2)}) %collective-permute-start.20) | collective-permute-done | bytes 65568 | tf_op jit(solution)/shard_map/ppermute | solution.py:42
  73.8 4.5 %collective-permute-done.21.refs_0_ = bf16[8,32,128]{2,1,0:T(8,128)(2,1)S(1)} collective-permute-done((bf16[8,32,128]{2,1,0:T(8,128)(2,1)S(1)}, bf16[8,32,128]{2,1,0:T(8,128)(2,1)S(1)}, u32[]{:S(2)}, u32[]{:S(2)}) %collective-permute-start.21) | collective-permute-done | bytes 65568 | tf_op jit(solution)/shard_map/ppermute | solution.py:42
  79.7 1.4 %shard_map.93 = (f32[32,1024]{1,0:T(8,128)}, f32[32,128]{1,0:T(8,128)}) custom-call(bf16[8,32,128]{2,1,0:T(8,128)(2,1)S(1)} %collective-permute-done.22.scale_ref, f32[32,1024]{1,0:T(8,128)S(1)} %shard_map.92.image_ref, f32[32,1024]{1,0:T(8,128)S(1)} %get-tuple-element.107.u_ref, f32[8,32,128]{2,1,0:T(8,128)S(1)} %get-tuple-element.112.scale_v_ref, ...), custom_call_target="tpu_custom_call" | custom-call | tf_op jit(solution)/shard_map/pallas_call | solution.py:347
  (65 shorter events, 18.0 us)
Async XLA Ops:
  0.6 7.9 %copy-start = (bf16[1024,256]{1,0:T(8,128)(2,1)S(1)}, bf16[1024,256]{1,0:T(8,128)(2,1)}, u32[]{:S(2)}) copy-start(bf16[1024,256]{1,0:T(8,128)(2,1)} %param.4) | copy-start | bytes 1572868
  1.6 7.6 %collective-permute-start = (bf16[144,256]{1,0:T(8,128)(2,1)S(1)}, bf16[144,256]{1,0:T(8,128)(2,1)S(1)}, u32[]{:S(2)}, u32[]{:S(2)}) collective-permute-start(bf16[144,256]{1,0:T(8,128)(2,1)S(1)} %shard_map.67), channel_id=1, source_target_pairs={{0,8},{1,5},{2,10},{3,7},{4,12},{5,1},{6,14},{7,3},{8,0},{9,13},{1... | collective-permute-start | bytes 221192 | tf_op jit(solution)/shard_map/ppermute | solution.py:42
  5.7 4.4 %collective-permute-start.1 = (bf16[144,256]{1,0:T(8,128)(2,1)S(1)}, bf16[144,256]{1,0:T(8,128)(2,1)S(1)}, u32[]{:S(2)}, u32[]{:S(2)}) collective-permute-start(bf16[144,256]{1,0:T(8,128)(2,1)S(1)} %shard_map.67), channel_id=1, source_target_pairs={{0,2},{1,3},{2,0},{3,1},{4,6},{5,7},{6,4},{7,5},{8,10},{9,11},{10,... | collective-permute-start | bytes 221192 | tf_op jit(solution)/shard_map/ppermute | solution.py:42
  10.1 6.0 %collective-permute-start.2 = (bf16[288,256]{1,0:T(8,128)(2,1)S(1)}, bf16[288,256]{1,0:T(8,128)(2,1)S(1)}, u32[]{:S(2)}, u32[]{:S(2)}) collective-permute-start(bf16[288,256]{1,0:T(8,128)(2,1)S(1)} %pad_maximum_fusion.1), channel_id=1, source_target_pairs={{0,4},{1,9},{2,6},{3,11},{4,0},{5,13},{6,2},{7,15},{8,12},{9,1},{1... | collective-permute-start | bytes 442376 | tf_op jit(solution)/shard_map/ppermute | solution.py:42
  11.7 4.4 %collective-permute-start.3 = (bf16[144,256]{1,0:T(8,128)(2,1)S(1)}, bf16[144,256]{1,0:T(8,128)(2,1)S(1)}, u32[]{:S(2)}, u32[]{:S(2)}) collective-permute-start(bf16[144,256]{1,0:T(8,128)(2,1)S(1)} %collective-permute-done), channel_id=1, source_target_pairs={{0,2},{1,3},{2,0},{3,1},{4,6},{5,7},{6,4},{7,5},{8,10},{9,11},{10,... | collective-permute-start | bytes 221192 | tf_op jit(solution)/shard_map/ppermute | solution.py:42
  16.1 3.7 %collective-permute-start.5 = (bf16[576,256]{1,0:T(8,128)(2,1)S(1)}, bf16[576,256]{1,0:T(8,128)(2,1)S(1)}, u32[]{:S(2)}, u32[]{:S(2)}) collective-permute-start(bf16[576,256]{1,0:T(8,128)(2,1)S(1)} %pad_maximum_fusion.held_ref.refs_9_.refs_0_), channel_id=1, source_target_pairs={{0,1},{1,0},{2,3},{3,2},{4,5},{5,4},{6,7},{7,6},{8,9},{9,8},{10,11... | collective-permute-start | bytes 884744 | tf_op jit(solution)/shard_map/ppermute | solution.py:42
  16.2 3.1 %collective-permute-start.6 = (bf16[288,256]{1,0:T(8,128)(2,1)S(1)}, bf16[288,256]{1,0:T(8,128)(2,1)S(1)}, u32[]{:S(2)}, u32[]{:S(2)}) collective-permute-start(bf16[288,256]{1,0:T(8,128)(2,1)S(1)} %constant_dynamic-update-slice_fusion.held_ref.refs_10_.refs_1_), channel_id=1, source_target_pairs={{0,1},{1,0},{2,3},{3,2},{4,5},{5,4},{6,7},{7,6},{8,9},{9,8},{10,11... | collective-permute-start | bytes 442376 | tf_op jit(solution)/shard_map/ppermute | solution.py:42
  16.8 5.8 %collective-permute-start.4 = (bf16[288,256]{1,0:T(8,128)(2,1)S(1)}, bf16[288,256]{1,0:T(8,128)(2,1)S(1)}, u32[]{:S(2)}, u32[]{:S(2)}) collective-permute-start(bf16[288,256]{1,0:T(8,128)(2,1)S(1)} %collective-permute-done.2), channel_id=1, source_target_pairs={{0,2},{1,3},{2,0},{3,1},{4,6},{5,7},{6,4},{7,5},{8,10},{9,11},{10,... | collective-permute-start | bytes 442376 | tf_op jit(solution)/shard_map/ppermute | solution.py:42
  22.6 1.4 %collective-permute-start.7 = (bf16[288,256]{1,0:T(8,128)(2,1)S(1)}, bf16[288,256]{1,0:T(8,128)(2,1)S(1)}, u32[]{:S(2)}, u32[]{:S(2)}) collective-permute-start(bf16[288,256]{1,0:T(8,128)(2,1)S(1)} %collective-permute-done.4.held_ref.refs_11_.refs_2_), channel_id=1, source_target_pairs={{0,1},{1,0},{2,3},{3,2},{4,5},{5,4},{6,7},{7,6},{8,9},{9,8},{10,11... | collective-permute-start | bytes 442376 | tf_op jit(solution)/shard_map/ppermute | solution.py:42
  25.1 1.3 %collective-permute-start.8 = (bf16[8,32,128]{2,1,0:T(8,128)(2,1)S(1)}, bf16[8,32,128]{2,1,0:T(8,128)(2,1)S(1)}, u32[]{:S(2)}, u32[]{:S(2)}) collective-permute-start(bf16[8,32,128]{2,1,0:T(8,128)(2,1)S(1)} %get-tuple-element.90), channel_id=1, source_target_pairs={{0,1},{1,0},{2,3},{3,2},{4,5},{5,4},{6,7},{7,6},{8,9},{9,8},{10,11... | collective-permute-start | bytes 196616 | tf_op jit(solution)/shard_map/ppermute | solution.py:42
  26.4 4.3 %collective-permute-start.9 = (bf16[8,32,128]{2,1,0:T(8,128)(2,1)S(1)}, bf16[8,32,128]{2,1,0:T(8,128)(2,1)S(1)}, u32[]{:S(2)}, u32[]{:S(2)}) collective-permute-start(bf16[8,32,128]{2,1,0:T(8,128)(2,1)S(1)} %get-tuple-element.119), channel_id=1, source_target_pairs={{0,2},{1,5},{2,0},{3,7},{4,6},{5,1},{6,4},{7,3},{8,10},{9,13},{10,... | collective-permute-start | bytes 196616 | tf_op jit(solution)/shard_map/ppermute | solution.py:42
  30.7 4.7 %collective-permute-start.10 = (bf16[8,32,128]{2,1,0:T(8,128)(2,1)S(1)}, bf16[8,32,128]{2,1,0:T(8,128)(2,1)S(1)}, u32[]{:S(2)}, u32[]{:S(2)}) collective-permute-start(bf16[8,32,128]{2,1,0:T(8,128)(2,1)S(1)} %get-tuple-element.92), channel_id=1, source_target_pairs={{0,4},{1,9},{2,6},{3,11},{4,0},{5,13},{6,2},{7,15},{8,12},{9,1},{1... | collective-permute-start | bytes 196616 | tf_op jit(solution)/shard_map/ppermute | solution.py:42
  35.4 5.8 %collective-permute-start.11 = (bf16[8,32,128]{2,1,0:T(8,128)(2,1)S(1)}, bf16[8,32,128]{2,1,0:T(8,128)(2,1)S(1)}, u32[]{:S(2)}, u32[]{:S(2)}) collective-permute-start(bf16[8,32,128]{2,1,0:T(8,128)(2,1)S(1)} %get-tuple-element.94), channel_id=1, source_target_pairs={{0,8},{1,3},{2,10},{3,1},{4,12},{5,7},{6,14},{7,5},{8,0},{9,11},{1... | collective-permute-start | bytes 196616 | tf_op jit(solution)/shard_map/ppermute | solution.py:42
  41.3 1.3 %collective-permute-start.12 = (bf16[8,32,128]{2,1,0:T(8,128)(2,1)S(1)}, bf16[8,32,128]{2,1,0:T(8,128)(2,1)S(1)}, u32[]{:S(2)}, u32[]{:S(2)}) collective-permute-start(bf16[8,32,128]{2,1,0:T(8,128)(2,1)S(1)} %shard_map.79.scale_ref), channel_id=1, source_target_pairs={{0,1},{1,0},{2,3},{3,2},{4,5},{5,4},{6,7},{7,6},{8,9},{9,8},{10,11... | collective-permute-start | bytes 196616 | tf_op jit(solution)/shard_map/ppermute | solution.py:42
  44.3 1.3 %collective-permute-start.13 = (bf16[8,32,128]{2,1,0:T(8,128)(2,1)S(1)}, bf16[8,32,128]{2,1,0:T(8,128)(2,1)S(1)}, u32[]{:S(2)}, u32[]{:S(2)}) collective-permute-start(bf16[8,32,128]{2,1,0:T(8,128)(2,1)S(1)} %get-tuple-element.97), channel_id=1, source_target_pairs={{0,1},{1,0},{2,3},{3,2},{4,5},{5,4},{6,7},{7,6},{8,9},{9,8},{10,11... | collective-permute-start | bytes 196616 | tf_op jit(solution)/shard_map/ppermute | solution.py:42
  45.6 4.3 %collective-permute-start.14 = (bf16[8,32,128]{2,1,0:T(8,128)(2,1)S(1)}, bf16[8,32,128]{2,1,0:T(8,128)(2,1)S(1)}, u32[]{:S(2)}, u32[]{:S(2)}) collective-permute-start(bf16[8,32,128]{2,1,0:T(8,128)(2,1)S(1)} %get-tuple-element.117), channel_id=1, source_target_pairs={{0,2},{1,5},{2,0},{3,7},{4,6},{5,1},{6,4},{7,3},{8,10},{9,13},{10,... | collective-permute-start | bytes 196616 | tf_op jit(solution)/shard_map/ppermute | solution.py:42
  50.0 4.7 %collective-permute-start.15 = (bf16[8,32,128]{2,1,0:T(8,128)(2,1)S(1)}, bf16[8,32,128]{2,1,0:T(8,128)(2,1)S(1)}, u32[]{:S(2)}, u32[]{:S(2)}) collective-permute-start(bf16[8,32,128]{2,1,0:T(8,128)(2,1)S(1)} %get-tuple-element.99), channel_id=1, source_target_pairs={{0,4},{1,9},{2,6},{3,11},{4,0},{5,13},{6,2},{7,15},{8,12},{9,1},{1... | collective-permute-start | bytes 196616 | tf_op jit(solution)/shard_map/ppermute | solution.py:42
  54.7 5.2 %collective-permute-start.16 = (bf16[8,32,128]{2,1,0:T(8,128)(2,1)S(1)}, bf16[8,32,128]{2,1,0:T(8,128)(2,1)S(1)}, u32[]{:S(2)}, u32[]{:S(2)}) collective-permute-start(bf16[8,32,128]{2,1,0:T(8,128)(2,1)S(1)} %get-tuple-element.101), channel_id=1, source_target_pairs={{0,8},{1,3},{2,10},{3,1},{4,12},{5,7},{6,14},{7,5},{8,0},{9,11},{1... | collective-permute-start | bytes 196616 | tf_op jit(solution)/shard_map/ppermute | solution.py:42
  59.9 1.3 %collective-permute-start.17 = (bf16[8,32,128]{2,1,0:T(8,128)(2,1)S(1)}, bf16[8,32,128]{2,1,0:T(8,128)(2,1)S(1)}, u32[]{:S(2)}, u32[]{:S(2)}) collective-permute-start(bf16[8,32,128]{2,1,0:T(8,128)(2,1)S(1)} %shard_map.85.scale_ref), channel_id=1, source_target_pairs={{0,1},{1,0},{2,3},{3,2},{4,5},{5,4},{6,7},{7,6},{8,9},{9,8},{10,11... | collective-permute-start | bytes 196616 | tf_op jit(solution)/shard_map/ppermute | solution.py:42
  62.7 1.3 %collective-permute-start.18 = (bf16[8,32,128]{2,1,0:T(8,128)(2,1)S(1)}, bf16[8,32,128]{2,1,0:T(8,128)(2,1)S(1)}, u32[]{:S(2)}, u32[]{:S(2)}) collective-permute-start(bf16[8,32,128]{2,1,0:T(8,128)(2,1)S(1)} %get-tuple-element.103), channel_id=1, source_target_pairs={{0,1},{1,0},{2,3},{3,2},{4,5},{5,4},{6,7},{7,6},{8,9},{9,8},{10,11... | collective-permute-start | bytes 196616 | tf_op jit(solution)/shard_map/ppermute | solution.py:42
  64.0 4.3 %collective-permute-start.19 = (bf16[8,32,128]{2,1,0:T(8,128)(2,1)S(1)}, bf16[8,32,128]{2,1,0:T(8,128)(2,1)S(1)}, u32[]{:S(2)}, u32[]{:S(2)}) collective-permute-start(bf16[8,32,128]{2,1,0:T(8,128)(2,1)S(1)} %get-tuple-element.115), channel_id=1, source_target_pairs={{0,2},{1,5},{2,0},{3,7},{4,6},{5,1},{6,4},{7,3},{8,10},{9,13},{10,... | collective-permute-start | bytes 196616 | tf_op jit(solution)/shard_map/ppermute | solution.py:42
  68.4 4.7 %collective-permute-start.20 = (bf16[8,32,128]{2,1,0:T(8,128)(2,1)S(1)}, bf16[8,32,128]{2,1,0:T(8,128)(2,1)S(1)}, u32[]{:S(2)}, u32[]{:S(2)}) collective-permute-start(bf16[8,32,128]{2,1,0:T(8,128)(2,1)S(1)} %get-tuple-element.105), channel_id=1, source_target_pairs={{0,4},{1,9},{2,6},{3,11},{4,0},{5,13},{6,2},{7,15},{8,12},{9,1},{1... | collective-permute-start | bytes 196616 | tf_op jit(solution)/shard_map/ppermute | solution.py:42
  73.1 5.2 %collective-permute-start.21 = (bf16[8,32,128]{2,1,0:T(8,128)(2,1)S(1)}, bf16[8,32,128]{2,1,0:T(8,128)(2,1)S(1)}, u32[]{:S(2)}, u32[]{:S(2)}) collective-permute-start(bf16[8,32,128]{2,1,0:T(8,128)(2,1)S(1)} %get-tuple-element.106), channel_id=1, source_target_pairs={{0,8},{1,3},{2,10},{3,1},{4,12},{5,7},{6,14},{7,5},{8,0},{9,11},{1... | collective-permute-start | bytes 196616 | tf_op jit(solution)/shard_map/ppermute | solution.py:42
  78.3 1.3 %collective-permute-start.22 = (bf16[8,32,128]{2,1,0:T(8,128)(2,1)S(1)}, bf16[8,32,128]{2,1,0:T(8,128)(2,1)S(1)}, u32[]{:S(2)}, u32[]{:S(2)}) collective-permute-start(bf16[8,32,128]{2,1,0:T(8,128)(2,1)S(1)} %get-tuple-element.111.scale_ref), channel_id=1, source_target_pairs={{0,1},{1,0},{2,3},{3,2},{4,5},{5,4},{6,7},{7,6},{8,9},{9,8},{10,11... | collective-permute-start | bytes 196616 | tf_op jit(solution)/shard_map/ppermute | solution.py:42
  (1 other events, 0.7 us)

commit v11 on v8

--- a/solution.py
+++ b/solution.py
@@ -26,7 +26,7 @@
 
 def rounds(core, top):
     bits = list(range(1, top))
-    bits = bits[core:] + bits[:core]
+    bits = bits[1 - core :] + bits[: 1 - core]
     return [bits[low : low + 2] for low in range(0, len(bits), 2)]
 
 

time: 77.9 us -> 76.6 us (0.983)
  waiting for transfers between devices: 34.2 us -> 30 us
  starting transfers between devices: 26.9 us -> 29.8 us
    ppermute x26, waiting for transfers between devices: 34.2 us -> 30 us  [exchange(): lax.ppermute(block, 'row', [(d, d ^ flips[d % len(flips)]) for d in range...]
    ppermute x26, starting transfers between devices: 26.9 us -> 29.8 us  [exchange(): lax.ppermute(block, 'row', [(d, d ^ flips[d % len(flips)]) for d in range...]
where the time goes in v11:
time: 76.6 us; the launch traced here: 76.4 us
  waiting for transfers between devices  30 us (39%)
  starting transfers between devices  29.8 us (39%)
  Pallas kernels  13 us (17%)
  other arithmetic  2.25 us (3%)
  between operations  0.9 us (1%)
    ppermute x26, waiting for transfers between devices, exchange(): lax.ppermute(block, 'row', [(d, d ^ flips[d % len(flips)]) for d in range...  30 us
    ppermute x26, starting transfers between devices, exchange(): lax.ppermute(block, 'row', [(d, d ^ flips[d % len(flips)]) for d in range...  29.8 us
    pallas_call x22, Pallas kernels, call(): pl.pallas_call(body, out_shape=[pltpu.VMEM(shape, dtype) for shape, dtype...  10.7 us
  transfers between devices with their start and end apart: 26, of which 22 were waited for; matrix products, arithmetic and copies ran while one was open for 3% of the time, Pallas kernels for 8%

profile of v11, /device:TPU:0, one launch (start us, length us, event | category | flops | bytes accessed | tf_op | source)
XLA Modules:
  0.0 76.4 jit_solution(4268544724232526276)
XLA Ops:
  1.6 4.1 %collective-permute-start = (bf16[144,256]{1,0:T(8,128)(2,1)S(1)}, bf16[144,256]{1,0:T(8,128)(2,1)S(1)}, u32[]{:S(2)}, u32[]{:S(2)}) collective-permute-start(bf16[144,256]{1,0:T(8,128)(2,1)S(1)} %shard_map.67), channel_id=1, source_target_pairs={{0,8},{1,5},{2,10},{3,7},{4,12},{5,1},{6,14},{7,3},{8,0},{9,13},{1... | collective-permute-start | bytes 221192 | tf_op jit(solution)/shard_map/ppermute | solution.py:42
  5.7 1.5 %collective-permute-start.1 = (bf16[144,256]{1,0:T(8,128)(2,1)S(1)}, bf16[144,256]{1,0:T(8,128)(2,1)S(1)}, u32[]{:S(2)}, u32[]{:S(2)}) collective-permute-start(bf16[144,256]{1,0:T(8,128)(2,1)S(1)} %shard_map.67), channel_id=1, source_target_pairs={{0,2},{1,3},{2,0},{3,1},{4,6},{5,7},{6,4},{7,5},{8,10},{9,11},{10,... | collective-permute-start | bytes 221192 | tf_op jit(solution)/shard_map/ppermute | solution.py:42
  10.1 1.6 %collective-permute-start.2 = (bf16[288,256]{1,0:T(8,128)(2,1)S(1)}, bf16[288,256]{1,0:T(8,128)(2,1)S(1)}, u32[]{:S(2)}, u32[]{:S(2)}) collective-permute-start(bf16[288,256]{1,0:T(8,128)(2,1)S(1)} %pad_maximum_fusion.1), channel_id=1, source_target_pairs={{0,4},{1,9},{2,6},{3,11},{4,0},{5,13},{6,2},{7,15},{8,12},{9,1},{1... | collective-permute-start | bytes 442376 | tf_op jit(solution)/shard_map/ppermute | solution.py:42
  11.7 1.5 %collective-permute-start.3 = (bf16[144,256]{1,0:T(8,128)(2,1)S(1)}, bf16[144,256]{1,0:T(8,128)(2,1)S(1)}, u32[]{:S(2)}, u32[]{:S(2)}) collective-permute-start(bf16[144,256]{1,0:T(8,128)(2,1)S(1)} %collective-permute-done), channel_id=1, source_target_pairs={{0,2},{1,3},{2,0},{3,1},{4,6},{5,7},{6,4},{7,5},{8,10},{9,11},{10,... | collective-permute-start | bytes 221192 | tf_op jit(solution)/shard_map/ppermute | solution.py:42
  13.2 2.8 %collective-permute-done.3 = bf16[144,256]{1,0:T(8,128)(2,1)S(1)} collective-permute-done((bf16[144,256]{1,0:T(8,128)(2,1)S(1)}, bf16[144,256]{1,0:T(8,128)(2,1)S(1)}, u32[]{:S(2)}, u32[]{:S(2)}) %collective-permute-start.3) | collective-permute-done | bytes 73760 | tf_op jit(solution)/shard_map/ppermute | solution.py:42
  16.8 1.5 %collective-permute-start.4 = (bf16[288,256]{1,0:T(8,128)(2,1)S(1)}, bf16[288,256]{1,0:T(8,128)(2,1)S(1)}, u32[]{:S(2)}, u32[]{:S(2)}) collective-permute-start(bf16[288,256]{1,0:T(8,128)(2,1)S(1)} %collective-permute-done.2), channel_id=1, source_target_pairs={{0,2},{1,3},{2,0},{3,1},{4,6},{5,7},{6,4},{7,5},{8,10},{9,11},{10,... | collective-permute-start | bytes 442376 | tf_op jit(solution)/shard_map/ppermute | solution.py:42
  20.4 2.2 %collective-permute-done.4.held_ref.refs_11_.refs_2_ = bf16[288,256]{1,0:T(8,128)(2,1)S(1)} collective-permute-done((bf16[288,256]{1,0:T(8,128)(2,1)S(1)}, bf16[288,256]{1,0:T(8,128)(2,1)S(1)}, u32[]{:S(2)}, u32[]{:S(2)}) %collective-permute-start.4) | collective-permute-done | bytes 147488 | tf_op jit(solution)/shard_map/ppermute | solution.py:42
  27.2 1.6 %collective-permute-start.10 = (bf16[8,32,128]{2,1,0:T(8,128)(2,1)S(1)}, bf16[8,32,128]{2,1,0:T(8,128)(2,1)S(1)}, u32[]{:S(2)}, u32[]{:S(2)}) collective-permute-start(bf16[8,32,128]{2,1,0:T(8,128)(2,1)S(1)} %get-tuple-element.107), channel_id=1, source_target_pairs={{0,8},{1,5},{2,10},{3,7},{4,12},{5,1},{6,14},{7,3},{8,0},{9,13},{1... | collective-permute-start | bytes 196616 | tf_op jit(solution)/shard_map/ppermute | solution.py:42
  28.8 2.0 %collective-permute-start.11 = (bf16[8,32,128]{2,1,0:T(8,128)(2,1)S(1)}, bf16[8,32,128]{2,1,0:T(8,128)(2,1)S(1)}, u32[]{:S(2)}, u32[]{:S(2)}) collective-permute-start(bf16[8,32,128]{2,1,0:T(8,128)(2,1)S(1)} %get-tuple-element.107), channel_id=1, source_target_pairs={{0,12},{1,7},{2,14},{3,5},{4,8},{5,3},{6,10},{7,1},{8,4},{9,15},{1... | collective-permute-start | bytes 196616 | tf_op jit(solution)/shard_map/ppermute | solution.py:42
  32.5 2.4 %collective-permute-done.11.refs_2_ = bf16[8,32,128]{2,1,0:T(8,128)(2,1)S(1)} collective-permute-done((bf16[8,32,128]{2,1,0:T(8,128)(2,1)S(1)}, bf16[8,32,128]{2,1,0:T(8,128)(2,1)S(1)}, u32[]{:S(2)}, u32[]{:S(2)}) %collective-permute-start.11) | collective-permute-done | bytes 65568 | tf_op jit(solution)/shard_map/ppermute | solution.py:42
  34.9 1.6 %collective-permute-start.12 = (bf16[8,32,128]{2,1,0:T(8,128)(2,1)S(1)}, bf16[8,32,128]{2,1,0:T(8,128)(2,1)S(1)}, u32[]{:S(2)}, u32[]{:S(2)}) collective-permute-start(bf16[8,32,128]{2,1,0:T(8,128)(2,1)S(1)} %get-tuple-element.86), channel_id=1, source_target_pairs={{0,2},{1,9},{2,0},{3,11},{4,6},{5,13},{6,4},{7,15},{8,10},{9,1},{1... | collective-permute-start | bytes 196616 | tf_op jit(solution)/shard_map/ppermute | solution.py:42
  36.6 2.6 %collective-permute-done.12.refs_0_ = bf16[8,32,128]{2,1,0:T(8,128)(2,1)S(1)} collective-permute-done((bf16[8,32,128]{2,1,0:T(8,128)(2,1)S(1)}, bf16[8,32,128]{2,1,0:T(8,128)(2,1)S(1)}, u32[]{:S(2)}, u32[]{:S(2)}) %collective-permute-start.12) | collective-permute-done | bytes 65568 | tf_op jit(solution)/shard_map/ppermute | solution.py:42
  40.6 1.7 %shard_map.80 = (f32[32,1024]{1,0:T(8,128)}, bf16[32,1024]{1,0:T(8,128)(2,1)S(1)}, bf16[8,32,128]{2,1,0:T(8,128)(2,1)S(1)}) custom-call(bf16[8,32,128]{2,1,0:T(8,128)(2,1)S(1)} %collective-permute-done.13.scale_ref, f32[32,1024]{1,0:T(8,128)S(1)} %shard_map.79.image_ref, f32[32,1024]{1,0:T(8,128)S(1)} %get-tuple-element.87.marg_ref, ...), custom_call_target="tpu_custom_call" | custom-call | flops 536870912 | bytes 2424832 | tf_op jit(solution)/shard_map/pallas_call | solution.py:48
  43.7 2.6 %collective-permute-start.16 = (bf16[8,32,128]{2,1,0:T(8,128)(2,1)S(1)}, bf16[8,32,128]{2,1,0:T(8,128)(2,1)S(1)}, u32[]{:S(2)}, u32[]{:S(2)}) collective-permute-start(bf16[8,32,128]{2,1,0:T(8,128)(2,1)S(1)} %get-tuple-element.105), channel_id=1, source_target_pairs={{0,8},{1,5},{2,10},{3,7},{4,12},{5,1},{6,14},{7,3},{8,0},{9,13},{1... | collective-permute-start | bytes 196616 | tf_op jit(solution)/shard_map/ppermute | solution.py:42
  46.2 1.8 %collective-permute-start.17 = (bf16[8,32,128]{2,1,0:T(8,128)(2,1)S(1)}, bf16[8,32,128]{2,1,0:T(8,128)(2,1)S(1)}, u32[]{:S(2)}, u32[]{:S(2)}) collective-permute-start(bf16[8,32,128]{2,1,0:T(8,128)(2,1)S(1)} %get-tuple-element.105), channel_id=1, source_target_pairs={{0,12},{1,7},{2,14},{3,5},{4,8},{5,3},{6,10},{7,1},{8,4},{9,15},{1... | collective-permute-start | bytes 196616 | tf_op jit(solution)/shard_map/ppermute | solution.py:42
  49.0 3.3 %collective-permute-done.17.refs_2_ = bf16[8,32,128]{2,1,0:T(8,128)(2,1)S(1)} collective-permute-done((bf16[8,32,128]{2,1,0:T(8,128)(2,1)S(1)}, bf16[8,32,128]{2,1,0:T(8,128)(2,1)S(1)}, u32[]{:S(2)}, u32[]{:S(2)}) %collective-permute-start.17) | collective-permute-done | bytes 65568 | tf_op jit(solution)/shard_map/ppermute | solution.py:42
  52.3 1.6 %collective-permute-start.18 = (bf16[8,32,128]{2,1,0:T(8,128)(2,1)S(1)}, bf16[8,32,128]{2,1,0:T(8,128)(2,1)S(1)}, u32[]{:S(2)}, u32[]{:S(2)}) collective-permute-start(bf16[8,32,128]{2,1,0:T(8,128)(2,1)S(1)} %get-tuple-element.91), channel_id=1, source_target_pairs={{0,2},{1,9},{2,0},{3,11},{4,6},{5,13},{6,4},{7,15},{8,10},{9,1},{1... | collective-permute-start | bytes 196616 | tf_op jit(solution)/shard_map/ppermute | solution.py:42
  54.0 2.7 %collective-permute-done.18.refs_0_ = bf16[8,32,128]{2,1,0:T(8,128)(2,1)S(1)} collective-permute-done((bf16[8,32,128]{2,1,0:T(8,128)(2,1)S(1)}, bf16[8,32,128]{2,1,0:T(8,128)(2,1)S(1)}, u32[]{:S(2)}, u32[]{:S(2)}) %collective-permute-start.18) | collective-permute-done | bytes 65568 | tf_op jit(solution)/shard_map/ppermute | solution.py:42
  58.0 1.5 %shard_map.85 = (f32[32,1024]{1,0:T(8,128)S(1)}, bf16[32,1024]{1,0:T(8,128)(2,1)S(1)}, bf16[8,32,128]{2,1,0:T(8,128)(2,1)S(1)}) custom-call(bf16[8,32,128]{2,1,0:T(8,128)(2,1)S(1)} %collective-permute-done.19.scale_ref, f32[32,1024]{1,0:T(8,128)S(1)} %shard_map.84.image_ref, f32[32,1024]{1,0:T(8,128)S(1)} %get-tuple-element.87.marg_ref, ...), custom_call_target="tpu_custom_call" | custom-call | flops 536870912 | bytes 2424832 | tf_op jit(solution)/shard_map/pallas_call | solution.py:48
  60.9 2.4 %collective-permute-start.22 = (bf16[8,32,128]{2,1,0:T(8,128)(2,1)S(1)}, bf16[8,32,128]{2,1,0:T(8,128)(2,1)S(1)}, u32[]{:S(2)}, u32[]{:S(2)}) collective-permute-start(bf16[8,32,128]{2,1,0:T(8,128)(2,1)S(1)} %get-tuple-element.103), channel_id=1, source_target_pairs={{0,8},{1,5},{2,10},{3,7},{4,12},{5,1},{6,14},{7,3},{8,0},{9,13},{1... | collective-permute-start | bytes 196616 | tf_op jit(solution)/shard_map/ppermute | solution.py:42
  63.3 2.0 %collective-permute-start.23 = (bf16[8,32,128]{2,1,0:T(8,128)(2,1)S(1)}, bf16[8,32,128]{2,1,0:T(8,128)(2,1)S(1)}, u32[]{:S(2)}, u32[]{:S(2)}) collective-permute-start(bf16[8,32,128]{2,1,0:T(8,128)(2,1)S(1)} %get-tuple-element.103), channel_id=1, source_target_pairs={{0,12},{1,7},{2,14},{3,5},{4,8},{5,3},{6,10},{7,1},{8,4},{9,15},{1... | collective-permute-start | bytes 196616 | tf_op jit(solution)/shard_map/ppermute | solution.py:42
  66.2 3.1 %collective-permute-done.23.refs_2_ = bf16[8,32,128]{2,1,0:T(8,128)(2,1)S(1)} collective-permute-done((bf16[8,32,128]{2,1,0:T(8,128)(2,1)S(1)}, bf16[8,32,128]{2,1,0:T(8,128)(2,1)S(1)}, u32[]{:S(2)}, u32[]{:S(2)}) %collective-permute-start.23) | collective-permute-done | bytes 65568 | tf_op jit(solution)/shard_map/ppermute | solution.py:42
  69.4 1.6 %collective-permute-start.24 = (bf16[8,32,128]{2,1,0:T(8,128)(2,1)S(1)}, bf16[8,32,128]{2,1,0:T(8,128)(2,1)S(1)}, u32[]{:S(2)}, u32[]{:S(2)}) collective-permute-start(bf16[8,32,128]{2,1,0:T(8,128)(2,1)S(1)} %get-tuple-element.94), channel_id=1, source_target_pairs={{0,2},{1,9},{2,0},{3,11},{4,6},{5,13},{6,4},{7,15},{8,10},{9,1},{1... | collective-permute-start | bytes 196616 | tf_op jit(solution)/shard_map/ppermute | solution.py:42
  71.7 2.0 %collective-permute-done.24.refs_0_ = bf16[8,32,128]{2,1,0:T(8,128)(2,1)S(1)} collective-permute-done((bf16[8,32,128]{2,1,0:T(8,128)(2,1)S(1)}, bf16[8,32,128]{2,1,0:T(8,128)(2,1)S(1)}, u32[]{:S(2)}, u32[]{:S(2)}) %collective-permute-start.24) | collective-permute-done | bytes 65568 | tf_op jit(solution)/shard_map/ppermute | solution.py:42
  (68 shorter events, 23.7 us)
Async XLA Ops:
  1.6 7.6 %collective-permute-start = (bf16[144,256]{1,0:T(8,128)(2,1)S(1)}, bf16[144,256]{1,0:T(8,128)(2,1)S(1)}, u32[]{:S(2)}, u32[]{:S(2)}) collective-permute-start(bf16[144,256]{1,0:T(8,128)(2,1)S(1)} %shard_map.67), channel_id=1, source_target_pairs={{0,8},{1,5},{2,10},{3,7},{4,12},{5,1},{6,14},{7,3},{8,0},{9,13},{1... | collective-permute-start | bytes 221192 | tf_op jit(solution)/shard_map/ppermute | solution.py:42
  5.7 4.4 %collective-permute-start.1 = (bf16[144,256]{1,0:T(8,128)(2,1)S(1)}, bf16[144,256]{1,0:T(8,128)(2,1)S(1)}, u32[]{:S(2)}, u32[]{:S(2)}) collective-permute-start(bf16[144,256]{1,0:T(8,128)(2,1)S(1)} %shard_map.67), channel_id=1, source_target_pairs={{0,2},{1,3},{2,0},{3,1},{4,6},{5,7},{6,4},{7,5},{8,10},{9,11},{10,... | collective-permute-start | bytes 221192 | tf_op jit(solution)/shard_map/ppermute | solution.py:42
  10.1 6.0 %collective-permute-start.2 = (bf16[288,256]{1,0:T(8,128)(2,1)S(1)}, bf16[288,256]{1,0:T(8,128)(2,1)S(1)}, u32[]{:S(2)}, u32[]{:S(2)}) collective-permute-start(bf16[288,256]{1,0:T(8,128)(2,1)S(1)} %pad_maximum_fusion.1), channel_id=1, source_target_pairs={{0,4},{1,9},{2,6},{3,11},{4,0},{5,13},{6,2},{7,15},{8,12},{9,1},{1... | collective-permute-start | bytes 442376 | tf_op jit(solution)/shard_map/ppermute | solution.py:42
  11.7 4.4 %collective-permute-start.3 = (bf16[144,256]{1,0:T(8,128)(2,1)S(1)}, bf16[144,256]{1,0:T(8,128)(2,1)S(1)}, u32[]{:S(2)}, u32[]{:S(2)}) collective-permute-start(bf16[144,256]{1,0:T(8,128)(2,1)S(1)} %collective-permute-done), channel_id=1, source_target_pairs={{0,2},{1,3},{2,0},{3,1},{4,6},{5,7},{6,4},{7,5},{8,10},{9,11},{10,... | collective-permute-start | bytes 221192 | tf_op jit(solution)/shard_map/ppermute | solution.py:42
  16.1 3.7 %collective-permute-start.5 = (bf16[576,256]{1,0:T(8,128)(2,1)S(1)}, bf16[576,256]{1,0:T(8,128)(2,1)S(1)}, u32[]{:S(2)}, u32[]{:S(2)}) collective-permute-start(bf16[576,256]{1,0:T(8,128)(2,1)S(1)} %pad_maximum_fusion.held_ref.refs_9_.refs_0_), channel_id=1, source_target_pairs={{0,1},{1,0},{2,3},{3,2},{4,5},{5,4},{6,7},{7,6},{8,9},{9,8},{10,11... | collective-permute-start | bytes 884744 | tf_op jit(solution)/shard_map/ppermute | solution.py:42
  16.2 3.1 %collective-permute-start.6 = (bf16[288,256]{1,0:T(8,128)(2,1)S(1)}, bf16[288,256]{1,0:T(8,128)(2,1)S(1)}, u32[]{:S(2)}, u32[]{:S(2)}) collective-permute-start(bf16[288,256]{1,0:T(8,128)(2,1)S(1)} %constant_dynamic-update-slice_fusion.held_ref.refs_10_.refs_1_), channel_id=1, source_target_pairs={{0,1},{1,0},{2,3},{3,2},{4,5},{5,4},{6,7},{7,6},{8,9},{9,8},{10,11... | collective-permute-start | bytes 442376 | tf_op jit(solution)/shard_map/ppermute | solution.py:42
  16.8 5.8 %collective-permute-start.4 = (bf16[288,256]{1,0:T(8,128)(2,1)S(1)}, bf16[288,256]{1,0:T(8,128)(2,1)S(1)}, u32[]{:S(2)}, u32[]{:S(2)}) collective-permute-start(bf16[288,256]{1,0:T(8,128)(2,1)S(1)} %collective-permute-done.2), channel_id=1, source_target_pairs={{0,2},{1,3},{2,0},{3,1},{4,6},{5,7},{6,4},{7,5},{8,10},{9,11},{10,... | collective-permute-start | bytes 442376 | tf_op jit(solution)/shard_map/ppermute | solution.py:42
  22.6 1.4 %collective-permute-start.7 = (bf16[288,256]{1,0:T(8,128)(2,1)S(1)}, bf16[288,256]{1,0:T(8,128)(2,1)S(1)}, u32[]{:S(2)}, u32[]{:S(2)}) collective-permute-start(bf16[288,256]{1,0:T(8,128)(2,1)S(1)} %collective-permute-done.4.held_ref.refs_11_.refs_2_), channel_id=1, source_target_pairs={{0,1},{1,0},{2,3},{3,2},{4,5},{5,4},{6,7},{7,6},{8,9},{9,8},{10,11... | collective-permute-start | bytes 442376 | tf_op jit(solution)/shard_map/ppermute | solution.py:42
  25.1 1.3 %collective-permute-start.8 = (bf16[8,32,128]{2,1,0:T(8,128)(2,1)S(1)}, bf16[8,32,128]{2,1,0:T(8,128)(2,1)S(1)}, u32[]{:S(2)}, u32[]{:S(2)}) collective-permute-start(bf16[8,32,128]{2,1,0:T(8,128)(2,1)S(1)} %get-tuple-element.84), channel_id=1, source_target_pairs={{0,1},{1,0},{2,3},{3,2},{4,5},{5,4},{6,7},{7,6},{8,9},{9,8},{10,11... | collective-permute-start | bytes 196616 | tf_op jit(solution)/shard_map/ppermute | solution.py:42
  26.4 4.7 %collective-permute-start.9 = (bf16[8,32,128]{2,1,0:T(8,128)(2,1)S(1)}, bf16[8,32,128]{2,1,0:T(8,128)(2,1)S(1)}, u32[]{:S(2)}, u32[]{:S(2)}) collective-permute-start(bf16[8,32,128]{2,1,0:T(8,128)(2,1)S(1)} %get-tuple-element.107), channel_id=1, source_target_pairs={{0,4},{1,3},{2,6},{3,1},{4,0},{5,7},{6,2},{7,5},{8,12},{9,11},{10,... | collective-permute-start | bytes 196616 | tf_op jit(solution)/shard_map/ppermute | solution.py:42
  27.2 5.3 %collective-permute-start.10 = (bf16[8,32,128]{2,1,0:T(8,128)(2,1)S(1)}, bf16[8,32,128]{2,1,0:T(8,128)(2,1)S(1)}, u32[]{:S(2)}, u32[]{:S(2)}) collective-permute-start(bf16[8,32,128]{2,1,0:T(8,128)(2,1)S(1)} %get-tuple-element.107), channel_id=1, source_target_pairs={{0,8},{1,5},{2,10},{3,7},{4,12},{5,1},{6,14},{7,3},{8,0},{9,13},{1... | collective-permute-start | bytes 196616 | tf_op jit(solution)/shard_map/ppermute | solution.py:42
  28.8 6.1 %collective-permute-start.11 = (bf16[8,32,128]{2,1,0:T(8,128)(2,1)S(1)}, bf16[8,32,128]{2,1,0:T(8,128)(2,1)S(1)}, u32[]{:S(2)}, u32[]{:S(2)}) collective-permute-start(bf16[8,32,128]{2,1,0:T(8,128)(2,1)S(1)} %get-tuple-element.107), channel_id=1, source_target_pairs={{0,12},{1,7},{2,14},{3,5},{4,8},{5,3},{6,10},{7,1},{8,4},{9,15},{1... | collective-permute-start | bytes 196616 | tf_op jit(solution)/shard_map/ppermute | solution.py:42
  34.9 4.3 %collective-permute-start.12 = (bf16[8,32,128]{2,1,0:T(8,128)(2,1)S(1)}, bf16[8,32,128]{2,1,0:T(8,128)(2,1)S(1)}, u32[]{:S(2)}, u32[]{:S(2)}) collective-permute-start(bf16[8,32,128]{2,1,0:T(8,128)(2,1)S(1)} %get-tuple-element.86), channel_id=1, source_target_pairs={{0,2},{1,9},{2,0},{3,11},{4,6},{5,13},{6,4},{7,15},{8,10},{9,1},{1... | collective-permute-start | bytes 196616 | tf_op jit(solution)/shard_map/ppermute | solution.py:42
  39.2 1.3 %collective-permute-start.13 = (bf16[8,32,128]{2,1,0:T(8,128)(2,1)S(1)}, bf16[8,32,128]{2,1,0:T(8,128)(2,1)S(1)}, u32[]{:S(2)}, u32[]{:S(2)}) collective-permute-start(bf16[8,32,128]{2,1,0:T(8,128)(2,1)S(1)} %shard_map.78.scale_ref), channel_id=1, source_target_pairs={{0,1},{1,0},{2,3},{3,2},{4,5},{5,4},{6,7},{7,6},{8,9},{9,8},{10,11... | collective-permute-start | bytes 196616 | tf_op jit(solution)/shard_map/ppermute | solution.py:42
  43.6 4.7 %collective-permute-start.15 = (bf16[8,32,128]{2,1,0:T(8,128)(2,1)S(1)}, bf16[8,32,128]{2,1,0:T(8,128)(2,1)S(1)}, u32[]{:S(2)}, u32[]{:S(2)}) collective-permute-start(bf16[8,32,128]{2,1,0:T(8,128)(2,1)S(1)} %get-tuple-element.105), channel_id=1, source_target_pairs={{0,4},{1,3},{2,6},{3,1},{4,0},{5,7},{6,2},{7,5},{8,12},{9,11},{10,... | collective-permute-start | bytes 196616 | tf_op jit(solution)/shard_map/ppermute | solution.py:42
  43.7 5.3 %collective-permute-start.16 = (bf16[8,32,128]{2,1,0:T(8,128)(2,1)S(1)}, bf16[8,32,128]{2,1,0:T(8,128)(2,1)S(1)}, u32[]{:S(2)}, u32[]{:S(2)}) collective-permute-start(bf16[8,32,128]{2,1,0:T(8,128)(2,1)S(1)} %get-tuple-element.105), channel_id=1, source_target_pairs={{0,8},{1,5},{2,10},{3,7},{4,12},{5,1},{6,14},{7,3},{8,0},{9,13},{1... | collective-permute-start | bytes 196616 | tf_op jit(solution)/shard_map/ppermute | solution.py:42
  46.2 6.1 %collective-permute-start.17 = (bf16[8,32,128]{2,1,0:T(8,128)(2,1)S(1)}, bf16[8,32,128]{2,1,0:T(8,128)(2,1)S(1)}, u32[]{:S(2)}, u32[]{:S(2)}) collective-permute-start(bf16[8,32,128]{2,1,0:T(8,128)(2,1)S(1)} %get-tuple-element.105), channel_id=1, source_target_pairs={{0,12},{1,7},{2,14},{3,5},{4,8},{5,3},{6,10},{7,1},{8,4},{9,15},{1... | collective-permute-start | bytes 196616 | tf_op jit(solution)/shard_map/ppermute | solution.py:42
  52.3 4.3 %collective-permute-start.18 = (bf16[8,32,128]{2,1,0:T(8,128)(2,1)S(1)}, bf16[8,32,128]{2,1,0:T(8,128)(2,1)S(1)}, u32[]{:S(2)}, u32[]{:S(2)}) collective-permute-start(bf16[8,32,128]{2,1,0:T(8,128)(2,1)S(1)} %get-tuple-element.91), channel_id=1, source_target_pairs={{0,2},{1,9},{2,0},{3,11},{4,6},{5,13},{6,4},{7,15},{8,10},{9,1},{1... | collective-permute-start | bytes 196616 | tf_op jit(solution)/shard_map/ppermute | solution.py:42
  56.7 1.3 %collective-permute-start.19 = (bf16[8,32,128]{2,1,0:T(8,128)(2,1)S(1)}, bf16[8,32,128]{2,1,0:T(8,128)(2,1)S(1)}, u32[]{:S(2)}, u32[]{:S(2)}) collective-permute-start(bf16[8,32,128]{2,1,0:T(8,128)(2,1)S(1)} %shard_map.83.scale_ref), channel_id=1, source_target_pairs={{0,1},{1,0},{2,3},{3,2},{4,5},{5,4},{6,7},{7,6},{8,9},{9,8},{10,11... | collective-permute-start | bytes 196616 | tf_op jit(solution)/shard_map/ppermute | solution.py:42
  60.8 4.6 %collective-permute-start.21 = (bf16[8,32,128]{2,1,0:T(8,128)(2,1)S(1)}, bf16[8,32,128]{2,1,0:T(8,128)(2,1)S(1)}, u32[]{:S(2)}, u32[]{:S(2)}) collective-permute-start(bf16[8,32,128]{2,1,0:T(8,128)(2,1)S(1)} %get-tuple-element.103), channel_id=1, source_target_pairs={{0,4},{1,3},{2,6},{3,1},{4,0},{5,7},{6,2},{7,5},{8,12},{9,11},{10,... | collective-permute-start | bytes 196616 | tf_op jit(solution)/shard_map/ppermute | solution.py:42
  60.9 5.3 %collective-permute-start.22 = (bf16[8,32,128]{2,1,0:T(8,128)(2,1)S(1)}, bf16[8,32,128]{2,1,0:T(8,128)(2,1)S(1)}, u32[]{:S(2)}, u32[]{:S(2)}) collective-permute-start(bf16[8,32,128]{2,1,0:T(8,128)(2,1)S(1)} %get-tuple-element.103), channel_id=1, source_target_pairs={{0,8},{1,5},{2,10},{3,7},{4,12},{5,1},{6,14},{7,3},{8,0},{9,13},{1... | collective-permute-start | bytes 196616 | tf_op jit(solution)/shard_map/ppermute | solution.py:42
  63.3 6.1 %collective-permute-start.23 = (bf16[8,32,128]{2,1,0:T(8,128)(2,1)S(1)}, bf16[8,32,128]{2,1,0:T(8,128)(2,1)S(1)}, u32[]{:S(2)}, u32[]{:S(2)}) collective-permute-start(bf16[8,32,128]{2,1,0:T(8,128)(2,1)S(1)} %get-tuple-element.103), channel_id=1, source_target_pairs={{0,12},{1,7},{2,14},{3,5},{4,8},{5,3},{6,10},{7,1},{8,4},{9,15},{1... | collective-permute-start | bytes 196616 | tf_op jit(solution)/shard_map/ppermute | solution.py:42
  69.4 4.3 %collective-permute-start.24 = (bf16[8,32,128]{2,1,0:T(8,128)(2,1)S(1)}, bf16[8,32,128]{2,1,0:T(8,128)(2,1)S(1)}, u32[]{:S(2)}, u32[]{:S(2)}) collective-permute-start(bf16[8,32,128]{2,1,0:T(8,128)(2,1)S(1)} %get-tuple-element.94), channel_id=1, source_target_pairs={{0,2},{1,9},{2,0},{3,11},{4,6},{5,13},{6,4},{7,15},{8,10},{9,1},{1... | collective-permute-start | bytes 196616 | tf_op jit(solution)/shard_map/ppermute | solution.py:42
  73.7 1.3 %collective-permute-start.25 = (bf16[8,32,128]{2,1,0:T(8,128)(2,1)S(1)}, bf16[8,32,128]{2,1,0:T(8,128)(2,1)S(1)}, u32[]{:S(2)}, u32[]{:S(2)}) collective-permute-start(bf16[8,32,128]{2,1,0:T(8,128)(2,1)S(1)} %get-tuple-element.99.scale_ref), channel_id=1, source_target_pairs={{0,1},{1,0},{2,3},{3,2},{4,5},{5,4},{6,7},{7,6},{8,9},{9,8},{10,11... | collective-permute-start | bytes 196616 | tf_op jit(solution)/shard_map/ppermute | solution.py:42
  (4 other events, 11.1 us)

commit v12 on v11

--- a/solution.py
+++ b/solution.py
@@ -19,14 +19,18 @@
 BF16 = jnp.bfloat16
 
 
-def slot_bits(core, top):
+def parity(index, top):
+    return sum(index // (1 << bit) % 2 for bit in range(top)) % 2
+
+
+def slot_bits(kind, top):
     layer = list(range(2, top))
-    return (layer if core else layer[::-1]) + [1]
-
-
-def rounds(core, top):
+    return (layer if kind else layer[::-1]) + [1]
+
+
+def rounds(kind, top):
     bits = list(range(1, top))
-    bits = bits[1 - core :] + bits[: 1 - core]
+    bits = bits[1 - kind :] + bits[: 1 - kind]
     return [bits[low : low + 2] for low in range(0, len(bits), 2)]
 
 
@@ -39,7 +43,17 @@
 
 def exchange(block, *flips):
     devices = lax.axis_size("row")
-    return lax.ppermute(block, "row", [(d, d ^ flips[d % len(flips)]) for d in range(devices)])
+    top = devices.bit_length() - 1
+    pairs = []
+    for d in range(devices):
+        flip = flips[parity(d, top) % len(flips)]
+        pairs.append((d, d ^ flip ^ parity(flip, top)))
+    return lax.ppermute(block, "row", pairs)
+
+
+def swap(block):
+    devices = lax.axis_size("row")
+    return lax.ppermute(block, "row", [(d, d ^ 1) for d in range(devices)])
 
 
 def call(body, outs, *args, flops=0):
@@ -210,11 +224,12 @@
     refs[-1][...] = image_of(refs[:-1], scale_ref)
 
 
-def step_body(scale_ref, image_ref, marg_ref, *refs):
-    kernels, (out_ref, rounded_ref, column_ref) = refs[:-3], refs[-3:]
+def step_body(scale_ref, image_ref, marg_ref, *refs, parts):
+    kernels, (rounded_ref, column_ref, *out_refs) = refs[:parts], refs[parts:]
     image = image_ref[...] + image_of(kernels, scale_ref)
     scale_u = marg_ref[...] / image
-    out_ref[...] = scale_u
+    for out_ref in out_refs:
+        out_ref[...] = scale_u
     rounded_ref[...] = scale_u.astype(BF16)
     put_column(scale_u.astype(BF16), kernels, column_ref)
 
@@ -229,12 +244,12 @@
 def slot_of(slot, flips, slots):
     top = slots.bit_length()
     found = []
-    for core, flip in enumerate(flips):
-        turned = sum(1 << i for i, bit in enumerate(slot_bits(core, top)) if flip >> bit & 1)
+    for kind, flip in enumerate(flips):
+        turned = sum(1 << i for i, bit in enumerate(slot_bits(kind, top)) if flip >> bit & 1)
         found.append(slot ^ turned)
     if found[0] == found[1]:
         return found[0]
-    return found[0] + lax.axis_index("row") % 2 * (found[1] - found[0])
+    return found[0] + parity(lax.axis_index("row"), top) * (found[1] - found[0])
 
 
 def total_of(slot, own_ref, got_refs, flips):
@@ -293,11 +308,11 @@
         held = jnp.concatenate([held, piece])
     later = exchange(piece, 2)
     near = [held, jnp.concatenate(across)]
-    far = [exchange(part, 1) for part in near]
+    far = [swap(part) for part in near]
     filled = [[fill(part) for part in side] for side in (near, far)]
     later, filled = lax.optimization_barrier((later, filled))
     near.append(later)
-    far.append(exchange(later, 1))
+    far.append(swap(later))
     for side, parts in zip((near, far), filled):
         parts.append(fill(side[-1]))
     near_kernels, near_sums = zip(*filled[0])
@@ -310,13 +325,14 @@
     )
     (tgt_marg,) = call(target_body, [(block, F32)], *near, *far, flops=half_flops)
     for step in range(ITERS):
+        last = step == ITERS - 1
         if step:
-            scale_u, scale_ub, far_column = call(
-                step_body,
-                [image_type, rounded_type, (block, BF16)],
+            scale_ub, far_column, *scale_u = call(
+                functools.partial(step_body, parts=len(far)),
+                [rounded_type, (block, BF16)] + [image_type] * last,
                 far_vb, image, cand_marg, *far_kernels, flops=2 * half_flops,
             )
-        got = exchange(far_column, 1)
+        got = swap(far_column)
         (column,) = call(
             column_body, [(block, F32)], scale_ub, *near_kernels, flops=half_flops
         )
@@ -331,19 +347,18 @@
                     functools.partial(sum_body, flips=flips),
                     [(block, F32), (block, BF16)], column, *found,
                 )
-        last = step == ITERS - 1
         if last:
-            potential = ENTROPY_TEMP * jnp.log(scale_u)
+            potential = ENTROPY_TEMP * jnp.log(scale_u[0])
             found, potential = lax.optimization_barrier((found, potential))
         scale_vb, *scale_v = call(
             functools.partial(scale_body, flips=flips),
             [(block, BF16)] + [(block, F32)] * last,
             column, tgt_marg, *found,
         )
-        far_vb = exchange(scale_vb, 1)
+        far_vb = swap(scale_vb)
         (image,) = call(image_body, [image_type], scale_vb, *near_kernels, flops=half_flops)
     space = pl.BlockSpec(memory_space=pltpu.VMEM)
-    args = [far_vb, image, scale_u, *scale_v, *far_kernels]
+    args = [far_vb, image, *scale_u, *scale_v, *far_kernels]
     mass, tgt_scaling = pl.pallas_call(
         functools.partial(last_body, candidates=float(cand_rows * devices)),
         out_shape=[

time: 76.6 us -> 73.7 us (0.962)
  starting transfers between devices: 29.8 us -> 23.8 us
  waiting for transfers between devices: 30 us -> 33.3 us
    ppermute x26, starting transfers between devices: 29.8 us -> 23.8 us  [the longest x17 22.3 us: exchange(): return lax.ppermute(block, 'row', pairs)]
    ppermute x26, waiting for transfers between devices: 30 us -> 33.3 us  [the longest x17 29 us: exchange(): return lax.ppermute(block, 'row', pairs)]
  transfers between devices with their start and end apart: 26 -> 26, of which waited for: 22 -> 20; matrix products, arithmetic and copies ran while one was open for 3% -> 3% of each run, Pallas kernels for 8% -> 8%
where the time goes in v12:
time: 73.7 us; the launch traced here: 73.5 us
  waiting for transfers between devices  33.3 us (45%)
  starting transfers between devices  23.8 us (32%)
  Pallas kernels  12.8 us (17%)
  other arithmetic  2.25 us (3%)
  between operations  0.88 us (1%)
    ppermute x17, waiting for transfers between devices, exchange(): return lax.ppermute(block, 'row', pairs)  29 us
    ppermute x17, starting transfers between devices, exchange(): return lax.ppermute(block, 'row', pairs)  22.3 us
    pallas_call x22, Pallas kernels, call(): pl.pallas_call(body, out_shape=[pltpu.VMEM(shape, dtype) for shape, dtype...  10.4 us
    ppermute x9, waiting for transfers between devices, swap(): return lax.ppermute(block, 'row', [(d, d ^ 1) for d in range(devices)])  4.32 us
  transfers between devices with their start and end apart: 26, of which 20 were waited for; matrix products, arithmetic and copies ran while one was open for 3% of the time, Pallas kernels for 8%

profile of v12, /device:TPU:0, one launch (start us, length us, event | category | flops | bytes accessed | tf_op | source)
XLA Modules:
  0.0 73.5 jit_solution(14061780457331928288)
XLA Ops:
  1.6 3.5 %collective-permute-start = (bf16[144,256]{1,0:T(8,128)(2,1)S(1)}, bf16[144,256]{1,0:T(8,128)(2,1)S(1)}, u32[]{:S(2)}, u32[]{:S(2)}) collective-permute-start(bf16[144,256]{1,0:T(8,128)(2,1)S(1)} %shard_map.67), channel_id=1, source_target_pairs={{0,9},{1,4},{2,7},{3,10},{4,1},{5,12},{6,15},{7,2},{8,13},{9,0},{1... | collective-permute-start | bytes 221192 | tf_op jit(solution)/shard_map/ppermute | solution.py:51
  5.1 1.8 %collective-permute-start.1 = (bf16[144,256]{1,0:T(8,128)(2,1)S(1)}, bf16[144,256]{1,0:T(8,128)(2,1)S(1)}, u32[]{:S(2)}, u32[]{:S(2)}) collective-permute-start(bf16[144,256]{1,0:T(8,128)(2,1)S(1)} %shard_map.67), channel_id=1, source_target_pairs={{0,3},{1,2},{2,1},{3,0},{4,7},{5,6},{6,5},{7,4},{8,11},{9,10},{10,... | collective-permute-start | bytes 221192 | tf_op jit(solution)/shard_map/ppermute | solution.py:51
  6.9 1.3 %fusion = f32[1024]{0:T(1024)S(1)} fusion(bf16[1024,256]{1,0:T(8,128)(2,1)} %param.4), kind=kLoop, calls=%fused_computation.2 | loop fusion | flops 785408 | bytes 528384 | tf_op jit(solution)/shard_map/reduce_sum | solution.py:74
  9.6 1.3 %collective-permute-start.2 = (bf16[288,256]{1,0:T(8,128)(2,1)S(1)}, bf16[288,256]{1,0:T(8,128)(2,1)S(1)}, u32[]{:S(2)}, u32[]{:S(2)}) collective-permute-start(bf16[288,256]{1,0:T(8,128)(2,1)S(1)} %pad_maximum_fusion.1), channel_id=1, source_target_pairs={{0,5},{1,8},{2,11},{3,6},{4,13},{5,0},{6,3},{7,14},{8,1},{9,12},{1... | collective-permute-start | bytes 442376 | tf_op jit(solution)/shard_map/ppermute | solution.py:51
  11.8 3.5 %collective-permute-done.3 = bf16[144,256]{1,0:T(8,128)(2,1)S(1)} collective-permute-done((bf16[144,256]{1,0:T(8,128)(2,1)S(1)}, bf16[144,256]{1,0:T(8,128)(2,1)S(1)}, u32[]{:S(2)}, u32[]{:S(2)}) %collective-permute-start.3) | collective-permute-done | bytes 73760 | tf_op jit(solution)/shard_map/ppermute | solution.py:51
  19.5 2.9 %collective-permute-done.4.held_ref.refs_11_.refs_2_ = bf16[288,256]{1,0:T(8,128)(2,1)S(1)} collective-permute-done((bf16[288,256]{1,0:T(8,128)(2,1)S(1)}, bf16[288,256]{1,0:T(8,128)(2,1)S(1)}, u32[]{:S(2)}, u32[]{:S(2)}) %collective-permute-start.4) | collective-permute-done | bytes 147488 | tf_op jit(solution)/shard_map/ppermute | solution.py:51
  26.3 2.1 %collective-permute-start.10 = (bf16[8,32,128]{2,1,0:T(8,128)(2,1)S(1)}, bf16[8,32,128]{2,1,0:T(8,128)(2,1)S(1)}, u32[]{:S(2)}, u32[]{:S(2)}) collective-permute-start(bf16[8,32,128]{2,1,0:T(8,128)(2,1)S(1)} %get-tuple-element.107), channel_id=1, source_target_pairs={{0,9},{1,4},{2,7},{3,10},{4,1},{5,12},{6,15},{7,2},{8,13},{9,0},{1... | collective-permute-start | bytes 196616 | tf_op jit(solution)/shard_map/ppermute | solution.py:51
  28.4 1.9 %collective-permute-start.11 = (bf16[8,32,128]{2,1,0:T(8,128)(2,1)S(1)}, bf16[8,32,128]{2,1,0:T(8,128)(2,1)S(1)}, u32[]{:S(2)}, u32[]{:S(2)}) collective-permute-start(bf16[8,32,128]{2,1,0:T(8,128)(2,1)S(1)} %get-tuple-element.107), channel_id=1, source_target_pairs={{0,12},{1,7},{2,4},{3,15},{4,2},{5,9},{6,10},{7,1},{8,14},{9,5},{1... | collective-permute-start | bytes 196616 | tf_op jit(solution)/shard_map/ppermute | solution.py:51
  30.9 3.6 %collective-permute-done.11.refs_2_ = bf16[8,32,128]{2,1,0:T(8,128)(2,1)S(1)} collective-permute-done((bf16[8,32,128]{2,1,0:T(8,128)(2,1)S(1)}, bf16[8,32,128]{2,1,0:T(8,128)(2,1)S(1)}, u32[]{:S(2)}, u32[]{:S(2)}) %collective-permute-start.11) | collective-permute-done | bytes 65568 | tf_op jit(solution)/shard_map/ppermute | solution.py:51
  34.9 3.4 %collective-permute-done.12.refs_0_ = bf16[8,32,128]{2,1,0:T(8,128)(2,1)S(1)} collective-permute-done((bf16[8,32,128]{2,1,0:T(8,128)(2,1)S(1)}, bf16[8,32,128]{2,1,0:T(8,128)(2,1)S(1)}, u32[]{:S(2)}, u32[]{:S(2)}) %collective-permute-start.12) | collective-permute-done | bytes 65568 | tf_op jit(solution)/shard_map/ppermute | solution.py:51
  39.6 1.5 %shard_map.80 = (bf16[32,1024]{1,0:T(8,128)(2,1)S(1)}, bf16[8,32,128]{2,1,0:T(8,128)(2,1)S(1)}) custom-call(bf16[8,32,128]{2,1,0:T(8,128)(2,1)S(1)} %collective-permute-done.13.scale_ref, f32[32,1024]{1,0:T(8,128)S(1)} %shard_map.79.image_ref, f32[32,1024]{1,0:T(8,128)S(1)} %get-tuple-element.87.marg_ref, bf16[1024,512]{1,0:T(8,128)(2,1)S(1)} %get-tuple-element.70.refs_0_, ...), custom_call_target="tpu_custom_call" | custom-call | flops 536870912 | bytes 2424832 | tf_op jit(solution)/shard_map/pallas_call | solution.py:62
  42.4 1.1 %collective-permute-start.15 = (bf16[8,32,128]{2,1,0:T(8,128)(2,1)S(1)}, bf16[8,32,128]{2,1,0:T(8,128)(2,1)S(1)}, u32[]{:S(2)}, u32[]{:S(2)}) collective-permute-start(bf16[8,32,128]{2,1,0:T(8,128)(2,1)S(1)} %get-tuple-element.105), channel_id=1, source_target_pairs={{0,5},{1,2},{2,1},{3,6},{4,7},{5,0},{6,3},{7,4},{8,11},{9,12},{10,... | collective-permute-start | bytes 196616 | tf_op jit(solution)/shard_map/ppermute | solution.py:51
  43.5 1.1 %collective-permute-start.16 = (bf16[8,32,128]{2,1,0:T(8,128)(2,1)S(1)}, bf16[8,32,128]{2,1,0:T(8,128)(2,1)S(1)}, u32[]{:S(2)}, u32[]{:S(2)}) collective-permute-start(bf16[8,32,128]{2,1,0:T(8,128)(2,1)S(1)} %get-tuple-element.105), channel_id=1, source_target_pairs={{0,9},{1,4},{2,7},{3,10},{4,1},{5,12},{6,15},{7,2},{8,13},{9,0},{1... | collective-permute-start | bytes 196616 | tf_op jit(solution)/shard_map/ppermute | solution.py:51
  44.7 1.9 %collective-permute-start.17 = (bf16[8,32,128]{2,1,0:T(8,128)(2,1)S(1)}, bf16[8,32,128]{2,1,0:T(8,128)(2,1)S(1)}, u32[]{:S(2)}, u32[]{:S(2)}) collective-permute-start(bf16[8,32,128]{2,1,0:T(8,128)(2,1)S(1)} %get-tuple-element.105), channel_id=1, source_target_pairs={{0,12},{1,7},{2,4},{3,15},{4,2},{5,9},{6,10},{7,1},{8,14},{9,5},{1... | collective-permute-start | bytes 196616 | tf_op jit(solution)/shard_map/ppermute | solution.py:51
  46.6 1.5 %collective-permute-done.16.refs_1_ = bf16[8,32,128]{2,1,0:T(8,128)(2,1)S(1)} collective-permute-done((bf16[8,32,128]{2,1,0:T(8,128)(2,1)S(1)}, bf16[8,32,128]{2,1,0:T(8,128)(2,1)S(1)}, u32[]{:S(2)}, u32[]{:S(2)}) %collective-permute-start.16) | collective-permute-done | bytes 65568 | tf_op jit(solution)/shard_map/ppermute | solution.py:51
  48.1 2.6 %collective-permute-done.17.refs_2_ = bf16[8,32,128]{2,1,0:T(8,128)(2,1)S(1)} collective-permute-done((bf16[8,32,128]{2,1,0:T(8,128)(2,1)S(1)}, bf16[8,32,128]{2,1,0:T(8,128)(2,1)S(1)}, u32[]{:S(2)}, u32[]{:S(2)}) %collective-permute-start.17) | collective-permute-done | bytes 65568 | tf_op jit(solution)/shard_map/ppermute | solution.py:51
  51.2 3.3 %collective-permute-done.18.refs_0_ = bf16[8,32,128]{2,1,0:T(8,128)(2,1)S(1)} collective-permute-done((bf16[8,32,128]{2,1,0:T(8,128)(2,1)S(1)}, bf16[8,32,128]{2,1,0:T(8,128)(2,1)S(1)}, u32[]{:S(2)}, u32[]{:S(2)}) %collective-permute-start.18) | collective-permute-done | bytes 65568 | tf_op jit(solution)/shard_map/ppermute | solution.py:51
  55.9 1.5 %shard_map.85 = (bf16[32,1024]{1,0:T(8,128)(2,1)S(1)}, bf16[8,32,128]{2,1,0:T(8,128)(2,1)S(1)}, f32[32,1024]{1,0:T(8,128)S(1)}) custom-call(bf16[8,32,128]{2,1,0:T(8,128)(2,1)S(1)} %collective-permute-done.19.scale_ref, f32[32,1024]{1,0:T(8,128)S(1)} %shard_map.84.image_ref, f32[32,1024]{1,0:T(8,128)S(1)} %get-tuple-element.87.marg_ref, ...), custom_call_target="tpu_custom_call" | custom-call | flops 536870912 | bytes 2424832 | tf_op jit(solution)/shard_map/pallas_call | solution.py:62
  59.8 1.2 %collective-permute-start.22 = (bf16[8,32,128]{2,1,0:T(8,128)(2,1)S(1)}, bf16[8,32,128]{2,1,0:T(8,128)(2,1)S(1)}, u32[]{:S(2)}, u32[]{:S(2)}) collective-permute-start(bf16[8,32,128]{2,1,0:T(8,128)(2,1)S(1)} %get-tuple-element.103), channel_id=1, source_target_pairs={{0,9},{1,4},{2,7},{3,10},{4,1},{5,12},{6,15},{7,2},{8,13},{9,0},{1... | collective-permute-start | bytes 196616 | tf_op jit(solution)/shard_map/ppermute | solution.py:51
  60.9 1.9 %collective-permute-start.23 = (bf16[8,32,128]{2,1,0:T(8,128)(2,1)S(1)}, bf16[8,32,128]{2,1,0:T(8,128)(2,1)S(1)}, u32[]{:S(2)}, u32[]{:S(2)}) collective-permute-start(bf16[8,32,128]{2,1,0:T(8,128)(2,1)S(1)} %get-tuple-element.103), channel_id=1, source_target_pairs={{0,12},{1,7},{2,4},{3,15},{4,2},{5,9},{6,10},{7,1},{8,14},{9,5},{1... | collective-permute-start | bytes 196616 | tf_op jit(solution)/shard_map/ppermute | solution.py:51
  62.8 1.6 %collective-permute-done.22.refs_1_ = bf16[8,32,128]{2,1,0:T(8,128)(2,1)S(1)} collective-permute-done((bf16[8,32,128]{2,1,0:T(8,128)(2,1)S(1)}, bf16[8,32,128]{2,1,0:T(8,128)(2,1)S(1)}, u32[]{:S(2)}, u32[]{:S(2)}) %collective-permute-start.22) | collective-permute-done | bytes 65568 | tf_op jit(solution)/shard_map/ppermute | solution.py:51
  64.5 2.5 %collective-permute-done.23.refs_2_ = bf16[8,32,128]{2,1,0:T(8,128)(2,1)S(1)} collective-permute-done((bf16[8,32,128]{2,1,0:T(8,128)(2,1)S(1)}, bf16[8,32,128]{2,1,0:T(8,128)(2,1)S(1)}, u32[]{:S(2)}, u32[]{:S(2)}) %collective-permute-start.23) | collective-permute-done | bytes 65568 | tf_op jit(solution)/shard_map/ppermute | solution.py:51
  68.4 2.4 %collective-permute-done.24.refs_0_ = bf16[8,32,128]{2,1,0:T(8,128)(2,1)S(1)} collective-permute-done((bf16[8,32,128]{2,1,0:T(8,128)(2,1)S(1)}, bf16[8,32,128]{2,1,0:T(8,128)(2,1)S(1)}, u32[]{:S(2)}, u32[]{:S(2)}) %collective-permute-start.24) | collective-permute-done | bytes 65568 | tf_op jit(solution)/shard_map/ppermute | solution.py:51
  72.1 1.4 %shard_map.90 = (f32[32,1024]{1,0:T(8,128)}, f32[32,128]{1,0:T(8,128)}) custom-call(bf16[8,32,128]{2,1,0:T(8,128)(2,1)S(1)} %collective-permute-done.25.scale_ref, f32[32,1024]{1,0:T(8,128)S(1)} %shard_map.89.image_ref, f32[32,1024]{1,0:T(8,128)S(1)} %get-tuple-element.95.u_ref, f32[8,32,128]{2,1,0:T(8,128)S(1)} %get-tuple-element.100.scale_v_ref, ...), custom_call_target="tpu_custom_call" | custom-call | tf_op jit(solution)/shard_map/pallas_call | solution.py:362
  (68 shorter events, 21.7 us)
Async XLA Ops:
  1.6 7.3 %collective-permute-start = (bf16[144,256]{1,0:T(8,128)(2,1)S(1)}, bf16[144,256]{1,0:T(8,128)(2,1)S(1)}, u32[]{:S(2)}, u32[]{:S(2)}) collective-permute-start(bf16[144,256]{1,0:T(8,128)(2,1)S(1)} %shard_map.67), channel_id=1, source_target_pairs={{0,9},{1,4},{2,7},{3,10},{4,1},{5,12},{6,15},{7,2},{8,13},{9,0},{1... | collective-permute-start | bytes 221192 | tf_op jit(solution)/shard_map/ppermute | solution.py:51
  5.1 4.4 %collective-permute-start.1 = (bf16[144,256]{1,0:T(8,128)(2,1)S(1)}, bf16[144,256]{1,0:T(8,128)(2,1)S(1)}, u32[]{:S(2)}, u32[]{:S(2)}) collective-permute-start(bf16[144,256]{1,0:T(8,128)(2,1)S(1)} %shard_map.67), channel_id=1, source_target_pairs={{0,3},{1,2},{2,1},{3,0},{4,7},{5,6},{6,5},{7,4},{8,11},{9,10},{10,... | collective-permute-start | bytes 221192 | tf_op jit(solution)/shard_map/ppermute | solution.py:51
  9.6 6.2 %collective-permute-start.2 = (bf16[288,256]{1,0:T(8,128)(2,1)S(1)}, bf16[288,256]{1,0:T(8,128)(2,1)S(1)}, u32[]{:S(2)}, u32[]{:S(2)}) collective-permute-start(bf16[288,256]{1,0:T(8,128)(2,1)S(1)} %pad_maximum_fusion.1), channel_id=1, source_target_pairs={{0,5},{1,8},{2,11},{3,6},{4,13},{5,0},{6,3},{7,14},{8,1},{9,12},{1... | collective-permute-start | bytes 442376 | tf_op jit(solution)/shard_map/ppermute | solution.py:51
  10.9 4.5 %collective-permute-start.3 = (bf16[144,256]{1,0:T(8,128)(2,1)S(1)}, bf16[144,256]{1,0:T(8,128)(2,1)S(1)}, u32[]{:S(2)}, u32[]{:S(2)}) collective-permute-start(bf16[144,256]{1,0:T(8,128)(2,1)S(1)} %collective-permute-done), channel_id=1, source_target_pairs={{0,3},{1,2},{2,1},{3,0},{4,7},{5,6},{6,5},{7,4},{8,11},{9,10},{10,... | collective-permute-start | bytes 221192 | tf_op jit(solution)/shard_map/ppermute | solution.py:51
  15.8 3.0 %collective-permute-start.5 = (bf16[576,256]{1,0:T(8,128)(2,1)S(1)}, bf16[576,256]{1,0:T(8,128)(2,1)S(1)}, u32[]{:S(2)}, u32[]{:S(2)}) collective-permute-start(bf16[576,256]{1,0:T(8,128)(2,1)S(1)} %pad_maximum_fusion.held_ref.refs_9_.refs_0_), channel_id=1, source_target_pairs={{0,1},{1,0},{2,3},{3,2},{4,5},{5,4},{6,7},{7,6},{8,9},{9,8},{10,11... | collective-permute-start | bytes 884744 | tf_op jit(solution)/shard_map/ppermute | solution.py:56
  15.9 2.5 %collective-permute-start.6 = (bf16[288,256]{1,0:T(8,128)(2,1)S(1)}, bf16[288,256]{1,0:T(8,128)(2,1)S(1)}, u32[]{:S(2)}, u32[]{:S(2)}) collective-permute-start(bf16[288,256]{1,0:T(8,128)(2,1)S(1)} %constant_dynamic-update-slice_fusion.held_ref.refs_10_.refs_1_), channel_id=1, source_target_pairs={{0,1},{1,0},{2,3},{3,2},{4,5},{5,4},{6,7},{7,6},{8,9},{9,8},{10,11... | collective-permute-start | bytes 442376 | tf_op jit(solution)/shard_map/ppermute | solution.py:56
  16.5 5.9 %collective-permute-start.4 = (bf16[288,256]{1,0:T(8,128)(2,1)S(1)}, bf16[288,256]{1,0:T(8,128)(2,1)S(1)}, u32[]{:S(2)}, u32[]{:S(2)}) collective-permute-start(bf16[288,256]{1,0:T(8,128)(2,1)S(1)} %collective-permute-done.2), channel_id=1, source_target_pairs={{0,3},{1,2},{2,1},{3,0},{4,7},{5,6},{6,5},{7,4},{8,11},{9,10},{10,... | collective-permute-start | bytes 442376 | tf_op jit(solution)/shard_map/ppermute | solution.py:51
  22.4 1.4 %collective-permute-start.7 = (bf16[288,256]{1,0:T(8,128)(2,1)S(1)}, bf16[288,256]{1,0:T(8,128)(2,1)S(1)}, u32[]{:S(2)}, u32[]{:S(2)}) collective-permute-start(bf16[288,256]{1,0:T(8,128)(2,1)S(1)} %collective-permute-done.4.held_ref.refs_11_.refs_2_), channel_id=1, source_target_pairs={{0,1},{1,0},{2,3},{3,2},{4,5},{5,4},{6,7},{7,6},{8,9},{9,8},{10,11... | collective-permute-start | bytes 442376 | tf_op jit(solution)/shard_map/ppermute | solution.py:56
  24.8 1.3 %collective-permute-start.8 = (bf16[8,32,128]{2,1,0:T(8,128)(2,1)S(1)}, bf16[8,32,128]{2,1,0:T(8,128)(2,1)S(1)}, u32[]{:S(2)}, u32[]{:S(2)}) collective-permute-start(bf16[8,32,128]{2,1,0:T(8,128)(2,1)S(1)} %get-tuple-element.84), channel_id=1, source_target_pairs={{0,1},{1,0},{2,3},{3,2},{4,5},{5,4},{6,7},{7,6},{8,9},{9,8},{10,11... | collective-permute-start | bytes 196616 | tf_op jit(solution)/shard_map/ppermute | solution.py:56
  26.1 4.2 %collective-permute-start.9 = (bf16[8,32,128]{2,1,0:T(8,128)(2,1)S(1)}, bf16[8,32,128]{2,1,0:T(8,128)(2,1)S(1)}, u32[]{:S(2)}, u32[]{:S(2)}) collective-permute-start(bf16[8,32,128]{2,1,0:T(8,128)(2,1)S(1)} %get-tuple-element.107), channel_id=1, source_target_pairs={{0,5},{1,2},{2,1},{3,6},{4,7},{5,0},{6,3},{7,4},{8,11},{9,12},{10,... | collective-permute-start | bytes 196616 | tf_op jit(solution)/shard_map/ppermute | solution.py:51
  26.3 4.6 %collective-permute-start.10 = (bf16[8,32,128]{2,1,0:T(8,128)(2,1)S(1)}, bf16[8,32,128]{2,1,0:T(8,128)(2,1)S(1)}, u32[]{:S(2)}, u32[]{:S(2)}) collective-permute-start(bf16[8,32,128]{2,1,0:T(8,128)(2,1)S(1)} %get-tuple-element.107), channel_id=1, source_target_pairs={{0,9},{1,4},{2,7},{3,10},{4,1},{5,12},{6,15},{7,2},{8,13},{9,0},{1... | collective-permute-start | bytes 196616 | tf_op jit(solution)/shard_map/ppermute | solution.py:51
  28.4 6.1 %collective-permute-start.11 = (bf16[8,32,128]{2,1,0:T(8,128)(2,1)S(1)}, bf16[8,32,128]{2,1,0:T(8,128)(2,1)S(1)}, u32[]{:S(2)}, u32[]{:S(2)}) collective-permute-start(bf16[8,32,128]{2,1,0:T(8,128)(2,1)S(1)} %get-tuple-element.107), channel_id=1, source_target_pairs={{0,12},{1,7},{2,4},{3,15},{4,2},{5,9},{6,10},{7,1},{8,14},{9,5},{1... | collective-permute-start | bytes 196616 | tf_op jit(solution)/shard_map/ppermute | solution.py:51
  34.5 3.8 %collective-permute-start.12 = (bf16[8,32,128]{2,1,0:T(8,128)(2,1)S(1)}, bf16[8,32,128]{2,1,0:T(8,128)(2,1)S(1)}, u32[]{:S(2)}, u32[]{:S(2)}) collective-permute-start(bf16[8,32,128]{2,1,0:T(8,128)(2,1)S(1)} %get-tuple-element.86), channel_id=1, source_target_pairs={{0,3},{1,8},{2,11},{3,0},{4,13},{5,6},{6,5},{7,14},{8,1},{9,10},{1... | collective-permute-start | bytes 196616 | tf_op jit(solution)/shard_map/ppermute | solution.py:51
  38.3 1.3 %collective-permute-start.13 = (bf16[8,32,128]{2,1,0:T(8,128)(2,1)S(1)}, bf16[8,32,128]{2,1,0:T(8,128)(2,1)S(1)}, u32[]{:S(2)}, u32[]{:S(2)}) collective-permute-start(bf16[8,32,128]{2,1,0:T(8,128)(2,1)S(1)} %shard_map.78.scale_ref), channel_id=1, source_target_pairs={{0,1},{1,0},{2,3},{3,2},{4,5},{5,4},{6,7},{7,6},{8,9},{9,8},{10,11... | collective-permute-start | bytes 196616 | tf_op jit(solution)/shard_map/ppermute | solution.py:56
  42.4 4.2 %collective-permute-start.15 = (bf16[8,32,128]{2,1,0:T(8,128)(2,1)S(1)}, bf16[8,32,128]{2,1,0:T(8,128)(2,1)S(1)}, u32[]{:S(2)}, u32[]{:S(2)}) collective-permute-start(bf16[8,32,128]{2,1,0:T(8,128)(2,1)S(1)} %get-tuple-element.105), channel_id=1, source_target_pairs={{0,5},{1,2},{2,1},{3,6},{4,7},{5,0},{6,3},{7,4},{8,11},{9,12},{10,... | collective-permute-start | bytes 196616 | tf_op jit(solution)/shard_map/ppermute | solution.py:51
  43.5 4.6 %collective-permute-start.16 = (bf16[8,32,128]{2,1,0:T(8,128)(2,1)S(1)}, bf16[8,32,128]{2,1,0:T(8,128)(2,1)S(1)}, u32[]{:S(2)}, u32[]{:S(2)}) collective-permute-start(bf16[8,32,128]{2,1,0:T(8,128)(2,1)S(1)} %get-tuple-element.105), channel_id=1, source_target_pairs={{0,9},{1,4},{2,7},{3,10},{4,1},{5,12},{6,15},{7,2},{8,13},{9,0},{1... | collective-permute-start | bytes 196616 | tf_op jit(solution)/shard_map/ppermute | solution.py:51
  44.7 6.1 %collective-permute-start.17 = (bf16[8,32,128]{2,1,0:T(8,128)(2,1)S(1)}, bf16[8,32,128]{2,1,0:T(8,128)(2,1)S(1)}, u32[]{:S(2)}, u32[]{:S(2)}) collective-permute-start(bf16[8,32,128]{2,1,0:T(8,128)(2,1)S(1)} %get-tuple-element.105), channel_id=1, source_target_pairs={{0,12},{1,7},{2,4},{3,15},{4,2},{5,9},{6,10},{7,1},{8,14},{9,5},{1... | collective-permute-start | bytes 196616 | tf_op jit(solution)/shard_map/ppermute | solution.py:51
  50.8 3.8 %collective-permute-start.18 = (bf16[8,32,128]{2,1,0:T(8,128)(2,1)S(1)}, bf16[8,32,128]{2,1,0:T(8,128)(2,1)S(1)}, u32[]{:S(2)}, u32[]{:S(2)}) collective-permute-start(bf16[8,32,128]{2,1,0:T(8,128)(2,1)S(1)} %get-tuple-element.91), channel_id=1, source_target_pairs={{0,3},{1,8},{2,11},{3,0},{4,13},{5,6},{6,5},{7,14},{8,1},{9,10},{1... | collective-permute-start | bytes 196616 | tf_op jit(solution)/shard_map/ppermute | solution.py:51
  54.5 1.3 %collective-permute-start.19 = (bf16[8,32,128]{2,1,0:T(8,128)(2,1)S(1)}, bf16[8,32,128]{2,1,0:T(8,128)(2,1)S(1)}, u32[]{:S(2)}, u32[]{:S(2)}) collective-permute-start(bf16[8,32,128]{2,1,0:T(8,128)(2,1)S(1)} %shard_map.83.scale_ref), channel_id=1, source_target_pairs={{0,1},{1,0},{2,3},{3,2},{4,5},{5,4},{6,7},{7,6},{8,9},{9,8},{10,11... | collective-permute-start | bytes 196616 | tf_op jit(solution)/shard_map/ppermute | solution.py:56
  58.7 4.2 %collective-permute-start.21 = (bf16[8,32,128]{2,1,0:T(8,128)(2,1)S(1)}, bf16[8,32,128]{2,1,0:T(8,128)(2,1)S(1)}, u32[]{:S(2)}, u32[]{:S(2)}) collective-permute-start(bf16[8,32,128]{2,1,0:T(8,128)(2,1)S(1)} %get-tuple-element.103), channel_id=1, source_target_pairs={{0,5},{1,2},{2,1},{3,6},{4,7},{5,0},{6,3},{7,4},{8,11},{9,12},{10,... | collective-permute-start | bytes 196616 | tf_op jit(solution)/shard_map/ppermute | solution.py:51
  59.8 4.7 %collective-permute-start.22 = (bf16[8,32,128]{2,1,0:T(8,128)(2,1)S(1)}, bf16[8,32,128]{2,1,0:T(8,128)(2,1)S(1)}, u32[]{:S(2)}, u32[]{:S(2)}) collective-permute-start(bf16[8,32,128]{2,1,0:T(8,128)(2,1)S(1)} %get-tuple-element.103), channel_id=1, source_target_pairs={{0,9},{1,4},{2,7},{3,10},{4,1},{5,12},{6,15},{7,2},{8,13},{9,0},{1... | collective-permute-start | bytes 196616 | tf_op jit(solution)/shard_map/ppermute | solution.py:51
  60.9 6.1 %collective-permute-start.23 = (bf16[8,32,128]{2,1,0:T(8,128)(2,1)S(1)}, bf16[8,32,128]{2,1,0:T(8,128)(2,1)S(1)}, u32[]{:S(2)}, u32[]{:S(2)}) collective-permute-start(bf16[8,32,128]{2,1,0:T(8,128)(2,1)S(1)} %get-tuple-element.103), channel_id=1, source_target_pairs={{0,12},{1,7},{2,4},{3,15},{4,2},{5,9},{6,10},{7,1},{8,14},{9,5},{1... | collective-permute-start | bytes 196616 | tf_op jit(solution)/shard_map/ppermute | solution.py:51
  67.0 3.8 %collective-permute-start.24 = (bf16[8,32,128]{2,1,0:T(8,128)(2,1)S(1)}, bf16[8,32,128]{2,1,0:T(8,128)(2,1)S(1)}, u32[]{:S(2)}, u32[]{:S(2)}) collective-permute-start(bf16[8,32,128]{2,1,0:T(8,128)(2,1)S(1)} %get-tuple-element.94), channel_id=1, source_target_pairs={{0,3},{1,8},{2,11},{3,0},{4,13},{5,6},{6,5},{7,14},{8,1},{9,10},{1... | collective-permute-start | bytes 196616 | tf_op jit(solution)/shard_map/ppermute | solution.py:51
  70.8 1.3 %collective-permute-start.25 = (bf16[8,32,128]{2,1,0:T(8,128)(2,1)S(1)}, bf16[8,32,128]{2,1,0:T(8,128)(2,1)S(1)}, u32[]{:S(2)}, u32[]{:S(2)}) collective-permute-start(bf16[8,32,128]{2,1,0:T(8,128)(2,1)S(1)} %get-tuple-element.99.scale_ref), channel_id=1, source_target_pairs={{0,1},{1,0},{2,3},{3,2},{4,5},{5,4},{6,7},{7,6},{8,9},{9,8},{10,11... | collective-permute-start | bytes 196616 | tf_op jit(solution)/shard_map/ppermute | solution.py:56
  (4 other events, 10.8 us)

commit v13 on v12

--- a/solution.py
+++ b/solution.py
@@ -28,9 +28,8 @@
     return (layer if kind else layer[::-1]) + [1]
 
 
-def rounds(kind, top):
+def rounds(top):
     bits = list(range(1, top))
-    bits = bits[1 - kind :] + bits[: 1 - kind]
     return [bits[low : low + 2] for low in range(0, len(bits), 2)]
 
 
@@ -338,9 +337,9 @@
         )
         column = column + got.astype(F32)
         sent = column.astype(BF16)
-        order = list(zip(rounds(0, top), rounds(1, top)))
-        for place, pair in enumerate(order):
-            flips = list(zip(*[flips_of(bits) for bits in pair]))
+        order = rounds(top)
+        for place, bits in enumerate(order):
+            flips = [(flip, flip) for flip in flips_of(bits)]
             found = [exchange(sent, *turn) for turn in flips]
             if place < len(order) - 1:
                 column, sent = call(

time: 73.7 us -> 78.3 us (1.062)
  waiting for transfers between devices: 33.3 us -> 40.7 us
  starting transfers between devices: 23.8 us -> 21 us
    ppermute x17, waiting for transfers between devices: 29 us -> 36.5 us  [exchange(): return lax.ppermute(block, 'row', pairs)]
    ppermute x17, starting transfers between devices: 22.3 us -> 19.3 us  [exchange(): return lax.ppermute(block, 'row', pairs)]
  transfers between devices with their start and end apart: 26 -> 26, of which waited for: 20 -> 23; matrix products, arithmetic and copies ran while one was open for 3% -> 3% of each run, Pallas kernels for 8% -> 8%
where the time goes in v13:
time: 78.3 us; the launch traced here: 78.1 us
  waiting for transfers between devices  40.7 us (52%)
  starting transfers between devices  21 us (27%)
  Pallas kernels  12.8 us (16%)
  other arithmetic  2.25 us (3%)
  between operations  0.88 us (1%)
    ppermute x17, waiting for transfers between devices, exchange(): return lax.ppermute(block, 'row', pairs)  36.5 us
    ppermute x17, starting transfers between devices, exchange(): return lax.ppermute(block, 'row', pairs)  19.3 us
    pallas_call x22, Pallas kernels, call(): pl.pallas_call(body, out_shape=[pltpu.VMEM(shape, dtype) for shape, dtype...  10.5 us
    ppermute x9, waiting for transfers between devices, swap(): return lax.ppermute(block, 'row', [(d, d ^ 1) for d in range(devices)])  4.14 us
    ppermute x9, starting transfers between devices, swap(): return lax.ppermute(block, 'row', [(d, d ^ 1) for d in range(devices)])  1.66 us
  transfers between devices with their start and end apart: 26, of which 23 were waited for; matrix products, arithmetic and copies ran while one was open for 3% of the time, Pallas kernels for 8%

profile of v13, /device:TPU:0, one launch (start us, length us, event | category | flops | bytes accessed | tf_op | source)
XLA Modules:
  0.0 78.1 jit_solution(11466194167735478246)
XLA Ops:
  0.6 1.0 %shard_map.67 = bf16[144,256]{1,0:T(8,128)(2,1)S(1)} custom-call(bf16[128,256]{1,0:T(8,128)(2,1)} %embed_hbm.1, s32[1,128]{1,0:T(1,128)} %bitcast.3, s32[1,1024]{1,0:T(1,128)} %bitcast.2), custom_call_target="tpu_custom_call" | custom-call | tf_op jit(solution)/shard_map/pallas_call | solution.py:112
  1.6 3.5 %collective-permute-start = (bf16[144,256]{1,0:T(8,128)(2,1)S(1)}, bf16[144,256]{1,0:T(8,128)(2,1)S(1)}, u32[]{:S(2)}, u32[]{:S(2)}) collective-permute-start(bf16[144,256]{1,0:T(8,128)(2,1)S(1)} %shard_map.67), channel_id=1, source_target_pairs={{0,9},{1,4},{2,7},{3,10},{4,1},{5,12},{6,15},{7,2},{8,13},{9,0},{1... | collective-permute-start | bytes 221192 | tf_op jit(solution)/shard_map/ppermute | solution.py:50
  5.1 1.8 %collective-permute-start.1 = (bf16[144,256]{1,0:T(8,128)(2,1)S(1)}, bf16[144,256]{1,0:T(8,128)(2,1)S(1)}, u32[]{:S(2)}, u32[]{:S(2)}) collective-permute-start(bf16[144,256]{1,0:T(8,128)(2,1)S(1)} %shard_map.67), channel_id=1, source_target_pairs={{0,3},{1,2},{2,1},{3,0},{4,7},{5,6},{6,5},{7,4},{8,11},{9,10},{10,... | collective-permute-start | bytes 221192 | tf_op jit(solution)/shard_map/ppermute | solution.py:50
  6.9 1.3 %fusion = f32[1024]{0:T(1024)S(1)} fusion(bf16[1024,256]{1,0:T(8,128)(2,1)} %param.4), kind=kLoop, calls=%fused_computation.2 | loop fusion | flops 785408 | bytes 528384 | tf_op jit(solution)/shard_map/reduce_sum | solution.py:73
  9.6 1.3 %collective-permute-start.2 = (bf16[288,256]{1,0:T(8,128)(2,1)S(1)}, bf16[288,256]{1,0:T(8,128)(2,1)S(1)}, u32[]{:S(2)}, u32[]{:S(2)}) collective-permute-start(bf16[288,256]{1,0:T(8,128)(2,1)S(1)} %pad_maximum_fusion.1), channel_id=1, source_target_pairs={{0,5},{1,8},{2,11},{3,6},{4,13},{5,0},{6,3},{7,14},{8,1},{9,12},{1... | collective-permute-start | bytes 442376 | tf_op jit(solution)/shard_map/ppermute | solution.py:50
  10.9 1.0 %collective-permute-start.3 = (bf16[144,256]{1,0:T(8,128)(2,1)S(1)}, bf16[144,256]{1,0:T(8,128)(2,1)S(1)}, u32[]{:S(2)}, u32[]{:S(2)}) collective-permute-start(bf16[144,256]{1,0:T(8,128)(2,1)S(1)} %collective-permute-done), channel_id=1, source_target_pairs={{0,3},{1,2},{2,1},{3,0},{4,7},{5,6},{6,5},{7,4},{8,11},{9,10},{10,... | collective-permute-start | bytes 221192 | tf_op jit(solution)/shard_map/ppermute | solution.py:50
  11.8 3.5 %collective-permute-done.3 = bf16[144,256]{1,0:T(8,128)(2,1)S(1)} collective-permute-done((bf16[144,256]{1,0:T(8,128)(2,1)S(1)}, bf16[144,256]{1,0:T(8,128)(2,1)S(1)}, u32[]{:S(2)}, u32[]{:S(2)}) %collective-permute-start.3) | collective-permute-done | bytes 73760 | tf_op jit(solution)/shard_map/ppermute | solution.py:50
  16.5 0.9 %collective-permute-start.4 = (bf16[288,256]{1,0:T(8,128)(2,1)S(1)}, bf16[288,256]{1,0:T(8,128)(2,1)S(1)}, u32[]{:S(2)}, u32[]{:S(2)}) collective-permute-start(bf16[288,256]{1,0:T(8,128)(2,1)S(1)} %collective-permute-done.2), channel_id=1, source_target_pairs={{0,3},{1,2},{2,1},{3,0},{4,7},{5,6},{6,5},{7,4},{8,11},{9,10},{10,... | collective-permute-start | bytes 442376 | tf_op jit(solution)/shard_map/ppermute | solution.py:50
  19.5 2.9 %collective-permute-done.4.held_ref.refs_11_.refs_2_ = bf16[288,256]{1,0:T(8,128)(2,1)S(1)} collective-permute-done((bf16[288,256]{1,0:T(8,128)(2,1)S(1)}, bf16[288,256]{1,0:T(8,128)(2,1)S(1)}, u32[]{:S(2)}, u32[]{:S(2)}) %collective-permute-start.4) | collective-permute-done | bytes 147488 | tf_op jit(solution)/shard_map/ppermute | solution.py:50
  26.1 0.9 %collective-permute-start.9 = (bf16[8,32,128]{2,1,0:T(8,128)(2,1)S(1)}, bf16[8,32,128]{2,1,0:T(8,128)(2,1)S(1)}, u32[]{:S(2)}, u32[]{:S(2)}) collective-permute-start(bf16[8,32,128]{2,1,0:T(8,128)(2,1)S(1)} %get-tuple-element.107), channel_id=1, source_target_pairs={{0,3},{1,2},{2,1},{3,0},{4,7},{5,6},{6,5},{7,4},{8,11},{9,10},{10,... | collective-permute-start | bytes 196616 | tf_op jit(solution)/shard_map/ppermute | solution.py:50
  27.3 2.0 %collective-permute-start.11 = (bf16[8,32,128]{2,1,0:T(8,128)(2,1)S(1)}, bf16[8,32,128]{2,1,0:T(8,128)(2,1)S(1)}, u32[]{:S(2)}, u32[]{:S(2)}) collective-permute-start(bf16[8,32,128]{2,1,0:T(8,128)(2,1)S(1)} %get-tuple-element.107), channel_id=1, source_target_pairs={{0,6},{1,7},{2,4},{3,5},{4,2},{5,3},{6,0},{7,1},{8,14},{9,15},{10,... | collective-permute-start | bytes 196616 | tf_op jit(solution)/shard_map/ppermute | solution.py:50
  29.4 0.8 %collective-permute-done.9.refs_0_ = bf16[8,32,128]{2,1,0:T(8,128)(2,1)S(1)} collective-permute-done((bf16[8,32,128]{2,1,0:T(8,128)(2,1)S(1)}, bf16[8,32,128]{2,1,0:T(8,128)(2,1)S(1)}, u32[]{:S(2)}, u32[]{:S(2)}) %collective-permute-start.9) | collective-permute-done | bytes 65568 | tf_op jit(solution)/shard_map/ppermute | solution.py:50
  31.0 2.2 %collective-permute-done.11.refs_2_ = bf16[8,32,128]{2,1,0:T(8,128)(2,1)S(1)} collective-permute-done((bf16[8,32,128]{2,1,0:T(8,128)(2,1)S(1)}, bf16[8,32,128]{2,1,0:T(8,128)(2,1)S(1)}, u32[]{:S(2)}, u32[]{:S(2)}) %collective-permute-start.11) | collective-permute-done | bytes 65568 | tf_op jit(solution)/shard_map/ppermute | solution.py:50
  34.0 5.8 %collective-permute-done.12.refs_0_ = bf16[8,32,128]{2,1,0:T(8,128)(2,1)S(1)} collective-permute-done((bf16[8,32,128]{2,1,0:T(8,128)(2,1)S(1)}, bf16[8,32,128]{2,1,0:T(8,128)(2,1)S(1)}, u32[]{:S(2)}, u32[]{:S(2)}) %collective-permute-start.12) | collective-permute-done | bytes 65568 | tf_op jit(solution)/shard_map/ppermute | solution.py:50
  41.1 1.5 %shard_map.80 = (bf16[32,1024]{1,0:T(8,128)(2,1)S(1)}, bf16[8,32,128]{2,1,0:T(8,128)(2,1)S(1)}) custom-call(bf16[8,32,128]{2,1,0:T(8,128)(2,1)S(1)} %collective-permute-done.13.scale_ref, f32[32,1024]{1,0:T(8,128)S(1)} %shard_map.79.image_ref, f32[32,1024]{1,0:T(8,128)S(1)} %get-tuple-element.87.marg_ref, bf16[1024,512]{1,0:T(8,128)(2,1)S(1)} %get-tuple-element.70.refs_0_, ...), custom_call_target="tpu_custom_call" | custom-call | flops 536870912 | bytes 2424832 | tf_op jit(solution)/shard_map/pallas_call | solution.py:61
  44.7 2.5 %collective-permute-start.17 = (bf16[8,32,128]{2,1,0:T(8,128)(2,1)S(1)}, bf16[8,32,128]{2,1,0:T(8,128)(2,1)S(1)}, u32[]{:S(2)}, u32[]{:S(2)}) collective-permute-start(bf16[8,32,128]{2,1,0:T(8,128)(2,1)S(1)} %get-tuple-element.105), channel_id=1, source_target_pairs={{0,6},{1,7},{2,4},{3,5},{4,2},{5,3},{6,0},{7,1},{8,14},{9,15},{10,... | collective-permute-start | bytes 196616 | tf_op jit(solution)/shard_map/ppermute | solution.py:50
  48.7 2.4 %collective-permute-done.17.refs_2_ = bf16[8,32,128]{2,1,0:T(8,128)(2,1)S(1)} collective-permute-done((bf16[8,32,128]{2,1,0:T(8,128)(2,1)S(1)}, bf16[8,32,128]{2,1,0:T(8,128)(2,1)S(1)}, u32[]{:S(2)}, u32[]{:S(2)}) %collective-permute-start.17) | collective-permute-done | bytes 65568 | tf_op jit(solution)/shard_map/ppermute | solution.py:50
  51.5 6.2 %collective-permute-done.18.refs_0_ = bf16[8,32,128]{2,1,0:T(8,128)(2,1)S(1)} collective-permute-done((bf16[8,32,128]{2,1,0:T(8,128)(2,1)S(1)}, bf16[8,32,128]{2,1,0:T(8,128)(2,1)S(1)}, u32[]{:S(2)}, u32[]{:S(2)}) %collective-permute-start.18) | collective-permute-done | bytes 65568 | tf_op jit(solution)/shard_map/ppermute | solution.py:50
  59.0 1.5 %shard_map.85 = (bf16[32,1024]{1,0:T(8,128)(2,1)S(1)}, bf16[8,32,128]{2,1,0:T(8,128)(2,1)S(1)}, f32[32,1024]{1,0:T(8,128)S(1)}) custom-call(bf16[8,32,128]{2,1,0:T(8,128)(2,1)S(1)} %collective-permute-done.19.scale_ref, f32[32,1024]{1,0:T(8,128)S(1)} %shard_map.84.image_ref, f32[32,1024]{1,0:T(8,128)S(1)} %get-tuple-element.87.marg_ref, ...), custom_call_target="tpu_custom_call" | custom-call | flops 536870912 | bytes 2424832 | tf_op jit(solution)/shard_map/pallas_call | solution.py:61
  62.6 2.5 %collective-permute-start.23 = (bf16[8,32,128]{2,1,0:T(8,128)(2,1)S(1)}, bf16[8,32,128]{2,1,0:T(8,128)(2,1)S(1)}, u32[]{:S(2)}, u32[]{:S(2)}) collective-permute-start(bf16[8,32,128]{2,1,0:T(8,128)(2,1)S(1)} %get-tuple-element.103), channel_id=1, source_target_pairs={{0,6},{1,7},{2,4},{3,5},{4,2},{5,3},{6,0},{7,1},{8,14},{9,15},{10,... | collective-permute-start | bytes 196616 | tf_op jit(solution)/shard_map/ppermute | solution.py:50
  65.1 0.8 %collective-permute-done.21.refs_0_ = bf16[8,32,128]{2,1,0:T(8,128)(2,1)S(1)} collective-permute-done((bf16[8,32,128]{2,1,0:T(8,128)(2,1)S(1)}, bf16[8,32,128]{2,1,0:T(8,128)(2,1)S(1)}, u32[]{:S(2)}, u32[]{:S(2)}) %collective-permute-start.21) | collective-permute-done | bytes 65568 | tf_op jit(solution)/shard_map/ppermute | solution.py:50
  66.6 2.4 %collective-permute-done.23.refs_2_ = bf16[8,32,128]{2,1,0:T(8,128)(2,1)S(1)} collective-permute-done((bf16[8,32,128]{2,1,0:T(8,128)(2,1)S(1)}, bf16[8,32,128]{2,1,0:T(8,128)(2,1)S(1)}, u32[]{:S(2)}, u32[]{:S(2)}) %collective-permute-start.23) | collective-permute-done | bytes 65568 | tf_op jit(solution)/shard_map/ppermute | solution.py:50
  69.7 5.6 %collective-permute-done.24.refs_0_ = bf16[8,32,128]{2,1,0:T(8,128)(2,1)S(1)} collective-permute-done((bf16[8,32,128]{2,1,0:T(8,128)(2,1)S(1)}, bf16[8,32,128]{2,1,0:T(8,128)(2,1)S(1)}, u32[]{:S(2)}, u32[]{:S(2)}) %collective-permute-start.24) | collective-permute-done | bytes 65568 | tf_op jit(solution)/shard_map/ppermute | solution.py:50
  76.7 1.4 %shard_map.90 = (f32[32,1024]{1,0:T(8,128)}, f32[32,128]{1,0:T(8,128)}) custom-call(bf16[8,32,128]{2,1,0:T(8,128)(2,1)S(1)} %collective-permute-done.25.scale_ref, f32[32,1024]{1,0:T(8,128)S(1)} %shard_map.89.image_ref, f32[32,1024]{1,0:T(8,128)S(1)} %get-tuple-element.95.u_ref, f32[8,32,128]{2,1,0:T(8,128)S(1)} %get-tuple-element.100.scale_v_ref, ...), custom_call_target="tpu_custom_call" | custom-call | tf_op jit(solution)/shard_map/pallas_call | solution.py:361
  (68 shorter events, 21.5 us)
Async XLA Ops:
  1.6 7.3 %collective-permute-start = (bf16[144,256]{1,0:T(8,128)(2,1)S(1)}, bf16[144,256]{1,0:T(8,128)(2,1)S(1)}, u32[]{:S(2)}, u32[]{:S(2)}) collective-permute-start(bf16[144,256]{1,0:T(8,128)(2,1)S(1)} %shard_map.67), channel_id=1, source_target_pairs={{0,9},{1,4},{2,7},{3,10},{4,1},{5,12},{6,15},{7,2},{8,13},{9,0},{1... | collective-permute-start | bytes 221192 | tf_op jit(solution)/shard_map/ppermute | solution.py:50
  5.1 4.4 %collective-permute-start.1 = (bf16[144,256]{1,0:T(8,128)(2,1)S(1)}, bf16[144,256]{1,0:T(8,128)(2,1)S(1)}, u32[]{:S(2)}, u32[]{:S(2)}) collective-permute-start(bf16[144,256]{1,0:T(8,128)(2,1)S(1)} %shard_map.67), channel_id=1, source_target_pairs={{0,3},{1,2},{2,1},{3,0},{4,7},{5,6},{6,5},{7,4},{8,11},{9,10},{10,... | collective-permute-start | bytes 221192 | tf_op jit(solution)/shard_map/ppermute | solution.py:50
  9.6 6.2 %collective-permute-start.2 = (bf16[288,256]{1,0:T(8,128)(2,1)S(1)}, bf16[288,256]{1,0:T(8,128)(2,1)S(1)}, u32[]{:S(2)}, u32[]{:S(2)}) collective-permute-start(bf16[288,256]{1,0:T(8,128)(2,1)S(1)} %pad_maximum_fusion.1), channel_id=1, source_target_pairs={{0,5},{1,8},{2,11},{3,6},{4,13},{5,0},{6,3},{7,14},{8,1},{9,12},{1... | collective-permute-start | bytes 442376 | tf_op jit(solution)/shard_map/ppermute | solution.py:50
  10.9 4.5 %collective-permute-start.3 = (bf16[144,256]{1,0:T(8,128)(2,1)S(1)}, bf16[144,256]{1,0:T(8,128)(2,1)S(1)}, u32[]{:S(2)}, u32[]{:S(2)}) collective-permute-start(bf16[144,256]{1,0:T(8,128)(2,1)S(1)} %collective-permute-done), channel_id=1, source_target_pairs={{0,3},{1,2},{2,1},{3,0},{4,7},{5,6},{6,5},{7,4},{8,11},{9,10},{10,... | collective-permute-start | bytes 221192 | tf_op jit(solution)/shard_map/ppermute | solution.py:50
  15.8 3.0 %collective-permute-start.5 = (bf16[576,256]{1,0:T(8,128)(2,1)S(1)}, bf16[576,256]{1,0:T(8,128)(2,1)S(1)}, u32[]{:S(2)}, u32[]{:S(2)}) collective-permute-start(bf16[576,256]{1,0:T(8,128)(2,1)S(1)} %pad_maximum_fusion.held_ref.refs_9_.refs_0_), channel_id=1, source_target_pairs={{0,1},{1,0},{2,3},{3,2},{4,5},{5,4},{6,7},{7,6},{8,9},{9,8},{10,11... | collective-permute-start | bytes 884744 | tf_op jit(solution)/shard_map/ppermute | solution.py:55
  15.9 2.5 %collective-permute-start.6 = (bf16[288,256]{1,0:T(8,128)(2,1)S(1)}, bf16[288,256]{1,0:T(8,128)(2,1)S(1)}, u32[]{:S(2)}, u32[]{:S(2)}) collective-permute-start(bf16[288,256]{1,0:T(8,128)(2,1)S(1)} %constant_dynamic-update-slice_fusion.held_ref.refs_10_.refs_1_), channel_id=1, source_target_pairs={{0,1},{1,0},{2,3},{3,2},{4,5},{5,4},{6,7},{7,6},{8,9},{9,8},{10,11... | collective-permute-start | bytes 442376 | tf_op jit(solution)/shard_map/ppermute | solution.py:55
  16.5 5.9 %collective-permute-start.4 = (bf16[288,256]{1,0:T(8,128)(2,1)S(1)}, bf16[288,256]{1,0:T(8,128)(2,1)S(1)}, u32[]{:S(2)}, u32[]{:S(2)}) collective-permute-start(bf16[288,256]{1,0:T(8,128)(2,1)S(1)} %collective-permute-done.2), channel_id=1, source_target_pairs={{0,3},{1,2},{2,1},{3,0},{4,7},{5,6},{6,5},{7,4},{8,11},{9,10},{10,... | collective-permute-start | bytes 442376 | tf_op jit(solution)/shard_map/ppermute | solution.py:50
  22.4 1.4 %collective-permute-start.7 = (bf16[288,256]{1,0:T(8,128)(2,1)S(1)}, bf16[288,256]{1,0:T(8,128)(2,1)S(1)}, u32[]{:S(2)}, u32[]{:S(2)}) collective-permute-start(bf16[288,256]{1,0:T(8,128)(2,1)S(1)} %collective-permute-done.4.held_ref.refs_11_.refs_2_), channel_id=1, source_target_pairs={{0,1},{1,0},{2,3},{3,2},{4,5},{5,4},{6,7},{7,6},{8,9},{9,8},{10,11... | collective-permute-start | bytes 442376 | tf_op jit(solution)/shard_map/ppermute | solution.py:55
  24.8 1.3 %collective-permute-start.8 = (bf16[8,32,128]{2,1,0:T(8,128)(2,1)S(1)}, bf16[8,32,128]{2,1,0:T(8,128)(2,1)S(1)}, u32[]{:S(2)}, u32[]{:S(2)}) collective-permute-start(bf16[8,32,128]{2,1,0:T(8,128)(2,1)S(1)} %get-tuple-element.84), channel_id=1, source_target_pairs={{0,1},{1,0},{2,3},{3,2},{4,5},{5,4},{6,7},{7,6},{8,9},{9,8},{10,11... | collective-permute-start | bytes 196616 | tf_op jit(solution)/shard_map/ppermute | solution.py:55
  26.1 4.1 %collective-permute-start.9 = (bf16[8,32,128]{2,1,0:T(8,128)(2,1)S(1)}, bf16[8,32,128]{2,1,0:T(8,128)(2,1)S(1)}, u32[]{:S(2)}, u32[]{:S(2)}) collective-permute-start(bf16[8,32,128]{2,1,0:T(8,128)(2,1)S(1)} %get-tuple-element.107), channel_id=1, source_target_pairs={{0,3},{1,2},{2,1},{3,0},{4,7},{5,6},{6,5},{7,4},{8,11},{9,10},{10,... | collective-permute-start | bytes 196616 | tf_op jit(solution)/shard_map/ppermute | solution.py:50
  27.1 3.9 %collective-permute-start.10 = (bf16[8,32,128]{2,1,0:T(8,128)(2,1)S(1)}, bf16[8,32,128]{2,1,0:T(8,128)(2,1)S(1)}, u32[]{:S(2)}, u32[]{:S(2)}) collective-permute-start(bf16[8,32,128]{2,1,0:T(8,128)(2,1)S(1)} %get-tuple-element.107), channel_id=1, source_target_pairs={{0,5},{1,4},{2,7},{3,6},{4,1},{5,0},{6,3},{7,2},{8,13},{9,12},{10,... | collective-permute-start | bytes 196616 | tf_op jit(solution)/shard_map/ppermute | solution.py:50
  27.3 5.9 %collective-permute-start.11 = (bf16[8,32,128]{2,1,0:T(8,128)(2,1)S(1)}, bf16[8,32,128]{2,1,0:T(8,128)(2,1)S(1)}, u32[]{:S(2)}, u32[]{:S(2)}) collective-permute-start(bf16[8,32,128]{2,1,0:T(8,128)(2,1)S(1)} %get-tuple-element.107), channel_id=1, source_target_pairs={{0,6},{1,7},{2,4},{3,5},{4,2},{5,3},{6,0},{7,1},{8,14},{9,15},{10,... | collective-permute-start | bytes 196616 | tf_op jit(solution)/shard_map/ppermute | solution.py:50
  33.3 6.5 %collective-permute-start.12 = (bf16[8,32,128]{2,1,0:T(8,128)(2,1)S(1)}, bf16[8,32,128]{2,1,0:T(8,128)(2,1)S(1)}, u32[]{:S(2)}, u32[]{:S(2)}) collective-permute-start(bf16[8,32,128]{2,1,0:T(8,128)(2,1)S(1)} %get-tuple-element.86), channel_id=1, source_target_pairs={{0,9},{1,8},{2,11},{3,10},{4,13},{5,12},{6,15},{7,14},{8,1},{9,0},... | collective-permute-start | bytes 196616 | tf_op jit(solution)/shard_map/ppermute | solution.py:50
  39.8 1.3 %collective-permute-start.13 = (bf16[8,32,128]{2,1,0:T(8,128)(2,1)S(1)}, bf16[8,32,128]{2,1,0:T(8,128)(2,1)S(1)}, u32[]{:S(2)}, u32[]{:S(2)}) collective-permute-start(bf16[8,32,128]{2,1,0:T(8,128)(2,1)S(1)} %shard_map.78.scale_ref), channel_id=1, source_target_pairs={{0,1},{1,0},{2,3},{3,2},{4,5},{5,4},{6,7},{7,6},{8,9},{9,8},{10,11... | collective-permute-start | bytes 196616 | tf_op jit(solution)/shard_map/ppermute | solution.py:55
  43.9 4.1 %collective-permute-start.15 = (bf16[8,32,128]{2,1,0:T(8,128)(2,1)S(1)}, bf16[8,32,128]{2,1,0:T(8,128)(2,1)S(1)}, u32[]{:S(2)}, u32[]{:S(2)}) collective-permute-start(bf16[8,32,128]{2,1,0:T(8,128)(2,1)S(1)} %get-tuple-element.105), channel_id=1, source_target_pairs={{0,3},{1,2},{2,1},{3,0},{4,7},{5,6},{6,5},{7,4},{8,11},{9,10},{10,... | collective-permute-start | bytes 196616 | tf_op jit(solution)/shard_map/ppermute | solution.py:50
  44.7 3.9 %collective-permute-start.16 = (bf16[8,32,128]{2,1,0:T(8,128)(2,1)S(1)}, bf16[8,32,128]{2,1,0:T(8,128)(2,1)S(1)}, u32[]{:S(2)}, u32[]{:S(2)}) collective-permute-start(bf16[8,32,128]{2,1,0:T(8,128)(2,1)S(1)} %get-tuple-element.105), channel_id=1, source_target_pairs={{0,5},{1,4},{2,7},{3,6},{4,1},{5,0},{6,3},{7,2},{8,13},{9,12},{10,... | collective-permute-start | bytes 196616 | tf_op jit(solution)/shard_map/ppermute | solution.py:50
  44.7 6.3 %collective-permute-start.17 = (bf16[8,32,128]{2,1,0:T(8,128)(2,1)S(1)}, bf16[8,32,128]{2,1,0:T(8,128)(2,1)S(1)}, u32[]{:S(2)}, u32[]{:S(2)}) collective-permute-start(bf16[8,32,128]{2,1,0:T(8,128)(2,1)S(1)} %get-tuple-element.105), channel_id=1, source_target_pairs={{0,6},{1,7},{2,4},{3,5},{4,2},{5,3},{6,0},{7,1},{8,14},{9,15},{10,... | collective-permute-start | bytes 196616 | tf_op jit(solution)/shard_map/ppermute | solution.py:50
  51.1 6.6 %collective-permute-start.18 = (bf16[8,32,128]{2,1,0:T(8,128)(2,1)S(1)}, bf16[8,32,128]{2,1,0:T(8,128)(2,1)S(1)}, u32[]{:S(2)}, u32[]{:S(2)}) collective-permute-start(bf16[8,32,128]{2,1,0:T(8,128)(2,1)S(1)} %get-tuple-element.91), channel_id=1, source_target_pairs={{0,9},{1,8},{2,11},{3,10},{4,13},{5,12},{6,15},{7,14},{8,1},{9,0},... | collective-permute-start | bytes 196616 | tf_op jit(solution)/shard_map/ppermute | solution.py:50
  57.7 1.3 %collective-permute-start.19 = (bf16[8,32,128]{2,1,0:T(8,128)(2,1)S(1)}, bf16[8,32,128]{2,1,0:T(8,128)(2,1)S(1)}, u32[]{:S(2)}, u32[]{:S(2)}) collective-permute-start(bf16[8,32,128]{2,1,0:T(8,128)(2,1)S(1)} %shard_map.83.scale_ref), channel_id=1, source_target_pairs={{0,1},{1,0},{2,3},{3,2},{4,5},{5,4},{6,7},{7,6},{8,9},{9,8},{10,11... | collective-permute-start | bytes 196616 | tf_op jit(solution)/shard_map/ppermute | solution.py:55
  61.8 4.1 %collective-permute-start.21 = (bf16[8,32,128]{2,1,0:T(8,128)(2,1)S(1)}, bf16[8,32,128]{2,1,0:T(8,128)(2,1)S(1)}, u32[]{:S(2)}, u32[]{:S(2)}) collective-permute-start(bf16[8,32,128]{2,1,0:T(8,128)(2,1)S(1)} %get-tuple-element.103), channel_id=1, source_target_pairs={{0,3},{1,2},{2,1},{3,0},{4,7},{5,6},{6,5},{7,4},{8,11},{9,10},{10,... | collective-permute-start | bytes 196616 | tf_op jit(solution)/shard_map/ppermute | solution.py:50
  62.6 3.9 %collective-permute-start.22 = (bf16[8,32,128]{2,1,0:T(8,128)(2,1)S(1)}, bf16[8,32,128]{2,1,0:T(8,128)(2,1)S(1)}, u32[]{:S(2)}, u32[]{:S(2)}) collective-permute-start(bf16[8,32,128]{2,1,0:T(8,128)(2,1)S(1)} %get-tuple-element.103), channel_id=1, source_target_pairs={{0,5},{1,4},{2,7},{3,6},{4,1},{5,0},{6,3},{7,2},{8,13},{9,12},{10,... | collective-permute-start | bytes 196616 | tf_op jit(solution)/shard_map/ppermute | solution.py:50
  62.6 6.3 %collective-permute-start.23 = (bf16[8,32,128]{2,1,0:T(8,128)(2,1)S(1)}, bf16[8,32,128]{2,1,0:T(8,128)(2,1)S(1)}, u32[]{:S(2)}, u32[]{:S(2)}) collective-permute-start(bf16[8,32,128]{2,1,0:T(8,128)(2,1)S(1)} %get-tuple-element.103), channel_id=1, source_target_pairs={{0,6},{1,7},{2,4},{3,5},{4,2},{5,3},{6,0},{7,1},{8,14},{9,15},{10,... | collective-permute-start | bytes 196616 | tf_op jit(solution)/shard_map/ppermute | solution.py:50
  69.0 6.4 %collective-permute-start.24 = (bf16[8,32,128]{2,1,0:T(8,128)(2,1)S(1)}, bf16[8,32,128]{2,1,0:T(8,128)(2,1)S(1)}, u32[]{:S(2)}, u32[]{:S(2)}) collective-permute-start(bf16[8,32,128]{2,1,0:T(8,128)(2,1)S(1)} %get-tuple-element.94), channel_id=1, source_target_pairs={{0,9},{1,8},{2,11},{3,10},{4,13},{5,12},{6,15},{7,14},{8,1},{9,0},... | collective-permute-start | bytes 196616 | tf_op jit(solution)/shard_map/ppermute | solution.py:50
  75.4 1.3 %collective-permute-start.25 = (bf16[8,32,128]{2,1,0:T(8,128)(2,1)S(1)}, bf16[8,32,128]{2,1,0:T(8,128)(2,1)S(1)}, u32[]{:S(2)}, u32[]{:S(2)}) collective-permute-start(bf16[8,32,128]{2,1,0:T(8,128)(2,1)S(1)} %get-tuple-element.99.scale_ref), channel_id=1, source_target_pairs={{0,1},{1,0},{2,3},{3,2},{4,5},{5,4},{6,7},{7,6},{8,9},{9,8},{10,11... | collective-permute-start | bytes 196616 | tf_op jit(solution)/shard_map/ppermute | solution.py:55
  (4 other events, 10.8 us)

commit v14 on v13

--- a/solution.py
+++ b/solution.py
@@ -28,9 +28,9 @@
     return (layer if kind else layer[::-1]) + [1]
 
 
-def rounds(top):
+def order(kind, top):
     bits = list(range(1, top))
-    return [bits[low : low + 2] for low in range(0, len(bits), 2)]
+    return bits[1 - kind :] + bits[: 1 - kind]
 
 
 def flips_of(bits):
@@ -240,38 +240,58 @@
     mass_ref[...] = candidates * u_ref[...] * image
 
 
-def slot_of(slot, flips, slots):
-    top = slots.bit_length()
+def spread(top):
+    return list(zip(*[flips_of(order(kind, top)[:2]) for kind in range(2)]))
+
+
+def slot_of(kept, flips, top):
     found = []
     for kind, flip in enumerate(flips):
-        turned = sum(1 << i for i, bit in enumerate(slot_bits(kind, top)) if flip >> bit & 1)
-        found.append(slot ^ turned)
+        own = sum(1 << bit for i, bit in enumerate(order(kind, top)[2:]) if kept >> i & 1)
+        bits = enumerate(slot_bits(kind, top))
+        found.append(sum(1 << i for i, bit in bits if (flip ^ own) >> bit & 1))
     if found[0] == found[1]:
         return found[0]
     return found[0] + parity(lax.axis_index("row"), top) * (found[1] - found[0])
 
 
-def total_of(slot, own_ref, got_refs, flips):
-    total = own_ref[slot]
-    for pair, got_ref in zip(flips, got_refs):
-        total += got_ref[slot_of(slot, pair, own_ref.shape[0])].astype(F32)
+def part_body(column_ref, got_ref, *out_refs, top):
+    for out_ref, flips in zip(out_refs, [(0, 0)] + spread(top)):
+        for kept in range(out_ref.shape[0]):
+            slot = slot_of(kept, flips, top)
+            total = column_ref[slot] + got_ref[slot].astype(F32)
+            out_ref[kept] = total.astype(out_ref.dtype)
+
+
+def total_of(kept, own_ref, got_refs, masks):
+    total = own_ref[kept]
+    for mask, got_ref in zip(masks, got_refs):
+        total += got_ref[kept ^ mask].astype(F32)
     return total
 
 
-def sum_body(own_ref, *refs, flips):
+def sum_body(own_ref, *refs, masks):
     *got_refs, total_ref, sent_ref = refs
-    for slot in range(own_ref.shape[0]):
-        total = total_of(slot, own_ref, got_refs, flips)
-        total_ref[slot] = total
-        sent_ref[slot] = total.astype(BF16)
-
-
-def scale_body(own_ref, marg_ref, *refs, flips):
-    got_refs, outs = refs[: len(flips)], refs[len(flips) :]
-    for slot in range(own_ref.shape[0]):
-        scale_v = marg_ref[slot] / total_of(slot, own_ref, got_refs, flips)
+    for kept in range(own_ref.shape[0]):
+        total = total_of(kept, own_ref, got_refs, masks)
+        total_ref[kept] = total
+        sent_ref[kept] = total.astype(BF16)
+
+
+def scale_body(own_ref, marg_ref, *refs, masks, top):
+    got_refs, outs = refs[: len(masks)], refs[len(masks) :]
+    for kept in range(own_ref.shape[0]):
+        marg = marg_ref[slot_of(kept, (0, 0), top)]
+        scale_v = marg / total_of(kept, own_ref, got_refs, masks)
         for out_ref in outs:
-            out_ref[slot] = scale_v.astype(out_ref.dtype)
+            out_ref[kept] = scale_v.astype(out_ref.dtype)
+
+
+def join_body(*refs, top):
+    *part_refs, out_ref = refs
+    for part_ref, flips in zip(part_refs, [(0, 0)] + spread(top)):
+        for kept in range(part_ref.shape[0]):
+            out_ref[slot_of(kept, flips, top)] = part_ref[kept]
 
 
 def shards(cand_embed, cand_labels, tgt_embed, tgt_labels):
@@ -282,6 +302,7 @@
     tgt_rows = tgt_embed.shape[0]
     cand_labels = cand_labels.reshape(1, cand_rows)
     block = (slots, CLASSES, tgt_rows)
+    kept = (slots // 4, CLASSES, tgt_rows)
     image_type = ((CLASSES, cand_rows), F32)
     rounded_type = ((CLASSES, cand_rows), BF16)
     half_flops = 2 * cand_rows * slots * tgt_rows * 128
@@ -335,25 +356,30 @@
         (column,) = call(
             column_body, [(block, F32)], scale_ub, *near_kernels, flops=half_flops
         )
-        column = column + got.astype(F32)
-        sent = column.astype(BF16)
-        order = rounds(top)
-        for place, bits in enumerate(order):
-            flips = [(flip, flip) for flip in flips_of(bits)]
-            found = [exchange(sent, *turn) for turn in flips]
-            if place < len(order) - 1:
-                column, sent = call(
-                    functools.partial(sum_body, flips=flips),
-                    [(block, F32), (block, BF16)], column, *found,
-                )
+        column, *sent = call(
+            functools.partial(part_body, top=top),
+            [(kept, F32)] + [(kept, BF16)] * 3, column, got,
+        )
+        found = [exchange(part, *flips) for part, flips in zip(sent, spread(top))]
+        masks = [0] * 3
+        for low in range(2, top - 1, 2):
+            column, sent = call(
+                functools.partial(sum_body, masks=masks),
+                [(kept, F32), (kept, BF16)], column, *found,
+            )
+            turns = [flips_of(order(kind, top)[low : low + 2]) for kind in range(2)]
+            found = [exchange(sent, *flips) for flips in zip(*turns)]
+            masks = flips_of(list(range(low - 2, low - 2 + len(turns[0]).bit_length())))
         if last:
             potential = ENTROPY_TEMP * jnp.log(scale_u[0])
             found, potential = lax.optimization_barrier((found, potential))
-        scale_vb, *scale_v = call(
-            functools.partial(scale_body, flips=flips),
-            [(block, BF16)] + [(block, F32)] * last,
+        own_vb, *scale_v = call(
+            functools.partial(scale_body, masks=masks, top=top),
+            [(kept, BF16)] + [(kept, F32)] * last,
             column, tgt_marg, *found,
         )
+        found = [exchange(own_vb, *flips) for flips in spread(top)]
+        (scale_vb,) = call(functools.partial(join_body, top=top), [(block, BF16)], own_vb, *found)
         far_vb = swap(scale_vb)
         (image,) = call(image_body, [image_type], scale_vb, *near_kernels, flops=half_flops)
     space = pl.BlockSpec(memory_space=pltpu.VMEM)

time: 78.3 us -> 94 us (1.20)
  starting transfers between devices: 21 us -> 35.1 us
  waiting for transfers between devices: 40.7 us -> 42.2 us
    ppermute x17 -> x26, starting transfers between devices: 19.3 us -> 33.7 us  [exchange(): return lax.ppermute(block, 'row', pairs)]
    ppermute x17 -> x26, waiting for transfers between devices: 36.5 us -> 37.9 us  [exchange(): return lax.ppermute(block, 'row', pairs)]
    pallas_call x22 -> x28, Pallas kernels: 10.5 us -> 10.5 us  [call(): pl.pallas_call(body, out_shape=[pltpu.VMEM(shape, dtype) for shape, dtype...]
  transfers between devices with their start and end apart: 26 -> 35, of which waited for: 23 -> 20; matrix products, arithmetic and copies ran while one was open for 3% -> 2% of each run, Pallas kernels for 8% -> 7%
where the time goes in v14:
time: 94 us; the launch traced here: 93.8 us
  waiting for transfers between devices  42.2 us (45%)
  starting transfers between devices  35.1 us (37%)
  Pallas kernels  12.8 us (14%)
  other arithmetic  2.19 us (2%)
  between operations  0.98 us (1%)
    ppermute x26, waiting for transfers between devices, exchange(): return lax.ppermute(block, 'row', pairs)  37.9 us
    ppermute x26, starting transfers between devices, exchange(): return lax.ppermute(block, 'row', pairs)  33.7 us
    pallas_call x28, Pallas kernels, call(): pl.pallas_call(body, out_shape=[pltpu.VMEM(shape, dtype) for shape, dtype...  10.5 us
    ppermute x9, waiting for transfers between devices, swap(): return lax.ppermute(block, 'row', [(d, d ^ 1) for d in range(devices)])  4.32 us
  transfers between devices with their start and end apart: 35, of which 20 were waited for; matrix products, arithmetic and copies ran while one was open for 2% of the time, Pallas kernels for 7%

profile of v14, /device:TPU:0, one launch (start us, length us, event | category | flops | bytes accessed | tf_op | source)
XLA Modules:
  0.0 93.8 jit_solution(8566049856833950283)
XLA Ops:
  1.6 3.5 %collective-permute-start = (bf16[144,256]{1,0:T(8,128)(2,1)S(1)}, bf16[144,256]{1,0:T(8,128)(2,1)S(1)}, u32[]{:S(2)}, u32[]{:S(2)}) collective-permute-start(bf16[144,256]{1,0:T(8,128)(2,1)S(1)} %shard_map.67), channel_id=1, source_target_pairs={{0,9},{1,4},{2,7},{3,10},{4,1},{5,12},{6,15},{7,2},{8,13},{9,0},{1... | collective-permute-start | bytes 221192 | tf_op jit(solution)/shard_map/ppermute | solution.py:50
  11.8 3.5 %collective-permute-done.3 = bf16[144,256]{1,0:T(8,128)(2,1)S(1)} collective-permute-done((bf16[144,256]{1,0:T(8,128)(2,1)S(1)}, bf16[144,256]{1,0:T(8,128)(2,1)S(1)}, u32[]{:S(2)}, u32[]{:S(2)}) %collective-permute-start.3) | collective-permute-done | bytes 73760 | tf_op jit(solution)/shard_map/ppermute | solution.py:50
  19.5 2.9 %collective-permute-done.4.held_ref.refs_11_.refs_2_ = bf16[288,256]{1,0:T(8,128)(2,1)S(1)} collective-permute-done((bf16[288,256]{1,0:T(8,128)(2,1)S(1)}, bf16[288,256]{1,0:T(8,128)(2,1)S(1)}, u32[]{:S(2)}, u32[]{:S(2)}) %collective-permute-start.4) | collective-permute-done | bytes 147488 | tf_op jit(solution)/shard_map/ppermute | solution.py:50
  26.3 2.1 %collective-permute-start.10 = (bf16[2,32,128]{2,1,0:T(8,128)(2,1)S(1)}, bf16[2,32,128]{2,1,0:T(8,128)(2,1)S(1)}, u32[]{:S(2)}, u32[]{:S(2)}) collective-permute-start(bf16[2,32,128]{2,1,0:T(8,128)(2,1)S(1)} %get-tuple-element.99), channel_id=1, source_target_pairs={{0,9},{1,4},{2,7},{3,10},{4,1},{5,12},{6,15},{7,2},{8,13},{9,0},{1... | collective-permute-start | bytes 49160 | tf_op jit(solution)/shard_map/ppermute | solution.py:50
  28.4 1.9 %collective-permute-start.11 = (bf16[2,32,128]{2,1,0:T(8,128)(2,1)S(1)}, bf16[2,32,128]{2,1,0:T(8,128)(2,1)S(1)}, u32[]{:S(2)}, u32[]{:S(2)}) collective-permute-start(bf16[2,32,128]{2,1,0:T(8,128)(2,1)S(1)} %get-tuple-element.100), channel_id=1, source_target_pairs={{0,12},{1,7},{2,4},{3,15},{4,2},{5,9},{6,10},{7,1},{8,14},{9,5},{1... | collective-permute-start | bytes 49160 | tf_op jit(solution)/shard_map/ppermute | solution.py:50
  30.3 3.6 %collective-permute-done.11.refs_2_ = bf16[2,32,128]{2,1,0:T(8,128)(2,1)S(1)} collective-permute-done((bf16[2,32,128]{2,1,0:T(8,128)(2,1)S(1)}, bf16[2,32,128]{2,1,0:T(8,128)(2,1)S(1)}, u32[]{:S(2)}, u32[]{:S(2)}) %collective-permute-start.11) | collective-permute-done | bytes 16416 | tf_op jit(solution)/shard_map/ppermute | solution.py:50
  34.2 3.0 %collective-permute-done.12.refs_0_ = bf16[2,32,128]{2,1,0:T(8,128)(2,1)S(1)} collective-permute-done((bf16[2,32,128]{2,1,0:T(8,128)(2,1)S(1)}, bf16[2,32,128]{2,1,0:T(8,128)(2,1)S(1)}, u32[]{:S(2)}, u32[]{:S(2)}) %collective-permute-start.12) | collective-permute-done | bytes 16416 | tf_op jit(solution)/shard_map/ppermute | solution.py:50
  37.3 2.2 %collective-permute-start.14 = (bf16[2,32,128]{2,1,0:T(8,128)(2,1)S(1)}, bf16[2,32,128]{2,1,0:T(8,128)(2,1)S(1)}, u32[]{:S(2)}, u32[]{:S(2)}) collective-permute-start(bf16[2,32,128]{2,1,0:T(8,128)(2,1)S(1)} %shard_map.79.refs_0_), channel_id=1, source_target_pairs={{0,9},{1,4},{2,7},{3,10},{4,1},{5,12},{6,15},{7,2},{8,13},{9,0},{1... | collective-permute-start | bytes 49160 | tf_op jit(solution)/shard_map/ppermute | solution.py:50
  39.5 1.9 %collective-permute-start.15 = (bf16[2,32,128]{2,1,0:T(8,128)(2,1)S(1)}, bf16[2,32,128]{2,1,0:T(8,128)(2,1)S(1)}, u32[]{:S(2)}, u32[]{:S(2)}) collective-permute-start(bf16[2,32,128]{2,1,0:T(8,128)(2,1)S(1)} %shard_map.79.refs_0_), channel_id=1, source_target_pairs={{0,12},{1,7},{2,4},{3,15},{4,2},{5,9},{6,10},{7,1},{8,14},{9,5},{1... | collective-permute-start | bytes 49160 | tf_op jit(solution)/shard_map/ppermute | solution.py:50
  41.4 3.6 %collective-permute-done.15.refs_3_ = bf16[2,32,128]{2,1,0:T(8,128)(2,1)S(1)} collective-permute-done((bf16[2,32,128]{2,1,0:T(8,128)(2,1)S(1)}, bf16[2,32,128]{2,1,0:T(8,128)(2,1)S(1)}, u32[]{:S(2)}, u32[]{:S(2)}) %collective-permute-start.15) | collective-permute-done | bytes 16416 | tf_op jit(solution)/shard_map/ppermute | solution.py:50
  49.3 2.2 %collective-permute-start.19 = (bf16[2,32,128]{2,1,0:T(8,128)(2,1)S(1)}, bf16[2,32,128]{2,1,0:T(8,128)(2,1)S(1)}, u32[]{:S(2)}, u32[]{:S(2)}) collective-permute-start(bf16[2,32,128]{2,1,0:T(8,128)(2,1)S(1)} %get-tuple-element.108), channel_id=1, source_target_pairs={{0,9},{1,4},{2,7},{3,10},{4,1},{5,12},{6,15},{7,2},{8,13},{9,0},{1... | collective-permute-start | bytes 49160 | tf_op jit(solution)/shard_map/ppermute | solution.py:50
  51.4 1.9 %collective-permute-start.20 = (bf16[2,32,128]{2,1,0:T(8,128)(2,1)S(1)}, bf16[2,32,128]{2,1,0:T(8,128)(2,1)S(1)}, u32[]{:S(2)}, u32[]{:S(2)}) collective-permute-start(bf16[2,32,128]{2,1,0:T(8,128)(2,1)S(1)} %get-tuple-element.109), channel_id=1, source_target_pairs={{0,12},{1,7},{2,4},{3,15},{4,2},{5,9},{6,10},{7,1},{8,14},{9,5},{1... | collective-permute-start | bytes 49160 | tf_op jit(solution)/shard_map/ppermute | solution.py:50
  53.4 3.6 %collective-permute-done.20.refs_2_ = bf16[2,32,128]{2,1,0:T(8,128)(2,1)S(1)} collective-permute-done((bf16[2,32,128]{2,1,0:T(8,128)(2,1)S(1)}, bf16[2,32,128]{2,1,0:T(8,128)(2,1)S(1)}, u32[]{:S(2)}, u32[]{:S(2)}) %collective-permute-start.20) | collective-permute-done | bytes 16416 | tf_op jit(solution)/shard_map/ppermute | solution.py:50
  57.1 3.2 %collective-permute-done.21.refs_0_ = bf16[2,32,128]{2,1,0:T(8,128)(2,1)S(1)} collective-permute-done((bf16[2,32,128]{2,1,0:T(8,128)(2,1)S(1)}, bf16[2,32,128]{2,1,0:T(8,128)(2,1)S(1)}, u32[]{:S(2)}, u32[]{:S(2)}) %collective-permute-start.21) | collective-permute-done | bytes 16416 | tf_op jit(solution)/shard_map/ppermute | solution.py:50
  60.3 2.2 %collective-permute-start.23 = (bf16[2,32,128]{2,1,0:T(8,128)(2,1)S(1)}, bf16[2,32,128]{2,1,0:T(8,128)(2,1)S(1)}, u32[]{:S(2)}, u32[]{:S(2)}) collective-permute-start(bf16[2,32,128]{2,1,0:T(8,128)(2,1)S(1)} %shard_map.86.refs_0_), channel_id=1, source_target_pairs={{0,9},{1,4},{2,7},{3,10},{4,1},{5,12},{6,15},{7,2},{8,13},{9,0},{1... | collective-permute-start | bytes 49160 | tf_op jit(solution)/shard_map/ppermute | solution.py:50
  62.5 1.9 %collective-permute-start.24 = (bf16[2,32,128]{2,1,0:T(8,128)(2,1)S(1)}, bf16[2,32,128]{2,1,0:T(8,128)(2,1)S(1)}, u32[]{:S(2)}, u32[]{:S(2)}) collective-permute-start(bf16[2,32,128]{2,1,0:T(8,128)(2,1)S(1)} %shard_map.86.refs_0_), channel_id=1, source_target_pairs={{0,12},{1,7},{2,4},{3,15},{4,2},{5,9},{6,10},{7,1},{8,14},{9,5},{1... | collective-permute-start | bytes 49160 | tf_op jit(solution)/shard_map/ppermute | solution.py:50
  64.5 3.6 %collective-permute-done.24.refs_3_ = bf16[2,32,128]{2,1,0:T(8,128)(2,1)S(1)} collective-permute-done((bf16[2,32,128]{2,1,0:T(8,128)(2,1)S(1)}, bf16[2,32,128]{2,1,0:T(8,128)(2,1)S(1)}, u32[]{:S(2)}, u32[]{:S(2)}) %collective-permute-start.24) | collective-permute-done | bytes 16416 | tf_op jit(solution)/shard_map/ppermute | solution.py:50
  72.3 2.2 %collective-permute-start.28 = (bf16[2,32,128]{2,1,0:T(8,128)(2,1)S(1)}, bf16[2,32,128]{2,1,0:T(8,128)(2,1)S(1)}, u32[]{:S(2)}, u32[]{:S(2)}) collective-permute-start(bf16[2,32,128]{2,1,0:T(8,128)(2,1)S(1)} %get-tuple-element.116), channel_id=1, source_target_pairs={{0,9},{1,4},{2,7},{3,10},{4,1},{5,12},{6,15},{7,2},{8,13},{9,0},{1... | collective-permute-start | bytes 49160 | tf_op jit(solution)/shard_map/ppermute | solution.py:50
  74.5 1.9 %collective-permute-start.29 = (bf16[2,32,128]{2,1,0:T(8,128)(2,1)S(1)}, bf16[2,32,128]{2,1,0:T(8,128)(2,1)S(1)}, u32[]{:S(2)}, u32[]{:S(2)}) collective-permute-start(bf16[2,32,128]{2,1,0:T(8,128)(2,1)S(1)} %get-tuple-element.117), channel_id=1, source_target_pairs={{0,12},{1,7},{2,4},{3,15},{4,2},{5,9},{6,10},{7,1},{8,14},{9,5},{1... | collective-permute-start | bytes 49160 | tf_op jit(solution)/shard_map/ppermute | solution.py:50
  76.4 3.6 %collective-permute-done.29.refs_2_ = bf16[2,32,128]{2,1,0:T(8,128)(2,1)S(1)} collective-permute-done((bf16[2,32,128]{2,1,0:T(8,128)(2,1)S(1)}, bf16[2,32,128]{2,1,0:T(8,128)(2,1)S(1)}, u32[]{:S(2)}, u32[]{:S(2)}) %collective-permute-start.29) | collective-permute-done | bytes 16416 | tf_op jit(solution)/shard_map/ppermute | solution.py:50
  80.8 2.5 %collective-permute-done.30.refs_0_ = bf16[2,32,128]{2,1,0:T(8,128)(2,1)S(1)} collective-permute-done((bf16[2,32,128]{2,1,0:T(8,128)(2,1)S(1)}, bf16[2,32,128]{2,1,0:T(8,128)(2,1)S(1)}, u32[]{:S(2)}, u32[]{:S(2)}) %collective-permute-start.30) | collective-permute-done | bytes 16416 | tf_op jit(solution)/shard_map/ppermute | solution.py:50
  83.4 2.2 %collective-permute-start.32 = (bf16[2,32,128]{2,1,0:T(8,128)(2,1)S(1)}, bf16[2,32,128]{2,1,0:T(8,128)(2,1)S(1)}, u32[]{:S(2)}, u32[]{:S(2)}) collective-permute-start(bf16[2,32,128]{2,1,0:T(8,128)(2,1)S(1)} %get-tuple-element.123.refs_0_), channel_id=1, source_target_pairs={{0,9},{1,4},{2,7},{3,10},{4,1},{5,12},{6,15},{7,2},{8,13},{9,0},{1... | collective-permute-start | bytes 49160 | tf_op jit(solution)/shard_map/ppermute | solution.py:50
  85.6 1.9 %collective-permute-start.33 = (bf16[2,32,128]{2,1,0:T(8,128)(2,1)S(1)}, bf16[2,32,128]{2,1,0:T(8,128)(2,1)S(1)}, u32[]{:S(2)}, u32[]{:S(2)}) collective-permute-start(bf16[2,32,128]{2,1,0:T(8,128)(2,1)S(1)} %get-tuple-element.123.refs_0_), channel_id=1, source_target_pairs={{0,12},{1,7},{2,4},{3,15},{4,2},{5,9},{6,10},{7,1},{8,14},{9,5},{1... | collective-permute-start | bytes 49160 | tf_op jit(solution)/shard_map/ppermute | solution.py:50
  87.5 3.6 %collective-permute-done.33.refs_3_ = bf16[2,32,128]{2,1,0:T(8,128)(2,1)S(1)} collective-permute-done((bf16[2,32,128]{2,1,0:T(8,128)(2,1)S(1)}, bf16[2,32,128]{2,1,0:T(8,128)(2,1)S(1)}, u32[]{:S(2)}, u32[]{:S(2)}) %collective-permute-start.33) | collective-permute-done | bytes 16416 | tf_op jit(solution)/shard_map/ppermute | solution.py:50
  (89 shorter events, 28.2 us)
Async XLA Ops:
  1.6 7.3 %collective-permute-start = (bf16[144,256]{1,0:T(8,128)(2,1)S(1)}, bf16[144,256]{1,0:T(8,128)(2,1)S(1)}, u32[]{:S(2)}, u32[]{:S(2)}) collective-permute-start(bf16[144,256]{1,0:T(8,128)(2,1)S(1)} %shard_map.67), channel_id=1, source_target_pairs={{0,9},{1,4},{2,7},{3,10},{4,1},{5,12},{6,15},{7,2},{8,13},{9,0},{1... | collective-permute-start | bytes 221192 | tf_op jit(solution)/shard_map/ppermute | solution.py:50
  5.1 4.4 %collective-permute-start.1 = (bf16[144,256]{1,0:T(8,128)(2,1)S(1)}, bf16[144,256]{1,0:T(8,128)(2,1)S(1)}, u32[]{:S(2)}, u32[]{:S(2)}) collective-permute-start(bf16[144,256]{1,0:T(8,128)(2,1)S(1)} %shard_map.67), channel_id=1, source_target_pairs={{0,3},{1,2},{2,1},{3,0},{4,7},{5,6},{6,5},{7,4},{8,11},{9,10},{10,... | collective-permute-start | bytes 221192 | tf_op jit(solution)/shard_map/ppermute | solution.py:50
  9.6 6.2 %collective-permute-start.2 = (bf16[288,256]{1,0:T(8,128)(2,1)S(1)}, bf16[288,256]{1,0:T(8,128)(2,1)S(1)}, u32[]{:S(2)}, u32[]{:S(2)}) collective-permute-start(bf16[288,256]{1,0:T(8,128)(2,1)S(1)} %pad_maximum_fusion.1), channel_id=1, source_target_pairs={{0,5},{1,8},{2,11},{3,6},{4,13},{5,0},{6,3},{7,14},{8,1},{9,12},{1... | collective-permute-start | bytes 442376 | tf_op jit(solution)/shard_map/ppermute | solution.py:50
  10.9 4.5 %collective-permute-start.3 = (bf16[144,256]{1,0:T(8,128)(2,1)S(1)}, bf16[144,256]{1,0:T(8,128)(2,1)S(1)}, u32[]{:S(2)}, u32[]{:S(2)}) collective-permute-start(bf16[144,256]{1,0:T(8,128)(2,1)S(1)} %collective-permute-done), channel_id=1, source_target_pairs={{0,3},{1,2},{2,1},{3,0},{4,7},{5,6},{6,5},{7,4},{8,11},{9,10},{10,... | collective-permute-start | bytes 221192 | tf_op jit(solution)/shard_map/ppermute | solution.py:50
  16.5 5.9 %collective-permute-start.4 = (bf16[288,256]{1,0:T(8,128)(2,1)S(1)}, bf16[288,256]{1,0:T(8,128)(2,1)S(1)}, u32[]{:S(2)}, u32[]{:S(2)}) collective-permute-start(bf16[288,256]{1,0:T(8,128)(2,1)S(1)} %collective-permute-done.2), channel_id=1, source_target_pairs={{0,3},{1,2},{2,1},{3,0},{4,7},{5,6},{6,5},{7,4},{8,11},{9,10},{10,... | collective-permute-start | bytes 442376 | tf_op jit(solution)/shard_map/ppermute | solution.py:50
  26.1 4.2 %collective-permute-start.9 = (bf16[2,32,128]{2,1,0:T(8,128)(2,1)S(1)}, bf16[2,32,128]{2,1,0:T(8,128)(2,1)S(1)}, u32[]{:S(2)}, u32[]{:S(2)}) collective-permute-start(bf16[2,32,128]{2,1,0:T(8,128)(2,1)S(1)} %get-tuple-element.98), channel_id=1, source_target_pairs={{0,5},{1,2},{2,1},{3,6},{4,7},{5,0},{6,3},{7,4},{8,11},{9,12},{10,... | collective-permute-start | bytes 49160 | tf_op jit(solution)/shard_map/ppermute | solution.py:50
  26.3 4.1 %collective-permute-start.10 = (bf16[2,32,128]{2,1,0:T(8,128)(2,1)S(1)}, bf16[2,32,128]{2,1,0:T(8,128)(2,1)S(1)}, u32[]{:S(2)}, u32[]{:S(2)}) collective-permute-start(bf16[2,32,128]{2,1,0:T(8,128)(2,1)S(1)} %get-tuple-element.99), channel_id=1, source_target_pairs={{0,9},{1,4},{2,7},{3,10},{4,1},{5,12},{6,15},{7,2},{8,13},{9,0},{1... | collective-permute-start | bytes 49160 | tf_op jit(solution)/shard_map/ppermute | solution.py:50
  28.4 5.5 %collective-permute-start.11 = (bf16[2,32,128]{2,1,0:T(8,128)(2,1)S(1)}, bf16[2,32,128]{2,1,0:T(8,128)(2,1)S(1)}, u32[]{:S(2)}, u32[]{:S(2)}) collective-permute-start(bf16[2,32,128]{2,1,0:T(8,128)(2,1)S(1)} %get-tuple-element.100), channel_id=1, source_target_pairs={{0,12},{1,7},{2,4},{3,15},{4,2},{5,9},{6,10},{7,1},{8,14},{9,5},{1... | collective-permute-start | bytes 49160 | tf_op jit(solution)/shard_map/ppermute | solution.py:50
  34.0 3.2 %collective-permute-start.12 = (bf16[2,32,128]{2,1,0:T(8,128)(2,1)S(1)}, bf16[2,32,128]{2,1,0:T(8,128)(2,1)S(1)}, u32[]{:S(2)}, u32[]{:S(2)}) collective-permute-start(bf16[2,32,128]{2,1,0:T(8,128)(2,1)S(1)} %get-tuple-element.102), channel_id=1, source_target_pairs={{0,3},{1,8},{2,11},{3,0},{4,13},{5,6},{6,5},{7,14},{8,1},{9,10},{1... | collective-permute-start | bytes 49160 | tf_op jit(solution)/shard_map/ppermute | solution.py:50
  37.2 4.2 %collective-permute-start.13 = (bf16[2,32,128]{2,1,0:T(8,128)(2,1)S(1)}, bf16[2,32,128]{2,1,0:T(8,128)(2,1)S(1)}, u32[]{:S(2)}, u32[]{:S(2)}) collective-permute-start(bf16[2,32,128]{2,1,0:T(8,128)(2,1)S(1)} %shard_map.79.refs_0_), channel_id=1, source_target_pairs={{0,5},{1,2},{2,1},{3,6},{4,7},{5,0},{6,3},{7,4},{8,11},{9,12},{10,... | collective-permute-start | bytes 49160 | tf_op jit(solution)/shard_map/ppermute | solution.py:50
  37.3 4.1 %collective-permute-start.14 = (bf16[2,32,128]{2,1,0:T(8,128)(2,1)S(1)}, bf16[2,32,128]{2,1,0:T(8,128)(2,1)S(1)}, u32[]{:S(2)}, u32[]{:S(2)}) collective-permute-start(bf16[2,32,128]{2,1,0:T(8,128)(2,1)S(1)} %shard_map.79.refs_0_), channel_id=1, source_target_pairs={{0,9},{1,4},{2,7},{3,10},{4,1},{5,12},{6,15},{7,2},{8,13},{9,0},{1... | collective-permute-start | bytes 49160 | tf_op jit(solution)/shard_map/ppermute | solution.py:50
  39.5 5.5 %collective-permute-start.15 = (bf16[2,32,128]{2,1,0:T(8,128)(2,1)S(1)}, bf16[2,32,128]{2,1,0:T(8,128)(2,1)S(1)}, u32[]{:S(2)}, u32[]{:S(2)}) collective-permute-start(bf16[2,32,128]{2,1,0:T(8,128)(2,1)S(1)} %shard_map.79.refs_0_), channel_id=1, source_target_pairs={{0,12},{1,7},{2,4},{3,15},{4,2},{5,9},{6,10},{7,1},{8,14},{9,5},{1... | collective-permute-start | bytes 49160 | tf_op jit(solution)/shard_map/ppermute | solution.py:50
  49.2 4.2 %collective-permute-start.18 = (bf16[2,32,128]{2,1,0:T(8,128)(2,1)S(1)}, bf16[2,32,128]{2,1,0:T(8,128)(2,1)S(1)}, u32[]{:S(2)}, u32[]{:S(2)}) collective-permute-start(bf16[2,32,128]{2,1,0:T(8,128)(2,1)S(1)} %get-tuple-element.107), channel_id=1, source_target_pairs={{0,5},{1,2},{2,1},{3,6},{4,7},{5,0},{6,3},{7,4},{8,11},{9,12},{10,... | collective-permute-start | bytes 49160 | tf_op jit(solution)/shard_map/ppermute | solution.py:50
  49.3 4.1 %collective-permute-start.19 = (bf16[2,32,128]{2,1,0:T(8,128)(2,1)S(1)}, bf16[2,32,128]{2,1,0:T(8,128)(2,1)S(1)}, u32[]{:S(2)}, u32[]{:S(2)}) collective-permute-start(bf16[2,32,128]{2,1,0:T(8,128)(2,1)S(1)} %get-tuple-element.108), channel_id=1, source_target_pairs={{0,9},{1,4},{2,7},{3,10},{4,1},{5,12},{6,15},{7,2},{8,13},{9,0},{1... | collective-permute-start | bytes 49160 | tf_op jit(solution)/shard_map/ppermute | solution.py:50
  51.4 5.5 %collective-permute-start.20 = (bf16[2,32,128]{2,1,0:T(8,128)(2,1)S(1)}, bf16[2,32,128]{2,1,0:T(8,128)(2,1)S(1)}, u32[]{:S(2)}, u32[]{:S(2)}) collective-permute-start(bf16[2,32,128]{2,1,0:T(8,128)(2,1)S(1)} %get-tuple-element.109), channel_id=1, source_target_pairs={{0,12},{1,7},{2,4},{3,15},{4,2},{5,9},{6,10},{7,1},{8,14},{9,5},{1... | collective-permute-start | bytes 49160 | tf_op jit(solution)/shard_map/ppermute | solution.py:50
  60.3 4.2 %collective-permute-start.22 = (bf16[2,32,128]{2,1,0:T(8,128)(2,1)S(1)}, bf16[2,32,128]{2,1,0:T(8,128)(2,1)S(1)}, u32[]{:S(2)}, u32[]{:S(2)}) collective-permute-start(bf16[2,32,128]{2,1,0:T(8,128)(2,1)S(1)} %shard_map.86.refs_0_), channel_id=1, source_target_pairs={{0,5},{1,2},{2,1},{3,6},{4,7},{5,0},{6,3},{7,4},{8,11},{9,12},{10,... | collective-permute-start | bytes 49160 | tf_op jit(solution)/shard_map/ppermute | solution.py:50
  60.3 4.1 %collective-permute-start.23 = (bf16[2,32,128]{2,1,0:T(8,128)(2,1)S(1)}, bf16[2,32,128]{2,1,0:T(8,128)(2,1)S(1)}, u32[]{:S(2)}, u32[]{:S(2)}) collective-permute-start(bf16[2,32,128]{2,1,0:T(8,128)(2,1)S(1)} %shard_map.86.refs_0_), channel_id=1, source_target_pairs={{0,9},{1,4},{2,7},{3,10},{4,1},{5,12},{6,15},{7,2},{8,13},{9,0},{1... | collective-permute-start | bytes 49160 | tf_op jit(solution)/shard_map/ppermute | solution.py:50
  62.5 5.5 %collective-permute-start.24 = (bf16[2,32,128]{2,1,0:T(8,128)(2,1)S(1)}, bf16[2,32,128]{2,1,0:T(8,128)(2,1)S(1)}, u32[]{:S(2)}, u32[]{:S(2)}) collective-permute-start(bf16[2,32,128]{2,1,0:T(8,128)(2,1)S(1)} %shard_map.86.refs_0_), channel_id=1, source_target_pairs={{0,12},{1,7},{2,4},{3,15},{4,2},{5,9},{6,10},{7,1},{8,14},{9,5},{1... | collective-permute-start | bytes 49160 | tf_op jit(solution)/shard_map/ppermute | solution.py:50
  72.2 4.2 %collective-permute-start.27 = (bf16[2,32,128]{2,1,0:T(8,128)(2,1)S(1)}, bf16[2,32,128]{2,1,0:T(8,128)(2,1)S(1)}, u32[]{:S(2)}, u32[]{:S(2)}) collective-permute-start(bf16[2,32,128]{2,1,0:T(8,128)(2,1)S(1)} %get-tuple-element.115), channel_id=1, source_target_pairs={{0,5},{1,2},{2,1},{3,6},{4,7},{5,0},{6,3},{7,4},{8,11},{9,12},{10,... | collective-permute-start | bytes 49160 | tf_op jit(solution)/shard_map/ppermute | solution.py:50
  72.3 4.1 %collective-permute-start.28 = (bf16[2,32,128]{2,1,0:T(8,128)(2,1)S(1)}, bf16[2,32,128]{2,1,0:T(8,128)(2,1)S(1)}, u32[]{:S(2)}, u32[]{:S(2)}) collective-permute-start(bf16[2,32,128]{2,1,0:T(8,128)(2,1)S(1)} %get-tuple-element.116), channel_id=1, source_target_pairs={{0,9},{1,4},{2,7},{3,10},{4,1},{5,12},{6,15},{7,2},{8,13},{9,0},{1... | collective-permute-start | bytes 49160 | tf_op jit(solution)/shard_map/ppermute | solution.py:50
  74.5 5.5 %collective-permute-start.29 = (bf16[2,32,128]{2,1,0:T(8,128)(2,1)S(1)}, bf16[2,32,128]{2,1,0:T(8,128)(2,1)S(1)}, u32[]{:S(2)}, u32[]{:S(2)}) collective-permute-start(bf16[2,32,128]{2,1,0:T(8,128)(2,1)S(1)} %get-tuple-element.117), channel_id=1, source_target_pairs={{0,12},{1,7},{2,4},{3,15},{4,2},{5,9},{6,10},{7,1},{8,14},{9,5},{1... | collective-permute-start | bytes 49160 | tf_op jit(solution)/shard_map/ppermute | solution.py:50
  83.3 4.2 %collective-permute-start.31 = (bf16[2,32,128]{2,1,0:T(8,128)(2,1)S(1)}, bf16[2,32,128]{2,1,0:T(8,128)(2,1)S(1)}, u32[]{:S(2)}, u32[]{:S(2)}) collective-permute-start(bf16[2,32,128]{2,1,0:T(8,128)(2,1)S(1)} %get-tuple-element.123.refs_0_), channel_id=1, source_target_pairs={{0,5},{1,2},{2,1},{3,6},{4,7},{5,0},{6,3},{7,4},{8,11},{9,12},{10,... | collective-permute-start | bytes 49160 | tf_op jit(solution)/shard_map/ppermute | solution.py:50
  83.4 4.1 %collective-permute-start.32 = (bf16[2,32,128]{2,1,0:T(8,128)(2,1)S(1)}, bf16[2,32,128]{2,1,0:T(8,128)(2,1)S(1)}, u32[]{:S(2)}, u32[]{:S(2)}) collective-permute-start(bf16[2,32,128]{2,1,0:T(8,128)(2,1)S(1)} %get-tuple-element.123.refs_0_), channel_id=1, source_target_pairs={{0,9},{1,4},{2,7},{3,10},{4,1},{5,12},{6,15},{7,2},{8,13},{9,0},{1... | collective-permute-start | bytes 49160 | tf_op jit(solution)/shard_map/ppermute | solution.py:50
  85.6 5.5 %collective-permute-start.33 = (bf16[2,32,128]{2,1,0:T(8,128)(2,1)S(1)}, bf16[2,32,128]{2,1,0:T(8,128)(2,1)S(1)}, u32[]{:S(2)}, u32[]{:S(2)}) collective-permute-start(bf16[2,32,128]{2,1,0:T(8,128)(2,1)S(1)} %get-tuple-element.123.refs_0_), channel_id=1, source_target_pairs={{0,12},{1,7},{2,4},{3,15},{4,2},{5,9},{6,10},{7,1},{8,14},{9,5},{1... | collective-permute-start | bytes 49160 | tf_op jit(solution)/shard_map/ppermute | solution.py:50
  (13 other events, 29.4 us)

commit v15 on v12

--- a/solution.py
+++ b/solution.py
@@ -127,31 +127,33 @@
     ])
 
 
-def fill_body(unit_ref, held_ref, kernel_ref, sums_ref, *, tgt_rows):
+def fill_body(own_ref, other_ref, held_ref, *out_refs, tgt_rows):
     rows = tgt_rows + EXTRA
-    cand_rows = unit_ref.shape[0]
-    per = TILE // tgt_rows
-    for col in range(0, kernel_ref.shape[1], TILE):
+    columns = out_refs[0].shape[1]
+    per = min(TILE, columns) // tgt_rows
+    tile = per * tgt_rows
+    for col in range(0, columns, tile):
         first = col // tgt_rows
         block = jnp.concatenate(
             [held_ref[pl.ds((first + s) * rows, tgt_rows), :] for s in range(per)]
         )
         tgt_unit = unit_rows(block)
-        for row in range(0, cand_rows, TILE):
-            scores = lax.dot_general(
-                unit_ref[row : row + TILE, :],
-                tgt_unit,
-                (((1,), (1,)), ((), ())),
-                preferred_element_type=F32,
-            )
-            tile = jnp.exp(INVERSE_TEMP * scores)
-            kernel_ref[row : row + TILE, col : col + TILE] = tile.astype(BF16)
-            sums = tile[:, :LANES]
-            for lane in range(LANES, TILE, LANES):
-                sums += tile[:, lane : lane + LANES]
-            if col:
-                sums += sums_ref[row : row + TILE, :]
-            sums_ref[row : row + TILE, :] = sums
+        for cand_ref, kernel_ref, sums_ref in zip((own_ref, other_ref), out_refs, out_refs[2:]):
+            for row in range(0, cand_ref.shape[0], TILE):
+                scores = lax.dot_general(
+                    cand_ref[row : row + TILE, :],
+                    tgt_unit,
+                    (((1,), (1,)), ((), ())),
+                    preferred_element_type=F32,
+                )
+                found = jnp.exp(INVERSE_TEMP * scores)
+                kernel_ref[row : row + TILE, col : col + tile] = found.astype(BF16)
+                sums = found[:, :LANES]
+                for lane in range(LANES, tile, LANES):
+                    sums += found[:, lane : lane + LANES]
+                if col:
+                    sums += sums_ref[row : row + TILE, :]
+                sums_ref[row : row + TILE, :] = sums
 
 
 def image_of(kernels, scale_ref):
@@ -167,14 +169,18 @@
     return image.T
 
 
-def put_column(scale_ub, kernels, out_ref):
-    width = out_ref.shape[2]
+def put_column(scale_ub, kernels, added, out_refs):
+    width = out_refs[0].shape[2]
     first = 0
     for kernel_ref in kernels:
         part = jnp.dot(scale_ub, kernel_ref[...], preferred_element_type=F32)
         slots = kernel_ref.shape[1] // width
         for s in range(slots):
-            out_ref[first + s] = part[:, s * width : (s + 1) * width].astype(out_ref.dtype)
+            piece = part[:, s * width : (s + 1) * width]
+            if added is not None:
+                piece += added[first + s]
+            for out_ref in out_refs:
+                out_ref[first + s] = piece.astype(out_ref.dtype)
         first += slots
 
 
@@ -185,60 +191,78 @@
             yield ref[pl.ds(s * rows + tgt_rows, EXTRA), :].astype(F32)
 
 
-def target_body(*refs):
+def sums_body(*refs, parts, tgt_rows):
+    *refs, out_ref = refs
+    each = (out_ref.shape[0] - 8) // 2
+    for place in range(2):
+        total = sum(ref[...] for ref in refs[place * parts : (place + 1) * parts])
+        row = jnp.sum(total.T, axis=0, keepdims=True)
+        for i in range(each):
+            out_ref[pl.ds(place * each + i, 1), :] = row[:, i * LANES : (i + 1) * LANES]
+    counts = jnp.zeros((EXTRA, LANES), F32)
+    labels = jnp.zeros((LANES, tgt_rows), F32)
+    for extra in extras(refs[2 * parts :], tgt_rows):
+        counts += extra[:, LANES:]
+        labels += hot(extra[:1, :LANES].astype(jnp.int32), LANES)
+    out_ref[pl.ds(2 * each, 8), :] = counts[:8] + counts[1:9]
+    out_ref[pl.ds(2 * each + 1, 1), :] = jnp.sum(labels.T, axis=0, keepdims=True)
+
+
+def count_of(place, mine_ref, got_ref):
+    row = mine_ref.shape[0] - 8 + place
+    count = mine_ref[pl.ds(row, 1), :] + got_ref[pl.ds(row, 1), :]
+    return jnp.broadcast_to(count, (LANES, LANES)).T[:CLASSES, :1]
+
+
+def first_body(own_weight, other_weight, mine_ref, got_ref, *refs, candidates):
+    *kernels, own_marg, other_marg, column_ref, sent_ref = refs
+    parts = len(kernels) // 2
+    each = (mine_ref.shape[0] - 8) // 2
+    total = candidates + 3.0 * count_of(0, mine_ref, got_ref)
+    for place, (weight_ref, marg_ref) in enumerate(
+        ((own_weight, own_marg), (other_weight, other_marg))
+    ):
+        rows = [
+            mine_ref[pl.ds(place * each + i, 1), :] + got_ref[pl.ds((1 - place) * each + i, 1), :]
+            for i in range(each)
+        ]
+        marg = weight_ref[...] / total
+        marg_ref[...] = marg
+        scale_ub = (marg / jnp.concatenate(rows, axis=1)).astype(BF16)
+        if place == 0:
+            put_column(scale_ub, kernels[:parts], None, (column_ref,))
+        else:
+            put_column(scale_ub, kernels[parts:], column_ref, (column_ref, sent_ref))
+
+
+def target_body(mine_ref, got_ref, *refs, targets):
     *held_refs, marg_ref = refs
-    slots, _, tgt_rows = marg_ref.shape
-    total = jnp.zeros((CLASSES, tgt_rows), F32)
-    for s, extra in enumerate(extras(held_refs, tgt_rows)):
-        weight = 1.0 + 3.0 * hot(extra[:1, :LANES].astype(jnp.int32))
-        total += weight
-        if s < slots:
-            marg_ref[s] = weight
-    total = jnp.sum(total, axis=1, keepdims=True)
-    for s in range(slots):
-        marg_ref[s] = marg_ref[s] / total
-
-
-def first_body(weight_ref, *refs, parts):
-    refs, (marg_ref, scale_ref, column_ref) = refs[:-3], refs[-3:]
-    kernels, sums_refs, held_refs = refs[:parts], refs[parts : 3 * parts], refs[3 * parts :]
-    counts = jnp.zeros((EXTRA, LANES), F32)
-    for extra in extras(held_refs, column_ref.shape[2]):
-        counts += extra[:, LANES:]
-    count = jnp.broadcast_to(counts[:1] + counts[1:2], (LANES, LANES)).T[:CLASSES, :1]
-    candidates = weight_ref.shape[1] * 2 * column_ref.shape[0]
-    marg = weight_ref[...] / (candidates + 3.0 * count)
-    marg_ref[...] = marg
-    sums = sum(ref[...] for ref in sums_refs)
-    image = jnp.sum(sums.T, axis=0, keepdims=True)
-    scale_ub = (marg / image).astype(BF16)
-    scale_ref[...] = scale_ub
-    put_column(scale_ub, kernels, column_ref)
-
-
-def column_body(scale_ref, *refs):
-    put_column(scale_ref[...], refs[:-1], refs[-1])
+    total = targets + 3.0 * count_of(1, mine_ref, got_ref)
+    for s, extra in enumerate(extras(held_refs, marg_ref.shape[2])):
+        marg_ref[s] = (1.0 + 3.0 * hot(extra[:1, :LANES].astype(jnp.int32))) / total
 
 
 def image_body(scale_ref, *refs):
     refs[-1][...] = image_of(refs[:-1], scale_ref)
 
 
-def step_body(scale_ref, image_ref, marg_ref, *refs, parts):
-    kernels, (rounded_ref, column_ref, *out_refs) = refs[:parts], refs[parts:]
-    image = image_ref[...] + image_of(kernels, scale_ref)
-    scale_u = marg_ref[...] / image
+def own_body(image_ref, got_ref, marg_ref, *refs, parts):
+    kernels, (column_ref, *out_refs) = refs[:parts], refs[parts:]
+    scale_u = marg_ref[...] / (image_ref[...] + got_ref[...])
     for out_ref in out_refs:
         out_ref[...] = scale_u
-    rounded_ref[...] = scale_u.astype(BF16)
-    put_column(scale_u.astype(BF16), kernels, column_ref)
-
-
-def last_body(scale_ref, image_ref, u_ref, scale_v_ref, *refs, candidates):
-    kernels, (mass_ref, own_ref) = refs[:-2], refs[-2:]
+    put_column(scale_u.astype(BF16), kernels, None, (column_ref,))
+
+
+def other_body(image_ref, got_ref, marg_ref, added_ref, *refs):
+    *kernels, column_ref, sent_ref = refs
+    scale_u = marg_ref[...] / (image_ref[...] + got_ref[...])
+    put_column(scale_u.astype(BF16), kernels, added_ref, (column_ref, sent_ref))
+
+
+def last_body(image_ref, got_ref, u_ref, scale_v_ref, mass_ref, own_ref, *, candidates):
     own_ref[...] = scale_v_ref[0]
-    image = image_ref[...] + image_of(kernels, scale_ref)
-    mass_ref[...] = candidates * u_ref[...] * image
+    mass_ref[...] = candidates * u_ref[...] * (image_ref[...] + got_ref[...])
 
 
 def slot_of(slot, flips, slots):
@@ -281,63 +305,70 @@
     slots = devices // 2
     cand_rows, width = cand_embed.shape
     tgt_rows = tgt_embed.shape[0]
+    label_rows = cand_labels.reshape(cand_rows // LANES, LANES)
     cand_labels = cand_labels.reshape(1, cand_rows)
     block = (slots, CLASSES, tgt_rows)
     image_type = ((CLASSES, cand_rows), F32)
-    rounded_type = ((CLASSES, cand_rows), BF16)
     half_flops = 2 * cand_rows * slots * tgt_rows * 128
 
     def fill(held):
         columns = held.shape[0] // (tgt_rows + EXTRA) * tgt_rows
         return call(
             functools.partial(fill_body, tgt_rows=tgt_rows),
-            [((cand_rows, columns), BF16), ((cand_rows, LANES), F32)],
-            cand_unit, held, flops=4 * 2 * cand_rows * columns * 128,
+            [((cand_rows, columns), BF16)] * 2 + [((cand_rows, LANES), F32)] * 2,
+            cand_unit, other_unit, held, flops=8 * 2 * cand_rows * columns * 128,
         )
 
     held = piece = pack(tgt_embed, tgt_labels.reshape(1, tgt_rows), cand_labels)
     cand_unit = unit_rows(cand_embed)
     weight = 1.0 + 3.0 * hot(cand_labels)
     across = []
+    other_unit = None
     for bits in list(zip(slot_bits(0, top), slot_bits(1, top)))[:-1]:
         turned = exchange(held, *[1 << bit for bit in bits])
         across.append(exchange(piece, 2))
-        piece, across, cand_unit, weight = lax.optimization_barrier(
-            (turned, across, cand_unit, weight)
+        piece, across, cand_unit, weight, other_unit = lax.optimization_barrier(
+            (turned, across, cand_unit, weight, other_unit)
         )
         held = jnp.concatenate([held, piece])
+        if other_unit is None:
+            other_unit = swap(cand_unit), swap(label_rows)
     later = exchange(piece, 2)
+    other_unit, other_labels = other_unit
+    other_weight = 1.0 + 3.0 * hot(other_labels.reshape(1, cand_rows))
     near = [held, jnp.concatenate(across)]
-    far = [swap(part) for part in near]
-    filled = [[fill(part) for part in side] for side in (near, far)]
-    later, filled = lax.optimization_barrier((later, filled))
+    filled = [fill(part) for part in near]
+    later, filled, other_weight = lax.optimization_barrier((later, filled, other_weight))
     near.append(later)
-    far.append(swap(later))
-    for side, parts in zip((near, far), filled):
-        parts.append(fill(side[-1]))
-    near_kernels, near_sums = zip(*filled[0])
-    far_kernels, far_sums = zip(*filled[1])
-
-    cand_marg, scale_ub, far_column = call(
-        functools.partial(first_body, parts=len(near)),
-        [image_type, rounded_type, (block, BF16)],
-        weight, *far_kernels, *near_sums, *far_sums, *near, *far, flops=half_flops,
+    filled.append(fill(later))
+    own_kernels, other_kernels, own_sums, other_sums = zip(*filled)
+
+    (mine,) = call(
+        functools.partial(sums_body, parts=len(near), tgt_rows=tgt_rows),
+        [((2 * cand_rows // LANES + 8, LANES), F32)], *own_sums, *other_sums, *near,
     )
-    (tgt_marg,) = call(target_body, [(block, F32)], *near, *far, flops=half_flops)
+    got = swap(mine)
+    own_marg, other_marg, column, sent = call(
+        functools.partial(first_body, candidates=float(cand_rows * devices)),
+        [image_type, image_type, (block, F32), (block, BF16)],
+        weight, other_weight, mine, got, *own_kernels, *other_kernels, flops=2 * half_flops,
+    )
+    (tgt_marg,) = call(
+        functools.partial(target_body, targets=float(tgt_rows * devices)),
+        [(block, F32)], mine, got, *near,
+    )
     for step in range(ITERS):
         last = step == ITERS - 1
         if step:
-            scale_ub, far_column, *scale_u = call(
-                functools.partial(step_body, parts=len(far)),
-                [rounded_type, (block, BF16)] + [image_type] * last,
-                far_vb, image, cand_marg, *far_kernels, flops=2 * half_flops,
+            column, *scale_u = call(
+                functools.partial(own_body, parts=len(near)),
+                [(block, F32)] + [image_type] * last,
+                own_image, own_got, own_marg, *own_kernels, flops=half_flops,
             )
-        got = swap(far_column)
-        (column,) = call(
-            column_body, [(block, F32)], scale_ub, *near_kernels, flops=half_flops
-        )
-        column = column + got.astype(F32)
-        sent = column.astype(BF16)
+            column, sent = call(
+                other_body, [(block, F32), (block, BF16)],
+                other_image, other_got, other_marg, column, *other_kernels, flops=half_flops,
+            )
         order = list(zip(rounds(0, top), rounds(1, top)))
         for place, pair in enumerate(order):
             flips = list(zip(*[flips_of(bits) for bits in pair]))
@@ -355,10 +386,15 @@
             [(block, BF16)] + [(block, F32)] * last,
             column, tgt_marg, *found,
         )
-        far_vb = swap(scale_vb)
-        (image,) = call(image_body, [image_type], scale_vb, *near_kernels, flops=half_flops)
+        (other_image,) = call(
+            image_body, [image_type], scale_vb, *other_kernels, flops=half_flops
+        )
+        own_got = swap(other_image)
+        (own_image,) = call(image_body, [image_type], scale_vb, *own_kernels, flops=half_flops)
+        if not last:
+            other_got = swap(own_image)
     space = pl.BlockSpec(memory_space=pltpu.VMEM)
-    args = [far_vb, image, *scale_u, *scale_v, *far_kernels]
+    args = [own_image, own_got, *scale_u, *scale_v]
     mass, tgt_scaling = pl.pallas_call(
         functools.partial(last_body, candidates=float(cand_rows * devices)),
         out_shape=[

time: 73.7 us -> 70.8 us (0.961)
  waiting for transfers between devices: 33.3 us -> 28.2 us
  starting transfers between devices: 23.8 us -> 27.2 us
  Pallas kernels: 12.8 us -> 11.7 us
    ppermute x17, waiting for transfers between devices: 29 us -> 24.8 us  [exchange(): return lax.ppermute(block, 'row', pairs)]
    ppermute x9 -> x8, starting transfers between devices: 1.47 us -> 4.25 us  [swap(): return lax.ppermute(block, 'row', [(d, d ^ 1) for d in range(devices)])]
    ppermute x9 -> x8, waiting for transfers between devices: 4.32 us -> 3.37 us  [swap(): return lax.ppermute(block, 'row', [(d, d ^ 1) for d in range(devices)])]
  transfers between devices with their start and end apart: 26 -> 25, of which waited for: 20 -> 20; matrix products, arithmetic and copies ran while one was open for 3% -> 3% of each run, Pallas kernels for 8% -> 7%
where the time goes in v15:
time: 70.8 us; the launch traced here: 70.6 us
  waiting for transfers between devices  28.2 us (40%)
  starting transfers between devices  27.2 us (38%)
  Pallas kernels  11.7 us (17%)
  other arithmetic  2.21 us (3%)
  between operations  0.83 us (1%)
    ppermute x17, waiting for transfers between devices, exchange(): return lax.ppermute(block, 'row', pairs)  24.8 us
    ppermute x17, starting transfers between devices, exchange(): return lax.ppermute(block, 'row', pairs)  23 us
    pallas_call x22, Pallas kernels, call(): pl.pallas_call(body, out_shape=[pltpu.VMEM(shape, dtype) for shape, dtype...  10 us
    ppermute x8, starting transfers between devices, swap(): return lax.ppermute(block, 'row', [(d, d ^ 1) for d in range(devices)])  4.25 us
    ppermute x8, waiting for transfers between devices, swap(): return lax.ppermute(block, 'row', [(d, d ^ 1) for d in range(devices)])  3.37 us
  transfers between devices with their start and end apart: 25, of which 20 were waited for; matrix products, arithmetic and copies ran while one was open for 3% of the time, Pallas kernels for 7%

profile of v15, /device:TPU:0, one launch (start us, length us, event | category | flops | bytes accessed | tf_op | source)
XLA Modules:
  0.0 70.6 jit_solution(15385252254970520913)
XLA Ops:
  0.6 1.0 %shard_map.67 = bf16[144,256]{1,0:T(8,128)(2,1)S(1)} custom-call(bf16[128,256]{1,0:T(8,128)(2,1)} %embed_hbm.1, s32[1,128]{1,0:T(1,128)} %bitcast.7, s32[1,1024]{1,0:T(1,128)} %bitcast.4), custom_call_target="tpu_custom_call" | custom-call | tf_op jit(solution)/shard_map/pallas_call | solution.py:113
  1.6 2.5 %collective-permute-start.1 = (bf16[144,256]{1,0:T(8,128)(2,1)S(1)}, bf16[144,256]{1,0:T(8,128)(2,1)S(1)}, u32[]{:S(2)}, u32[]{:S(2)}) collective-permute-start(bf16[144,256]{1,0:T(8,128)(2,1)S(1)} %shard_map.67), channel_id=1, source_target_pairs={{0,3},{1,2},{2,1},{3,0},{4,7},{5,6},{6,5},{7,4},{8,11},{9,10},{10,... | collective-permute-start | bytes 221192 | tf_op jit(solution)/shard_map/ppermute | solution.py:51
  4.1 2.9 %collective-permute-start = (bf16[144,256]{1,0:T(8,128)(2,1)S(1)}, bf16[144,256]{1,0:T(8,128)(2,1)S(1)}, u32[]{:S(2)}, u32[]{:S(2)}) collective-permute-start(bf16[144,256]{1,0:T(8,128)(2,1)S(1)} %shard_map.67), channel_id=1, source_target_pairs={{0,9},{1,4},{2,7},{3,10},{4,1},{5,12},{6,15},{7,2},{8,13},{9,0},{1... | collective-permute-start | bytes 221192 | tf_op jit(solution)/shard_map/ppermute | solution.py:51
  6.9 1.3 %fusion = f32[1024]{0:T(1024)S(1)} fusion(bf16[1024,256]{1,0:T(8,128)(2,1)} %param.4), kind=kLoop, calls=%fused_computation.2 | loop fusion | flops 785408 | bytes 528384 | tf_op jit(solution)/shard_map/reduce_sum | solution.py:74
  9.3 1.5 %collective-permute-start.2 = (bf16[288,256]{1,0:T(8,128)(2,1)S(1)}, bf16[288,256]{1,0:T(8,128)(2,1)S(1)}, u32[]{:S(2)}, u32[]{:S(2)}) collective-permute-start(bf16[288,256]{1,0:T(8,128)(2,1)S(1)} %pad_maximum_fusion.1), channel_id=1, source_target_pairs={{0,5},{1,8},{2,11},{3,6},{4,13},{5,0},{6,3},{7,14},{8,1},{9,12},{1... | collective-permute-start | bytes 442376 | tf_op jit(solution)/shard_map/ppermute | solution.py:51
  11.1 1.8 %collective-permute-start.5 = (s32[8,128]{1,0:T(8,128)S(1)}, s32[8,128]{1,0:T(8,128)S(1)}, u32[]{:S(2)}, u32[]{:S(2)}) collective-permute-start(s32[8,128]{1,0:T(8,128)S(1)} %bitcast.5), channel_id=1, source_target_pairs={{0,1},{1,0},{2,3},{3,2},{4,5},{5,4},{6,7},{7,6},{8,9},{9,8},{10,11... | collective-permute-start | bytes 12296 | tf_op jit(solution)/shard_map/ppermute | solution.py:56
  14.9 1.0 %collective-permute-start.6 = (bf16[288,256]{1,0:T(8,128)(2,1)S(1)}, bf16[288,256]{1,0:T(8,128)(2,1)S(1)}, u32[]{:S(2)}, u32[]{:S(2)}) collective-permute-start(bf16[288,256]{1,0:T(8,128)(2,1)S(1)} %collective-permute-done.2), channel_id=1, source_target_pairs={{0,3},{1,2},{2,1},{3,0},{4,7},{5,6},{6,5},{7,4},{8,11},{9,10},{10,... | collective-permute-start | bytes 442376 | tf_op jit(solution)/shard_map/ppermute | solution.py:51
  16.6 1.0 %shard_map.68 = (bf16[1024,512]{1,0:T(8,128)(2,1)S(1)}, bf16[1024,512]{1,0:T(8,128)(2,1)S(1)}, f32[1024,128]{1,0:T(8,128)S(1)}, f32[1024,128]{1,0:T(8,128)S(1)}) custom-call(bf16[1024,256]{1,0:T(8,128)(2,1)S(1)} %fusion.2.own_ref, bf16[1024,256]{1,0:T(8,128)(2,1)S(1)} %collective-permute-done.4.other_ref, ...), custom_call_target="tpu_custom_call" | custom-call | flops 1073741824 | bytes 1343488 | tf_op jit(solution)/shard_map/pallas_call | solution.py:62
  17.6 2.5 %collective-permute-done.6.held_ref.refs_8_.refs_2_ = bf16[288,256]{1,0:T(8,128)(2,1)S(1)} collective-permute-done((bf16[288,256]{1,0:T(8,128)(2,1)S(1)}, bf16[288,256]{1,0:T(8,128)(2,1)S(1)}, u32[]{:S(2)}, u32[]{:S(2)}) %collective-permute-start.6) | collective-permute-done | bytes 147488 | tf_op jit(solution)/shard_map/ppermute | solution.py:51
  21.0 1.0 %collective-permute-start.7 = (f32[24,128]{1,0:T(8,128)S(1)}, f32[24,128]{1,0:T(8,128)S(1)}, u32[]{:S(2)}, u32[]{:S(2)}) collective-permute-start(f32[24,128]{1,0:T(8,128)S(1)} %shard_map.71.mine_ref), channel_id=1, source_target_pairs={{0,1},{1,0},{2,3},{3,2},{4,5},{5,4},{6,7},{7,6},{8,9},{9,8},{10,11... | collective-permute-start | bytes 36872 | tf_op jit(solution)/shard_map/ppermute | solution.py:56
  22.9 0.9 %shard_map.72 = (f32[32,1024]{1,0:T(8,128)S(1)}, f32[32,1024]{1,0:T(8,128)S(1)}, f32[8,32,128]{2,1,0:T(8,128)S(1)}, bf16[8,32,128]{2,1,0:T(8,128)(2,1)S(1)}) custom-call(f32[32,1024]{1,0:T(8,128)S(1)} %select_add_fusion.1.own_weight, f32[32,1024]{1,0:T(8,128)S(1)} %select_add_fusion.other_weight, f32[24,128]{1,0:T(8,128)S(1)} %shard_map.71.mine_ref, ...), custom_call_target="tpu_custom_call" | custom-call | flops 536870912 | bytes 4481024 | tf_op jit(solution)/shard_map/pallas_call | solution.py:62
  23.8 3.7 %collective-permute-start.10 = (bf16[8,32,128]{2,1,0:T(8,128)(2,1)S(1)}, bf16[8,32,128]{2,1,0:T(8,128)(2,1)S(1)}, u32[]{:S(2)}, u32[]{:S(2)}) collective-permute-start(bf16[8,32,128]{2,1,0:T(8,128)(2,1)S(1)} %get-tuple-element.92), channel_id=1, source_target_pairs={{0,12},{1,7},{2,4},{3,15},{4,2},{5,9},{6,10},{7,1},{8,14},{9,5},{1... | collective-permute-start | bytes 196616 | tf_op jit(solution)/shard_map/ppermute | solution.py:51
  28.1 2.5 %collective-permute-done.10.refs_2_ = bf16[8,32,128]{2,1,0:T(8,128)(2,1)S(1)} collective-permute-done((bf16[8,32,128]{2,1,0:T(8,128)(2,1)S(1)}, bf16[8,32,128]{2,1,0:T(8,128)(2,1)S(1)}, u32[]{:S(2)}, u32[]{:S(2)}) %collective-permute-start.10) | collective-permute-done | bytes 65568 | tf_op jit(solution)/shard_map/ppermute | solution.py:51
  30.6 2.3 %collective-permute-done.9.refs_1_ = bf16[8,32,128]{2,1,0:T(8,128)(2,1)S(1)} collective-permute-done((bf16[8,32,128]{2,1,0:T(8,128)(2,1)S(1)}, bf16[8,32,128]{2,1,0:T(8,128)(2,1)S(1)}, u32[]{:S(2)}, u32[]{:S(2)}) %collective-permute-start.9) | collective-permute-done | bytes 65568 | tf_op jit(solution)/shard_map/ppermute | solution.py:51
  33.3 3.4 %collective-permute-done.11.refs_0_ = bf16[8,32,128]{2,1,0:T(8,128)(2,1)S(1)} collective-permute-done((bf16[8,32,128]{2,1,0:T(8,128)(2,1)S(1)}, bf16[8,32,128]{2,1,0:T(8,128)(2,1)S(1)}, u32[]{:S(2)}, u32[]{:S(2)}) %collective-permute-start.11) | collective-permute-done | bytes 65568 | tf_op jit(solution)/shard_map/ppermute | solution.py:51
  40.2 3.4 %collective-permute-start.16 = (bf16[8,32,128]{2,1,0:T(8,128)(2,1)S(1)}, bf16[8,32,128]{2,1,0:T(8,128)(2,1)S(1)}, u32[]{:S(2)}, u32[]{:S(2)}) collective-permute-start(bf16[8,32,128]{2,1,0:T(8,128)(2,1)S(1)} %get-tuple-element.98), channel_id=1, source_target_pairs={{0,12},{1,7},{2,4},{3,15},{4,2},{5,9},{6,10},{7,1},{8,14},{9,5},{1... | collective-permute-start | bytes 196616 | tf_op jit(solution)/shard_map/ppermute | solution.py:51
  44.3 2.4 %collective-permute-done.16.refs_2_ = bf16[8,32,128]{2,1,0:T(8,128)(2,1)S(1)} collective-permute-done((bf16[8,32,128]{2,1,0:T(8,128)(2,1)S(1)}, bf16[8,32,128]{2,1,0:T(8,128)(2,1)S(1)}, u32[]{:S(2)}, u32[]{:S(2)}) %collective-permute-start.16) | collective-permute-done | bytes 65568 | tf_op jit(solution)/shard_map/ppermute | solution.py:51
  46.7 1.5 %collective-permute-done.15.refs_1_ = bf16[8,32,128]{2,1,0:T(8,128)(2,1)S(1)} collective-permute-done((bf16[8,32,128]{2,1,0:T(8,128)(2,1)S(1)}, bf16[8,32,128]{2,1,0:T(8,128)(2,1)S(1)}, u32[]{:S(2)}, u32[]{:S(2)}) %collective-permute-start.15) | collective-permute-done | bytes 65568 | tf_op jit(solution)/shard_map/ppermute | solution.py:51
  48.3 1.5 %collective-permute-start.17 = (bf16[8,32,128]{2,1,0:T(8,128)(2,1)S(1)}, bf16[8,32,128]{2,1,0:T(8,128)(2,1)S(1)}, u32[]{:S(2)}, u32[]{:S(2)}) collective-permute-start(bf16[8,32,128]{2,1,0:T(8,128)(2,1)S(1)} %get-tuple-element.100), channel_id=1, source_target_pairs={{0,3},{1,8},{2,11},{3,0},{4,13},{5,6},{6,5},{7,14},{8,1},{9,10},{1... | collective-permute-start | bytes 196616 | tf_op jit(solution)/shard_map/ppermute | solution.py:51
  49.7 2.3 %collective-permute-done.17.refs_0_ = bf16[8,32,128]{2,1,0:T(8,128)(2,1)S(1)} collective-permute-done((bf16[8,32,128]{2,1,0:T(8,128)(2,1)S(1)}, bf16[8,32,128]{2,1,0:T(8,128)(2,1)S(1)}, u32[]{:S(2)}, u32[]{:S(2)}) %collective-permute-start.17) | collective-permute-done | bytes 65568 | tf_op jit(solution)/shard_map/ppermute | solution.py:51
  55.5 3.9 %collective-permute-start.22 = (bf16[8,32,128]{2,1,0:T(8,128)(2,1)S(1)}, bf16[8,32,128]{2,1,0:T(8,128)(2,1)S(1)}, u32[]{:S(2)}, u32[]{:S(2)}) collective-permute-start(bf16[8,32,128]{2,1,0:T(8,128)(2,1)S(1)} %get-tuple-element.103), channel_id=1, source_target_pairs={{0,12},{1,7},{2,4},{3,15},{4,2},{5,9},{6,10},{7,1},{8,14},{9,5},{1... | collective-permute-start | bytes 196616 | tf_op jit(solution)/shard_map/ppermute | solution.py:51
  59.7 2.5 %collective-permute-done.22.refs_2_ = bf16[8,32,128]{2,1,0:T(8,128)(2,1)S(1)} collective-permute-done((bf16[8,32,128]{2,1,0:T(8,128)(2,1)S(1)}, bf16[8,32,128]{2,1,0:T(8,128)(2,1)S(1)}, u32[]{:S(2)}, u32[]{:S(2)}) %collective-permute-start.22) | collective-permute-done | bytes 65568 | tf_op jit(solution)/shard_map/ppermute | solution.py:51
  62.3 1.7 %collective-permute-done.21.refs_1_ = bf16[8,32,128]{2,1,0:T(8,128)(2,1)S(1)} collective-permute-done((bf16[8,32,128]{2,1,0:T(8,128)(2,1)S(1)}, bf16[8,32,128]{2,1,0:T(8,128)(2,1)S(1)}, u32[]{:S(2)}, u32[]{:S(2)}) %collective-permute-start.21) | collective-permute-done | bytes 65568 | tf_op jit(solution)/shard_map/ppermute | solution.py:51
  65.3 2.5 %collective-permute-done.23.refs_0_ = bf16[8,32,128]{2,1,0:T(8,128)(2,1)S(1)} collective-permute-done((bf16[8,32,128]{2,1,0:T(8,128)(2,1)S(1)}, bf16[8,32,128]{2,1,0:T(8,128)(2,1)S(1)}, u32[]{:S(2)}, u32[]{:S(2)}) %collective-permute-start.23) | collective-permute-done | bytes 65568 | tf_op jit(solution)/shard_map/ppermute | solution.py:51
  (64 shorter events, 19.0 us)
Async XLA Ops:
  1.6 7.3 %collective-permute-start.1 = (bf16[144,256]{1,0:T(8,128)(2,1)S(1)}, bf16[144,256]{1,0:T(8,128)(2,1)S(1)}, u32[]{:S(2)}, u32[]{:S(2)}) collective-permute-start(bf16[144,256]{1,0:T(8,128)(2,1)S(1)} %shard_map.67), channel_id=1, source_target_pairs={{0,3},{1,2},{2,1},{3,0},{4,7},{5,6},{6,5},{7,4},{8,11},{9,10},{10,... | collective-permute-start | bytes 221192 | tf_op jit(solution)/shard_map/ppermute | solution.py:51
  4.1 5.0 %collective-permute-start = (bf16[144,256]{1,0:T(8,128)(2,1)S(1)}, bf16[144,256]{1,0:T(8,128)(2,1)S(1)}, u32[]{:S(2)}, u32[]{:S(2)}) collective-permute-start(bf16[144,256]{1,0:T(8,128)(2,1)S(1)} %shard_map.67), channel_id=1, source_target_pairs={{0,9},{1,4},{2,7},{3,10},{4,1},{5,12},{6,15},{7,2},{8,13},{9,0},{1... | collective-permute-start | bytes 221192 | tf_op jit(solution)/shard_map/ppermute | solution.py:51
  9.1 5.8 %collective-permute-start.4 = (bf16[1024,256]{1,0:T(8,128)(2,1)S(1)}, bf16[1024,256]{1,0:T(8,128)(2,1)S(1)}, u32[]{:S(2)}, u32[]{:S(2)}) collective-permute-start(bf16[1024,256]{1,0:T(8,128)(2,1)S(1)} %fusion.2.own_ref), channel_id=1, source_target_pairs={{0,1},{1,0},{2,3},{3,2},{4,5},{5,4},{6,7},{7,6},{8,9},{9,8},{10,11... | collective-permute-start | bytes 1572872 | tf_op jit(solution)/shard_map/ppermute | solution.py:56
  9.3 5.6 %collective-permute-start.2 = (bf16[288,256]{1,0:T(8,128)(2,1)S(1)}, bf16[288,256]{1,0:T(8,128)(2,1)S(1)}, u32[]{:S(2)}, u32[]{:S(2)}) collective-permute-start(bf16[288,256]{1,0:T(8,128)(2,1)S(1)} %pad_maximum_fusion.1), channel_id=1, source_target_pairs={{0,5},{1,8},{2,11},{3,6},{4,13},{5,0},{6,3},{7,14},{8,1},{9,12},{1... | collective-permute-start | bytes 442376 | tf_op jit(solution)/shard_map/ppermute | solution.py:51
  10.9 3.8 %collective-permute-start.3 = (bf16[144,256]{1,0:T(8,128)(2,1)S(1)}, bf16[144,256]{1,0:T(8,128)(2,1)S(1)}, u32[]{:S(2)}, u32[]{:S(2)}) collective-permute-start(bf16[144,256]{1,0:T(8,128)(2,1)S(1)} %collective-permute-done), channel_id=1, source_target_pairs={{0,3},{1,2},{2,1},{3,0},{4,7},{5,6},{6,5},{7,4},{8,11},{9,10},{10,... | collective-permute-start | bytes 221192 | tf_op jit(solution)/shard_map/ppermute | solution.py:51
  11.1 2.6 %collective-permute-start.5 = (s32[8,128]{1,0:T(8,128)S(1)}, s32[8,128]{1,0:T(8,128)S(1)}, u32[]{:S(2)}, u32[]{:S(2)}) collective-permute-start(s32[8,128]{1,0:T(8,128)S(1)} %bitcast.5), channel_id=1, source_target_pairs={{0,1},{1,0},{2,3},{3,2},{4,5},{5,4},{6,7},{7,6},{8,9},{9,8},{10,11... | collective-permute-start | bytes 12296 | tf_op jit(solution)/shard_map/ppermute | solution.py:56
  14.9 5.1 %collective-permute-start.6 = (bf16[288,256]{1,0:T(8,128)(2,1)S(1)}, bf16[288,256]{1,0:T(8,128)(2,1)S(1)}, u32[]{:S(2)}, u32[]{:S(2)}) collective-permute-start(bf16[288,256]{1,0:T(8,128)(2,1)S(1)} %collective-permute-done.2), channel_id=1, source_target_pairs={{0,3},{1,2},{2,1},{3,0},{4,7},{5,6},{6,5},{7,4},{8,11},{9,10},{10,... | collective-permute-start | bytes 442376 | tf_op jit(solution)/shard_map/ppermute | solution.py:51
  21.0 1.8 %collective-permute-start.7 = (f32[24,128]{1,0:T(8,128)S(1)}, f32[24,128]{1,0:T(8,128)S(1)}, u32[]{:S(2)}, u32[]{:S(2)}) collective-permute-start(f32[24,128]{1,0:T(8,128)S(1)} %shard_map.71.mine_ref), channel_id=1, source_target_pairs={{0,1},{1,0},{2,3},{3,2},{4,5},{5,4},{6,7},{7,6},{8,9},{9,8},{10,11... | collective-permute-start | bytes 36872 | tf_op jit(solution)/shard_map/ppermute | solution.py:56
  23.8 6.8 %collective-permute-start.10 = (bf16[8,32,128]{2,1,0:T(8,128)(2,1)S(1)}, bf16[8,32,128]{2,1,0:T(8,128)(2,1)S(1)}, u32[]{:S(2)}, u32[]{:S(2)}) collective-permute-start(bf16[8,32,128]{2,1,0:T(8,128)(2,1)S(1)} %get-tuple-element.92), channel_id=1, source_target_pairs={{0,12},{1,7},{2,4},{3,15},{4,2},{5,9},{6,10},{7,1},{8,14},{9,5},{1... | collective-permute-start | bytes 196616 | tf_op jit(solution)/shard_map/ppermute | solution.py:51
  27.6 5.3 %collective-permute-start.9 = (bf16[8,32,128]{2,1,0:T(8,128)(2,1)S(1)}, bf16[8,32,128]{2,1,0:T(8,128)(2,1)S(1)}, u32[]{:S(2)}, u32[]{:S(2)}) collective-permute-start(bf16[8,32,128]{2,1,0:T(8,128)(2,1)S(1)} %get-tuple-element.92), channel_id=1, source_target_pairs={{0,9},{1,4},{2,7},{3,10},{4,1},{5,12},{6,15},{7,2},{8,13},{9,0},{1... | collective-permute-start | bytes 196616 | tf_op jit(solution)/shard_map/ppermute | solution.py:51
  27.9 5.0 %collective-permute-start.8 = (bf16[8,32,128]{2,1,0:T(8,128)(2,1)S(1)}, bf16[8,32,128]{2,1,0:T(8,128)(2,1)S(1)}, u32[]{:S(2)}, u32[]{:S(2)}) collective-permute-start(bf16[8,32,128]{2,1,0:T(8,128)(2,1)S(1)} %get-tuple-element.92), channel_id=1, source_target_pairs={{0,5},{1,2},{2,1},{3,6},{4,7},{5,0},{6,3},{7,4},{8,11},{9,12},{10,... | collective-permute-start | bytes 196616 | tf_op jit(solution)/shard_map/ppermute | solution.py:51
  32.9 3.8 %collective-permute-start.11 = (bf16[8,32,128]{2,1,0:T(8,128)(2,1)S(1)}, bf16[8,32,128]{2,1,0:T(8,128)(2,1)S(1)}, u32[]{:S(2)}, u32[]{:S(2)}) collective-permute-start(bf16[8,32,128]{2,1,0:T(8,128)(2,1)S(1)} %get-tuple-element.94), channel_id=1, source_target_pairs={{0,3},{1,8},{2,11},{3,0},{4,13},{5,6},{6,5},{7,14},{8,1},{9,10},{1... | collective-permute-start | bytes 196616 | tf_op jit(solution)/shard_map/ppermute | solution.py:51
  37.4 1.4 %collective-permute-start.13 = (f32[32,1024]{1,0:T(8,128)S(1)}, f32[32,1024]{1,0:T(8,128)S(1)}, u32[]{:S(2)}, u32[]{:S(2)}) collective-permute-start(f32[32,1024]{1,0:T(8,128)S(1)} %shard_map.76.image_ref), channel_id=1, source_target_pairs={{0,1},{1,0},{2,3},{3,2},{4,5},{5,4},{6,7},{7,6},{8,9},{9,8},{10,11... | collective-permute-start | bytes 393224 | tf_op jit(solution)/shard_map/ppermute | solution.py:56
  38.2 1.5 %collective-permute-start.12 = (f32[32,1024]{1,0:T(8,128)S(1)}, f32[32,1024]{1,0:T(8,128)S(1)}, u32[]{:S(2)}, u32[]{:S(2)}) collective-permute-start(f32[32,1024]{1,0:T(8,128)S(1)} %shard_map.77.image_ref), channel_id=1, source_target_pairs={{0,1},{1,0},{2,3},{3,2},{4,5},{5,4},{6,7},{7,6},{8,9},{9,8},{10,11... | collective-permute-start | bytes 393224 | tf_op jit(solution)/shard_map/ppermute | solution.py:56
  40.2 6.5 %collective-permute-start.16 = (bf16[8,32,128]{2,1,0:T(8,128)(2,1)S(1)}, bf16[8,32,128]{2,1,0:T(8,128)(2,1)S(1)}, u32[]{:S(2)}, u32[]{:S(2)}) collective-permute-start(bf16[8,32,128]{2,1,0:T(8,128)(2,1)S(1)} %get-tuple-element.98), channel_id=1, source_target_pairs={{0,12},{1,7},{2,4},{3,15},{4,2},{5,9},{6,10},{7,1},{8,14},{9,5},{1... | collective-permute-start | bytes 196616 | tf_op jit(solution)/shard_map/ppermute | solution.py:51
  43.6 4.6 %collective-permute-start.15 = (bf16[8,32,128]{2,1,0:T(8,128)(2,1)S(1)}, bf16[8,32,128]{2,1,0:T(8,128)(2,1)S(1)}, u32[]{:S(2)}, u32[]{:S(2)}) collective-permute-start(bf16[8,32,128]{2,1,0:T(8,128)(2,1)S(1)} %get-tuple-element.98), channel_id=1, source_target_pairs={{0,9},{1,4},{2,7},{3,10},{4,1},{5,12},{6,15},{7,2},{8,13},{9,0},{1... | collective-permute-start | bytes 196616 | tf_op jit(solution)/shard_map/ppermute | solution.py:51
  43.6 4.6 %collective-permute-start.14 = (bf16[8,32,128]{2,1,0:T(8,128)(2,1)S(1)}, bf16[8,32,128]{2,1,0:T(8,128)(2,1)S(1)}, u32[]{:S(2)}, u32[]{:S(2)}) collective-permute-start(bf16[8,32,128]{2,1,0:T(8,128)(2,1)S(1)} %get-tuple-element.98), channel_id=1, source_target_pairs={{0,5},{1,2},{2,1},{3,6},{4,7},{5,0},{6,3},{7,4},{8,11},{9,12},{10,... | collective-permute-start | bytes 196616 | tf_op jit(solution)/shard_map/ppermute | solution.py:51
  48.3 3.8 %collective-permute-start.17 = (bf16[8,32,128]{2,1,0:T(8,128)(2,1)S(1)}, bf16[8,32,128]{2,1,0:T(8,128)(2,1)S(1)}, u32[]{:S(2)}, u32[]{:S(2)}) collective-permute-start(bf16[8,32,128]{2,1,0:T(8,128)(2,1)S(1)} %get-tuple-element.100), channel_id=1, source_target_pairs={{0,3},{1,8},{2,11},{3,0},{4,13},{5,6},{6,5},{7,14},{8,1},{9,10},{1... | collective-permute-start | bytes 196616 | tf_op jit(solution)/shard_map/ppermute | solution.py:51
  52.8 1.4 %collective-permute-start.19 = (f32[32,1024]{1,0:T(8,128)S(1)}, f32[32,1024]{1,0:T(8,128)S(1)}, u32[]{:S(2)}, u32[]{:S(2)}) collective-permute-start(f32[32,1024]{1,0:T(8,128)S(1)} %shard_map.82.image_ref), channel_id=1, source_target_pairs={{0,1},{1,0},{2,3},{3,2},{4,5},{5,4},{6,7},{7,6},{8,9},{9,8},{10,11... | collective-permute-start | bytes 393224 | tf_op jit(solution)/shard_map/ppermute | solution.py:56
  53.5 1.5 %collective-permute-start.18 = (f32[32,1024]{1,0:T(8,128)S(1)}, f32[32,1024]{1,0:T(8,128)S(1)}, u32[]{:S(2)}, u32[]{:S(2)}) collective-permute-start(f32[32,1024]{1,0:T(8,128)S(1)} %shard_map.83.image_ref), channel_id=1, source_target_pairs={{0,1},{1,0},{2,3},{3,2},{4,5},{5,4},{6,7},{7,6},{8,9},{9,8},{10,11... | collective-permute-start | bytes 393224 | tf_op jit(solution)/shard_map/ppermute | solution.py:56
  55.5 6.8 %collective-permute-start.22 = (bf16[8,32,128]{2,1,0:T(8,128)(2,1)S(1)}, bf16[8,32,128]{2,1,0:T(8,128)(2,1)S(1)}, u32[]{:S(2)}, u32[]{:S(2)}) collective-permute-start(bf16[8,32,128]{2,1,0:T(8,128)(2,1)S(1)} %get-tuple-element.103), channel_id=1, source_target_pairs={{0,12},{1,7},{2,4},{3,15},{4,2},{5,9},{6,10},{7,1},{8,14},{9,5},{1... | collective-permute-start | bytes 196616 | tf_op jit(solution)/shard_map/ppermute | solution.py:51
  59.4 4.6 %collective-permute-start.21 = (bf16[8,32,128]{2,1,0:T(8,128)(2,1)S(1)}, bf16[8,32,128]{2,1,0:T(8,128)(2,1)S(1)}, u32[]{:S(2)}, u32[]{:S(2)}) collective-permute-start(bf16[8,32,128]{2,1,0:T(8,128)(2,1)S(1)} %get-tuple-element.103), channel_id=1, source_target_pairs={{0,9},{1,4},{2,7},{3,10},{4,1},{5,12},{6,15},{7,2},{8,13},{9,0},{1... | collective-permute-start | bytes 196616 | tf_op jit(solution)/shard_map/ppermute | solution.py:51
  59.4 4.6 %collective-permute-start.20 = (bf16[8,32,128]{2,1,0:T(8,128)(2,1)S(1)}, bf16[8,32,128]{2,1,0:T(8,128)(2,1)S(1)}, u32[]{:S(2)}, u32[]{:S(2)}) collective-permute-start(bf16[8,32,128]{2,1,0:T(8,128)(2,1)S(1)} %get-tuple-element.103), channel_id=1, source_target_pairs={{0,5},{1,2},{2,1},{3,6},{4,7},{5,0},{6,3},{7,4},{8,11},{9,12},{10,... | collective-permute-start | bytes 196616 | tf_op jit(solution)/shard_map/ppermute | solution.py:51
  64.0 3.8 %collective-permute-start.23 = (bf16[8,32,128]{2,1,0:T(8,128)(2,1)S(1)}, bf16[8,32,128]{2,1,0:T(8,128)(2,1)S(1)}, u32[]{:S(2)}, u32[]{:S(2)}) collective-permute-start(bf16[8,32,128]{2,1,0:T(8,128)(2,1)S(1)} %get-tuple-element.104), channel_id=1, source_target_pairs={{0,3},{1,8},{2,11},{3,0},{4,13},{5,6},{6,5},{7,14},{8,1},{9,10},{1... | collective-permute-start | bytes 196616 | tf_op jit(solution)/shard_map/ppermute | solution.py:51
  (3 other events, 9.7 us)

commit v16 on v15

--- a/solution.py
+++ b/solution.py
@@ -127,17 +127,26 @@
     ])
 
 
-def fill_body(own_ref, other_ref, held_ref, *out_refs, tgt_rows):
-    rows = tgt_rows + EXTRA
-    columns = out_refs[0].shape[1]
-    per = min(TILE, columns) // tgt_rows
-    tile = per * tgt_rows
-    for col in range(0, columns, tile):
-        first = col // tgt_rows
+def unit_body(*refs):
+    for in_ref, out_ref in zip(refs, refs[2:]):
+        for row in range(0, in_ref.shape[0], TILE):
+            out_ref[row : row + TILE, :] = unit_rows(in_ref[row : row + TILE, :])
+
+
+def block_of(refs, place, tgt_rows, extra=False):
+    ref, first = refs[place[0]], place[1] * (tgt_rows + EXTRA)
+    return ref[pl.ds(first + tgt_rows, EXTRA) if extra else pl.ds(first, tgt_rows), :]
+
+
+def fill_body(own_ref, other_ref, *refs, places, tgt_rows):
+    held_refs, out_refs = refs[:-4], refs[-4:]
+    per = TILE // tgt_rows
+    for first in range(0, len(places), per):
         block = jnp.concatenate(
-            [held_ref[pl.ds((first + s) * rows, tgt_rows), :] for s in range(per)]
+            [block_of(held_refs, place, tgt_rows) for place in places[first : first + per]]
         )
         tgt_unit = unit_rows(block)
+        col, tile = first * tgt_rows, block.shape[0]
         for cand_ref, kernel_ref, sums_ref in zip((own_ref, other_ref), out_refs, out_refs[2:]):
             for row in range(0, cand_ref.shape[0], TILE):
                 scores = lax.dot_general(
@@ -184,14 +193,7 @@
         first += slots
 
 
-def extras(refs, tgt_rows):
-    rows = tgt_rows + EXTRA
-    for ref in refs:
-        for s in range(ref.shape[0] // rows):
-            yield ref[pl.ds(s * rows + tgt_rows, EXTRA), :].astype(F32)
-
-
-def sums_body(*refs, parts, tgt_rows):
+def sums_body(*refs, parts, places, tgt_rows):
     *refs, out_ref = refs
     each = (out_ref.shape[0] - 8) // 2
     for place in range(2):
@@ -201,7 +203,8 @@
             out_ref[pl.ds(place * each + i, 1), :] = row[:, i * LANES : (i + 1) * LANES]
     counts = jnp.zeros((EXTRA, LANES), F32)
     labels = jnp.zeros((LANES, tgt_rows), F32)
-    for extra in extras(refs[2 * parts :], tgt_rows):
+    for place in places:
+        extra = block_of(refs[2 * parts :], place, tgt_rows, extra=True).astype(F32)
         counts += extra[:, LANES:]
         labels += hot(extra[:1, :LANES].astype(jnp.int32), LANES)
     out_ref[pl.ds(2 * each, 8), :] = counts[:8] + counts[1:9]
@@ -235,10 +238,11 @@
             put_column(scale_ub, kernels[parts:], column_ref, (column_ref, sent_ref))
 
 
-def target_body(mine_ref, got_ref, *refs, targets):
+def target_body(mine_ref, got_ref, *refs, places, targets):
     *held_refs, marg_ref = refs
     total = targets + 3.0 * count_of(1, mine_ref, got_ref)
-    for s, extra in enumerate(extras(held_refs, marg_ref.shape[2])):
+    for s, place in enumerate(places):
+        extra = block_of(held_refs, place, marg_ref.shape[2], extra=True).astype(F32)
         marg_ref[s] = (1.0 + 3.0 * hot(extra[:1, :LANES].astype(jnp.int32))) / total
 
 
@@ -311,41 +315,60 @@
     image_type = ((CLASSES, cand_rows), F32)
     half_flops = 2 * cand_rows * slots * tgt_rows * 128
 
-    def fill(held):
-        columns = held.shape[0] // (tgt_rows + EXTRA) * tgt_rows
+    def found_at(blocks):
+        arrays = []
+        for array, _ in blocks:
+            if not any(array is known for known in arrays):
+                arrays.append(array)
+        number = {id(array): i for i, array in enumerate(arrays)}
+        return arrays, [(number[id(array)], place) for array, place in blocks]
+
+    def fill(blocks):
+        arrays, places = found_at(blocks)
+        columns = len(blocks) * tgt_rows
         return call(
-            functools.partial(fill_body, tgt_rows=tgt_rows),
+            functools.partial(fill_body, places=places, tgt_rows=tgt_rows),
             [((cand_rows, columns), BF16)] * 2 + [((cand_rows, LANES), F32)] * 2,
-            cand_unit, other_unit, held, flops=8 * 2 * cand_rows * columns * 128,
+            cand_unit, other_unit, *arrays, flops=8 * 2 * cand_rows * columns * 128,
         )
 
-    held = piece = pack(tgt_embed, tgt_labels.reshape(1, tgt_rows), cand_labels)
-    cand_unit = unit_rows(cand_embed)
-    weight = 1.0 + 3.0 * hot(cand_labels)
+    held = pack(tgt_embed, tgt_labels.reshape(1, tgt_rows), cand_labels)
+    piece, cand_embed, label_rows = lax.optimization_barrier((held, cand_embed, label_rows))
+    swapped = swap(cand_embed), swap(label_rows)
     across = []
-    other_unit = None
-    for bits in list(zip(slot_bits(0, top), slot_bits(1, top)))[:-1]:
+    stages = list(zip(slot_bits(0, top), slot_bits(1, top)))[:-1]
+    for bits in stages[:-1]:
         turned = exchange(held, *[1 << bit for bit in bits])
         across.append(exchange(piece, 2))
-        piece, across, cand_unit, weight, other_unit = lax.optimization_barrier(
-            (turned, across, cand_unit, weight, other_unit)
-        )
+        piece, across, swapped = lax.optimization_barrier((turned, across, swapped))
         held = jnp.concatenate([held, piece])
-        if other_unit is None:
-            other_unit = swap(cand_unit), swap(label_rows)
-    later = exchange(piece, 2)
-    other_unit, other_labels = other_unit
-    other_weight = 1.0 + 3.0 * hot(other_labels.reshape(1, cand_rows))
-    near = [held, jnp.concatenate(across)]
-    filled = [fill(part) for part in near]
-    later, filled, other_weight = lax.optimization_barrier((later, filled, other_weight))
-    near.append(later)
-    filled.append(fill(later))
+    height = tgt_rows + EXTRA
+    half = held.shape[0] // height
+    known = sum(part.shape[0] for part in across) // height
+    sent = jnp.concatenate([held] + across)
+    turned = exchange(sent, *[1 << bit for bit in stages[-1]])
+    beside = exchange(piece, 2)
+    cand_unit, other_unit = call(unit_body, [(cand_embed.shape, BF16)] * 2, cand_embed, swapped[0])
+    weight = 1.0 + 3.0 * hot(cand_labels)
+    other_weight = 1.0 + 3.0 * hot(swapped[1].reshape(1, cand_rows))
+    turned, beside, cand_unit, other_unit, weight, other_weight = lax.optimization_barrier(
+        (turned, beside, cand_unit, other_unit, weight, other_weight)
+    )
+    later = exchange(turned[known * height : half * height], 2)
+    blocks = [(sent, i) for i in range(half)] + [(turned, i) for i in range(half)]
+    blocks += [(sent, half + i) for i in range(known)]
+    blocks += [(beside, i) for i in range(half - known)]
+    filled = [fill(blocks[: 2 * half]), fill(blocks[2 * half :])]
+    later, filled = lax.optimization_barrier((later, filled))
+    blocks += [(turned, half + i) for i in range(known)]
+    blocks += [(later, i) for i in range(half - known)]
+    filled.append(fill(blocks[3 * half :]))
     own_kernels, other_kernels, own_sums, other_sums = zip(*filled)
+    arrays, places = found_at(blocks)
 
     (mine,) = call(
-        functools.partial(sums_body, parts=len(near), tgt_rows=tgt_rows),
-        [((2 * cand_rows // LANES + 8, LANES), F32)], *own_sums, *other_sums, *near,
+        functools.partial(sums_body, parts=len(filled), places=places, tgt_rows=tgt_rows),
+        [((2 * cand_rows // LANES + 8, LANES), F32)], *own_sums, *other_sums, *arrays,
     )
     got = swap(mine)
     own_marg, other_marg, column, sent = call(
@@ -354,14 +377,14 @@
         weight, other_weight, mine, got, *own_kernels, *other_kernels, flops=2 * half_flops,
     )
     (tgt_marg,) = call(
-        functools.partial(target_body, targets=float(tgt_rows * devices)),
-        [(block, F32)], mine, got, *near,
+        functools.partial(target_body, places=places, targets=float(tgt_rows * devices)),
+        [(block, F32)], mine, got, *arrays,
     )
     for step in range(ITERS):
         last = step == ITERS - 1
         if step:
             column, *scale_u = call(
-                functools.partial(own_body, parts=len(near)),
+                functools.partial(own_body, parts=len(own_kernels)),
                 [(block, F32)] + [image_type] * last,
                 own_image, own_got, own_marg, *own_kernels, flops=half_flops,
             )

time: 70.8 us -> 73.1 us (1.032)
  waiting for transfers between devices: 28.2 us -> 30.6 us
  starting transfers between devices: 27.2 us -> 28.1 us
  other arithmetic: 2.21 us -> 1.42 us
    ppermute x17, waiting for transfers between devices: 24.8 us -> 27.8 us  [exchange(): return lax.ppermute(block, 'row', pairs)]
    reduce_sum x1 -> x0, other arithmetic: 1.25 us -> none  [unit_rows(): meansq = jnp.mean(widened * widened, axis=1, keepdims=True)]
    pallas_call x22 -> x23, Pallas kernels: 10 us -> 10.4 us  [call(): pl.pallas_call(body, out_shape=[pltpu.VMEM(shape, dtype) for shape, dtype...]
  transfers between devices with their start and end apart: 25 -> 25, of which waited for: 20 -> 20; matrix products, arithmetic and copies ran while one was open for 3% -> 2% of each run, Pallas kernels for 7% -> 7%
where the time goes in v16:
time: 73.1 us; the launch traced here: 72.9 us
  waiting for transfers between devices  30.6 us (42%)
  starting transfers between devices  28.1 us (38%)
  Pallas kernels  12.1 us (17%)
  other arithmetic  1.42 us (2%)
  between operations  0.78 us (1%)
    ppermute x17, waiting for transfers between devices, exchange(): return lax.ppermute(block, 'row', pairs)  27.8 us
    ppermute x17, starting transfers between devices, exchange(): return lax.ppermute(block, 'row', pairs)  23.2 us
    pallas_call x23, Pallas kernels, call(): pl.pallas_call(body, out_shape=[pltpu.VMEM(shape, dtype) for shape, dtype...  10.4 us
    ppermute x8, starting transfers between devices, swap(): return lax.ppermute(block, 'row', [(d, d ^ 1) for d in range(devices)])  4.94 us
    ppermute x8, waiting for transfers between devices, swap(): return lax.ppermute(block, 'row', [(d, d ^ 1) for d in range(devices)])  2.76 us
  transfers between devices with their start and end apart: 25, of which 20 were waited for; matrix products, arithmetic and copies ran while one was open for 2% of the time, Pallas kernels for 7%

profile of v16, /device:TPU:0, one launch (start us, length us, event | category | flops | bytes accessed | tf_op | source)
XLA Modules:
  0.0 72.9 jit_solution(16329184868691226909)
XLA Ops:
  2.1 3.7 %collective-permute-start = (bf16[144,256]{1,0:T(8,128)(2,1)S(1)}, bf16[144,256]{1,0:T(8,128)(2,1)S(1)}, u32[]{:S(2)}, u32[]{:S(2)}) collective-permute-start(bf16[144,256]{1,0:T(8,128)(2,1)S(1)} %shard_map.67), channel_id=1, source_target_pairs={{0,9},{1,4},{2,7},{3,10},{4,1},{5,12},{6,15},{7,2},{8,13},{9,0},{1... | collective-permute-start | bytes 221192 | tf_op jit(solution)/shard_map/ppermute | solution.py:51
  5.8 1.2 %collective-permute-start.1 = (bf16[144,256]{1,0:T(8,128)(2,1)S(1)}, bf16[144,256]{1,0:T(8,128)(2,1)S(1)}, u32[]{:S(2)}, u32[]{:S(2)}) collective-permute-start(bf16[144,256]{1,0:T(8,128)(2,1)S(1)} %shard_map.67), channel_id=1, source_target_pairs={{0,3},{1,2},{2,1},{3,0},{4,7},{5,6},{6,5},{7,4},{8,11},{9,10},{10,... | collective-permute-start | bytes 221192 | tf_op jit(solution)/shard_map/ppermute | solution.py:51
  7.8 2.0 %collective-permute-done.1 = bf16[144,256]{1,0:T(8,128)(2,1)S(1)} collective-permute-done((bf16[144,256]{1,0:T(8,128)(2,1)S(1)}, bf16[144,256]{1,0:T(8,128)(2,1)S(1)}, u32[]{:S(2)}, u32[]{:S(2)}) %collective-permute-start.1) | collective-permute-done | bytes 73760 | tf_op jit(solution)/shard_map/ppermute | solution.py:51
  9.8 1.8 %collective-permute-start.5 = (bf16[144,256]{1,0:T(8,128)(2,1)S(1)}, bf16[144,256]{1,0:T(8,128)(2,1)S(1)}, u32[]{:S(2)}, u32[]{:S(2)}) collective-permute-start(bf16[144,256]{1,0:T(8,128)(2,1)S(1)} %collective-permute-done), channel_id=1, source_target_pairs={{0,3},{1,2},{2,1},{3,0},{4,7},{5,6},{6,5},{7,4},{8,11},{9,10},{10,... | collective-permute-start | bytes 221192 | tf_op jit(solution)/shard_map/ppermute | solution.py:51
  11.6 1.1 %collective-permute-start.4 = (bf16[432,256]{1,0:T(8,128)(2,1)S(1)}, bf16[432,256]{1,0:T(8,128)(2,1)S(1)}, u32[]{:S(2)}, u32[]{:S(2)}) collective-permute-start(bf16[432,256]{1,0:T(8,128)(2,1)S(1)} %pad_maximum_fusion.refs_0_.refs_6_), channel_id=1, source_target_pairs={{0,5},{1,8},{2,11},{3,6},{4,13},{5,0},{6,3},{7,14},{8,1},{9,12},{1... | collective-permute-start | bytes 663560 | tf_op jit(solution)/shard_map/ppermute | solution.py:51
  13.9 4.6 %collective-permute-done.4.refs_1_.refs_0_.refs_7_ = bf16[432,256]{1,0:T(8,128)(2,1)S(1)} collective-permute-done((bf16[432,256]{1,0:T(8,128)(2,1)S(1)}, bf16[432,256]{1,0:T(8,128)(2,1)S(1)}, u32[]{:S(2)}, u32[]{:S(2)}) %collective-permute-start.4) | collective-permute-done | bytes 221216 | tf_op jit(solution)/shard_map/ppermute | solution.py:51
  21.0 1.3 %collective-permute-done.6.refs_1_.refs_9_.refs_3_ = bf16[144,256]{1,0:T(8,128)(2,1)S(1)} collective-permute-done((bf16[144,256]{1,0:T(8,128)(2,1)S(1)}, bf16[144,256]{1,0:T(8,128)(2,1)S(1)}, u32[]{:S(2)}, u32[]{:S(2)}) %collective-permute-start.6) | collective-permute-done | bytes 73760 | tf_op jit(solution)/shard_map/ppermute | solution.py:51
  23.3 2.0 %collective-permute-start.7 = (f32[24,128]{1,0:T(8,128)S(1)}, f32[24,128]{1,0:T(8,128)S(1)}, u32[]{:S(2)}, u32[]{:S(2)}) collective-permute-start(f32[24,128]{1,0:T(8,128)S(1)} %shard_map.72.mine_ref), channel_id=1, source_target_pairs={{0,1},{1,0},{2,3},{3,2},{4,5},{5,4},{6,7},{7,6},{8,9},{9,8},{10,11... | collective-permute-start | bytes 36872 | tf_op jit(solution)/shard_map/ppermute | solution.py:56
  27.0 1.6 %collective-permute-start.10 = (bf16[8,32,128]{2,1,0:T(8,128)(2,1)S(1)}, bf16[8,32,128]{2,1,0:T(8,128)(2,1)S(1)}, u32[]{:S(2)}, u32[]{:S(2)}) collective-permute-start(bf16[8,32,128]{2,1,0:T(8,128)(2,1)S(1)} %get-tuple-element.98), channel_id=1, source_target_pairs={{0,12},{1,7},{2,4},{3,15},{4,2},{5,9},{6,10},{7,1},{8,14},{9,5},{1... | collective-permute-start | bytes 196616 | tf_op jit(solution)/shard_map/ppermute | solution.py:51
  28.6 1.3 %collective-permute-start.9 = (bf16[8,32,128]{2,1,0:T(8,128)(2,1)S(1)}, bf16[8,32,128]{2,1,0:T(8,128)(2,1)S(1)}, u32[]{:S(2)}, u32[]{:S(2)}) collective-permute-start(bf16[8,32,128]{2,1,0:T(8,128)(2,1)S(1)} %get-tuple-element.98), channel_id=1, source_target_pairs={{0,9},{1,4},{2,7},{3,10},{4,1},{5,12},{6,15},{7,2},{8,13},{9,0},{1... | collective-permute-start | bytes 196616 | tf_op jit(solution)/shard_map/ppermute | solution.py:51
  29.9 1.2 %collective-permute-start.8 = (bf16[8,32,128]{2,1,0:T(8,128)(2,1)S(1)}, bf16[8,32,128]{2,1,0:T(8,128)(2,1)S(1)}, u32[]{:S(2)}, u32[]{:S(2)}) collective-permute-start(bf16[8,32,128]{2,1,0:T(8,128)(2,1)S(1)} %get-tuple-element.98), channel_id=1, source_target_pairs={{0,5},{1,2},{2,1},{3,6},{4,7},{5,0},{6,3},{7,4},{8,11},{9,12},{10,... | collective-permute-start | bytes 196616 | tf_op jit(solution)/shard_map/ppermute | solution.py:51
  31.1 2.3 %collective-permute-done.10.refs_2_ = bf16[8,32,128]{2,1,0:T(8,128)(2,1)S(1)} collective-permute-done((bf16[8,32,128]{2,1,0:T(8,128)(2,1)S(1)}, bf16[8,32,128]{2,1,0:T(8,128)(2,1)S(1)}, u32[]{:S(2)}, u32[]{:S(2)}) %collective-permute-start.10) | collective-permute-done | bytes 65568 | tf_op jit(solution)/shard_map/ppermute | solution.py:51
  35.3 3.0 %collective-permute-done.11.refs_0_ = bf16[8,32,128]{2,1,0:T(8,128)(2,1)S(1)} collective-permute-done((bf16[8,32,128]{2,1,0:T(8,128)(2,1)S(1)}, bf16[8,32,128]{2,1,0:T(8,128)(2,1)S(1)}, u32[]{:S(2)}, u32[]{:S(2)}) %collective-permute-start.11) | collective-permute-done | bytes 65568 | tf_op jit(solution)/shard_map/ppermute | solution.py:51
  41.8 2.0 %collective-permute-start.16 = (bf16[8,32,128]{2,1,0:T(8,128)(2,1)S(1)}, bf16[8,32,128]{2,1,0:T(8,128)(2,1)S(1)}, u32[]{:S(2)}, u32[]{:S(2)}) collective-permute-start(bf16[8,32,128]{2,1,0:T(8,128)(2,1)S(1)} %get-tuple-element.104), channel_id=1, source_target_pairs={{0,12},{1,7},{2,4},{3,15},{4,2},{5,9},{6,10},{7,1},{8,14},{9,5},{1... | collective-permute-start | bytes 196616 | tf_op jit(solution)/shard_map/ppermute | solution.py:51
  44.2 1.8 %collective-permute-start.14 = (bf16[8,32,128]{2,1,0:T(8,128)(2,1)S(1)}, bf16[8,32,128]{2,1,0:T(8,128)(2,1)S(1)}, u32[]{:S(2)}, u32[]{:S(2)}) collective-permute-start(bf16[8,32,128]{2,1,0:T(8,128)(2,1)S(1)} %get-tuple-element.104), channel_id=1, source_target_pairs={{0,5},{1,2},{2,1},{3,6},{4,7},{5,0},{6,3},{7,4},{8,11},{9,12},{10,... | collective-permute-start | bytes 196616 | tf_op jit(solution)/shard_map/ppermute | solution.py:51
  46.0 2.2 %collective-permute-done.16.refs_2_ = bf16[8,32,128]{2,1,0:T(8,128)(2,1)S(1)} collective-permute-done((bf16[8,32,128]{2,1,0:T(8,128)(2,1)S(1)}, bf16[8,32,128]{2,1,0:T(8,128)(2,1)S(1)}, u32[]{:S(2)}, u32[]{:S(2)}) %collective-permute-start.16) | collective-permute-done | bytes 65568 | tf_op jit(solution)/shard_map/ppermute | solution.py:51
  50.0 1.4 %collective-permute-start.17 = (bf16[8,32,128]{2,1,0:T(8,128)(2,1)S(1)}, bf16[8,32,128]{2,1,0:T(8,128)(2,1)S(1)}, u32[]{:S(2)}, u32[]{:S(2)}) collective-permute-start(bf16[8,32,128]{2,1,0:T(8,128)(2,1)S(1)} %get-tuple-element.106), channel_id=1, source_target_pairs={{0,3},{1,8},{2,11},{3,0},{4,13},{5,6},{6,5},{7,14},{8,1},{9,10},{1... | collective-permute-start | bytes 196616 | tf_op jit(solution)/shard_map/ppermute | solution.py:51
  51.3 2.4 %collective-permute-done.17.refs_0_ = bf16[8,32,128]{2,1,0:T(8,128)(2,1)S(1)} collective-permute-done((bf16[8,32,128]{2,1,0:T(8,128)(2,1)S(1)}, bf16[8,32,128]{2,1,0:T(8,128)(2,1)S(1)}, u32[]{:S(2)}, u32[]{:S(2)}) %collective-permute-start.17) | collective-permute-done | bytes 65568 | tf_op jit(solution)/shard_map/ppermute | solution.py:51
  54.5 1.6 %collective-permute-start.19 = (f32[32,1024]{1,0:T(8,128)S(1)}, f32[32,1024]{1,0:T(8,128)S(1)}, u32[]{:S(2)}, u32[]{:S(2)}) collective-permute-start(f32[32,1024]{1,0:T(8,128)S(1)} %shard_map.83.image_ref), channel_id=1, source_target_pairs={{0,1},{1,0},{2,3},{3,2},{4,5},{5,4},{6,7},{7,6},{8,9},{9,8},{10,11... | collective-permute-start | bytes 393224 | tf_op jit(solution)/shard_map/ppermute | solution.py:56
  58.6 1.5 %collective-permute-start.22 = (bf16[8,32,128]{2,1,0:T(8,128)(2,1)S(1)}, bf16[8,32,128]{2,1,0:T(8,128)(2,1)S(1)}, u32[]{:S(2)}, u32[]{:S(2)}) collective-permute-start(bf16[8,32,128]{2,1,0:T(8,128)(2,1)S(1)} %get-tuple-element.109), channel_id=1, source_target_pairs={{0,12},{1,7},{2,4},{3,15},{4,2},{5,9},{6,10},{7,1},{8,14},{9,5},{1... | collective-permute-start | bytes 196616 | tf_op jit(solution)/shard_map/ppermute | solution.py:51
  60.2 2.6 %collective-permute-start.20 = (bf16[8,32,128]{2,1,0:T(8,128)(2,1)S(1)}, bf16[8,32,128]{2,1,0:T(8,128)(2,1)S(1)}, u32[]{:S(2)}, u32[]{:S(2)}) collective-permute-start(bf16[8,32,128]{2,1,0:T(8,128)(2,1)S(1)} %get-tuple-element.109), channel_id=1, source_target_pairs={{0,5},{1,2},{2,1},{3,6},{4,7},{5,0},{6,3},{7,4},{8,11},{9,12},{10,... | collective-permute-start | bytes 196616 | tf_op jit(solution)/shard_map/ppermute | solution.py:51
  62.8 2.1 %collective-permute-done.22.refs_2_ = bf16[8,32,128]{2,1,0:T(8,128)(2,1)S(1)} collective-permute-done((bf16[8,32,128]{2,1,0:T(8,128)(2,1)S(1)}, bf16[8,32,128]{2,1,0:T(8,128)(2,1)S(1)}, u32[]{:S(2)}, u32[]{:S(2)}) %collective-permute-start.22) | collective-permute-done | bytes 65568 | tf_op jit(solution)/shard_map/ppermute | solution.py:51
  64.9 1.3 %collective-permute-done.21.refs_1_ = bf16[8,32,128]{2,1,0:T(8,128)(2,1)S(1)} collective-permute-done((bf16[8,32,128]{2,1,0:T(8,128)(2,1)S(1)}, bf16[8,32,128]{2,1,0:T(8,128)(2,1)S(1)}, u32[]{:S(2)}, u32[]{:S(2)}) %collective-permute-start.21) | collective-permute-done | bytes 65568 | tf_op jit(solution)/shard_map/ppermute | solution.py:51
  67.1 3.0 %collective-permute-done.23.refs_0_ = bf16[8,32,128]{2,1,0:T(8,128)(2,1)S(1)} collective-permute-done((bf16[8,32,128]{2,1,0:T(8,128)(2,1)S(1)}, bf16[8,32,128]{2,1,0:T(8,128)(2,1)S(1)}, u32[]{:S(2)}, u32[]{:S(2)}) %collective-permute-start.23) | collective-permute-done | bytes 65568 | tf_op jit(solution)/shard_map/ppermute | solution.py:51
  (58 shorter events, 23.2 us)
Async XLA Ops:
  1.6 8.1 %collective-permute-start.2 = (bf16[1024,256]{1,0:T(8,128)(2,1)}, bf16[1024,256]{1,0:T(8,128)(2,1)S(1)}, u32[]{:S(2)}, u32[]{:S(2)}) collective-permute-start(bf16[1024,256]{1,0:T(8,128)(2,1)} %refs_0_), channel_id=1, source_target_pairs={{0,1},{1,0},{2,3},{3,2},{4,5},{5,4},{6,7},{7,6},{8,9},{9,8},{10,11... | collective-permute-start | bytes 1572872 | tf_op jit(solution)/shard_map/ppermute | solution.py:56
  2.1 7.6 %collective-permute-start = (bf16[144,256]{1,0:T(8,128)(2,1)S(1)}, bf16[144,256]{1,0:T(8,128)(2,1)S(1)}, u32[]{:S(2)}, u32[]{:S(2)}) collective-permute-start(bf16[144,256]{1,0:T(8,128)(2,1)S(1)} %shard_map.67), channel_id=1, source_target_pairs={{0,9},{1,4},{2,7},{3,10},{4,1},{5,12},{6,15},{7,2},{8,13},{9,0},{1... | collective-permute-start | bytes 221192 | tf_op jit(solution)/shard_map/ppermute | solution.py:51
  5.8 1.9 %collective-permute-start.3 = (s32[8,128]{1,0:T(8,128)}, s32[8,128]{1,0:T(8,128)S(1)}, u32[]{:S(2)}, u32[]{:S(2)}) collective-permute-start(s32[8,128]{1,0:T(8,128)} %bitcast.5), channel_id=1, source_target_pairs={{0,1},{1,0},{2,3},{3,2},{4,5},{5,4},{6,7},{7,6},{8,9},{9,8},{10,11... | collective-permute-start | bytes 12296 | tf_op jit(solution)/shard_map/ppermute | solution.py:56
  5.8 3.9 %collective-permute-start.1 = (bf16[144,256]{1,0:T(8,128)(2,1)S(1)}, bf16[144,256]{1,0:T(8,128)(2,1)S(1)}, u32[]{:S(2)}, u32[]{:S(2)}) collective-permute-start(bf16[144,256]{1,0:T(8,128)(2,1)S(1)} %shard_map.67), channel_id=1, source_target_pairs={{0,3},{1,2},{2,1},{3,0},{4,7},{5,6},{6,5},{7,4},{8,11},{9,10},{10,... | collective-permute-start | bytes 221192 | tf_op jit(solution)/shard_map/ppermute | solution.py:51
  9.8 4.1 %collective-permute-start.5 = (bf16[144,256]{1,0:T(8,128)(2,1)S(1)}, bf16[144,256]{1,0:T(8,128)(2,1)S(1)}, u32[]{:S(2)}, u32[]{:S(2)}) collective-permute-start(bf16[144,256]{1,0:T(8,128)(2,1)S(1)} %collective-permute-done), channel_id=1, source_target_pairs={{0,3},{1,2},{2,1},{3,0},{4,7},{5,6},{6,5},{7,4},{8,11},{9,10},{10,... | collective-permute-start | bytes 221192 | tf_op jit(solution)/shard_map/ppermute | solution.py:51
  11.6 6.9 %collective-permute-start.4 = (bf16[432,256]{1,0:T(8,128)(2,1)S(1)}, bf16[432,256]{1,0:T(8,128)(2,1)S(1)}, u32[]{:S(2)}, u32[]{:S(2)}) collective-permute-start(bf16[432,256]{1,0:T(8,128)(2,1)S(1)} %pad_maximum_fusion.refs_0_.refs_6_), channel_id=1, source_target_pairs={{0,5},{1,8},{2,11},{3,6},{4,13},{5,0},{6,3},{7,14},{8,1},{9,12},{1... | collective-permute-start | bytes 663560 | tf_op jit(solution)/shard_map/ppermute | solution.py:51
  18.5 3.8 %collective-permute-start.6 = (bf16[144,256]{1,0:T(8,128)(2,1)S(1)}, bf16[144,256]{1,0:T(8,128)(2,1)S(1)}, u32[]{:S(2)}, u32[]{:S(2)}) collective-permute-start(bf16[144,256]{1,0:T(8,128)(2,1)S(1)} %slice.3), channel_id=1, source_target_pairs={{0,3},{1,2},{2,1},{3,0},{4,7},{5,6},{6,5},{7,4},{8,11},{9,10},{10,... | collective-permute-start | bytes 221192 | tf_op jit(solution)/shard_map/ppermute | solution.py:51
  23.3 2.8 %collective-permute-start.7 = (f32[24,128]{1,0:T(8,128)S(1)}, f32[24,128]{1,0:T(8,128)S(1)}, u32[]{:S(2)}, u32[]{:S(2)}) collective-permute-start(f32[24,128]{1,0:T(8,128)S(1)} %shard_map.72.mine_ref), channel_id=1, source_target_pairs={{0,1},{1,0},{2,3},{3,2},{4,5},{5,4},{6,7},{7,6},{8,9},{9,8},{10,11... | collective-permute-start | bytes 36872 | tf_op jit(solution)/shard_map/ppermute | solution.py:56
  27.0 6.5 %collective-permute-start.10 = (bf16[8,32,128]{2,1,0:T(8,128)(2,1)S(1)}, bf16[8,32,128]{2,1,0:T(8,128)(2,1)S(1)}, u32[]{:S(2)}, u32[]{:S(2)}) collective-permute-start(bf16[8,32,128]{2,1,0:T(8,128)(2,1)S(1)} %get-tuple-element.98), channel_id=1, source_target_pairs={{0,12},{1,7},{2,4},{3,15},{4,2},{5,9},{6,10},{7,1},{8,14},{9,5},{1... | collective-permute-start | bytes 196616 | tf_op jit(solution)/shard_map/ppermute | solution.py:51
  28.6 5.9 %collective-permute-start.9 = (bf16[8,32,128]{2,1,0:T(8,128)(2,1)S(1)}, bf16[8,32,128]{2,1,0:T(8,128)(2,1)S(1)}, u32[]{:S(2)}, u32[]{:S(2)}) collective-permute-start(bf16[8,32,128]{2,1,0:T(8,128)(2,1)S(1)} %get-tuple-element.98), channel_id=1, source_target_pairs={{0,9},{1,4},{2,7},{3,10},{4,1},{5,12},{6,15},{7,2},{8,13},{9,0},{1... | collective-permute-start | bytes 196616 | tf_op jit(solution)/shard_map/ppermute | solution.py:51
  29.9 4.6 %collective-permute-start.8 = (bf16[8,32,128]{2,1,0:T(8,128)(2,1)S(1)}, bf16[8,32,128]{2,1,0:T(8,128)(2,1)S(1)}, u32[]{:S(2)}, u32[]{:S(2)}) collective-permute-start(bf16[8,32,128]{2,1,0:T(8,128)(2,1)S(1)} %get-tuple-element.98), channel_id=1, source_target_pairs={{0,5},{1,2},{2,1},{3,6},{4,7},{5,0},{6,3},{7,4},{8,11},{9,12},{10,... | collective-permute-start | bytes 196616 | tf_op jit(solution)/shard_map/ppermute | solution.py:51
  34.6 3.8 %collective-permute-start.11 = (bf16[8,32,128]{2,1,0:T(8,128)(2,1)S(1)}, bf16[8,32,128]{2,1,0:T(8,128)(2,1)S(1)}, u32[]{:S(2)}, u32[]{:S(2)}) collective-permute-start(bf16[8,32,128]{2,1,0:T(8,128)(2,1)S(1)} %get-tuple-element.100), channel_id=1, source_target_pairs={{0,3},{1,8},{2,11},{3,0},{4,13},{5,6},{6,5},{7,14},{8,1},{9,10},{1... | collective-permute-start | bytes 196616 | tf_op jit(solution)/shard_map/ppermute | solution.py:51
  39.1 1.4 %collective-permute-start.13 = (f32[32,1024]{1,0:T(8,128)S(1)}, f32[32,1024]{1,0:T(8,128)S(1)}, u32[]{:S(2)}, u32[]{:S(2)}) collective-permute-start(f32[32,1024]{1,0:T(8,128)S(1)} %shard_map.77.image_ref), channel_id=1, source_target_pairs={{0,1},{1,0},{2,3},{3,2},{4,5},{5,4},{6,7},{7,6},{8,9},{9,8},{10,11... | collective-permute-start | bytes 393224 | tf_op jit(solution)/shard_map/ppermute | solution.py:56
  39.9 1.5 %collective-permute-start.12 = (f32[32,1024]{1,0:T(8,128)S(1)}, f32[32,1024]{1,0:T(8,128)S(1)}, u32[]{:S(2)}, u32[]{:S(2)}) collective-permute-start(f32[32,1024]{1,0:T(8,128)S(1)} %shard_map.78.image_ref), channel_id=1, source_target_pairs={{0,1},{1,0},{2,3},{3,2},{4,5},{5,4},{6,7},{7,6},{8,9},{9,8},{10,11... | collective-permute-start | bytes 393224 | tf_op jit(solution)/shard_map/ppermute | solution.py:56
  41.8 6.3 %collective-permute-start.16 = (bf16[8,32,128]{2,1,0:T(8,128)(2,1)S(1)}, bf16[8,32,128]{2,1,0:T(8,128)(2,1)S(1)}, u32[]{:S(2)}, u32[]{:S(2)}) collective-permute-start(bf16[8,32,128]{2,1,0:T(8,128)(2,1)S(1)} %get-tuple-element.104), channel_id=1, source_target_pairs={{0,12},{1,7},{2,4},{3,15},{4,2},{5,9},{6,10},{7,1},{8,14},{9,5},{1... | collective-permute-start | bytes 196616 | tf_op jit(solution)/shard_map/ppermute | solution.py:51
  43.8 5.4 %collective-permute-start.15 = (bf16[8,32,128]{2,1,0:T(8,128)(2,1)S(1)}, bf16[8,32,128]{2,1,0:T(8,128)(2,1)S(1)}, u32[]{:S(2)}, u32[]{:S(2)}) collective-permute-start(bf16[8,32,128]{2,1,0:T(8,128)(2,1)S(1)} %get-tuple-element.104), channel_id=1, source_target_pairs={{0,9},{1,4},{2,7},{3,10},{4,1},{5,12},{6,15},{7,2},{8,13},{9,0},{1... | collective-permute-start | bytes 196616 | tf_op jit(solution)/shard_map/ppermute | solution.py:51
  44.2 5.7 %collective-permute-start.14 = (bf16[8,32,128]{2,1,0:T(8,128)(2,1)S(1)}, bf16[8,32,128]{2,1,0:T(8,128)(2,1)S(1)}, u32[]{:S(2)}, u32[]{:S(2)}) collective-permute-start(bf16[8,32,128]{2,1,0:T(8,128)(2,1)S(1)} %get-tuple-element.104), channel_id=1, source_target_pairs={{0,5},{1,2},{2,1},{3,6},{4,7},{5,0},{6,3},{7,4},{8,11},{9,12},{10,... | collective-permute-start | bytes 196616 | tf_op jit(solution)/shard_map/ppermute | solution.py:51
  50.0 3.8 %collective-permute-start.17 = (bf16[8,32,128]{2,1,0:T(8,128)(2,1)S(1)}, bf16[8,32,128]{2,1,0:T(8,128)(2,1)S(1)}, u32[]{:S(2)}, u32[]{:S(2)}) collective-permute-start(bf16[8,32,128]{2,1,0:T(8,128)(2,1)S(1)} %get-tuple-element.106), channel_id=1, source_target_pairs={{0,3},{1,8},{2,11},{3,0},{4,13},{5,6},{6,5},{7,14},{8,1},{9,10},{1... | collective-permute-start | bytes 196616 | tf_op jit(solution)/shard_map/ppermute | solution.py:51
  54.5 2.6 %collective-permute-start.19 = (f32[32,1024]{1,0:T(8,128)S(1)}, f32[32,1024]{1,0:T(8,128)S(1)}, u32[]{:S(2)}, u32[]{:S(2)}) collective-permute-start(f32[32,1024]{1,0:T(8,128)S(1)} %shard_map.83.image_ref), channel_id=1, source_target_pairs={{0,1},{1,0},{2,3},{3,2},{4,5},{5,4},{6,7},{7,6},{8,9},{9,8},{10,11... | collective-permute-start | bytes 393224 | tf_op jit(solution)/shard_map/ppermute | solution.py:56
  56.8 1.4 %collective-permute-start.18 = (f32[32,1024]{1,0:T(8,128)S(1)}, f32[32,1024]{1,0:T(8,128)S(1)}, u32[]{:S(2)}, u32[]{:S(2)}) collective-permute-start(f32[32,1024]{1,0:T(8,128)S(1)} %shard_map.84.image_ref), channel_id=1, source_target_pairs={{0,1},{1,0},{2,3},{3,2},{4,5},{5,4},{6,7},{7,6},{8,9},{9,8},{10,11... | collective-permute-start | bytes 393224 | tf_op jit(solution)/shard_map/ppermute | solution.py:56
  58.6 6.3 %collective-permute-start.22 = (bf16[8,32,128]{2,1,0:T(8,128)(2,1)S(1)}, bf16[8,32,128]{2,1,0:T(8,128)(2,1)S(1)}, u32[]{:S(2)}, u32[]{:S(2)}) collective-permute-start(bf16[8,32,128]{2,1,0:T(8,128)(2,1)S(1)} %get-tuple-element.109), channel_id=1, source_target_pairs={{0,12},{1,7},{2,4},{3,15},{4,2},{5,9},{6,10},{7,1},{8,14},{9,5},{1... | collective-permute-start | bytes 196616 | tf_op jit(solution)/shard_map/ppermute | solution.py:51
  60.2 6.1 %collective-permute-start.21 = (bf16[8,32,128]{2,1,0:T(8,128)(2,1)S(1)}, bf16[8,32,128]{2,1,0:T(8,128)(2,1)S(1)}, u32[]{:S(2)}, u32[]{:S(2)}) collective-permute-start(bf16[8,32,128]{2,1,0:T(8,128)(2,1)S(1)} %get-tuple-element.109), channel_id=1, source_target_pairs={{0,9},{1,4},{2,7},{3,10},{4,1},{5,12},{6,15},{7,2},{8,13},{9,0},{1... | collective-permute-start | bytes 196616 | tf_op jit(solution)/shard_map/ppermute | solution.py:51
  60.2 6.1 %collective-permute-start.20 = (bf16[8,32,128]{2,1,0:T(8,128)(2,1)S(1)}, bf16[8,32,128]{2,1,0:T(8,128)(2,1)S(1)}, u32[]{:S(2)}, u32[]{:S(2)}) collective-permute-start(bf16[8,32,128]{2,1,0:T(8,128)(2,1)S(1)} %get-tuple-element.109), channel_id=1, source_target_pairs={{0,5},{1,2},{2,1},{3,6},{4,7},{5,0},{6,3},{7,4},{8,11},{9,12},{10,... | collective-permute-start | bytes 196616 | tf_op jit(solution)/shard_map/ppermute | solution.py:51
  66.3 3.8 %collective-permute-start.23 = (bf16[8,32,128]{2,1,0:T(8,128)(2,1)S(1)}, bf16[8,32,128]{2,1,0:T(8,128)(2,1)S(1)}, u32[]{:S(2)}, u32[]{:S(2)}) collective-permute-start(bf16[8,32,128]{2,1,0:T(8,128)(2,1)S(1)} %get-tuple-element.110), channel_id=1, source_target_pairs={{0,3},{1,8},{2,11},{3,0},{4,13},{5,6},{6,5},{7,14},{8,1},{9,10},{1... | collective-permute-start | bytes 196616 | tf_op jit(solution)/shard_map/ppermute | solution.py:51
  (2 other events, 13.4 us)

commit v17 on v15

--- a/solution.py
+++ b/solution.py
@@ -125,6 +125,11 @@
         pltpu.with_memory_space_constraint(a, pltpu.HBM)
         for a in (tgt_embed, tgt_labels, cand_labels)
     ])
+
+
+def unit_body(in_ref, out_ref):
+    for row in range(0, in_ref.shape[0], TILE):
+        out_ref[row : row + TILE, :] = unit_rows(in_ref[row : row + TILE, :])
 
 
 def fill_body(own_ref, other_ref, held_ref, *out_refs, tgt_rows):
@@ -320,21 +325,23 @@
         )
 
     held = piece = pack(tgt_embed, tgt_labels.reshape(1, tgt_rows), cand_labels)
-    cand_unit = unit_rows(cand_embed)
-    weight = 1.0 + 3.0 * hot(cand_labels)
     across = []
-    other_unit = None
-    for bits in list(zip(slot_bits(0, top), slot_bits(1, top)))[:-1]:
+    stages = list(zip(slot_bits(0, top), slot_bits(1, top)))[:-1]
+    for place, bits in enumerate(stages):
         turned = exchange(held, *[1 << bit for bit in bits])
         across.append(exchange(piece, 2))
-        piece, across, cand_unit, weight, other_unit = lax.optimization_barrier(
-            (turned, across, cand_unit, weight, other_unit)
-        )
+        if place == len(stages) - 1:
+            (cand_unit,) = call(unit_body, [(cand_embed.shape, BF16)], cand_embed)
+            other_unit, other_labels = swap(cand_unit), swap(label_rows)
+            weight = 1.0 + 3.0 * hot(cand_labels)
+            turned, across, weight = lax.optimization_barrier((turned, across, weight))
+        else:
+            turned, across, cand_embed, cand_labels, label_rows = lax.optimization_barrier(
+                (turned, across, cand_embed, cand_labels, label_rows)
+            )
+        piece = turned
         held = jnp.concatenate([held, piece])
-        if other_unit is None:
-            other_unit = swap(cand_unit), swap(label_rows)
     later = exchange(piece, 2)
-    other_unit, other_labels = other_unit
     other_weight = 1.0 + 3.0 * hot(other_labels.reshape(1, cand_rows))
     near = [held, jnp.concatenate(across)]
     filled = [fill(part) for part in near]

time: 70.8 us -> 71.4 us (level)
  starting transfers between devices: 27.2 us -> 30.1 us
  other arithmetic: 2.21 us -> 0.75 us
    ppermute x17, starting transfers between devices: 23 us -> 25.8 us  [exchange(): return lax.ppermute(block, 'row', pairs)]
    reduce_sum x1 -> x0, other arithmetic: 1.25 us -> none  [unit_rows(): meansq = jnp.mean(widened * widened, axis=1, keepdims=True)]
    ppermute x8, waiting for transfers between devices: 3.37 us -> 2.55 us  [swap(): return lax.ppermute(block, 'row', [(d, d ^ 1) for d in range(devices)])]
    pallas_call x22 -> x23, Pallas kernels: 10 us -> 10.2 us  [call(): pl.pallas_call(body, out_shape=[pltpu.VMEM(shape, dtype) for shape, dtype...]
  transfers between devices with their start and end apart: 25 -> 25, of which waited for: 20 -> 19; matrix products, arithmetic and copies ran while one was open for 3% -> 1% of each run, Pallas kernels for 7% -> 7%
where the time goes in v17:
time: 71.4 us; the launch traced here: 71.2 us
  starting transfers between devices  30.1 us (42%)
  waiting for transfers between devices  27.6 us (39%)
  Pallas kernels  11.9 us (17%)
  between operations  0.81 us (1%)
  other arithmetic  0.75 us (1%)
    ppermute x17, starting transfers between devices, exchange(): return lax.ppermute(block, 'row', pairs)  25.8 us
    ppermute x17, waiting for transfers between devices, exchange(): return lax.ppermute(block, 'row', pairs)  25.1 us
    pallas_call x23, Pallas kernels, call(): pl.pallas_call(body, out_shape=[pltpu.VMEM(shape, dtype) for shape, dtype...  10.2 us
    ppermute x8, starting transfers between devices, swap(): return lax.ppermute(block, 'row', [(d, d ^ 1) for d in range(devices)])  4.39 us
    ppermute x8, waiting for transfers between devices, swap(): return lax.ppermute(block, 'row', [(d, d ^ 1) for d in range(devices)])  2.55 us
  transfers between devices with their start and end apart: 25, of which 19 were waited for; matrix products, arithmetic and copies ran while one was open for 1% of the time, Pallas kernels for 7%

profile of v17, /device:TPU:0, one launch (start us, length us, event | category | flops | bytes accessed | tf_op | source)
XLA Modules:
  0.0 71.2 jit_solution(4741944871669337172)
XLA Ops:
  0.7 1.0 %shard_map.67 = bf16[144,256]{1,0:T(8,128)(2,1)S(1)} custom-call(bf16[128,256]{1,0:T(8,128)(2,1)} %embed_hbm.1, s32[1,128]{1,0:T(1,128)} %bitcast.8, s32[1,1024]{1,0:T(1,128)} %bitcast.5), custom_call_target="tpu_custom_call" | custom-call | tf_op jit(solution)/shard_map/pallas_call | solution.py:113
  1.6 2.5 %collective-permute-start.1 = (bf16[144,256]{1,0:T(8,128)(2,1)S(1)}, bf16[144,256]{1,0:T(8,128)(2,1)S(1)}, u32[]{:S(2)}, u32[]{:S(2)}) collective-permute-start(bf16[144,256]{1,0:T(8,128)(2,1)S(1)} %shard_map.67), channel_id=1, source_target_pairs={{0,3},{1,2},{2,1},{3,0},{4,7},{5,6},{6,5},{7,4},{8,11},{9,10},{10,... | collective-permute-start | bytes 221192 | tf_op jit(solution)/shard_map/ppermute | solution.py:51
  4.1 2.9 %collective-permute-start = (bf16[144,256]{1,0:T(8,128)(2,1)S(1)}, bf16[144,256]{1,0:T(8,128)(2,1)S(1)}, u32[]{:S(2)}, u32[]{:S(2)}) collective-permute-start(bf16[144,256]{1,0:T(8,128)(2,1)S(1)} %shard_map.67), channel_id=1, source_target_pairs={{0,9},{1,4},{2,7},{3,10},{4,1},{5,12},{6,15},{7,2},{8,13},{9,0},{1... | collective-permute-start | bytes 221192 | tf_op jit(solution)/shard_map/ppermute | solution.py:51
  7.0 2.1 %collective-permute-done = bf16[144,256]{1,0:T(8,128)(2,1)S(1)} collective-permute-done((bf16[144,256]{1,0:T(8,128)(2,1)S(1)}, bf16[144,256]{1,0:T(8,128)(2,1)S(1)}, u32[]{:S(2)}, u32[]{:S(2)}) %collective-permute-start) | collective-permute-done | bytes 73760 | tf_op jit(solution)/shard_map/ppermute | solution.py:51
  9.4 1.8 %collective-permute-start.2 = (bf16[288,256]{1,0:T(8,128)(2,1)S(1)}, bf16[288,256]{1,0:T(8,128)(2,1)S(1)}, u32[]{:S(2)}, u32[]{:S(2)}) collective-permute-start(bf16[288,256]{1,0:T(8,128)(2,1)S(1)} %pad_maximum_fusion.1), channel_id=1, source_target_pairs={{0,5},{1,8},{2,11},{3,6},{4,13},{5,0},{6,3},{7,14},{8,1},{9,12},{1... | collective-permute-start | bytes 442376 | tf_op jit(solution)/shard_map/ppermute | solution.py:51
  11.4 1.8 %collective-permute-start.5 = (bf16[1024,256]{1,0:T(8,128)(2,1)S(1)}, bf16[1024,256]{1,0:T(8,128)(2,1)S(1)}, u32[]{:S(2)}, u32[]{:S(2)}) collective-permute-start(bf16[1024,256]{1,0:T(8,128)(2,1)S(1)} %shard_map.68.own_ref), channel_id=1, source_target_pairs={{0,1},{1,0},{2,3},{3,2},{4,5},{5,4},{6,7},{7,6},{8,9},{9,8},{10,11... | collective-permute-start | bytes 1572872 | tf_op jit(solution)/shard_map/ppermute | solution.py:56
  14.3 3.1 %collective-permute-start.4 = (bf16[288,256]{1,0:T(8,128)(2,1)S(1)}, bf16[288,256]{1,0:T(8,128)(2,1)S(1)}, u32[]{:S(2)}, u32[]{:S(2)}) collective-permute-start(bf16[288,256]{1,0:T(8,128)(2,1)S(1)} %collective-permute-done.2), channel_id=1, source_target_pairs={{0,3},{1,2},{2,1},{3,0},{4,7},{5,6},{6,5},{7,4},{8,11},{9,10},{10,... | collective-permute-start | bytes 442376 | tf_op jit(solution)/shard_map/ppermute | solution.py:51
  18.0 1.0 %shard_map.69 = (bf16[1024,512]{1,0:T(8,128)(2,1)S(1)}, bf16[1024,512]{1,0:T(8,128)(2,1)S(1)}, f32[1024,128]{1,0:T(8,128)S(1)}, f32[1024,128]{1,0:T(8,128)S(1)}) custom-call(bf16[1024,256]{1,0:T(8,128)(2,1)S(1)} %shard_map.68.own_ref, bf16[1024,256]{1,0:T(8,128)(2,1)S(1)} %collective-permute-done.5.other_ref, ...), custom_call_target="tpu_custom_call" | custom-call | flops 1073741824 | bytes 1343488 | tf_op jit(solution)/shard_map/pallas_call | solution.py:62
  19.0 1.6 %collective-permute-done.4.held_ref.refs_8_.refs_2_ = bf16[288,256]{1,0:T(8,128)(2,1)S(1)} collective-permute-done((bf16[288,256]{1,0:T(8,128)(2,1)S(1)}, bf16[288,256]{1,0:T(8,128)(2,1)S(1)}, u32[]{:S(2)}, u32[]{:S(2)}) %collective-permute-start.4) | collective-permute-done | bytes 147488 | tf_op jit(solution)/shard_map/ppermute | solution.py:51
  21.6 1.1 %collective-permute-start.7 = (f32[24,128]{1,0:T(8,128)S(1)}, f32[24,128]{1,0:T(8,128)S(1)}, u32[]{:S(2)}, u32[]{:S(2)}) collective-permute-start(f32[24,128]{1,0:T(8,128)S(1)} %shard_map.72.mine_ref), channel_id=1, source_target_pairs={{0,1},{1,0},{2,3},{3,2},{4,5},{5,4},{6,7},{7,6},{8,9},{9,8},{10,11... | collective-permute-start | bytes 36872 | tf_op jit(solution)/shard_map/ppermute | solution.py:56
  24.5 3.9 %collective-permute-start.10 = (bf16[8,32,128]{2,1,0:T(8,128)(2,1)S(1)}, bf16[8,32,128]{2,1,0:T(8,128)(2,1)S(1)}, u32[]{:S(2)}, u32[]{:S(2)}) collective-permute-start(bf16[8,32,128]{2,1,0:T(8,128)(2,1)S(1)} %get-tuple-element.88), channel_id=1, source_target_pairs={{0,12},{1,7},{2,4},{3,15},{4,2},{5,9},{6,10},{7,1},{8,14},{9,5},{1... | collective-permute-start | bytes 196616 | tf_op jit(solution)/shard_map/ppermute | solution.py:51
  28.7 2.5 %collective-permute-done.10.refs_2_ = bf16[8,32,128]{2,1,0:T(8,128)(2,1)S(1)} collective-permute-done((bf16[8,32,128]{2,1,0:T(8,128)(2,1)S(1)}, bf16[8,32,128]{2,1,0:T(8,128)(2,1)S(1)}, u32[]{:S(2)}, u32[]{:S(2)}) %collective-permute-start.10) | collective-permute-done | bytes 65568 | tf_op jit(solution)/shard_map/ppermute | solution.py:51
  31.2 2.3 %collective-permute-done.9.refs_1_ = bf16[8,32,128]{2,1,0:T(8,128)(2,1)S(1)} collective-permute-done((bf16[8,32,128]{2,1,0:T(8,128)(2,1)S(1)}, bf16[8,32,128]{2,1,0:T(8,128)(2,1)S(1)}, u32[]{:S(2)}, u32[]{:S(2)}) %collective-permute-start.9) | collective-permute-done | bytes 65568 | tf_op jit(solution)/shard_map/ppermute | solution.py:51
  33.5 1.1 %collective-permute-start.11 = (bf16[8,32,128]{2,1,0:T(8,128)(2,1)S(1)}, bf16[8,32,128]{2,1,0:T(8,128)(2,1)S(1)}, u32[]{:S(2)}, u32[]{:S(2)}) collective-permute-start(bf16[8,32,128]{2,1,0:T(8,128)(2,1)S(1)} %get-tuple-element.90), channel_id=1, source_target_pairs={{0,3},{1,8},{2,11},{3,0},{4,13},{5,6},{6,5},{7,14},{8,1},{9,10},{1... | collective-permute-start | bytes 196616 | tf_op jit(solution)/shard_map/ppermute | solution.py:51
  34.8 2.5 %collective-permute-done.11.refs_0_ = bf16[8,32,128]{2,1,0:T(8,128)(2,1)S(1)} collective-permute-done((bf16[8,32,128]{2,1,0:T(8,128)(2,1)S(1)}, bf16[8,32,128]{2,1,0:T(8,128)(2,1)S(1)}, u32[]{:S(2)}, u32[]{:S(2)}) %collective-permute-start.11) | collective-permute-done | bytes 65568 | tf_op jit(solution)/shard_map/ppermute | solution.py:51
  40.8 3.4 %collective-permute-start.16 = (bf16[8,32,128]{2,1,0:T(8,128)(2,1)S(1)}, bf16[8,32,128]{2,1,0:T(8,128)(2,1)S(1)}, u32[]{:S(2)}, u32[]{:S(2)}) collective-permute-start(bf16[8,32,128]{2,1,0:T(8,128)(2,1)S(1)} %get-tuple-element.94), channel_id=1, source_target_pairs={{0,12},{1,7},{2,4},{3,15},{4,2},{5,9},{6,10},{7,1},{8,14},{9,5},{1... | collective-permute-start | bytes 196616 | tf_op jit(solution)/shard_map/ppermute | solution.py:51
  44.9 2.2 %collective-permute-done.16.refs_2_ = bf16[8,32,128]{2,1,0:T(8,128)(2,1)S(1)} collective-permute-done((bf16[8,32,128]{2,1,0:T(8,128)(2,1)S(1)}, bf16[8,32,128]{2,1,0:T(8,128)(2,1)S(1)}, u32[]{:S(2)}, u32[]{:S(2)}) %collective-permute-start.16) | collective-permute-done | bytes 65568 | tf_op jit(solution)/shard_map/ppermute | solution.py:51
  47.1 1.6 %collective-permute-done.15.refs_1_ = bf16[8,32,128]{2,1,0:T(8,128)(2,1)S(1)} collective-permute-done((bf16[8,32,128]{2,1,0:T(8,128)(2,1)S(1)}, bf16[8,32,128]{2,1,0:T(8,128)(2,1)S(1)}, u32[]{:S(2)}, u32[]{:S(2)}) %collective-permute-start.15) | collective-permute-done | bytes 65568 | tf_op jit(solution)/shard_map/ppermute | solution.py:51
  48.8 1.2 %collective-permute-start.17 = (bf16[8,32,128]{2,1,0:T(8,128)(2,1)S(1)}, bf16[8,32,128]{2,1,0:T(8,128)(2,1)S(1)}, u32[]{:S(2)}, u32[]{:S(2)}) collective-permute-start(bf16[8,32,128]{2,1,0:T(8,128)(2,1)S(1)} %get-tuple-element.96), channel_id=1, source_target_pairs={{0,3},{1,8},{2,11},{3,0},{4,13},{5,6},{6,5},{7,14},{8,1},{9,10},{1... | collective-permute-start | bytes 196616 | tf_op jit(solution)/shard_map/ppermute | solution.py:51
  50.0 2.5 %collective-permute-done.17.refs_0_ = bf16[8,32,128]{2,1,0:T(8,128)(2,1)S(1)} collective-permute-done((bf16[8,32,128]{2,1,0:T(8,128)(2,1)S(1)}, bf16[8,32,128]{2,1,0:T(8,128)(2,1)S(1)}, u32[]{:S(2)}, u32[]{:S(2)}) %collective-permute-start.17) | collective-permute-done | bytes 65568 | tf_op jit(solution)/shard_map/ppermute | solution.py:51
  56.0 3.9 %collective-permute-start.22 = (bf16[8,32,128]{2,1,0:T(8,128)(2,1)S(1)}, bf16[8,32,128]{2,1,0:T(8,128)(2,1)S(1)}, u32[]{:S(2)}, u32[]{:S(2)}) collective-permute-start(bf16[8,32,128]{2,1,0:T(8,128)(2,1)S(1)} %get-tuple-element.99), channel_id=1, source_target_pairs={{0,12},{1,7},{2,4},{3,15},{4,2},{5,9},{6,10},{7,1},{8,14},{9,5},{1... | collective-permute-start | bytes 196616 | tf_op jit(solution)/shard_map/ppermute | solution.py:51
  60.3 2.2 %collective-permute-done.22.refs_2_ = bf16[8,32,128]{2,1,0:T(8,128)(2,1)S(1)} collective-permute-done((bf16[8,32,128]{2,1,0:T(8,128)(2,1)S(1)}, bf16[8,32,128]{2,1,0:T(8,128)(2,1)S(1)}, u32[]{:S(2)}, u32[]{:S(2)}) %collective-permute-start.22) | collective-permute-done | bytes 65568 | tf_op jit(solution)/shard_map/ppermute | solution.py:51
  62.5 2.0 %collective-permute-done.21.refs_1_ = bf16[8,32,128]{2,1,0:T(8,128)(2,1)S(1)} collective-permute-done((bf16[8,32,128]{2,1,0:T(8,128)(2,1)S(1)}, bf16[8,32,128]{2,1,0:T(8,128)(2,1)S(1)}, u32[]{:S(2)}, u32[]{:S(2)}) %collective-permute-start.21) | collective-permute-done | bytes 65568 | tf_op jit(solution)/shard_map/ppermute | solution.py:51
  65.9 2.5 %collective-permute-done.23.refs_0_ = bf16[8,32,128]{2,1,0:T(8,128)(2,1)S(1)} collective-permute-done((bf16[8,32,128]{2,1,0:T(8,128)(2,1)S(1)}, bf16[8,32,128]{2,1,0:T(8,128)(2,1)S(1)}, u32[]{:S(2)}, u32[]{:S(2)}) %collective-permute-start.23) | collective-permute-done | bytes 65568 | tf_op jit(solution)/shard_map/ppermute | solution.py:51
  (62 shorter events, 17.9 us)
Async XLA Ops:
  1.6 5.3 %collective-permute-start.1 = (bf16[144,256]{1,0:T(8,128)(2,1)S(1)}, bf16[144,256]{1,0:T(8,128)(2,1)S(1)}, u32[]{:S(2)}, u32[]{:S(2)}) collective-permute-start(bf16[144,256]{1,0:T(8,128)(2,1)S(1)} %shard_map.67), channel_id=1, source_target_pairs={{0,3},{1,2},{2,1},{3,0},{4,7},{5,6},{6,5},{7,4},{8,11},{9,10},{10,... | collective-permute-start | bytes 221192 | tf_op jit(solution)/shard_map/ppermute | solution.py:51
  4.1 5.0 %collective-permute-start = (bf16[144,256]{1,0:T(8,128)(2,1)S(1)}, bf16[144,256]{1,0:T(8,128)(2,1)S(1)}, u32[]{:S(2)}, u32[]{:S(2)}) collective-permute-start(bf16[144,256]{1,0:T(8,128)(2,1)S(1)} %shard_map.67), channel_id=1, source_target_pairs={{0,9},{1,4},{2,7},{3,10},{4,1},{5,12},{6,15},{7,2},{8,13},{9,0},{1... | collective-permute-start | bytes 221192 | tf_op jit(solution)/shard_map/ppermute | solution.py:51
  9.1 4.1 %collective-permute-start.6 = (s32[8,128]{1,0:T(8,128)}, s32[8,128]{1,0:T(8,128)S(1)}, u32[]{:S(2)}, u32[]{:S(2)}) collective-permute-start(s32[8,128]{1,0:T(8,128)} %bitcast.6), channel_id=1, source_target_pairs={{0,1},{1,0},{2,3},{3,2},{4,5},{5,4},{6,7},{7,6},{8,9},{9,8},{10,11... | collective-permute-start | bytes 12296 | tf_op jit(solution)/shard_map/ppermute | solution.py:56
  9.3 4.2 %collective-permute-start.3 = (bf16[144,256]{1,0:T(8,128)(2,1)S(1)}, bf16[144,256]{1,0:T(8,128)(2,1)S(1)}, u32[]{:S(2)}, u32[]{:S(2)}) collective-permute-start(bf16[144,256]{1,0:T(8,128)(2,1)S(1)} %collective-permute-done), channel_id=1, source_target_pairs={{0,3},{1,2},{2,1},{3,0},{4,7},{5,6},{6,5},{7,4},{8,11},{9,10},{10,... | collective-permute-start | bytes 221192 | tf_op jit(solution)/shard_map/ppermute | solution.py:51
  9.4 4.9 %collective-permute-start.2 = (bf16[288,256]{1,0:T(8,128)(2,1)S(1)}, bf16[288,256]{1,0:T(8,128)(2,1)S(1)}, u32[]{:S(2)}, u32[]{:S(2)}) collective-permute-start(bf16[288,256]{1,0:T(8,128)(2,1)S(1)} %pad_maximum_fusion.1), channel_id=1, source_target_pairs={{0,5},{1,8},{2,11},{3,6},{4,13},{5,0},{6,3},{7,14},{8,1},{9,12},{1... | collective-permute-start | bytes 442376 | tf_op jit(solution)/shard_map/ppermute | solution.py:51
  11.4 6.0 %collective-permute-start.5 = (bf16[1024,256]{1,0:T(8,128)(2,1)S(1)}, bf16[1024,256]{1,0:T(8,128)(2,1)S(1)}, u32[]{:S(2)}, u32[]{:S(2)}) collective-permute-start(bf16[1024,256]{1,0:T(8,128)(2,1)S(1)} %shard_map.68.own_ref), channel_id=1, source_target_pairs={{0,1},{1,0},{2,3},{3,2},{4,5},{5,4},{6,7},{7,6},{8,9},{9,8},{10,11... | collective-permute-start | bytes 1572872 | tf_op jit(solution)/shard_map/ppermute | solution.py:56
  14.3 6.3 %collective-permute-start.4 = (bf16[288,256]{1,0:T(8,128)(2,1)S(1)}, bf16[288,256]{1,0:T(8,128)(2,1)S(1)}, u32[]{:S(2)}, u32[]{:S(2)}) collective-permute-start(bf16[288,256]{1,0:T(8,128)(2,1)S(1)} %collective-permute-done.2), channel_id=1, source_target_pairs={{0,3},{1,2},{2,1},{3,0},{4,7},{5,6},{6,5},{7,4},{8,11},{9,10},{10,... | collective-permute-start | bytes 442376 | tf_op jit(solution)/shard_map/ppermute | solution.py:51
  21.6 1.9 %collective-permute-start.7 = (f32[24,128]{1,0:T(8,128)S(1)}, f32[24,128]{1,0:T(8,128)S(1)}, u32[]{:S(2)}, u32[]{:S(2)}) collective-permute-start(f32[24,128]{1,0:T(8,128)S(1)} %shard_map.72.mine_ref), channel_id=1, source_target_pairs={{0,1},{1,0},{2,3},{3,2},{4,5},{5,4},{6,7},{7,6},{8,9},{9,8},{10,11... | collective-permute-start | bytes 36872 | tf_op jit(solution)/shard_map/ppermute | solution.py:56
  24.5 6.7 %collective-permute-start.10 = (bf16[8,32,128]{2,1,0:T(8,128)(2,1)S(1)}, bf16[8,32,128]{2,1,0:T(8,128)(2,1)S(1)}, u32[]{:S(2)}, u32[]{:S(2)}) collective-permute-start(bf16[8,32,128]{2,1,0:T(8,128)(2,1)S(1)} %get-tuple-element.88), channel_id=1, source_target_pairs={{0,12},{1,7},{2,4},{3,15},{4,2},{5,9},{6,10},{7,1},{8,14},{9,5},{1... | collective-permute-start | bytes 196616 | tf_op jit(solution)/shard_map/ppermute | solution.py:51
  28.4 5.1 %collective-permute-start.9 = (bf16[8,32,128]{2,1,0:T(8,128)(2,1)S(1)}, bf16[8,32,128]{2,1,0:T(8,128)(2,1)S(1)}, u32[]{:S(2)}, u32[]{:S(2)}) collective-permute-start(bf16[8,32,128]{2,1,0:T(8,128)(2,1)S(1)} %get-tuple-element.88), channel_id=1, source_target_pairs={{0,9},{1,4},{2,7},{3,10},{4,1},{5,12},{6,15},{7,2},{8,13},{9,0},{1... | collective-permute-start | bytes 196616 | tf_op jit(solution)/shard_map/ppermute | solution.py:51
  28.4 5.1 %collective-permute-start.8 = (bf16[8,32,128]{2,1,0:T(8,128)(2,1)S(1)}, bf16[8,32,128]{2,1,0:T(8,128)(2,1)S(1)}, u32[]{:S(2)}, u32[]{:S(2)}) collective-permute-start(bf16[8,32,128]{2,1,0:T(8,128)(2,1)S(1)} %get-tuple-element.88), channel_id=1, source_target_pairs={{0,5},{1,2},{2,1},{3,6},{4,7},{5,0},{6,3},{7,4},{8,11},{9,12},{10,... | collective-permute-start | bytes 196616 | tf_op jit(solution)/shard_map/ppermute | solution.py:51
  33.5 3.8 %collective-permute-start.11 = (bf16[8,32,128]{2,1,0:T(8,128)(2,1)S(1)}, bf16[8,32,128]{2,1,0:T(8,128)(2,1)S(1)}, u32[]{:S(2)}, u32[]{:S(2)}) collective-permute-start(bf16[8,32,128]{2,1,0:T(8,128)(2,1)S(1)} %get-tuple-element.90), channel_id=1, source_target_pairs={{0,3},{1,8},{2,11},{3,0},{4,13},{5,6},{6,5},{7,14},{8,1},{9,10},{1... | collective-permute-start | bytes 196616 | tf_op jit(solution)/shard_map/ppermute | solution.py:51
  38.0 1.4 %collective-permute-start.13 = (f32[32,1024]{1,0:T(8,128)S(1)}, f32[32,1024]{1,0:T(8,128)S(1)}, u32[]{:S(2)}, u32[]{:S(2)}) collective-permute-start(f32[32,1024]{1,0:T(8,128)S(1)} %shard_map.77.image_ref), channel_id=1, source_target_pairs={{0,1},{1,0},{2,3},{3,2},{4,5},{5,4},{6,7},{7,6},{8,9},{9,8},{10,11... | collective-permute-start | bytes 393224 | tf_op jit(solution)/shard_map/ppermute | solution.py:56
  38.8 1.5 %collective-permute-start.12 = (f32[32,1024]{1,0:T(8,128)S(1)}, f32[32,1024]{1,0:T(8,128)S(1)}, u32[]{:S(2)}, u32[]{:S(2)}) collective-permute-start(f32[32,1024]{1,0:T(8,128)S(1)} %shard_map.78.image_ref), channel_id=1, source_target_pairs={{0,1},{1,0},{2,3},{3,2},{4,5},{5,4},{6,7},{7,6},{8,9},{9,8},{10,11... | collective-permute-start | bytes 393224 | tf_op jit(solution)/shard_map/ppermute | solution.py:56
  40.8 6.3 %collective-permute-start.16 = (bf16[8,32,128]{2,1,0:T(8,128)(2,1)S(1)}, bf16[8,32,128]{2,1,0:T(8,128)(2,1)S(1)}, u32[]{:S(2)}, u32[]{:S(2)}) collective-permute-start(bf16[8,32,128]{2,1,0:T(8,128)(2,1)S(1)} %get-tuple-element.94), channel_id=1, source_target_pairs={{0,12},{1,7},{2,4},{3,15},{4,2},{5,9},{6,10},{7,1},{8,14},{9,5},{1... | collective-permute-start | bytes 196616 | tf_op jit(solution)/shard_map/ppermute | solution.py:51
  44.1 4.6 %collective-permute-start.15 = (bf16[8,32,128]{2,1,0:T(8,128)(2,1)S(1)}, bf16[8,32,128]{2,1,0:T(8,128)(2,1)S(1)}, u32[]{:S(2)}, u32[]{:S(2)}) collective-permute-start(bf16[8,32,128]{2,1,0:T(8,128)(2,1)S(1)} %get-tuple-element.94), channel_id=1, source_target_pairs={{0,9},{1,4},{2,7},{3,10},{4,1},{5,12},{6,15},{7,2},{8,13},{9,0},{1... | collective-permute-start | bytes 196616 | tf_op jit(solution)/shard_map/ppermute | solution.py:51
  44.1 4.6 %collective-permute-start.14 = (bf16[8,32,128]{2,1,0:T(8,128)(2,1)S(1)}, bf16[8,32,128]{2,1,0:T(8,128)(2,1)S(1)}, u32[]{:S(2)}, u32[]{:S(2)}) collective-permute-start(bf16[8,32,128]{2,1,0:T(8,128)(2,1)S(1)} %get-tuple-element.94), channel_id=1, source_target_pairs={{0,5},{1,2},{2,1},{3,6},{4,7},{5,0},{6,3},{7,4},{8,11},{9,12},{10,... | collective-permute-start | bytes 196616 | tf_op jit(solution)/shard_map/ppermute | solution.py:51
  48.8 3.8 %collective-permute-start.17 = (bf16[8,32,128]{2,1,0:T(8,128)(2,1)S(1)}, bf16[8,32,128]{2,1,0:T(8,128)(2,1)S(1)}, u32[]{:S(2)}, u32[]{:S(2)}) collective-permute-start(bf16[8,32,128]{2,1,0:T(8,128)(2,1)S(1)} %get-tuple-element.96), channel_id=1, source_target_pairs={{0,3},{1,8},{2,11},{3,0},{4,13},{5,6},{6,5},{7,14},{8,1},{9,10},{1... | collective-permute-start | bytes 196616 | tf_op jit(solution)/shard_map/ppermute | solution.py:51
  53.3 1.4 %collective-permute-start.19 = (f32[32,1024]{1,0:T(8,128)S(1)}, f32[32,1024]{1,0:T(8,128)S(1)}, u32[]{:S(2)}, u32[]{:S(2)}) collective-permute-start(f32[32,1024]{1,0:T(8,128)S(1)} %shard_map.83.image_ref), channel_id=1, source_target_pairs={{0,1},{1,0},{2,3},{3,2},{4,5},{5,4},{6,7},{7,6},{8,9},{9,8},{10,11... | collective-permute-start | bytes 393224 | tf_op jit(solution)/shard_map/ppermute | solution.py:56
  54.1 1.5 %collective-permute-start.18 = (f32[32,1024]{1,0:T(8,128)S(1)}, f32[32,1024]{1,0:T(8,128)S(1)}, u32[]{:S(2)}, u32[]{:S(2)}) collective-permute-start(f32[32,1024]{1,0:T(8,128)S(1)} %shard_map.84.image_ref), channel_id=1, source_target_pairs={{0,1},{1,0},{2,3},{3,2},{4,5},{5,4},{6,7},{7,6},{8,9},{9,8},{10,11... | collective-permute-start | bytes 393224 | tf_op jit(solution)/shard_map/ppermute | solution.py:56
  56.0 6.5 %collective-permute-start.22 = (bf16[8,32,128]{2,1,0:T(8,128)(2,1)S(1)}, bf16[8,32,128]{2,1,0:T(8,128)(2,1)S(1)}, u32[]{:S(2)}, u32[]{:S(2)}) collective-permute-start(bf16[8,32,128]{2,1,0:T(8,128)(2,1)S(1)} %get-tuple-element.99), channel_id=1, source_target_pairs={{0,12},{1,7},{2,4},{3,15},{4,2},{5,9},{6,10},{7,1},{8,14},{9,5},{1... | collective-permute-start | bytes 196616 | tf_op jit(solution)/shard_map/ppermute | solution.py:51
  60.0 4.6 %collective-permute-start.21 = (bf16[8,32,128]{2,1,0:T(8,128)(2,1)S(1)}, bf16[8,32,128]{2,1,0:T(8,128)(2,1)S(1)}, u32[]{:S(2)}, u32[]{:S(2)}) collective-permute-start(bf16[8,32,128]{2,1,0:T(8,128)(2,1)S(1)} %get-tuple-element.99), channel_id=1, source_target_pairs={{0,9},{1,4},{2,7},{3,10},{4,1},{5,12},{6,15},{7,2},{8,13},{9,0},{1... | collective-permute-start | bytes 196616 | tf_op jit(solution)/shard_map/ppermute | solution.py:51
  60.0 4.6 %collective-permute-start.20 = (bf16[8,32,128]{2,1,0:T(8,128)(2,1)S(1)}, bf16[8,32,128]{2,1,0:T(8,128)(2,1)S(1)}, u32[]{:S(2)}, u32[]{:S(2)}) collective-permute-start(bf16[8,32,128]{2,1,0:T(8,128)(2,1)S(1)} %get-tuple-element.99), channel_id=1, source_target_pairs={{0,5},{1,2},{2,1},{3,6},{4,7},{5,0},{6,3},{7,4},{8,11},{9,12},{10,... | collective-permute-start | bytes 196616 | tf_op jit(solution)/shard_map/ppermute | solution.py:51
  64.6 3.8 %collective-permute-start.23 = (bf16[8,32,128]{2,1,0:T(8,128)(2,1)S(1)}, bf16[8,32,128]{2,1,0:T(8,128)(2,1)S(1)}, u32[]{:S(2)}, u32[]{:S(2)}) collective-permute-start(bf16[8,32,128]{2,1,0:T(8,128)(2,1)S(1)} %get-tuple-element.100), channel_id=1, source_target_pairs={{0,3},{1,8},{2,11},{3,0},{4,13},{5,6},{6,5},{7,14},{8,1},{9,10},{1... | collective-permute-start | bytes 196616 | tf_op jit(solution)/shard_map/ppermute | solution.py:51
  (3 other events, 20.6 us)

commit v18 on v15

--- a/solution.py
+++ b/solution.py
@@ -156,19 +156,6 @@
                 sums_ref[row : row + TILE, :] = sums
 
 
-def image_of(kernels, scale_ref):
-    image = 0.0
-    first = 0
-    for kernel_ref in kernels:
-        slots = kernel_ref.shape[1] // scale_ref.shape[2]
-        scale_v = jnp.concatenate([scale_ref[s] for s in range(first, first + slots)], axis=1)
-        image += lax.dot_general(
-            kernel_ref[...], scale_v, (((1,), (1,)), ((), ())), preferred_element_type=F32
-        )
-        first += slots
-    return image.T
-
-
 def put_column(scale_ub, kernels, added, out_refs):
     width = out_refs[0].shape[2]
     first = 0
@@ -243,7 +230,22 @@
 
 
 def image_body(scale_ref, *refs):
-    refs[-1][...] = image_of(refs[:-1], scale_ref)
+    *kernels, image_ref = refs
+    step = min(512, image_ref.shape[1])
+    for row in range(0, image_ref.shape[1], step):
+        image = 0.0
+        first = 0
+        for kernel_ref in kernels:
+            slots = kernel_ref.shape[1] // scale_ref.shape[2]
+            scale_v = jnp.concatenate([scale_ref[s] for s in range(first, first + slots)], axis=1)
+            image += lax.dot_general(
+                kernel_ref[row : row + step, :],
+                scale_v,
+                (((1,), (1,)), ((), ())),
+                preferred_element_type=F32,
+            )
+            first += slots
+        image_ref[:, row : row + step] = image.T
 
 
 def own_body(image_ref, got_ref, marg_ref, *refs, parts):

time: 70.8 us -> 71 us (level)
  transfers between devices with their start and end apart: 25 -> 25, of which waited for: 20 -> 18; matrix products, arithmetic and copies ran while one was open for 3% -> 3% of each run, Pallas kernels for 7% -> 7%
where the time goes in v18:
time: 71 us; the launch traced here: 70.8 us
  waiting for transfers between devices  28.2 us (40%)
  starting transfers between devices  27.3 us (38%)
  Pallas kernels  11.8 us (17%)
  other arithmetic  2.21 us (3%)
  between operations  0.83 us (1%)
    ppermute x17, waiting for transfers between devices, exchange(): return lax.ppermute(block, 'row', pairs)  24.8 us
    ppermute x17, starting transfers between devices, exchange(): return lax.ppermute(block, 'row', pairs)  23 us
    pallas_call x22, Pallas kernels, call(): pl.pallas_call(body, out_shape=[pltpu.VMEM(shape, dtype) for shape, dtype...  10.1 us
    ppermute x8, starting transfers between devices, swap(): return lax.ppermute(block, 'row', [(d, d ^ 1) for d in range(devices)])  4.31 us
    ppermute x8, waiting for transfers between devices, swap(): return lax.ppermute(block, 'row', [(d, d ^ 1) for d in range(devices)])  3.35 us
  transfers between devices with their start and end apart: 25, of which 18 were waited for; matrix products, arithmetic and copies ran while one was open for 3% of the time, Pallas kernels for 7%

profile of v18, /device:TPU:0, one launch (start us, length us, event | category | flops | bytes accessed | tf_op | source)
XLA Modules:
  0.0 70.8 jit_solution(17615870784379309253)
XLA Ops:
  0.6 1.0 %shard_map.67 = bf16[144,256]{1,0:T(8,128)(2,1)S(1)} custom-call(bf16[128,256]{1,0:T(8,128)(2,1)} %embed_hbm.1, s32[1,128]{1,0:T(1,128)} %bitcast.7, s32[1,1024]{1,0:T(1,128)} %bitcast.4), custom_call_target="tpu_custom_call" | custom-call | tf_op jit(solution)/shard_map/pallas_call | solution.py:113
  1.6 2.5 %collective-permute-start.1 = (bf16[144,256]{1,0:T(8,128)(2,1)S(1)}, bf16[144,256]{1,0:T(8,128)(2,1)S(1)}, u32[]{:S(2)}, u32[]{:S(2)}) collective-permute-start(bf16[144,256]{1,0:T(8,128)(2,1)S(1)} %shard_map.67), channel_id=1, source_target_pairs={{0,3},{1,2},{2,1},{3,0},{4,7},{5,6},{6,5},{7,4},{8,11},{9,10},{10,... | collective-permute-start | bytes 221192 | tf_op jit(solution)/shard_map/ppermute | solution.py:51
  4.1 2.9 %collective-permute-start = (bf16[144,256]{1,0:T(8,128)(2,1)S(1)}, bf16[144,256]{1,0:T(8,128)(2,1)S(1)}, u32[]{:S(2)}, u32[]{:S(2)}) collective-permute-start(bf16[144,256]{1,0:T(8,128)(2,1)S(1)} %shard_map.67), channel_id=1, source_target_pairs={{0,9},{1,4},{2,7},{3,10},{4,1},{5,12},{6,15},{7,2},{8,13},{9,0},{1... | collective-permute-start | bytes 221192 | tf_op jit(solution)/shard_map/ppermute | solution.py:51
  6.9 1.3 %fusion = f32[1024]{0:T(1024)S(1)} fusion(bf16[1024,256]{1,0:T(8,128)(2,1)} %param.4), kind=kLoop, calls=%fused_computation.2 | loop fusion | flops 785408 | bytes 528384 | tf_op jit(solution)/shard_map/reduce_sum | solution.py:74
  9.3 1.5 %collective-permute-start.2 = (bf16[288,256]{1,0:T(8,128)(2,1)S(1)}, bf16[288,256]{1,0:T(8,128)(2,1)S(1)}, u32[]{:S(2)}, u32[]{:S(2)}) collective-permute-start(bf16[288,256]{1,0:T(8,128)(2,1)S(1)} %pad_maximum_fusion.1), channel_id=1, source_target_pairs={{0,5},{1,8},{2,11},{3,6},{4,13},{5,0},{6,3},{7,14},{8,1},{9,12},{1... | collective-permute-start | bytes 442376 | tf_op jit(solution)/shard_map/ppermute | solution.py:51
  11.1 1.8 %collective-permute-start.5 = (s32[8,128]{1,0:T(8,128)S(1)}, s32[8,128]{1,0:T(8,128)S(1)}, u32[]{:S(2)}, u32[]{:S(2)}) collective-permute-start(s32[8,128]{1,0:T(8,128)S(1)} %bitcast.5), channel_id=1, source_target_pairs={{0,1},{1,0},{2,3},{3,2},{4,5},{5,4},{6,7},{7,6},{8,9},{9,8},{10,11... | collective-permute-start | bytes 12296 | tf_op jit(solution)/shard_map/ppermute | solution.py:56
  14.9 1.0 %collective-permute-start.6 = (bf16[288,256]{1,0:T(8,128)(2,1)S(1)}, bf16[288,256]{1,0:T(8,128)(2,1)S(1)}, u32[]{:S(2)}, u32[]{:S(2)}) collective-permute-start(bf16[288,256]{1,0:T(8,128)(2,1)S(1)} %collective-permute-done.2), channel_id=1, source_target_pairs={{0,3},{1,2},{2,1},{3,0},{4,7},{5,6},{6,5},{7,4},{8,11},{9,10},{10,... | collective-permute-start | bytes 442376 | tf_op jit(solution)/shard_map/ppermute | solution.py:51
  16.6 1.0 %shard_map.68 = (bf16[1024,512]{1,0:T(8,128)(2,1)S(1)}, bf16[1024,512]{1,0:T(8,128)(2,1)S(1)}, f32[1024,128]{1,0:T(8,128)S(1)}, f32[1024,128]{1,0:T(8,128)S(1)}) custom-call(bf16[1024,256]{1,0:T(8,128)(2,1)S(1)} %fusion.2.own_ref, bf16[1024,256]{1,0:T(8,128)(2,1)S(1)} %collective-permute-done.4.other_ref, ...), custom_call_target="tpu_custom_call" | custom-call | flops 1073741824 | bytes 1343488 | tf_op jit(solution)/shard_map/pallas_call | solution.py:62
  17.6 2.5 %collective-permute-done.6.held_ref.refs_8_.refs_2_ = bf16[288,256]{1,0:T(8,128)(2,1)S(1)} collective-permute-done((bf16[288,256]{1,0:T(8,128)(2,1)S(1)}, bf16[288,256]{1,0:T(8,128)(2,1)S(1)}, u32[]{:S(2)}, u32[]{:S(2)}) %collective-permute-start.6) | collective-permute-done | bytes 147488 | tf_op jit(solution)/shard_map/ppermute | solution.py:51
  21.0 1.0 %collective-permute-start.7 = (f32[24,128]{1,0:T(8,128)S(1)}, f32[24,128]{1,0:T(8,128)S(1)}, u32[]{:S(2)}, u32[]{:S(2)}) collective-permute-start(f32[24,128]{1,0:T(8,128)S(1)} %shard_map.71.mine_ref), channel_id=1, source_target_pairs={{0,1},{1,0},{2,3},{3,2},{4,5},{5,4},{6,7},{7,6},{8,9},{9,8},{10,11... | collective-permute-start | bytes 36872 | tf_op jit(solution)/shard_map/ppermute | solution.py:56
  22.9 0.9 %shard_map.72 = (f32[32,1024]{1,0:T(8,128)S(1)}, f32[32,1024]{1,0:T(8,128)S(1)}, f32[8,32,128]{2,1,0:T(8,128)S(1)}, bf16[8,32,128]{2,1,0:T(8,128)(2,1)S(1)}) custom-call(f32[32,1024]{1,0:T(8,128)S(1)} %select_add_fusion.1.own_weight, f32[32,1024]{1,0:T(8,128)S(1)} %select_add_fusion.other_weight, f32[24,128]{1,0:T(8,128)S(1)} %shard_map.71.mine_ref, ...), custom_call_target="tpu_custom_call" | custom-call | flops 536870912 | bytes 4481024 | tf_op jit(solution)/shard_map/pallas_call | solution.py:62
  23.8 3.7 %collective-permute-start.10 = (bf16[8,32,128]{2,1,0:T(8,128)(2,1)S(1)}, bf16[8,32,128]{2,1,0:T(8,128)(2,1)S(1)}, u32[]{:S(2)}, u32[]{:S(2)}) collective-permute-start(bf16[8,32,128]{2,1,0:T(8,128)(2,1)S(1)} %get-tuple-element.92), channel_id=1, source_target_pairs={{0,12},{1,7},{2,4},{3,15},{4,2},{5,9},{6,10},{7,1},{8,14},{9,5},{1... | collective-permute-start | bytes 196616 | tf_op jit(solution)/shard_map/ppermute | solution.py:51
  28.1 2.5 %collective-permute-done.10.refs_2_ = bf16[8,32,128]{2,1,0:T(8,128)(2,1)S(1)} collective-permute-done((bf16[8,32,128]{2,1,0:T(8,128)(2,1)S(1)}, bf16[8,32,128]{2,1,0:T(8,128)(2,1)S(1)}, u32[]{:S(2)}, u32[]{:S(2)}) %collective-permute-start.10) | collective-permute-done | bytes 65568 | tf_op jit(solution)/shard_map/ppermute | solution.py:51
  30.6 2.3 %collective-permute-done.9.refs_1_ = bf16[8,32,128]{2,1,0:T(8,128)(2,1)S(1)} collective-permute-done((bf16[8,32,128]{2,1,0:T(8,128)(2,1)S(1)}, bf16[8,32,128]{2,1,0:T(8,128)(2,1)S(1)}, u32[]{:S(2)}, u32[]{:S(2)}) %collective-permute-start.9) | collective-permute-done | bytes 65568 | tf_op jit(solution)/shard_map/ppermute | solution.py:51
  33.3 3.4 %collective-permute-done.11.refs_0_ = bf16[8,32,128]{2,1,0:T(8,128)(2,1)S(1)} collective-permute-done((bf16[8,32,128]{2,1,0:T(8,128)(2,1)S(1)}, bf16[8,32,128]{2,1,0:T(8,128)(2,1)S(1)}, u32[]{:S(2)}, u32[]{:S(2)}) %collective-permute-start.11) | collective-permute-done | bytes 65568 | tf_op jit(solution)/shard_map/ppermute | solution.py:51
  40.2 3.4 %collective-permute-start.16 = (bf16[8,32,128]{2,1,0:T(8,128)(2,1)S(1)}, bf16[8,32,128]{2,1,0:T(8,128)(2,1)S(1)}, u32[]{:S(2)}, u32[]{:S(2)}) collective-permute-start(bf16[8,32,128]{2,1,0:T(8,128)(2,1)S(1)} %get-tuple-element.98), channel_id=1, source_target_pairs={{0,12},{1,7},{2,4},{3,15},{4,2},{5,9},{6,10},{7,1},{8,14},{9,5},{1... | collective-permute-start | bytes 196616 | tf_op jit(solution)/shard_map/ppermute | solution.py:51
  44.4 2.4 %collective-permute-done.16.refs_2_ = bf16[8,32,128]{2,1,0:T(8,128)(2,1)S(1)} collective-permute-done((bf16[8,32,128]{2,1,0:T(8,128)(2,1)S(1)}, bf16[8,32,128]{2,1,0:T(8,128)(2,1)S(1)}, u32[]{:S(2)}, u32[]{:S(2)}) %collective-permute-start.16) | collective-permute-done | bytes 65568 | tf_op jit(solution)/shard_map/ppermute | solution.py:51
  46.8 1.4 %collective-permute-done.15.refs_1_ = bf16[8,32,128]{2,1,0:T(8,128)(2,1)S(1)} collective-permute-done((bf16[8,32,128]{2,1,0:T(8,128)(2,1)S(1)}, bf16[8,32,128]{2,1,0:T(8,128)(2,1)S(1)}, u32[]{:S(2)}, u32[]{:S(2)}) %collective-permute-start.15) | collective-permute-done | bytes 65568 | tf_op jit(solution)/shard_map/ppermute | solution.py:51
  48.3 1.5 %collective-permute-start.17 = (bf16[8,32,128]{2,1,0:T(8,128)(2,1)S(1)}, bf16[8,32,128]{2,1,0:T(8,128)(2,1)S(1)}, u32[]{:S(2)}, u32[]{:S(2)}) collective-permute-start(bf16[8,32,128]{2,1,0:T(8,128)(2,1)S(1)} %get-tuple-element.100), channel_id=1, source_target_pairs={{0,3},{1,8},{2,11},{3,0},{4,13},{5,6},{6,5},{7,14},{8,1},{9,10},{1... | collective-permute-start | bytes 196616 | tf_op jit(solution)/shard_map/ppermute | solution.py:51
  49.8 2.3 %collective-permute-done.17.refs_0_ = bf16[8,32,128]{2,1,0:T(8,128)(2,1)S(1)} collective-permute-done((bf16[8,32,128]{2,1,0:T(8,128)(2,1)S(1)}, bf16[8,32,128]{2,1,0:T(8,128)(2,1)S(1)}, u32[]{:S(2)}, u32[]{:S(2)}) %collective-permute-start.17) | collective-permute-done | bytes 65568 | tf_op jit(solution)/shard_map/ppermute | solution.py:51
  55.6 3.9 %collective-permute-start.22 = (bf16[8,32,128]{2,1,0:T(8,128)(2,1)S(1)}, bf16[8,32,128]{2,1,0:T(8,128)(2,1)S(1)}, u32[]{:S(2)}, u32[]{:S(2)}) collective-permute-start(bf16[8,32,128]{2,1,0:T(8,128)(2,1)S(1)} %get-tuple-element.103), channel_id=1, source_target_pairs={{0,12},{1,7},{2,4},{3,15},{4,2},{5,9},{6,10},{7,1},{8,14},{9,5},{1... | collective-permute-start | bytes 196616 | tf_op jit(solution)/shard_map/ppermute | solution.py:51
  59.9 2.5 %collective-permute-done.22.refs_2_ = bf16[8,32,128]{2,1,0:T(8,128)(2,1)S(1)} collective-permute-done((bf16[8,32,128]{2,1,0:T(8,128)(2,1)S(1)}, bf16[8,32,128]{2,1,0:T(8,128)(2,1)S(1)}, u32[]{:S(2)}, u32[]{:S(2)}) %collective-permute-start.22) | collective-permute-done | bytes 65568 | tf_op jit(solution)/shard_map/ppermute | solution.py:51
  62.4 1.7 %collective-permute-done.21.refs_1_ = bf16[8,32,128]{2,1,0:T(8,128)(2,1)S(1)} collective-permute-done((bf16[8,32,128]{2,1,0:T(8,128)(2,1)S(1)}, bf16[8,32,128]{2,1,0:T(8,128)(2,1)S(1)}, u32[]{:S(2)}, u32[]{:S(2)}) %collective-permute-start.21) | collective-permute-done | bytes 65568 | tf_op jit(solution)/shard_map/ppermute | solution.py:51
  65.4 2.5 %collective-permute-done.23.refs_0_ = bf16[8,32,128]{2,1,0:T(8,128)(2,1)S(1)} collective-permute-done((bf16[8,32,128]{2,1,0:T(8,128)(2,1)S(1)}, bf16[8,32,128]{2,1,0:T(8,128)(2,1)S(1)}, u32[]{:S(2)}, u32[]{:S(2)}) %collective-permute-start.23) | collective-permute-done | bytes 65568 | tf_op jit(solution)/shard_map/ppermute | solution.py:51
  (64 shorter events, 19.2 us)
Async XLA Ops:
  1.6 7.3 %collective-permute-start.1 = (bf16[144,256]{1,0:T(8,128)(2,1)S(1)}, bf16[144,256]{1,0:T(8,128)(2,1)S(1)}, u32[]{:S(2)}, u32[]{:S(2)}) collective-permute-start(bf16[144,256]{1,0:T(8,128)(2,1)S(1)} %shard_map.67), channel_id=1, source_target_pairs={{0,3},{1,2},{2,1},{3,0},{4,7},{5,6},{6,5},{7,4},{8,11},{9,10},{10,... | collective-permute-start | bytes 221192 | tf_op jit(solution)/shard_map/ppermute | solution.py:51
  4.1 5.0 %collective-permute-start = (bf16[144,256]{1,0:T(8,128)(2,1)S(1)}, bf16[144,256]{1,0:T(8,128)(2,1)S(1)}, u32[]{:S(2)}, u32[]{:S(2)}) collective-permute-start(bf16[144,256]{1,0:T(8,128)(2,1)S(1)} %shard_map.67), channel_id=1, source_target_pairs={{0,9},{1,4},{2,7},{3,10},{4,1},{5,12},{6,15},{7,2},{8,13},{9,0},{1... | collective-permute-start | bytes 221192 | tf_op jit(solution)/shard_map/ppermute | solution.py:51
  9.1 5.8 %collective-permute-start.4 = (bf16[1024,256]{1,0:T(8,128)(2,1)S(1)}, bf16[1024,256]{1,0:T(8,128)(2,1)S(1)}, u32[]{:S(2)}, u32[]{:S(2)}) collective-permute-start(bf16[1024,256]{1,0:T(8,128)(2,1)S(1)} %fusion.2.own_ref), channel_id=1, source_target_pairs={{0,1},{1,0},{2,3},{3,2},{4,5},{5,4},{6,7},{7,6},{8,9},{9,8},{10,11... | collective-permute-start | bytes 1572872 | tf_op jit(solution)/shard_map/ppermute | solution.py:56
  9.3 5.6 %collective-permute-start.2 = (bf16[288,256]{1,0:T(8,128)(2,1)S(1)}, bf16[288,256]{1,0:T(8,128)(2,1)S(1)}, u32[]{:S(2)}, u32[]{:S(2)}) collective-permute-start(bf16[288,256]{1,0:T(8,128)(2,1)S(1)} %pad_maximum_fusion.1), channel_id=1, source_target_pairs={{0,5},{1,8},{2,11},{3,6},{4,13},{5,0},{6,3},{7,14},{8,1},{9,12},{1... | collective-permute-start | bytes 442376 | tf_op jit(solution)/shard_map/ppermute | solution.py:51
  10.9 3.8 %collective-permute-start.3 = (bf16[144,256]{1,0:T(8,128)(2,1)S(1)}, bf16[144,256]{1,0:T(8,128)(2,1)S(1)}, u32[]{:S(2)}, u32[]{:S(2)}) collective-permute-start(bf16[144,256]{1,0:T(8,128)(2,1)S(1)} %collective-permute-done), channel_id=1, source_target_pairs={{0,3},{1,2},{2,1},{3,0},{4,7},{5,6},{6,5},{7,4},{8,11},{9,10},{10,... | collective-permute-start | bytes 221192 | tf_op jit(solution)/shard_map/ppermute | solution.py:51
  11.1 2.6 %collective-permute-start.5 = (s32[8,128]{1,0:T(8,128)S(1)}, s32[8,128]{1,0:T(8,128)S(1)}, u32[]{:S(2)}, u32[]{:S(2)}) collective-permute-start(s32[8,128]{1,0:T(8,128)S(1)} %bitcast.5), channel_id=1, source_target_pairs={{0,1},{1,0},{2,3},{3,2},{4,5},{5,4},{6,7},{7,6},{8,9},{9,8},{10,11... | collective-permute-start | bytes 12296 | tf_op jit(solution)/shard_map/ppermute | solution.py:56
  14.9 5.1 %collective-permute-start.6 = (bf16[288,256]{1,0:T(8,128)(2,1)S(1)}, bf16[288,256]{1,0:T(8,128)(2,1)S(1)}, u32[]{:S(2)}, u32[]{:S(2)}) collective-permute-start(bf16[288,256]{1,0:T(8,128)(2,1)S(1)} %collective-permute-done.2), channel_id=1, source_target_pairs={{0,3},{1,2},{2,1},{3,0},{4,7},{5,6},{6,5},{7,4},{8,11},{9,10},{10,... | collective-permute-start | bytes 442376 | tf_op jit(solution)/shard_map/ppermute | solution.py:51
  21.0 1.8 %collective-permute-start.7 = (f32[24,128]{1,0:T(8,128)S(1)}, f32[24,128]{1,0:T(8,128)S(1)}, u32[]{:S(2)}, u32[]{:S(2)}) collective-permute-start(f32[24,128]{1,0:T(8,128)S(1)} %shard_map.71.mine_ref), channel_id=1, source_target_pairs={{0,1},{1,0},{2,3},{3,2},{4,5},{5,4},{6,7},{7,6},{8,9},{9,8},{10,11... | collective-permute-start | bytes 36872 | tf_op jit(solution)/shard_map/ppermute | solution.py:56
  23.8 6.8 %collective-permute-start.10 = (bf16[8,32,128]{2,1,0:T(8,128)(2,1)S(1)}, bf16[8,32,128]{2,1,0:T(8,128)(2,1)S(1)}, u32[]{:S(2)}, u32[]{:S(2)}) collective-permute-start(bf16[8,32,128]{2,1,0:T(8,128)(2,1)S(1)} %get-tuple-element.92), channel_id=1, source_target_pairs={{0,12},{1,7},{2,4},{3,15},{4,2},{5,9},{6,10},{7,1},{8,14},{9,5},{1... | collective-permute-start | bytes 196616 | tf_op jit(solution)/shard_map/ppermute | solution.py:51
  27.6 5.3 %collective-permute-start.9 = (bf16[8,32,128]{2,1,0:T(8,128)(2,1)S(1)}, bf16[8,32,128]{2,1,0:T(8,128)(2,1)S(1)}, u32[]{:S(2)}, u32[]{:S(2)}) collective-permute-start(bf16[8,32,128]{2,1,0:T(8,128)(2,1)S(1)} %get-tuple-element.92), channel_id=1, source_target_pairs={{0,9},{1,4},{2,7},{3,10},{4,1},{5,12},{6,15},{7,2},{8,13},{9,0},{1... | collective-permute-start | bytes 196616 | tf_op jit(solution)/shard_map/ppermute | solution.py:51
  27.9 5.0 %collective-permute-start.8 = (bf16[8,32,128]{2,1,0:T(8,128)(2,1)S(1)}, bf16[8,32,128]{2,1,0:T(8,128)(2,1)S(1)}, u32[]{:S(2)}, u32[]{:S(2)}) collective-permute-start(bf16[8,32,128]{2,1,0:T(8,128)(2,1)S(1)} %get-tuple-element.92), channel_id=1, source_target_pairs={{0,5},{1,2},{2,1},{3,6},{4,7},{5,0},{6,3},{7,4},{8,11},{9,12},{10,... | collective-permute-start | bytes 196616 | tf_op jit(solution)/shard_map/ppermute | solution.py:51
  32.9 3.8 %collective-permute-start.11 = (bf16[8,32,128]{2,1,0:T(8,128)(2,1)S(1)}, bf16[8,32,128]{2,1,0:T(8,128)(2,1)S(1)}, u32[]{:S(2)}, u32[]{:S(2)}) collective-permute-start(bf16[8,32,128]{2,1,0:T(8,128)(2,1)S(1)} %get-tuple-element.94), channel_id=1, source_target_pairs={{0,3},{1,8},{2,11},{3,0},{4,13},{5,6},{6,5},{7,14},{8,1},{9,10},{1... | collective-permute-start | bytes 196616 | tf_op jit(solution)/shard_map/ppermute | solution.py:51
  37.5 1.4 %collective-permute-start.13 = (f32[32,1024]{1,0:T(8,128)S(1)}, f32[32,1024]{1,0:T(8,128)S(1)}, u32[]{:S(2)}, u32[]{:S(2)}) collective-permute-start(f32[32,1024]{1,0:T(8,128)S(1)} %shard_map.76.image_ref), channel_id=1, source_target_pairs={{0,1},{1,0},{2,3},{3,2},{4,5},{5,4},{6,7},{7,6},{8,9},{9,8},{10,11... | collective-permute-start | bytes 393224 | tf_op jit(solution)/shard_map/ppermute | solution.py:56
  38.3 1.5 %collective-permute-start.12 = (f32[32,1024]{1,0:T(8,128)S(1)}, f32[32,1024]{1,0:T(8,128)S(1)}, u32[]{:S(2)}, u32[]{:S(2)}) collective-permute-start(f32[32,1024]{1,0:T(8,128)S(1)} %shard_map.77.image_ref), channel_id=1, source_target_pairs={{0,1},{1,0},{2,3},{3,2},{4,5},{5,4},{6,7},{7,6},{8,9},{9,8},{10,11... | collective-permute-start | bytes 393224 | tf_op jit(solution)/shard_map/ppermute | solution.py:56
  40.2 6.6 %collective-permute-start.16 = (bf16[8,32,128]{2,1,0:T(8,128)(2,1)S(1)}, bf16[8,32,128]{2,1,0:T(8,128)(2,1)S(1)}, u32[]{:S(2)}, u32[]{:S(2)}) collective-permute-start(bf16[8,32,128]{2,1,0:T(8,128)(2,1)S(1)} %get-tuple-element.98), channel_id=1, source_target_pairs={{0,12},{1,7},{2,4},{3,15},{4,2},{5,9},{6,10},{7,1},{8,14},{9,5},{1... | collective-permute-start | bytes 196616 | tf_op jit(solution)/shard_map/ppermute | solution.py:51
  43.7 4.6 %collective-permute-start.15 = (bf16[8,32,128]{2,1,0:T(8,128)(2,1)S(1)}, bf16[8,32,128]{2,1,0:T(8,128)(2,1)S(1)}, u32[]{:S(2)}, u32[]{:S(2)}) collective-permute-start(bf16[8,32,128]{2,1,0:T(8,128)(2,1)S(1)} %get-tuple-element.98), channel_id=1, source_target_pairs={{0,9},{1,4},{2,7},{3,10},{4,1},{5,12},{6,15},{7,2},{8,13},{9,0},{1... | collective-permute-start | bytes 196616 | tf_op jit(solution)/shard_map/ppermute | solution.py:51
  43.7 4.6 %collective-permute-start.14 = (bf16[8,32,128]{2,1,0:T(8,128)(2,1)S(1)}, bf16[8,32,128]{2,1,0:T(8,128)(2,1)S(1)}, u32[]{:S(2)}, u32[]{:S(2)}) collective-permute-start(bf16[8,32,128]{2,1,0:T(8,128)(2,1)S(1)} %get-tuple-element.98), channel_id=1, source_target_pairs={{0,5},{1,2},{2,1},{3,6},{4,7},{5,0},{6,3},{7,4},{8,11},{9,12},{10,... | collective-permute-start | bytes 196616 | tf_op jit(solution)/shard_map/ppermute | solution.py:51
  48.3 3.8 %collective-permute-start.17 = (bf16[8,32,128]{2,1,0:T(8,128)(2,1)S(1)}, bf16[8,32,128]{2,1,0:T(8,128)(2,1)S(1)}, u32[]{:S(2)}, u32[]{:S(2)}) collective-permute-start(bf16[8,32,128]{2,1,0:T(8,128)(2,1)S(1)} %get-tuple-element.100), channel_id=1, source_target_pairs={{0,3},{1,8},{2,11},{3,0},{4,13},{5,6},{6,5},{7,14},{8,1},{9,10},{1... | collective-permute-start | bytes 196616 | tf_op jit(solution)/shard_map/ppermute | solution.py:51
  52.8 1.4 %collective-permute-start.19 = (f32[32,1024]{1,0:T(8,128)S(1)}, f32[32,1024]{1,0:T(8,128)S(1)}, u32[]{:S(2)}, u32[]{:S(2)}) collective-permute-start(f32[32,1024]{1,0:T(8,128)S(1)} %shard_map.82.image_ref), channel_id=1, source_target_pairs={{0,1},{1,0},{2,3},{3,2},{4,5},{5,4},{6,7},{7,6},{8,9},{9,8},{10,11... | collective-permute-start | bytes 393224 | tf_op jit(solution)/shard_map/ppermute | solution.py:56
  53.6 1.5 %collective-permute-start.18 = (f32[32,1024]{1,0:T(8,128)S(1)}, f32[32,1024]{1,0:T(8,128)S(1)}, u32[]{:S(2)}, u32[]{:S(2)}) collective-permute-start(f32[32,1024]{1,0:T(8,128)S(1)} %shard_map.83.image_ref), channel_id=1, source_target_pairs={{0,1},{1,0},{2,3},{3,2},{4,5},{5,4},{6,7},{7,6},{8,9},{9,8},{10,11... | collective-permute-start | bytes 393224 | tf_op jit(solution)/shard_map/ppermute | solution.py:56
  55.6 6.8 %collective-permute-start.22 = (bf16[8,32,128]{2,1,0:T(8,128)(2,1)S(1)}, bf16[8,32,128]{2,1,0:T(8,128)(2,1)S(1)}, u32[]{:S(2)}, u32[]{:S(2)}) collective-permute-start(bf16[8,32,128]{2,1,0:T(8,128)(2,1)S(1)} %get-tuple-element.103), channel_id=1, source_target_pairs={{0,12},{1,7},{2,4},{3,15},{4,2},{5,9},{6,10},{7,1},{8,14},{9,5},{1... | collective-permute-start | bytes 196616 | tf_op jit(solution)/shard_map/ppermute | solution.py:51
  59.5 4.6 %collective-permute-start.21 = (bf16[8,32,128]{2,1,0:T(8,128)(2,1)S(1)}, bf16[8,32,128]{2,1,0:T(8,128)(2,1)S(1)}, u32[]{:S(2)}, u32[]{:S(2)}) collective-permute-start(bf16[8,32,128]{2,1,0:T(8,128)(2,1)S(1)} %get-tuple-element.103), channel_id=1, source_target_pairs={{0,9},{1,4},{2,7},{3,10},{4,1},{5,12},{6,15},{7,2},{8,13},{9,0},{1... | collective-permute-start | bytes 196616 | tf_op jit(solution)/shard_map/ppermute | solution.py:51
  59.5 4.6 %collective-permute-start.20 = (bf16[8,32,128]{2,1,0:T(8,128)(2,1)S(1)}, bf16[8,32,128]{2,1,0:T(8,128)(2,1)S(1)}, u32[]{:S(2)}, u32[]{:S(2)}) collective-permute-start(bf16[8,32,128]{2,1,0:T(8,128)(2,1)S(1)} %get-tuple-element.103), channel_id=1, source_target_pairs={{0,5},{1,2},{2,1},{3,6},{4,7},{5,0},{6,3},{7,4},{8,11},{9,12},{10,... | collective-permute-start | bytes 196616 | tf_op jit(solution)/shard_map/ppermute | solution.py:51
  64.2 3.8 %collective-permute-start.23 = (bf16[8,32,128]{2,1,0:T(8,128)(2,1)S(1)}, bf16[8,32,128]{2,1,0:T(8,128)(2,1)S(1)}, u32[]{:S(2)}, u32[]{:S(2)}) collective-permute-start(bf16[8,32,128]{2,1,0:T(8,128)(2,1)S(1)} %get-tuple-element.104), channel_id=1, source_target_pairs={{0,3},{1,8},{2,11},{3,0},{4,13},{5,6},{6,5},{7,14},{8,1},{9,10},{1... | collective-permute-start | bytes 196616 | tf_op jit(solution)/shard_map/ppermute | solution.py:51
  (3 other events, 9.7 us)

commit v19 on v15

--- a/solution.py
+++ b/solution.py
@@ -156,17 +156,21 @@
                 sums_ref[row : row + TILE, :] = sums
 
 
-def image_of(kernels, scale_ref):
-    image = 0.0
-    first = 0
-    for kernel_ref in kernels:
-        slots = kernel_ref.shape[1] // scale_ref.shape[2]
-        scale_v = jnp.concatenate([scale_ref[s] for s in range(first, first + slots)], axis=1)
-        image += lax.dot_general(
-            kernel_ref[...], scale_v, (((1,), (1,)), ((), ())), preferred_element_type=F32
-        )
-        first += slots
-    return image.T
+def turned_body(own_ref, other_ref, held_ref, *out_refs, tgt_rows):
+    rows = tgt_rows + EXTRA
+    for s in range(held_ref.shape[0] // rows):
+        tgt_unit = unit_rows(held_ref[pl.ds(s * rows, tgt_rows), :])
+        for cand_ref, out_ref in zip((own_ref, other_ref), out_refs):
+            for row in range(0, cand_ref.shape[0], TILE):
+                scores = lax.dot_general(
+                    tgt_unit,
+                    cand_ref[row : row + TILE, :],
+                    (((1,), (1,)), ((), ())),
+                    preferred_element_type=F32,
+                )
+                out_ref[s * tgt_rows : (s + 1) * tgt_rows, row : row + TILE] = jnp.exp(
+                    INVERSE_TEMP * scores
+                ).astype(BF16)
 
 
 def put_column(scale_ub, kernels, added, out_refs):
@@ -243,7 +247,15 @@
 
 
 def image_body(scale_ref, *refs):
-    refs[-1][...] = image_of(refs[:-1], scale_ref)
+    *turned, image_ref = refs
+    image = 0.0
+    first = 0
+    for turned_ref in turned:
+        slots = turned_ref.shape[0] // scale_ref.shape[2]
+        scale_v = jnp.concatenate([scale_ref[s] for s in range(first, first + slots)], axis=1)
+        image += jnp.dot(scale_v, turned_ref[...], preferred_element_type=F32)
+        first += slots
+    image_ref[...] = image
 
 
 def own_body(image_ref, got_ref, marg_ref, *refs, parts):
@@ -353,6 +365,20 @@
         [image_type, image_type, (block, F32), (block, BF16)],
         weight, other_weight, mine, got, *own_kernels, *other_kernels, flops=2 * half_flops,
     )
+    sent, cand_unit, other_unit, near = lax.optimization_barrier(
+        (sent, cand_unit, other_unit, near)
+    )
+    turned = []
+    for part in near:
+        columns = part.shape[0] // (tgt_rows + EXTRA) * tgt_rows
+        turned.append(
+            call(
+                functools.partial(turned_body, tgt_rows=tgt_rows),
+                [((columns, cand_rows), BF16)] * 2,
+                cand_unit, other_unit, part, flops=8 * 2 * cand_rows * columns * 128,
+            )
+        )
+    own_turned, other_turned = zip(*turned)
     (tgt_marg,) = call(
         functools.partial(target_body, targets=float(tgt_rows * devices)),
         [(block, F32)], mine, got, *near,
@@ -387,10 +413,10 @@
             column, tgt_marg, *found,
         )
         (other_image,) = call(
-            image_body, [image_type], scale_vb, *other_kernels, flops=half_flops
+            image_body, [image_type], scale_vb, *other_turned, flops=half_flops
         )
         own_got = swap(other_image)
-        (own_image,) = call(image_body, [image_type], scale_vb, *own_kernels, flops=half_flops)
+        (own_image,) = call(image_body, [image_type], scale_vb, *own_turned, flops=half_flops)
         if not last:
             other_got = swap(own_image)
     space = pl.BlockSpec(memory_space=pltpu.VMEM)

time: 70.8 us -> 70.8 us (level)
  waiting for transfers between devices: 28.2 us -> 24.4 us
  starting transfers between devices: 27.2 us -> 29.4 us
  Pallas kernels: 11.7 us -> 13.3 us
    ppermute x17, waiting for transfers between devices: 24.8 us -> 20.8 us  [exchange(): return lax.ppermute(block, 'row', pairs)]
    ppermute x17, starting transfers between devices: 23 us -> 25.6 us  [exchange(): return lax.ppermute(block, 'row', pairs)]
    pallas_call x22 -> x25, Pallas kernels: 10 us -> 11.6 us  [call(): pl.pallas_call(body, out_shape=[pltpu.VMEM(shape, dtype) for shape, dtype...]
  transfers between devices with their start and end apart: 25 -> 25, of which waited for: 20 -> 19; matrix products, arithmetic and copies ran while one was open for 3% -> 3% of each run, Pallas kernels for 7% -> 10%
where the time goes in v19:
time: 70.8 us; the launch traced here: 70.6 us
  starting transfers between devices  29.4 us (42%)
  waiting for transfers between devices  24.4 us (34%)
  Pallas kernels  13.3 us (19%)
  other arithmetic  2.21 us (3%)
  between operations  0.85 us (1%)
    ppermute x17, starting transfers between devices, exchange(): return lax.ppermute(block, 'row', pairs)  25.6 us
    ppermute x17, waiting for transfers between devices, exchange(): return lax.ppermute(block, 'row', pairs)  20.8 us
    pallas_call x25, Pallas kernels, call(): pl.pallas_call(body, out_shape=[pltpu.VMEM(shape, dtype) for shape, dtype...  11.6 us
    ppermute x8, starting transfers between devices, swap(): return lax.ppermute(block, 'row', [(d, d ^ 1) for d in range(devices)])  3.79 us
    ppermute x8, waiting for transfers between devices, swap(): return lax.ppermute(block, 'row', [(d, d ^ 1) for d in range(devices)])  3.63 us
  transfers between devices with their start and end apart: 25, of which 19 were waited for; matrix products, arithmetic and copies ran while one was open for 3% of the time, Pallas kernels for 10%

profile of v19, /device:TPU:0, one launch (start us, length us, event | category | flops | bytes accessed | tf_op | source)
XLA Modules:
  0.0 70.6 jit_solution(12507242694145035009)
XLA Ops:
  1.6 3.5 %collective-permute-start = (bf16[144,256]{1,0:T(8,128)(2,1)S(1)}, bf16[144,256]{1,0:T(8,128)(2,1)S(1)}, u32[]{:S(2)}, u32[]{:S(2)}) collective-permute-start(bf16[144,256]{1,0:T(8,128)(2,1)S(1)} %shard_map.67), channel_id=1, source_target_pairs={{0,9},{1,4},{2,7},{3,10},{4,1},{5,12},{6,15},{7,2},{8,13},{9,0},{1... | collective-permute-start | bytes 221192 | tf_op jit(solution)/shard_map/ppermute | solution.py:51
  5.1 1.8 %collective-permute-start.1 = (bf16[144,256]{1,0:T(8,128)(2,1)S(1)}, bf16[144,256]{1,0:T(8,128)(2,1)S(1)}, u32[]{:S(2)}, u32[]{:S(2)}) collective-permute-start(bf16[144,256]{1,0:T(8,128)(2,1)S(1)} %shard_map.67), channel_id=1, source_target_pairs={{0,3},{1,2},{2,1},{3,0},{4,7},{5,6},{6,5},{7,4},{8,11},{9,10},{10,... | collective-permute-start | bytes 221192 | tf_op jit(solution)/shard_map/ppermute | solution.py:51
  6.9 1.3 %fusion = f32[1024]{0:T(1024)S(1)} fusion(bf16[1024,256]{1,0:T(8,128)(2,1)} %param.4), kind=kLoop, calls=%fused_computation.2 | loop fusion | flops 785408 | bytes 528384 | tf_op jit(solution)/shard_map/reduce_sum | solution.py:74
  9.6 1.3 %collective-permute-start.2 = (bf16[288,256]{1,0:T(8,128)(2,1)S(1)}, bf16[288,256]{1,0:T(8,128)(2,1)S(1)}, u32[]{:S(2)}, u32[]{:S(2)}) collective-permute-start(bf16[288,256]{1,0:T(8,128)(2,1)S(1)} %pad_maximum_fusion.1), channel_id=1, source_target_pairs={{0,5},{1,8},{2,11},{3,6},{4,13},{5,0},{6,3},{7,14},{8,1},{9,12},{1... | collective-permute-start | bytes 442376 | tf_op jit(solution)/shard_map/ppermute | solution.py:51
  13.3 2.0 %collective-permute-done.3 = bf16[144,256]{1,0:T(8,128)(2,1)S(1)} collective-permute-done((bf16[144,256]{1,0:T(8,128)(2,1)S(1)}, bf16[144,256]{1,0:T(8,128)(2,1)S(1)}, u32[]{:S(2)}, u32[]{:S(2)}) %collective-permute-start.3) | collective-permute-done | bytes 73760 | tf_op jit(solution)/shard_map/ppermute | solution.py:51
  15.3 1.7 %collective-permute-start.6 = (bf16[288,256]{1,0:T(8,128)(2,1)S(1)}, bf16[288,256]{1,0:T(8,128)(2,1)S(1)}, u32[]{:S(2)}, u32[]{:S(2)}) collective-permute-start(bf16[288,256]{1,0:T(8,128)(2,1)S(1)} %collective-permute-done.2), channel_id=1, source_target_pairs={{0,3},{1,2},{2,1},{3,0},{4,7},{5,6},{6,5},{7,4},{8,11},{9,10},{10,... | collective-permute-start | bytes 442376 | tf_op jit(solution)/shard_map/ppermute | solution.py:51
  18.7 2.3 %collective-permute-done.6.held_ref.refs_8_.refs_2_ = bf16[288,256]{1,0:T(8,128)(2,1)S(1)} collective-permute-done((bf16[288,256]{1,0:T(8,128)(2,1)S(1)}, bf16[288,256]{1,0:T(8,128)(2,1)S(1)}, u32[]{:S(2)}, u32[]{:S(2)}) %collective-permute-start.6) | collective-permute-done | bytes 147488 | tf_op jit(solution)/shard_map/ppermute | solution.py:51
  24.6 1.7 %collective-permute-start.8 = (bf16[8,32,128]{2,1,0:T(8,128)(2,1)S(1)}, bf16[8,32,128]{2,1,0:T(8,128)(2,1)S(1)}, u32[]{:S(2)}, u32[]{:S(2)}) collective-permute-start(bf16[8,32,128]{2,1,0:T(8,128)(2,1)S(1)} %get-tuple-element.105), channel_id=1, source_target_pairs={{0,5},{1,2},{2,1},{3,6},{4,7},{5,0},{6,3},{7,4},{8,11},{9,12},{10,... | collective-permute-start | bytes 196616 | tf_op jit(solution)/shard_map/ppermute | solution.py:51
  26.6 2.1 %collective-permute-start.10 = (bf16[8,32,128]{2,1,0:T(8,128)(2,1)S(1)}, bf16[8,32,128]{2,1,0:T(8,128)(2,1)S(1)}, u32[]{:S(2)}, u32[]{:S(2)}) collective-permute-start(bf16[8,32,128]{2,1,0:T(8,128)(2,1)S(1)} %get-tuple-element.105), channel_id=1, source_target_pairs={{0,12},{1,7},{2,4},{3,15},{4,2},{5,9},{6,10},{7,1},{8,14},{9,5},{1... | collective-permute-start | bytes 196616 | tf_op jit(solution)/shard_map/ppermute | solution.py:51
  28.7 1.5 %shard_map.76 = (bf16[512,1024]{1,0:T(8,128)(2,1)S(1)}, bf16[512,1024]{1,0:T(8,128)(2,1)S(1)}) custom-call(bf16[1024,256]{1,0:T(8,128)(2,1)S(1)} %fusion.2.own_ref, bf16[1024,256]{1,0:T(8,128)(2,1)S(1)} %collective-permute-done.4.other_ref, bf16[576,256]{1,0:T(8,128)(2,1)S(1)} %pad_maximum_fusion.held_ref.refs_6_.refs_0_), custom_call_target="tpu_custom_call" | custom-call | flops 1073741824 | bytes 1343488 | tf_op jit(solution)/shard_map/pallas_call | solution.py:62
  30.3 1.3 %collective-permute-done.9.refs_1_ = bf16[8,32,128]{2,1,0:T(8,128)(2,1)S(1)} collective-permute-done((bf16[8,32,128]{2,1,0:T(8,128)(2,1)S(1)}, bf16[8,32,128]{2,1,0:T(8,128)(2,1)S(1)}, u32[]{:S(2)}, u32[]{:S(2)}) %collective-permute-start.9) | collective-permute-done | bytes 65568 | tf_op jit(solution)/shard_map/ppermute | solution.py:51
  31.6 1.3 %collective-permute-done.10.refs_2_ = bf16[8,32,128]{2,1,0:T(8,128)(2,1)S(1)} collective-permute-done((bf16[8,32,128]{2,1,0:T(8,128)(2,1)S(1)}, bf16[8,32,128]{2,1,0:T(8,128)(2,1)S(1)}, u32[]{:S(2)}, u32[]{:S(2)}) %collective-permute-start.10) | collective-permute-done | bytes 65568 | tf_op jit(solution)/shard_map/ppermute | solution.py:51
  32.9 1.8 %collective-permute-start.11 = (bf16[8,32,128]{2,1,0:T(8,128)(2,1)S(1)}, bf16[8,32,128]{2,1,0:T(8,128)(2,1)S(1)}, u32[]{:S(2)}, u32[]{:S(2)}) collective-permute-start(bf16[8,32,128]{2,1,0:T(8,128)(2,1)S(1)} %get-tuple-element.110), channel_id=1, source_target_pairs={{0,3},{1,8},{2,11},{3,0},{4,13},{5,6},{6,5},{7,14},{8,1},{9,10},{1... | collective-permute-start | bytes 196616 | tf_op jit(solution)/shard_map/ppermute | solution.py:51
  40.1 1.6 %collective-permute-start.14 = (bf16[8,32,128]{2,1,0:T(8,128)(2,1)S(1)}, bf16[8,32,128]{2,1,0:T(8,128)(2,1)S(1)}, u32[]{:S(2)}, u32[]{:S(2)}) collective-permute-start(bf16[8,32,128]{2,1,0:T(8,128)(2,1)S(1)} %get-tuple-element.122), channel_id=1, source_target_pairs={{0,5},{1,2},{2,1},{3,6},{4,7},{5,0},{6,3},{7,4},{8,11},{9,12},{10,... | collective-permute-start | bytes 196616 | tf_op jit(solution)/shard_map/ppermute | solution.py:51
  41.7 1.2 %collective-permute-start.15 = (bf16[8,32,128]{2,1,0:T(8,128)(2,1)S(1)}, bf16[8,32,128]{2,1,0:T(8,128)(2,1)S(1)}, u32[]{:S(2)}, u32[]{:S(2)}) collective-permute-start(bf16[8,32,128]{2,1,0:T(8,128)(2,1)S(1)} %get-tuple-element.122), channel_id=1, source_target_pairs={{0,9},{1,4},{2,7},{3,10},{4,1},{5,12},{6,15},{7,2},{8,13},{9,0},{1... | collective-permute-start | bytes 196616 | tf_op jit(solution)/shard_map/ppermute | solution.py:51
  42.8 1.4 %collective-permute-start.16 = (bf16[8,32,128]{2,1,0:T(8,128)(2,1)S(1)}, bf16[8,32,128]{2,1,0:T(8,128)(2,1)S(1)}, u32[]{:S(2)}, u32[]{:S(2)}) collective-permute-start(bf16[8,32,128]{2,1,0:T(8,128)(2,1)S(1)} %get-tuple-element.122), channel_id=1, source_target_pairs={{0,12},{1,7},{2,4},{3,15},{4,2},{5,9},{6,10},{7,1},{8,14},{9,5},{1... | collective-permute-start | bytes 196616 | tf_op jit(solution)/shard_map/ppermute | solution.py:51
  44.2 2.1 %collective-permute-done.15.refs_1_ = bf16[8,32,128]{2,1,0:T(8,128)(2,1)S(1)} collective-permute-done((bf16[8,32,128]{2,1,0:T(8,128)(2,1)S(1)}, bf16[8,32,128]{2,1,0:T(8,128)(2,1)S(1)}, u32[]{:S(2)}, u32[]{:S(2)}) %collective-permute-start.15) | collective-permute-done | bytes 65568 | tf_op jit(solution)/shard_map/ppermute | solution.py:51
  46.4 2.6 %collective-permute-done.16.refs_2_ = bf16[8,32,128]{2,1,0:T(8,128)(2,1)S(1)} collective-permute-done((bf16[8,32,128]{2,1,0:T(8,128)(2,1)S(1)}, bf16[8,32,128]{2,1,0:T(8,128)(2,1)S(1)}, u32[]{:S(2)}, u32[]{:S(2)}) %collective-permute-start.16) | collective-permute-done | bytes 65568 | tf_op jit(solution)/shard_map/ppermute | solution.py:51
  49.3 3.5 %collective-permute-done.17.refs_0_ = bf16[8,32,128]{2,1,0:T(8,128)(2,1)S(1)} collective-permute-done((bf16[8,32,128]{2,1,0:T(8,128)(2,1)S(1)}, bf16[8,32,128]{2,1,0:T(8,128)(2,1)S(1)}, u32[]{:S(2)}, u32[]{:S(2)}) %collective-permute-start.17) | collective-permute-done | bytes 65568 | tf_op jit(solution)/shard_map/ppermute | solution.py:51
  57.5 2.4 %collective-permute-start.22 = (bf16[8,32,128]{2,1,0:T(8,128)(2,1)S(1)}, bf16[8,32,128]{2,1,0:T(8,128)(2,1)S(1)}, u32[]{:S(2)}, u32[]{:S(2)}) collective-permute-start(bf16[8,32,128]{2,1,0:T(8,128)(2,1)S(1)} %get-tuple-element.127), channel_id=1, source_target_pairs={{0,12},{1,7},{2,4},{3,15},{4,2},{5,9},{6,10},{7,1},{8,14},{9,5},{1... | collective-permute-start | bytes 196616 | tf_op jit(solution)/shard_map/ppermute | solution.py:51
  59.9 1.6 %collective-permute-done.21.refs_1_ = bf16[8,32,128]{2,1,0:T(8,128)(2,1)S(1)} collective-permute-done((bf16[8,32,128]{2,1,0:T(8,128)(2,1)S(1)}, bf16[8,32,128]{2,1,0:T(8,128)(2,1)S(1)}, u32[]{:S(2)}, u32[]{:S(2)}) %collective-permute-start.21) | collective-permute-done | bytes 65568 | tf_op jit(solution)/shard_map/ppermute | solution.py:51
  61.5 2.2 %collective-permute-done.22.refs_2_ = bf16[8,32,128]{2,1,0:T(8,128)(2,1)S(1)} collective-permute-done((bf16[8,32,128]{2,1,0:T(8,128)(2,1)S(1)}, bf16[8,32,128]{2,1,0:T(8,128)(2,1)S(1)}, u32[]{:S(2)}, u32[]{:S(2)}) %collective-permute-start.22) | collective-permute-done | bytes 65568 | tf_op jit(solution)/shard_map/ppermute | solution.py:51
  63.7 1.8 %collective-permute-start.23 = (bf16[8,32,128]{2,1,0:T(8,128)(2,1)S(1)}, bf16[8,32,128]{2,1,0:T(8,128)(2,1)S(1)}, u32[]{:S(2)}, u32[]{:S(2)}) collective-permute-start(bf16[8,32,128]{2,1,0:T(8,128)(2,1)S(1)} %get-tuple-element.128), channel_id=1, source_target_pairs={{0,3},{1,8},{2,11},{3,0},{4,13},{5,6},{6,5},{7,14},{8,1},{9,10},{1... | collective-permute-start | bytes 196616 | tf_op jit(solution)/shard_map/ppermute | solution.py:51
  66.2 1.3 %collective-permute-done.23.refs_0_ = bf16[8,32,128]{2,1,0:T(8,128)(2,1)S(1)} collective-permute-done((bf16[8,32,128]{2,1,0:T(8,128)(2,1)S(1)}, bf16[8,32,128]{2,1,0:T(8,128)(2,1)S(1)}, u32[]{:S(2)}, u32[]{:S(2)}) %collective-permute-start.23) | collective-permute-done | bytes 65568 | tf_op jit(solution)/shard_map/ppermute | solution.py:51
  (67 shorter events, 24.6 us)
Async XLA Ops:
  1.6 7.3 %collective-permute-start = (bf16[144,256]{1,0:T(8,128)(2,1)S(1)}, bf16[144,256]{1,0:T(8,128)(2,1)S(1)}, u32[]{:S(2)}, u32[]{:S(2)}) collective-permute-start(bf16[144,256]{1,0:T(8,128)(2,1)S(1)} %shard_map.67), channel_id=1, source_target_pairs={{0,9},{1,4},{2,7},{3,10},{4,1},{5,12},{6,15},{7,2},{8,13},{9,0},{1... | collective-permute-start | bytes 221192 | tf_op jit(solution)/shard_map/ppermute | solution.py:51
  5.1 4.4 %collective-permute-start.1 = (bf16[144,256]{1,0:T(8,128)(2,1)S(1)}, bf16[144,256]{1,0:T(8,128)(2,1)S(1)}, u32[]{:S(2)}, u32[]{:S(2)}) collective-permute-start(bf16[144,256]{1,0:T(8,128)(2,1)S(1)} %shard_map.67), channel_id=1, source_target_pairs={{0,3},{1,2},{2,1},{3,0},{4,7},{5,6},{6,5},{7,4},{8,11},{9,10},{10,... | collective-permute-start | bytes 221192 | tf_op jit(solution)/shard_map/ppermute | solution.py:51
  9.6 5.8 %collective-permute-start.4 = (bf16[1024,256]{1,0:T(8,128)(2,1)S(1)}, bf16[1024,256]{1,0:T(8,128)(2,1)S(1)}, u32[]{:S(2)}, u32[]{:S(2)}) collective-permute-start(bf16[1024,256]{1,0:T(8,128)(2,1)S(1)} %fusion.2.own_ref), channel_id=1, source_target_pairs={{0,1},{1,0},{2,3},{3,2},{4,5},{5,4},{6,7},{7,6},{8,9},{9,8},{10,11... | collective-permute-start | bytes 1572872 | tf_op jit(solution)/shard_map/ppermute | solution.py:56
  9.6 5.7 %collective-permute-start.2 = (bf16[288,256]{1,0:T(8,128)(2,1)S(1)}, bf16[288,256]{1,0:T(8,128)(2,1)S(1)}, u32[]{:S(2)}, u32[]{:S(2)}) collective-permute-start(bf16[288,256]{1,0:T(8,128)(2,1)S(1)} %pad_maximum_fusion.1), channel_id=1, source_target_pairs={{0,5},{1,8},{2,11},{3,6},{4,13},{5,0},{6,3},{7,14},{8,1},{9,12},{1... | collective-permute-start | bytes 442376 | tf_op jit(solution)/shard_map/ppermute | solution.py:51
  10.9 4.4 %collective-permute-start.3 = (bf16[144,256]{1,0:T(8,128)(2,1)S(1)}, bf16[144,256]{1,0:T(8,128)(2,1)S(1)}, u32[]{:S(2)}, u32[]{:S(2)}) collective-permute-start(bf16[144,256]{1,0:T(8,128)(2,1)S(1)} %collective-permute-done), channel_id=1, source_target_pairs={{0,3},{1,2},{2,1},{3,0},{4,7},{5,6},{6,5},{7,4},{8,11},{9,10},{10,... | collective-permute-start | bytes 221192 | tf_op jit(solution)/shard_map/ppermute | solution.py:51
  11.8 1.5 %collective-permute-start.5 = (s32[8,128]{1,0:T(8,128)S(1)}, s32[8,128]{1,0:T(8,128)S(1)}, u32[]{:S(2)}, u32[]{:S(2)}) collective-permute-start(s32[8,128]{1,0:T(8,128)S(1)} %bitcast.5), channel_id=1, source_target_pairs={{0,1},{1,0},{2,3},{3,2},{4,5},{5,4},{6,7},{7,6},{8,9},{9,8},{10,11... | collective-permute-start | bytes 12296 | tf_op jit(solution)/shard_map/ppermute | solution.py:56
  15.3 5.7 %collective-permute-start.6 = (bf16[288,256]{1,0:T(8,128)(2,1)S(1)}, bf16[288,256]{1,0:T(8,128)(2,1)S(1)}, u32[]{:S(2)}, u32[]{:S(2)}) collective-permute-start(bf16[288,256]{1,0:T(8,128)(2,1)S(1)} %collective-permute-done.2), channel_id=1, source_target_pairs={{0,3},{1,2},{2,1},{3,0},{4,7},{5,6},{6,5},{7,4},{8,11},{9,10},{10,... | collective-permute-start | bytes 442376 | tf_op jit(solution)/shard_map/ppermute | solution.py:51
  22.0 1.7 %collective-permute-start.7 = (f32[24,128]{1,0:T(8,128)S(1)}, f32[24,128]{1,0:T(8,128)S(1)}, u32[]{:S(2)}, u32[]{:S(2)}) collective-permute-start(f32[24,128]{1,0:T(8,128)S(1)} %shard_map.71.mine_ref), channel_id=1, source_target_pairs={{0,1},{1,0},{2,3},{3,2},{4,5},{5,4},{6,7},{7,6},{8,9},{9,8},{10,11... | collective-permute-start | bytes 36872 | tf_op jit(solution)/shard_map/ppermute | solution.py:56
  24.6 5.7 %collective-permute-start.8 = (bf16[8,32,128]{2,1,0:T(8,128)(2,1)S(1)}, bf16[8,32,128]{2,1,0:T(8,128)(2,1)S(1)}, u32[]{:S(2)}, u32[]{:S(2)}) collective-permute-start(bf16[8,32,128]{2,1,0:T(8,128)(2,1)S(1)} %get-tuple-element.105), channel_id=1, source_target_pairs={{0,5},{1,2},{2,1},{3,6},{4,7},{5,0},{6,3},{7,4},{8,11},{9,12},{10,... | collective-permute-start | bytes 196616 | tf_op jit(solution)/shard_map/ppermute | solution.py:51
  26.3 5.3 %collective-permute-start.9 = (bf16[8,32,128]{2,1,0:T(8,128)(2,1)S(1)}, bf16[8,32,128]{2,1,0:T(8,128)(2,1)S(1)}, u32[]{:S(2)}, u32[]{:S(2)}) collective-permute-start(bf16[8,32,128]{2,1,0:T(8,128)(2,1)S(1)} %get-tuple-element.105), channel_id=1, source_target_pairs={{0,9},{1,4},{2,7},{3,10},{4,1},{5,12},{6,15},{7,2},{8,13},{9,0},{1... | collective-permute-start | bytes 196616 | tf_op jit(solution)/shard_map/ppermute | solution.py:51
  26.6 6.2 %collective-permute-start.10 = (bf16[8,32,128]{2,1,0:T(8,128)(2,1)S(1)}, bf16[8,32,128]{2,1,0:T(8,128)(2,1)S(1)}, u32[]{:S(2)}, u32[]{:S(2)}) collective-permute-start(bf16[8,32,128]{2,1,0:T(8,128)(2,1)S(1)} %get-tuple-element.105), channel_id=1, source_target_pairs={{0,12},{1,7},{2,4},{3,15},{4,2},{5,9},{6,10},{7,1},{8,14},{9,5},{1... | collective-permute-start | bytes 196616 | tf_op jit(solution)/shard_map/ppermute | solution.py:51
  32.9 3.8 %collective-permute-start.11 = (bf16[8,32,128]{2,1,0:T(8,128)(2,1)S(1)}, bf16[8,32,128]{2,1,0:T(8,128)(2,1)S(1)}, u32[]{:S(2)}, u32[]{:S(2)}) collective-permute-start(bf16[8,32,128]{2,1,0:T(8,128)(2,1)S(1)} %get-tuple-element.110), channel_id=1, source_target_pairs={{0,3},{1,8},{2,11},{3,0},{4,13},{5,6},{6,5},{7,14},{8,1},{9,10},{1... | collective-permute-start | bytes 196616 | tf_op jit(solution)/shard_map/ppermute | solution.py:51
  37.1 1.6 %collective-permute-start.13 = (f32[32,1024]{1,0:T(8,128)S(1)}, f32[32,1024]{1,0:T(8,128)S(1)}, u32[]{:S(2)}, u32[]{:S(2)}) collective-permute-start(f32[32,1024]{1,0:T(8,128)S(1)} %shard_map.79.image_ref), channel_id=1, source_target_pairs={{0,1},{1,0},{2,3},{3,2},{4,5},{5,4},{6,7},{7,6},{8,9},{9,8},{10,11... | collective-permute-start | bytes 393224 | tf_op jit(solution)/shard_map/ppermute | solution.py:56
  40.1 4.2 %collective-permute-start.14 = (bf16[8,32,128]{2,1,0:T(8,128)(2,1)S(1)}, bf16[8,32,128]{2,1,0:T(8,128)(2,1)S(1)}, u32[]{:S(2)}, u32[]{:S(2)}) collective-permute-start(bf16[8,32,128]{2,1,0:T(8,128)(2,1)S(1)} %get-tuple-element.122), channel_id=1, source_target_pairs={{0,5},{1,2},{2,1},{3,6},{4,7},{5,0},{6,3},{7,4},{8,11},{9,12},{10,... | collective-permute-start | bytes 196616 | tf_op jit(solution)/shard_map/ppermute | solution.py:51
  41.7 4.7 %collective-permute-start.15 = (bf16[8,32,128]{2,1,0:T(8,128)(2,1)S(1)}, bf16[8,32,128]{2,1,0:T(8,128)(2,1)S(1)}, u32[]{:S(2)}, u32[]{:S(2)}) collective-permute-start(bf16[8,32,128]{2,1,0:T(8,128)(2,1)S(1)} %get-tuple-element.122), channel_id=1, source_target_pairs={{0,9},{1,4},{2,7},{3,10},{4,1},{5,12},{6,15},{7,2},{8,13},{9,0},{1... | collective-permute-start | bytes 196616 | tf_op jit(solution)/shard_map/ppermute | solution.py:51
  42.8 6.1 %collective-permute-start.16 = (bf16[8,32,128]{2,1,0:T(8,128)(2,1)S(1)}, bf16[8,32,128]{2,1,0:T(8,128)(2,1)S(1)}, u32[]{:S(2)}, u32[]{:S(2)}) collective-permute-start(bf16[8,32,128]{2,1,0:T(8,128)(2,1)S(1)} %get-tuple-element.122), channel_id=1, source_target_pairs={{0,12},{1,7},{2,4},{3,15},{4,2},{5,9},{6,10},{7,1},{8,14},{9,5},{1... | collective-permute-start | bytes 196616 | tf_op jit(solution)/shard_map/ppermute | solution.py:51
  49.0 3.8 %collective-permute-start.17 = (bf16[8,32,128]{2,1,0:T(8,128)(2,1)S(1)}, bf16[8,32,128]{2,1,0:T(8,128)(2,1)S(1)}, u32[]{:S(2)}, u32[]{:S(2)}) collective-permute-start(bf16[8,32,128]{2,1,0:T(8,128)(2,1)S(1)} %get-tuple-element.124), channel_id=1, source_target_pairs={{0,3},{1,8},{2,11},{3,0},{4,13},{5,6},{6,5},{7,14},{8,1},{9,10},{1... | collective-permute-start | bytes 196616 | tf_op jit(solution)/shard_map/ppermute | solution.py:51
  53.2 1.4 %collective-permute-start.19 = (f32[32,1024]{1,0:T(8,128)S(1)}, f32[32,1024]{1,0:T(8,128)S(1)}, u32[]{:S(2)}, u32[]{:S(2)}) collective-permute-start(f32[32,1024]{1,0:T(8,128)S(1)} %shard_map.85.image_ref), channel_id=1, source_target_pairs={{0,1},{1,0},{2,3},{3,2},{4,5},{5,4},{6,7},{7,6},{8,9},{9,8},{10,11... | collective-permute-start | bytes 393224 | tf_op jit(solution)/shard_map/ppermute | solution.py:56
  53.8 1.5 %collective-permute-start.18 = (f32[32,1024]{1,0:T(8,128)S(1)}, f32[32,1024]{1,0:T(8,128)S(1)}, u32[]{:S(2)}, u32[]{:S(2)}) collective-permute-start(f32[32,1024]{1,0:T(8,128)S(1)} %shard_map.86.image_ref), channel_id=1, source_target_pairs={{0,1},{1,0},{2,3},{3,2},{4,5},{5,4},{6,7},{7,6},{8,9},{9,8},{10,11... | collective-permute-start | bytes 393224 | tf_op jit(solution)/shard_map/ppermute | solution.py:56
  55.7 4.2 %collective-permute-start.20 = (bf16[8,32,128]{2,1,0:T(8,128)(2,1)S(1)}, bf16[8,32,128]{2,1,0:T(8,128)(2,1)S(1)}, u32[]{:S(2)}, u32[]{:S(2)}) collective-permute-start(bf16[8,32,128]{2,1,0:T(8,128)(2,1)S(1)} %get-tuple-element.127), channel_id=1, source_target_pairs={{0,5},{1,2},{2,1},{3,6},{4,7},{5,0},{6,3},{7,4},{8,11},{9,12},{10,... | collective-permute-start | bytes 196616 | tf_op jit(solution)/shard_map/ppermute | solution.py:51
  56.8 4.6 %collective-permute-start.21 = (bf16[8,32,128]{2,1,0:T(8,128)(2,1)S(1)}, bf16[8,32,128]{2,1,0:T(8,128)(2,1)S(1)}, u32[]{:S(2)}, u32[]{:S(2)}) collective-permute-start(bf16[8,32,128]{2,1,0:T(8,128)(2,1)S(1)} %get-tuple-element.127), channel_id=1, source_target_pairs={{0,9},{1,4},{2,7},{3,10},{4,1},{5,12},{6,15},{7,2},{8,13},{9,0},{1... | collective-permute-start | bytes 196616 | tf_op jit(solution)/shard_map/ppermute | solution.py:51
  57.5 6.2 %collective-permute-start.22 = (bf16[8,32,128]{2,1,0:T(8,128)(2,1)S(1)}, bf16[8,32,128]{2,1,0:T(8,128)(2,1)S(1)}, u32[]{:S(2)}, u32[]{:S(2)}) collective-permute-start(bf16[8,32,128]{2,1,0:T(8,128)(2,1)S(1)} %get-tuple-element.127), channel_id=1, source_target_pairs={{0,12},{1,7},{2,4},{3,15},{4,2},{5,9},{6,10},{7,1},{8,14},{9,5},{1... | collective-permute-start | bytes 196616 | tf_op jit(solution)/shard_map/ppermute | solution.py:51
  63.7 3.8 %collective-permute-start.23 = (bf16[8,32,128]{2,1,0:T(8,128)(2,1)S(1)}, bf16[8,32,128]{2,1,0:T(8,128)(2,1)S(1)}, u32[]{:S(2)}, u32[]{:S(2)}) collective-permute-start(bf16[8,32,128]{2,1,0:T(8,128)(2,1)S(1)} %get-tuple-element.128), channel_id=1, source_target_pairs={{0,3},{1,8},{2,11},{3,0},{4,13},{5,6},{6,5},{7,14},{8,1},{9,10},{1... | collective-permute-start | bytes 196616 | tf_op jit(solution)/shard_map/ppermute | solution.py:51
  67.9 2.0 %collective-permute-start.24 = (f32[32,1024]{1,0:T(8,128)S(1)}, f32[32,1024]{1,0:T(8,128)S(1)}, u32[]{:S(2)}, u32[]{:S(2)}) collective-permute-start(f32[32,1024]{1,0:T(8,128)S(1)} %shard_map.92), channel_id=1, source_target_pairs={{0,1},{1,0},{2,3},{3,2},{4,5},{5,4},{6,7},{7,6},{8,9},{9,8},{10,11... | collective-permute-start | bytes 393224 | tf_op jit(solution)/shard_map/ppermute | solution.py:56
  (3 other events, 9.7 us)

commit v20 on v19

--- a/solution.py
+++ b/solution.py
@@ -158,8 +158,16 @@
 
 def turned_body(own_ref, other_ref, held_ref, *out_refs, tgt_rows):
     rows = tgt_rows + EXTRA
-    for s in range(held_ref.shape[0] // rows):
-        tgt_unit = unit_rows(held_ref[pl.ds(s * rows, tgt_rows), :])
+    columns = out_refs[0].shape[0]
+    per = min(TILE, columns) // tgt_rows
+    tile = per * tgt_rows
+    for col in range(0, columns, tile):
+        first = col // tgt_rows
+        tgt_unit = unit_rows(
+            jnp.concatenate(
+                [held_ref[pl.ds((first + s) * rows, tgt_rows), :] for s in range(per)]
+            )
+        )
         for cand_ref, out_ref in zip((own_ref, other_ref), out_refs):
             for row in range(0, cand_ref.shape[0], TILE):
                 scores = lax.dot_general(
@@ -168,7 +176,7 @@
                     (((1,), (1,)), ((), ())),
                     preferred_element_type=F32,
                 )
-                out_ref[s * tgt_rows : (s + 1) * tgt_rows, row : row + TILE] = jnp.exp(
+                out_ref[col : col + tile, row : row + TILE] = jnp.exp(
                     INVERSE_TEMP * scores
                 ).astype(BF16)
 

time: 70.8 us -> 70.8 us (level)
  waiting for transfers between devices: 24.4 us -> 25.8 us
  Pallas kernels: 13.3 us -> 11.9 us
    ppermute x17, waiting for transfers between devices: 20.8 us -> 22.2 us  [exchange(): return lax.ppermute(block, 'row', pairs)]
    pallas_call x25, Pallas kernels: 11.6 us -> 10.2 us  [call(): pl.pallas_call(body, out_shape=[pltpu.VMEM(shape, dtype) for shape, dtype...]
  transfers between devices with their start and end apart: 25 -> 25, of which waited for: 19 -> 19; matrix products, arithmetic and copies ran while one was open for 3% -> 3% of each run, Pallas kernels for 10% -> 8%
where the time goes in v20:
time: 70.8 us; the launch traced here: 70.6 us
  starting transfers between devices  29.4 us (42%)
  waiting for transfers between devices  25.8 us (36%)
  Pallas kernels  11.9 us (17%)
  other arithmetic  2.21 us (3%)
  between operations  0.85 us (1%)
    ppermute x17, starting transfers between devices, exchange(): return lax.ppermute(block, 'row', pairs)  25.6 us
    ppermute x17, waiting for transfers between devices, exchange(): return lax.ppermute(block, 'row', pairs)  22.2 us
    pallas_call x25, Pallas kernels, call(): pl.pallas_call(body, out_shape=[pltpu.VMEM(shape, dtype) for shape, dtype...  10.2 us
    ppermute x8, starting transfers between devices, swap(): return lax.ppermute(block, 'row', [(d, d ^ 1) for d in range(devices)])  3.79 us
    ppermute x8, waiting for transfers between devices, swap(): return lax.ppermute(block, 'row', [(d, d ^ 1) for d in range(devices)])  3.63 us
  transfers between devices with their start and end apart: 25, of which 19 were waited for; matrix products, arithmetic and copies ran while one was open for 3% of the time, Pallas kernels for 8%

profile of v20, /device:TPU:0, one launch (start us, length us, event | category | flops | bytes accessed | tf_op | source)
XLA Modules:
  0.0 70.6 jit_solution(9948380322528236509)
XLA Ops:
  1.6 3.5 %collective-permute-start = (bf16[144,256]{1,0:T(8,128)(2,1)S(1)}, bf16[144,256]{1,0:T(8,128)(2,1)S(1)}, u32[]{:S(2)}, u32[]{:S(2)}) collective-permute-start(bf16[144,256]{1,0:T(8,128)(2,1)S(1)} %shard_map.67), channel_id=1, source_target_pairs={{0,9},{1,4},{2,7},{3,10},{4,1},{5,12},{6,15},{7,2},{8,13},{9,0},{1... | collective-permute-start | bytes 221192 | tf_op jit(solution)/shard_map/ppermute | solution.py:51
  5.1 1.8 %collective-permute-start.1 = (bf16[144,256]{1,0:T(8,128)(2,1)S(1)}, bf16[144,256]{1,0:T(8,128)(2,1)S(1)}, u32[]{:S(2)}, u32[]{:S(2)}) collective-permute-start(bf16[144,256]{1,0:T(8,128)(2,1)S(1)} %shard_map.67), channel_id=1, source_target_pairs={{0,3},{1,2},{2,1},{3,0},{4,7},{5,6},{6,5},{7,4},{8,11},{9,10},{10,... | collective-permute-start | bytes 221192 | tf_op jit(solution)/shard_map/ppermute | solution.py:51
  6.9 1.3 %fusion = f32[1024]{0:T(1024)S(1)} fusion(bf16[1024,256]{1,0:T(8,128)(2,1)} %param.4), kind=kLoop, calls=%fused_computation.2 | loop fusion | flops 785408 | bytes 528384 | tf_op jit(solution)/shard_map/reduce_sum | solution.py:74
  9.6 1.3 %collective-permute-start.2 = (bf16[288,256]{1,0:T(8,128)(2,1)S(1)}, bf16[288,256]{1,0:T(8,128)(2,1)S(1)}, u32[]{:S(2)}, u32[]{:S(2)}) collective-permute-start(bf16[288,256]{1,0:T(8,128)(2,1)S(1)} %pad_maximum_fusion.1), channel_id=1, source_target_pairs={{0,5},{1,8},{2,11},{3,6},{4,13},{5,0},{6,3},{7,14},{8,1},{9,12},{1... | collective-permute-start | bytes 442376 | tf_op jit(solution)/shard_map/ppermute | solution.py:51
  13.3 2.0 %collective-permute-done.3 = bf16[144,256]{1,0:T(8,128)(2,1)S(1)} collective-permute-done((bf16[144,256]{1,0:T(8,128)(2,1)S(1)}, bf16[144,256]{1,0:T(8,128)(2,1)S(1)}, u32[]{:S(2)}, u32[]{:S(2)}) %collective-permute-start.3) | collective-permute-done | bytes 73760 | tf_op jit(solution)/shard_map/ppermute | solution.py:51
  15.3 1.7 %collective-permute-start.6 = (bf16[288,256]{1,0:T(8,128)(2,1)S(1)}, bf16[288,256]{1,0:T(8,128)(2,1)S(1)}, u32[]{:S(2)}, u32[]{:S(2)}) collective-permute-start(bf16[288,256]{1,0:T(8,128)(2,1)S(1)} %collective-permute-done.2), channel_id=1, source_target_pairs={{0,3},{1,2},{2,1},{3,0},{4,7},{5,6},{6,5},{7,4},{8,11},{9,10},{10,... | collective-permute-start | bytes 442376 | tf_op jit(solution)/shard_map/ppermute | solution.py:51
  18.7 2.3 %collective-permute-done.6.held_ref.refs_8_.refs_2_ = bf16[288,256]{1,0:T(8,128)(2,1)S(1)} collective-permute-done((bf16[288,256]{1,0:T(8,128)(2,1)S(1)}, bf16[288,256]{1,0:T(8,128)(2,1)S(1)}, u32[]{:S(2)}, u32[]{:S(2)}) %collective-permute-start.6) | collective-permute-done | bytes 147488 | tf_op jit(solution)/shard_map/ppermute | solution.py:51
  24.6 1.7 %collective-permute-start.8 = (bf16[8,32,128]{2,1,0:T(8,128)(2,1)S(1)}, bf16[8,32,128]{2,1,0:T(8,128)(2,1)S(1)}, u32[]{:S(2)}, u32[]{:S(2)}) collective-permute-start(bf16[8,32,128]{2,1,0:T(8,128)(2,1)S(1)} %get-tuple-element.105), channel_id=1, source_target_pairs={{0,5},{1,2},{2,1},{3,6},{4,7},{5,0},{6,3},{7,4},{8,11},{9,12},{10,... | collective-permute-start | bytes 196616 | tf_op jit(solution)/shard_map/ppermute | solution.py:51
  26.6 2.1 %collective-permute-start.10 = (bf16[8,32,128]{2,1,0:T(8,128)(2,1)S(1)}, bf16[8,32,128]{2,1,0:T(8,128)(2,1)S(1)}, u32[]{:S(2)}, u32[]{:S(2)}) collective-permute-start(bf16[8,32,128]{2,1,0:T(8,128)(2,1)S(1)} %get-tuple-element.105), channel_id=1, source_target_pairs={{0,12},{1,7},{2,4},{3,15},{4,2},{5,9},{6,10},{7,1},{8,14},{9,5},{1... | collective-permute-start | bytes 196616 | tf_op jit(solution)/shard_map/ppermute | solution.py:51
  29.6 2.0 %collective-permute-done.9.refs_1_ = bf16[8,32,128]{2,1,0:T(8,128)(2,1)S(1)} collective-permute-done((bf16[8,32,128]{2,1,0:T(8,128)(2,1)S(1)}, bf16[8,32,128]{2,1,0:T(8,128)(2,1)S(1)}, u32[]{:S(2)}, u32[]{:S(2)}) %collective-permute-start.9) | collective-permute-done | bytes 65568 | tf_op jit(solution)/shard_map/ppermute | solution.py:51
  31.6 1.3 %collective-permute-done.10.refs_2_ = bf16[8,32,128]{2,1,0:T(8,128)(2,1)S(1)} collective-permute-done((bf16[8,32,128]{2,1,0:T(8,128)(2,1)S(1)}, bf16[8,32,128]{2,1,0:T(8,128)(2,1)S(1)}, u32[]{:S(2)}, u32[]{:S(2)}) %collective-permute-start.10) | collective-permute-done | bytes 65568 | tf_op jit(solution)/shard_map/ppermute | solution.py:51
  32.9 1.8 %collective-permute-start.11 = (bf16[8,32,128]{2,1,0:T(8,128)(2,1)S(1)}, bf16[8,32,128]{2,1,0:T(8,128)(2,1)S(1)}, u32[]{:S(2)}, u32[]{:S(2)}) collective-permute-start(bf16[8,32,128]{2,1,0:T(8,128)(2,1)S(1)} %get-tuple-element.110), channel_id=1, source_target_pairs={{0,3},{1,8},{2,11},{3,0},{4,13},{5,6},{6,5},{7,14},{8,1},{9,10},{1... | collective-permute-start | bytes 196616 | tf_op jit(solution)/shard_map/ppermute | solution.py:51
  40.1 1.6 %collective-permute-start.14 = (bf16[8,32,128]{2,1,0:T(8,128)(2,1)S(1)}, bf16[8,32,128]{2,1,0:T(8,128)(2,1)S(1)}, u32[]{:S(2)}, u32[]{:S(2)}) collective-permute-start(bf16[8,32,128]{2,1,0:T(8,128)(2,1)S(1)} %get-tuple-element.122), channel_id=1, source_target_pairs={{0,5},{1,2},{2,1},{3,6},{4,7},{5,0},{6,3},{7,4},{8,11},{9,12},{10,... | collective-permute-start | bytes 196616 | tf_op jit(solution)/shard_map/ppermute | solution.py:51
  41.7 1.2 %collective-permute-start.15 = (bf16[8,32,128]{2,1,0:T(8,128)(2,1)S(1)}, bf16[8,32,128]{2,1,0:T(8,128)(2,1)S(1)}, u32[]{:S(2)}, u32[]{:S(2)}) collective-permute-start(bf16[8,32,128]{2,1,0:T(8,128)(2,1)S(1)} %get-tuple-element.122), channel_id=1, source_target_pairs={{0,9},{1,4},{2,7},{3,10},{4,1},{5,12},{6,15},{7,2},{8,13},{9,0},{1... | collective-permute-start | bytes 196616 | tf_op jit(solution)/shard_map/ppermute | solution.py:51
  42.8 1.4 %collective-permute-start.16 = (bf16[8,32,128]{2,1,0:T(8,128)(2,1)S(1)}, bf16[8,32,128]{2,1,0:T(8,128)(2,1)S(1)}, u32[]{:S(2)}, u32[]{:S(2)}) collective-permute-start(bf16[8,32,128]{2,1,0:T(8,128)(2,1)S(1)} %get-tuple-element.122), channel_id=1, source_target_pairs={{0,12},{1,7},{2,4},{3,15},{4,2},{5,9},{6,10},{7,1},{8,14},{9,5},{1... | collective-permute-start | bytes 196616 | tf_op jit(solution)/shard_map/ppermute | solution.py:51
  44.2 2.1 %collective-permute-done.15.refs_1_ = bf16[8,32,128]{2,1,0:T(8,128)(2,1)S(1)} collective-permute-done((bf16[8,32,128]{2,1,0:T(8,128)(2,1)S(1)}, bf16[8,32,128]{2,1,0:T(8,128)(2,1)S(1)}, u32[]{:S(2)}, u32[]{:S(2)}) %collective-permute-start.15) | collective-permute-done | bytes 65568 | tf_op jit(solution)/shard_map/ppermute | solution.py:51
  46.4 2.6 %collective-permute-done.16.refs_2_ = bf16[8,32,128]{2,1,0:T(8,128)(2,1)S(1)} collective-permute-done((bf16[8,32,128]{2,1,0:T(8,128)(2,1)S(1)}, bf16[8,32,128]{2,1,0:T(8,128)(2,1)S(1)}, u32[]{:S(2)}, u32[]{:S(2)}) %collective-permute-start.16) | collective-permute-done | bytes 65568 | tf_op jit(solution)/shard_map/ppermute | solution.py:51
  49.3 3.5 %collective-permute-done.17.refs_0_ = bf16[8,32,128]{2,1,0:T(8,128)(2,1)S(1)} collective-permute-done((bf16[8,32,128]{2,1,0:T(8,128)(2,1)S(1)}, bf16[8,32,128]{2,1,0:T(8,128)(2,1)S(1)}, u32[]{:S(2)}, u32[]{:S(2)}) %collective-permute-start.17) | collective-permute-done | bytes 65568 | tf_op jit(solution)/shard_map/ppermute | solution.py:51
  55.7 1.1 %collective-permute-start.20 = (bf16[8,32,128]{2,1,0:T(8,128)(2,1)S(1)}, bf16[8,32,128]{2,1,0:T(8,128)(2,1)S(1)}, u32[]{:S(2)}, u32[]{:S(2)}) collective-permute-start(bf16[8,32,128]{2,1,0:T(8,128)(2,1)S(1)} %get-tuple-element.127), channel_id=1, source_target_pairs={{0,5},{1,2},{2,1},{3,6},{4,7},{5,0},{6,3},{7,4},{8,11},{9,12},{10,... | collective-permute-start | bytes 196616 | tf_op jit(solution)/shard_map/ppermute | solution.py:51
  57.5 2.4 %collective-permute-start.22 = (bf16[8,32,128]{2,1,0:T(8,128)(2,1)S(1)}, bf16[8,32,128]{2,1,0:T(8,128)(2,1)S(1)}, u32[]{:S(2)}, u32[]{:S(2)}) collective-permute-start(bf16[8,32,128]{2,1,0:T(8,128)(2,1)S(1)} %get-tuple-element.127), channel_id=1, source_target_pairs={{0,12},{1,7},{2,4},{3,15},{4,2},{5,9},{6,10},{7,1},{8,14},{9,5},{1... | collective-permute-start | bytes 196616 | tf_op jit(solution)/shard_map/ppermute | solution.py:51
  59.9 1.6 %collective-permute-done.21.refs_1_ = bf16[8,32,128]{2,1,0:T(8,128)(2,1)S(1)} collective-permute-done((bf16[8,32,128]{2,1,0:T(8,128)(2,1)S(1)}, bf16[8,32,128]{2,1,0:T(8,128)(2,1)S(1)}, u32[]{:S(2)}, u32[]{:S(2)}) %collective-permute-start.21) | collective-permute-done | bytes 65568 | tf_op jit(solution)/shard_map/ppermute | solution.py:51
  61.5 2.2 %collective-permute-done.22.refs_2_ = bf16[8,32,128]{2,1,0:T(8,128)(2,1)S(1)} collective-permute-done((bf16[8,32,128]{2,1,0:T(8,128)(2,1)S(1)}, bf16[8,32,128]{2,1,0:T(8,128)(2,1)S(1)}, u32[]{:S(2)}, u32[]{:S(2)}) %collective-permute-start.22) | collective-permute-done | bytes 65568 | tf_op jit(solution)/shard_map/ppermute | solution.py:51
  63.7 1.8 %collective-permute-start.23 = (bf16[8,32,128]{2,1,0:T(8,128)(2,1)S(1)}, bf16[8,32,128]{2,1,0:T(8,128)(2,1)S(1)}, u32[]{:S(2)}, u32[]{:S(2)}) collective-permute-start(bf16[8,32,128]{2,1,0:T(8,128)(2,1)S(1)} %get-tuple-element.128), channel_id=1, source_target_pairs={{0,3},{1,8},{2,11},{3,0},{4,13},{5,6},{6,5},{7,14},{8,1},{9,10},{1... | collective-permute-start | bytes 196616 | tf_op jit(solution)/shard_map/ppermute | solution.py:51
  66.2 1.3 %collective-permute-done.23.refs_0_ = bf16[8,32,128]{2,1,0:T(8,128)(2,1)S(1)} collective-permute-done((bf16[8,32,128]{2,1,0:T(8,128)(2,1)S(1)}, bf16[8,32,128]{2,1,0:T(8,128)(2,1)S(1)}, u32[]{:S(2)}, u32[]{:S(2)}) %collective-permute-start.23) | collective-permute-done | bytes 65568 | tf_op jit(solution)/shard_map/ppermute | solution.py:51
  (67 shorter events, 24.3 us)
Async XLA Ops:
  1.6 7.3 %collective-permute-start = (bf16[144,256]{1,0:T(8,128)(2,1)S(1)}, bf16[144,256]{1,0:T(8,128)(2,1)S(1)}, u32[]{:S(2)}, u32[]{:S(2)}) collective-permute-start(bf16[144,256]{1,0:T(8,128)(2,1)S(1)} %shard_map.67), channel_id=1, source_target_pairs={{0,9},{1,4},{2,7},{3,10},{4,1},{5,12},{6,15},{7,2},{8,13},{9,0},{1... | collective-permute-start | bytes 221192 | tf_op jit(solution)/shard_map/ppermute | solution.py:51
  5.1 4.4 %collective-permute-start.1 = (bf16[144,256]{1,0:T(8,128)(2,1)S(1)}, bf16[144,256]{1,0:T(8,128)(2,1)S(1)}, u32[]{:S(2)}, u32[]{:S(2)}) collective-permute-start(bf16[144,256]{1,0:T(8,128)(2,1)S(1)} %shard_map.67), channel_id=1, source_target_pairs={{0,3},{1,2},{2,1},{3,0},{4,7},{5,6},{6,5},{7,4},{8,11},{9,10},{10,... | collective-permute-start | bytes 221192 | tf_op jit(solution)/shard_map/ppermute | solution.py:51
  9.6 5.8 %collective-permute-start.4 = (bf16[1024,256]{1,0:T(8,128)(2,1)S(1)}, bf16[1024,256]{1,0:T(8,128)(2,1)S(1)}, u32[]{:S(2)}, u32[]{:S(2)}) collective-permute-start(bf16[1024,256]{1,0:T(8,128)(2,1)S(1)} %fusion.2.own_ref), channel_id=1, source_target_pairs={{0,1},{1,0},{2,3},{3,2},{4,5},{5,4},{6,7},{7,6},{8,9},{9,8},{10,11... | collective-permute-start | bytes 1572872 | tf_op jit(solution)/shard_map/ppermute | solution.py:56
  9.6 5.7 %collective-permute-start.2 = (bf16[288,256]{1,0:T(8,128)(2,1)S(1)}, bf16[288,256]{1,0:T(8,128)(2,1)S(1)}, u32[]{:S(2)}, u32[]{:S(2)}) collective-permute-start(bf16[288,256]{1,0:T(8,128)(2,1)S(1)} %pad_maximum_fusion.1), channel_id=1, source_target_pairs={{0,5},{1,8},{2,11},{3,6},{4,13},{5,0},{6,3},{7,14},{8,1},{9,12},{1... | collective-permute-start | bytes 442376 | tf_op jit(solution)/shard_map/ppermute | solution.py:51
  10.9 4.4 %collective-permute-start.3 = (bf16[144,256]{1,0:T(8,128)(2,1)S(1)}, bf16[144,256]{1,0:T(8,128)(2,1)S(1)}, u32[]{:S(2)}, u32[]{:S(2)}) collective-permute-start(bf16[144,256]{1,0:T(8,128)(2,1)S(1)} %collective-permute-done), channel_id=1, source_target_pairs={{0,3},{1,2},{2,1},{3,0},{4,7},{5,6},{6,5},{7,4},{8,11},{9,10},{10,... | collective-permute-start | bytes 221192 | tf_op jit(solution)/shard_map/ppermute | solution.py:51
  11.8 1.5 %collective-permute-start.5 = (s32[8,128]{1,0:T(8,128)S(1)}, s32[8,128]{1,0:T(8,128)S(1)}, u32[]{:S(2)}, u32[]{:S(2)}) collective-permute-start(s32[8,128]{1,0:T(8,128)S(1)} %bitcast.5), channel_id=1, source_target_pairs={{0,1},{1,0},{2,3},{3,2},{4,5},{5,4},{6,7},{7,6},{8,9},{9,8},{10,11... | collective-permute-start | bytes 12296 | tf_op jit(solution)/shard_map/ppermute | solution.py:56
  15.3 5.7 %collective-permute-start.6 = (bf16[288,256]{1,0:T(8,128)(2,1)S(1)}, bf16[288,256]{1,0:T(8,128)(2,1)S(1)}, u32[]{:S(2)}, u32[]{:S(2)}) collective-permute-start(bf16[288,256]{1,0:T(8,128)(2,1)S(1)} %collective-permute-done.2), channel_id=1, source_target_pairs={{0,3},{1,2},{2,1},{3,0},{4,7},{5,6},{6,5},{7,4},{8,11},{9,10},{10,... | collective-permute-start | bytes 442376 | tf_op jit(solution)/shard_map/ppermute | solution.py:51
  22.0 1.7 %collective-permute-start.7 = (f32[24,128]{1,0:T(8,128)S(1)}, f32[24,128]{1,0:T(8,128)S(1)}, u32[]{:S(2)}, u32[]{:S(2)}) collective-permute-start(f32[24,128]{1,0:T(8,128)S(1)} %shard_map.71.mine_ref), channel_id=1, source_target_pairs={{0,1},{1,0},{2,3},{3,2},{4,5},{5,4},{6,7},{7,6},{8,9},{9,8},{10,11... | collective-permute-start | bytes 36872 | tf_op jit(solution)/shard_map/ppermute | solution.py:56
  24.6 5.0 %collective-permute-start.8 = (bf16[8,32,128]{2,1,0:T(8,128)(2,1)S(1)}, bf16[8,32,128]{2,1,0:T(8,128)(2,1)S(1)}, u32[]{:S(2)}, u32[]{:S(2)}) collective-permute-start(bf16[8,32,128]{2,1,0:T(8,128)(2,1)S(1)} %get-tuple-element.105), channel_id=1, source_target_pairs={{0,5},{1,2},{2,1},{3,6},{4,7},{5,0},{6,3},{7,4},{8,11},{9,12},{10,... | collective-permute-start | bytes 196616 | tf_op jit(solution)/shard_map/ppermute | solution.py:51
  26.3 5.3 %collective-permute-start.9 = (bf16[8,32,128]{2,1,0:T(8,128)(2,1)S(1)}, bf16[8,32,128]{2,1,0:T(8,128)(2,1)S(1)}, u32[]{:S(2)}, u32[]{:S(2)}) collective-permute-start(bf16[8,32,128]{2,1,0:T(8,128)(2,1)S(1)} %get-tuple-element.105), channel_id=1, source_target_pairs={{0,9},{1,4},{2,7},{3,10},{4,1},{5,12},{6,15},{7,2},{8,13},{9,0},{1... | collective-permute-start | bytes 196616 | tf_op jit(solution)/shard_map/ppermute | solution.py:51
  26.6 6.2 %collective-permute-start.10 = (bf16[8,32,128]{2,1,0:T(8,128)(2,1)S(1)}, bf16[8,32,128]{2,1,0:T(8,128)(2,1)S(1)}, u32[]{:S(2)}, u32[]{:S(2)}) collective-permute-start(bf16[8,32,128]{2,1,0:T(8,128)(2,1)S(1)} %get-tuple-element.105), channel_id=1, source_target_pairs={{0,12},{1,7},{2,4},{3,15},{4,2},{5,9},{6,10},{7,1},{8,14},{9,5},{1... | collective-permute-start | bytes 196616 | tf_op jit(solution)/shard_map/ppermute | solution.py:51
  32.9 3.8 %collective-permute-start.11 = (bf16[8,32,128]{2,1,0:T(8,128)(2,1)S(1)}, bf16[8,32,128]{2,1,0:T(8,128)(2,1)S(1)}, u32[]{:S(2)}, u32[]{:S(2)}) collective-permute-start(bf16[8,32,128]{2,1,0:T(8,128)(2,1)S(1)} %get-tuple-element.110), channel_id=1, source_target_pairs={{0,3},{1,8},{2,11},{3,0},{4,13},{5,6},{6,5},{7,14},{8,1},{9,10},{1... | collective-permute-start | bytes 196616 | tf_op jit(solution)/shard_map/ppermute | solution.py:51
  37.1 1.6 %collective-permute-start.13 = (f32[32,1024]{1,0:T(8,128)S(1)}, f32[32,1024]{1,0:T(8,128)S(1)}, u32[]{:S(2)}, u32[]{:S(2)}) collective-permute-start(f32[32,1024]{1,0:T(8,128)S(1)} %shard_map.79.image_ref), channel_id=1, source_target_pairs={{0,1},{1,0},{2,3},{3,2},{4,5},{5,4},{6,7},{7,6},{8,9},{9,8},{10,11... | collective-permute-start | bytes 393224 | tf_op jit(solution)/shard_map/ppermute | solution.py:56
  40.1 4.2 %collective-permute-start.14 = (bf16[8,32,128]{2,1,0:T(8,128)(2,1)S(1)}, bf16[8,32,128]{2,1,0:T(8,128)(2,1)S(1)}, u32[]{:S(2)}, u32[]{:S(2)}) collective-permute-start(bf16[8,32,128]{2,1,0:T(8,128)(2,1)S(1)} %get-tuple-element.122), channel_id=1, source_target_pairs={{0,5},{1,2},{2,1},{3,6},{4,7},{5,0},{6,3},{7,4},{8,11},{9,12},{10,... | collective-permute-start | bytes 196616 | tf_op jit(solution)/shard_map/ppermute | solution.py:51
  41.7 4.7 %collective-permute-start.15 = (bf16[8,32,128]{2,1,0:T(8,128)(2,1)S(1)}, bf16[8,32,128]{2,1,0:T(8,128)(2,1)S(1)}, u32[]{:S(2)}, u32[]{:S(2)}) collective-permute-start(bf16[8,32,128]{2,1,0:T(8,128)(2,1)S(1)} %get-tuple-element.122), channel_id=1, source_target_pairs={{0,9},{1,4},{2,7},{3,10},{4,1},{5,12},{6,15},{7,2},{8,13},{9,0},{1... | collective-permute-start | bytes 196616 | tf_op jit(solution)/shard_map/ppermute | solution.py:51
  42.8 6.1 %collective-permute-start.16 = (bf16[8,32,128]{2,1,0:T(8,128)(2,1)S(1)}, bf16[8,32,128]{2,1,0:T(8,128)(2,1)S(1)}, u32[]{:S(2)}, u32[]{:S(2)}) collective-permute-start(bf16[8,32,128]{2,1,0:T(8,128)(2,1)S(1)} %get-tuple-element.122), channel_id=1, source_target_pairs={{0,12},{1,7},{2,4},{3,15},{4,2},{5,9},{6,10},{7,1},{8,14},{9,5},{1... | collective-permute-start | bytes 196616 | tf_op jit(solution)/shard_map/ppermute | solution.py:51
  49.0 3.8 %collective-permute-start.17 = (bf16[8,32,128]{2,1,0:T(8,128)(2,1)S(1)}, bf16[8,32,128]{2,1,0:T(8,128)(2,1)S(1)}, u32[]{:S(2)}, u32[]{:S(2)}) collective-permute-start(bf16[8,32,128]{2,1,0:T(8,128)(2,1)S(1)} %get-tuple-element.124), channel_id=1, source_target_pairs={{0,3},{1,8},{2,11},{3,0},{4,13},{5,6},{6,5},{7,14},{8,1},{9,10},{1... | collective-permute-start | bytes 196616 | tf_op jit(solution)/shard_map/ppermute | solution.py:51
  53.2 1.4 %collective-permute-start.19 = (f32[32,1024]{1,0:T(8,128)S(1)}, f32[32,1024]{1,0:T(8,128)S(1)}, u32[]{:S(2)}, u32[]{:S(2)}) collective-permute-start(f32[32,1024]{1,0:T(8,128)S(1)} %shard_map.85.image_ref), channel_id=1, source_target_pairs={{0,1},{1,0},{2,3},{3,2},{4,5},{5,4},{6,7},{7,6},{8,9},{9,8},{10,11... | collective-permute-start | bytes 393224 | tf_op jit(solution)/shard_map/ppermute | solution.py:56
  53.8 1.5 %collective-permute-start.18 = (f32[32,1024]{1,0:T(8,128)S(1)}, f32[32,1024]{1,0:T(8,128)S(1)}, u32[]{:S(2)}, u32[]{:S(2)}) collective-permute-start(f32[32,1024]{1,0:T(8,128)S(1)} %shard_map.86.image_ref), channel_id=1, source_target_pairs={{0,1},{1,0},{2,3},{3,2},{4,5},{5,4},{6,7},{7,6},{8,9},{9,8},{10,11... | collective-permute-start | bytes 393224 | tf_op jit(solution)/shard_map/ppermute | solution.py:56
  55.7 4.2 %collective-permute-start.20 = (bf16[8,32,128]{2,1,0:T(8,128)(2,1)S(1)}, bf16[8,32,128]{2,1,0:T(8,128)(2,1)S(1)}, u32[]{:S(2)}, u32[]{:S(2)}) collective-permute-start(bf16[8,32,128]{2,1,0:T(8,128)(2,1)S(1)} %get-tuple-element.127), channel_id=1, source_target_pairs={{0,5},{1,2},{2,1},{3,6},{4,7},{5,0},{6,3},{7,4},{8,11},{9,12},{10,... | collective-permute-start | bytes 196616 | tf_op jit(solution)/shard_map/ppermute | solution.py:51
  56.8 4.6 %collective-permute-start.21 = (bf16[8,32,128]{2,1,0:T(8,128)(2,1)S(1)}, bf16[8,32,128]{2,1,0:T(8,128)(2,1)S(1)}, u32[]{:S(2)}, u32[]{:S(2)}) collective-permute-start(bf16[8,32,128]{2,1,0:T(8,128)(2,1)S(1)} %get-tuple-element.127), channel_id=1, source_target_pairs={{0,9},{1,4},{2,7},{3,10},{4,1},{5,12},{6,15},{7,2},{8,13},{9,0},{1... | collective-permute-start | bytes 196616 | tf_op jit(solution)/shard_map/ppermute | solution.py:51
  57.5 6.2 %collective-permute-start.22 = (bf16[8,32,128]{2,1,0:T(8,128)(2,1)S(1)}, bf16[8,32,128]{2,1,0:T(8,128)(2,1)S(1)}, u32[]{:S(2)}, u32[]{:S(2)}) collective-permute-start(bf16[8,32,128]{2,1,0:T(8,128)(2,1)S(1)} %get-tuple-element.127), channel_id=1, source_target_pairs={{0,12},{1,7},{2,4},{3,15},{4,2},{5,9},{6,10},{7,1},{8,14},{9,5},{1... | collective-permute-start | bytes 196616 | tf_op jit(solution)/shard_map/ppermute | solution.py:51
  63.7 3.8 %collective-permute-start.23 = (bf16[8,32,128]{2,1,0:T(8,128)(2,1)S(1)}, bf16[8,32,128]{2,1,0:T(8,128)(2,1)S(1)}, u32[]{:S(2)}, u32[]{:S(2)}) collective-permute-start(bf16[8,32,128]{2,1,0:T(8,128)(2,1)S(1)} %get-tuple-element.128), channel_id=1, source_target_pairs={{0,3},{1,8},{2,11},{3,0},{4,13},{5,6},{6,5},{7,14},{8,1},{9,10},{1... | collective-permute-start | bytes 196616 | tf_op jit(solution)/shard_map/ppermute | solution.py:51
  67.9 2.0 %collective-permute-start.24 = (f32[32,1024]{1,0:T(8,128)S(1)}, f32[32,1024]{1,0:T(8,128)S(1)}, u32[]{:S(2)}, u32[]{:S(2)}) collective-permute-start(f32[32,1024]{1,0:T(8,128)S(1)} %shard_map.92), channel_id=1, source_target_pairs={{0,1},{1,0},{2,3},{3,2},{4,5},{5,4},{6,7},{7,6},{8,9},{9,8},{10,11... | collective-permute-start | bytes 393224 | tf_op jit(solution)/shard_map/ppermute | solution.py:56
  (3 other events, 9.7 us)

commit v21 on v20

--- a/solution.py
+++ b/solution.py
@@ -255,7 +255,7 @@
 
 
 def image_body(scale_ref, *refs):
-    *turned, image_ref = refs
+    *turned, image_ref, sent_ref = refs
     image = 0.0
     first = 0
     for turned_ref in turned:
@@ -264,11 +264,12 @@
         image += jnp.dot(scale_v, turned_ref[...], preferred_element_type=F32)
         first += slots
     image_ref[...] = image
+    sent_ref[...] = image.astype(BF16)
 
 
 def own_body(image_ref, got_ref, marg_ref, *refs, parts):
     kernels, (column_ref, *out_refs) = refs[:parts], refs[parts:]
-    scale_u = marg_ref[...] / (image_ref[...] + got_ref[...])
+    scale_u = marg_ref[...] / (image_ref[...] + got_ref[...].astype(F32))
     for out_ref in out_refs:
         out_ref[...] = scale_u
     put_column(scale_u.astype(BF16), kernels, None, (column_ref,))
@@ -276,13 +277,13 @@
 
 def other_body(image_ref, got_ref, marg_ref, added_ref, *refs):
     *kernels, column_ref, sent_ref = refs
-    scale_u = marg_ref[...] / (image_ref[...] + got_ref[...])
+    scale_u = marg_ref[...] / (image_ref[...] + got_ref[...].astype(F32))
     put_column(scale_u.astype(BF16), kernels, added_ref, (column_ref, sent_ref))
 
 
 def last_body(image_ref, got_ref, u_ref, scale_v_ref, mass_ref, own_ref, *, candidates):
     own_ref[...] = scale_v_ref[0]
-    mass_ref[...] = candidates * u_ref[...] * (image_ref[...] + got_ref[...])
+    mass_ref[...] = candidates * u_ref[...] * (image_ref[...] + got_ref[...].astype(F32))
 
 
 def slot_of(slot, flips, slots):
@@ -420,13 +421,12 @@
             [(block, BF16)] + [(block, F32)] * last,
             column, tgt_marg, *found,
         )
-        (other_image,) = call(
-            image_body, [image_type], scale_vb, *other_turned, flops=half_flops
-        )
-        own_got = swap(other_image)
-        (own_image,) = call(image_body, [image_type], scale_vb, *own_turned, flops=half_flops)
+        both = [image_type, ((CLASSES, cand_rows), BF16)]
+        other_image, sent = call(image_body, both, scale_vb, *other_turned, flops=half_flops)
+        own_got = swap(sent)
+        own_image, sent = call(image_body, both, scale_vb, *own_turned, flops=half_flops)
         if not last:
-            other_got = swap(own_image)
+            other_got = swap(sent)
     space = pl.BlockSpec(memory_space=pltpu.VMEM)
     args = [own_image, own_got, *scale_u, *scale_v]
     mass, tgt_scaling = pl.pallas_call(

time: 70.8 us -> 71.5 us (level)
  Pallas kernels: 11.9 us -> 13.2 us
    pallas_call x25, Pallas kernels: 10.2 us -> 11.6 us  [call(): pl.pallas_call(body, out_shape=[pltpu.VMEM(shape, dtype) for shape, dtype...]
  transfers between devices with their start and end apart: 25 -> 25, of which waited for: 19 -> 18; matrix products, arithmetic and copies ran while one was open for 3% -> 3% of each run, Pallas kernels for 8% -> 9%
where the time goes in v21:
time: 71.5 us; the launch traced here: 71.2 us
  starting transfers between devices  29.4 us (41%)
  waiting for transfers between devices  25.1 us (35%)
  Pallas kernels  13.2 us (18%)
  other arithmetic  2.21 us (3%)
  between operations  0.85 us (1%)
    ppermute x17, starting transfers between devices, exchange(): return lax.ppermute(block, 'row', pairs)  25.6 us
    ppermute x17, waiting for transfers between devices, exchange(): return lax.ppermute(block, 'row', pairs)  22.1 us
    pallas_call x25, Pallas kernels, call(): pl.pallas_call(body, out_shape=[pltpu.VMEM(shape, dtype) for shape, dtype...  11.6 us
    ppermute x8, starting transfers between devices, swap(): return lax.ppermute(block, 'row', [(d, d ^ 1) for d in range(devices)])  3.79 us
    ppermute x8, waiting for transfers between devices, swap(): return lax.ppermute(block, 'row', [(d, d ^ 1) for d in range(devices)])  2.92 us
  transfers between devices with their start and end apart: 25, of which 18 were waited for; matrix products, arithmetic and copies ran while one was open for 3% of the time, Pallas kernels for 9%

profile of v21, /device:TPU:0, one launch (start us, length us, event | category | flops | bytes accessed | tf_op | source)
XLA Modules:
  0.0 71.2 jit_solution(5290841058570836916)
XLA Ops:
  1.6 3.5 %collective-permute-start = (bf16[144,256]{1,0:T(8,128)(2,1)S(1)}, bf16[144,256]{1,0:T(8,128)(2,1)S(1)}, u32[]{:S(2)}, u32[]{:S(2)}) collective-permute-start(bf16[144,256]{1,0:T(8,128)(2,1)S(1)} %shard_map.67), channel_id=1, source_target_pairs={{0,9},{1,4},{2,7},{3,10},{4,1},{5,12},{6,15},{7,2},{8,13},{9,0},{1... | collective-permute-start | bytes 221192 | tf_op jit(solution)/shard_map/ppermute | solution.py:51
  5.1 1.8 %collective-permute-start.1 = (bf16[144,256]{1,0:T(8,128)(2,1)S(1)}, bf16[144,256]{1,0:T(8,128)(2,1)S(1)}, u32[]{:S(2)}, u32[]{:S(2)}) collective-permute-start(bf16[144,256]{1,0:T(8,128)(2,1)S(1)} %shard_map.67), channel_id=1, source_target_pairs={{0,3},{1,2},{2,1},{3,0},{4,7},{5,6},{6,5},{7,4},{8,11},{9,10},{10,... | collective-permute-start | bytes 221192 | tf_op jit(solution)/shard_map/ppermute | solution.py:51
  6.9 1.3 %fusion = f32[1024]{0:T(1024)S(1)} fusion(bf16[1024,256]{1,0:T(8,128)(2,1)} %param.4), kind=kLoop, calls=%fused_computation.2 | loop fusion | flops 785408 | bytes 528384 | tf_op jit(solution)/shard_map/reduce_sum | solution.py:74
  9.6 1.3 %collective-permute-start.2 = (bf16[288,256]{1,0:T(8,128)(2,1)S(1)}, bf16[288,256]{1,0:T(8,128)(2,1)S(1)}, u32[]{:S(2)}, u32[]{:S(2)}) collective-permute-start(bf16[288,256]{1,0:T(8,128)(2,1)S(1)} %pad_maximum_fusion.1), channel_id=1, source_target_pairs={{0,5},{1,8},{2,11},{3,6},{4,13},{5,0},{6,3},{7,14},{8,1},{9,12},{1... | collective-permute-start | bytes 442376 | tf_op jit(solution)/shard_map/ppermute | solution.py:51
  13.3 2.0 %collective-permute-done.3 = bf16[144,256]{1,0:T(8,128)(2,1)S(1)} collective-permute-done((bf16[144,256]{1,0:T(8,128)(2,1)S(1)}, bf16[144,256]{1,0:T(8,128)(2,1)S(1)}, u32[]{:S(2)}, u32[]{:S(2)}) %collective-permute-start.3) | collective-permute-done | bytes 73760 | tf_op jit(solution)/shard_map/ppermute | solution.py:51
  15.3 1.7 %collective-permute-start.6 = (bf16[288,256]{1,0:T(8,128)(2,1)S(1)}, bf16[288,256]{1,0:T(8,128)(2,1)S(1)}, u32[]{:S(2)}, u32[]{:S(2)}) collective-permute-start(bf16[288,256]{1,0:T(8,128)(2,1)S(1)} %collective-permute-done.2), channel_id=1, source_target_pairs={{0,3},{1,2},{2,1},{3,0},{4,7},{5,6},{6,5},{7,4},{8,11},{9,10},{10,... | collective-permute-start | bytes 442376 | tf_op jit(solution)/shard_map/ppermute | solution.py:51
  18.7 2.3 %collective-permute-done.6.held_ref.refs_8_.refs_2_ = bf16[288,256]{1,0:T(8,128)(2,1)S(1)} collective-permute-done((bf16[288,256]{1,0:T(8,128)(2,1)S(1)}, bf16[288,256]{1,0:T(8,128)(2,1)S(1)}, u32[]{:S(2)}, u32[]{:S(2)}) %collective-permute-start.6) | collective-permute-done | bytes 147488 | tf_op jit(solution)/shard_map/ppermute | solution.py:51
  24.6 1.7 %collective-permute-start.8 = (bf16[8,32,128]{2,1,0:T(8,128)(2,1)S(1)}, bf16[8,32,128]{2,1,0:T(8,128)(2,1)S(1)}, u32[]{:S(2)}, u32[]{:S(2)}) collective-permute-start(bf16[8,32,128]{2,1,0:T(8,128)(2,1)S(1)} %get-tuple-element.115), channel_id=1, source_target_pairs={{0,5},{1,2},{2,1},{3,6},{4,7},{5,0},{6,3},{7,4},{8,11},{9,12},{10,... | collective-permute-start | bytes 196616 | tf_op jit(solution)/shard_map/ppermute | solution.py:51
  26.7 2.1 %collective-permute-start.10 = (bf16[8,32,128]{2,1,0:T(8,128)(2,1)S(1)}, bf16[8,32,128]{2,1,0:T(8,128)(2,1)S(1)}, u32[]{:S(2)}, u32[]{:S(2)}) collective-permute-start(bf16[8,32,128]{2,1,0:T(8,128)(2,1)S(1)} %get-tuple-element.115), channel_id=1, source_target_pairs={{0,12},{1,7},{2,4},{3,15},{4,2},{5,9},{6,10},{7,1},{8,14},{9,5},{1... | collective-permute-start | bytes 196616 | tf_op jit(solution)/shard_map/ppermute | solution.py:51
  29.6 2.0 %collective-permute-done.9.refs_1_ = bf16[8,32,128]{2,1,0:T(8,128)(2,1)S(1)} collective-permute-done((bf16[8,32,128]{2,1,0:T(8,128)(2,1)S(1)}, bf16[8,32,128]{2,1,0:T(8,128)(2,1)S(1)}, u32[]{:S(2)}, u32[]{:S(2)}) %collective-permute-start.9) | collective-permute-done | bytes 65568 | tf_op jit(solution)/shard_map/ppermute | solution.py:51
  31.6 1.3 %collective-permute-done.10.refs_2_ = bf16[8,32,128]{2,1,0:T(8,128)(2,1)S(1)} collective-permute-done((bf16[8,32,128]{2,1,0:T(8,128)(2,1)S(1)}, bf16[8,32,128]{2,1,0:T(8,128)(2,1)S(1)}, u32[]{:S(2)}, u32[]{:S(2)}) %collective-permute-start.10) | collective-permute-done | bytes 65568 | tf_op jit(solution)/shard_map/ppermute | solution.py:51
  32.9 1.8 %collective-permute-start.11 = (bf16[8,32,128]{2,1,0:T(8,128)(2,1)S(1)}, bf16[8,32,128]{2,1,0:T(8,128)(2,1)S(1)}, u32[]{:S(2)}, u32[]{:S(2)}) collective-permute-start(bf16[8,32,128]{2,1,0:T(8,128)(2,1)S(1)} %get-tuple-element.120), channel_id=1, source_target_pairs={{0,3},{1,8},{2,11},{3,0},{4,13},{5,6},{6,5},{7,14},{8,1},{9,10},{1... | collective-permute-start | bytes 196616 | tf_op jit(solution)/shard_map/ppermute | solution.py:51
  40.0 1.6 %collective-permute-start.14 = (bf16[8,32,128]{2,1,0:T(8,128)(2,1)S(1)}, bf16[8,32,128]{2,1,0:T(8,128)(2,1)S(1)}, u32[]{:S(2)}, u32[]{:S(2)}) collective-permute-start(bf16[8,32,128]{2,1,0:T(8,128)(2,1)S(1)} %get-tuple-element.136), channel_id=1, source_target_pairs={{0,5},{1,2},{2,1},{3,6},{4,7},{5,0},{6,3},{7,4},{8,11},{9,12},{10,... | collective-permute-start | bytes 196616 | tf_op jit(solution)/shard_map/ppermute | solution.py:51
  41.6 1.2 %collective-permute-start.15 = (bf16[8,32,128]{2,1,0:T(8,128)(2,1)S(1)}, bf16[8,32,128]{2,1,0:T(8,128)(2,1)S(1)}, u32[]{:S(2)}, u32[]{:S(2)}) collective-permute-start(bf16[8,32,128]{2,1,0:T(8,128)(2,1)S(1)} %get-tuple-element.136), channel_id=1, source_target_pairs={{0,9},{1,4},{2,7},{3,10},{4,1},{5,12},{6,15},{7,2},{8,13},{9,0},{1... | collective-permute-start | bytes 196616 | tf_op jit(solution)/shard_map/ppermute | solution.py:51
  42.8 1.4 %collective-permute-start.16 = (bf16[8,32,128]{2,1,0:T(8,128)(2,1)S(1)}, bf16[8,32,128]{2,1,0:T(8,128)(2,1)S(1)}, u32[]{:S(2)}, u32[]{:S(2)}) collective-permute-start(bf16[8,32,128]{2,1,0:T(8,128)(2,1)S(1)} %get-tuple-element.136), channel_id=1, source_target_pairs={{0,12},{1,7},{2,4},{3,15},{4,2},{5,9},{6,10},{7,1},{8,14},{9,5},{1... | collective-permute-start | bytes 196616 | tf_op jit(solution)/shard_map/ppermute | solution.py:51
  44.2 2.1 %collective-permute-done.15.refs_1_ = bf16[8,32,128]{2,1,0:T(8,128)(2,1)S(1)} collective-permute-done((bf16[8,32,128]{2,1,0:T(8,128)(2,1)S(1)}, bf16[8,32,128]{2,1,0:T(8,128)(2,1)S(1)}, u32[]{:S(2)}, u32[]{:S(2)}) %collective-permute-start.15) | collective-permute-done | bytes 65568 | tf_op jit(solution)/shard_map/ppermute | solution.py:51
  46.3 2.6 %collective-permute-done.16.refs_2_ = bf16[8,32,128]{2,1,0:T(8,128)(2,1)S(1)} collective-permute-done((bf16[8,32,128]{2,1,0:T(8,128)(2,1)S(1)}, bf16[8,32,128]{2,1,0:T(8,128)(2,1)S(1)}, u32[]{:S(2)}, u32[]{:S(2)}) %collective-permute-start.16) | collective-permute-done | bytes 65568 | tf_op jit(solution)/shard_map/ppermute | solution.py:51
  49.2 3.5 %collective-permute-done.17.refs_0_ = bf16[8,32,128]{2,1,0:T(8,128)(2,1)S(1)} collective-permute-done((bf16[8,32,128]{2,1,0:T(8,128)(2,1)S(1)}, bf16[8,32,128]{2,1,0:T(8,128)(2,1)S(1)}, u32[]{:S(2)}, u32[]{:S(2)}) %collective-permute-start.17) | collective-permute-done | bytes 65568 | tf_op jit(solution)/shard_map/ppermute | solution.py:51
  57.3 2.4 %collective-permute-start.22 = (bf16[8,32,128]{2,1,0:T(8,128)(2,1)S(1)}, bf16[8,32,128]{2,1,0:T(8,128)(2,1)S(1)}, u32[]{:S(2)}, u32[]{:S(2)}) collective-permute-start(bf16[8,32,128]{2,1,0:T(8,128)(2,1)S(1)} %get-tuple-element.145), channel_id=1, source_target_pairs={{0,12},{1,7},{2,4},{3,15},{4,2},{5,9},{6,10},{7,1},{8,14},{9,5},{1... | collective-permute-start | bytes 196616 | tf_op jit(solution)/shard_map/ppermute | solution.py:51
  59.8 1.6 %collective-permute-done.21.refs_1_ = bf16[8,32,128]{2,1,0:T(8,128)(2,1)S(1)} collective-permute-done((bf16[8,32,128]{2,1,0:T(8,128)(2,1)S(1)}, bf16[8,32,128]{2,1,0:T(8,128)(2,1)S(1)}, u32[]{:S(2)}, u32[]{:S(2)}) %collective-permute-start.21) | collective-permute-done | bytes 65568 | tf_op jit(solution)/shard_map/ppermute | solution.py:51
  61.3 2.2 %collective-permute-done.22.refs_2_ = bf16[8,32,128]{2,1,0:T(8,128)(2,1)S(1)} collective-permute-done((bf16[8,32,128]{2,1,0:T(8,128)(2,1)S(1)}, bf16[8,32,128]{2,1,0:T(8,128)(2,1)S(1)}, u32[]{:S(2)}, u32[]{:S(2)}) %collective-permute-start.22) | collective-permute-done | bytes 65568 | tf_op jit(solution)/shard_map/ppermute | solution.py:51
  63.6 1.8 %collective-permute-start.23 = (bf16[8,32,128]{2,1,0:T(8,128)(2,1)S(1)}, bf16[8,32,128]{2,1,0:T(8,128)(2,1)S(1)}, u32[]{:S(2)}, u32[]{:S(2)}) collective-permute-start(bf16[8,32,128]{2,1,0:T(8,128)(2,1)S(1)} %get-tuple-element.146), channel_id=1, source_target_pairs={{0,3},{1,8},{2,11},{3,0},{4,13},{5,6},{6,5},{7,14},{8,1},{9,10},{1... | collective-permute-start | bytes 196616 | tf_op jit(solution)/shard_map/ppermute | solution.py:51
  66.0 1.3 %collective-permute-done.23.refs_0_ = bf16[8,32,128]{2,1,0:T(8,128)(2,1)S(1)} collective-permute-done((bf16[8,32,128]{2,1,0:T(8,128)(2,1)S(1)}, bf16[8,32,128]{2,1,0:T(8,128)(2,1)S(1)}, u32[]{:S(2)}, u32[]{:S(2)}) %collective-permute-start.23) | collective-permute-done | bytes 65568 | tf_op jit(solution)/shard_map/ppermute | solution.py:51
  67.3 1.1 %shard_map.92 = (f32[32,1024]{1,0:T(8,128)}, bf16[32,1024]{1,0:T(8,128)(2,1)S(1)}) custom-call(bf16[8,32,128]{2,1,0:T(8,128)(2,1)S(1)} %get-tuple-element.151.scale_ref, bf16[512,1024]{1,0:T(8,128)(2,1)S(1)} %get-tuple-element.123.refs_0_, bf16[256,1024]{1,0:T(8,128)(2,1)S(1)} %get-tuple-element.124.refs_1_, bf16[256,1024]{1,0:T(8,128)(2,1)S(1)} %get-tuple-element.125.refs_2_), custom_call_target="tpu_custom_call" | custom-call | flops 268435456 | bytes 2162688 | tf_op jit(solution)/shard_map/pallas_call | solution.py:62
  (67 shorter events, 24.9 us)
Async XLA Ops:
  1.6 7.3 %collective-permute-start = (bf16[144,256]{1,0:T(8,128)(2,1)S(1)}, bf16[144,256]{1,0:T(8,128)(2,1)S(1)}, u32[]{:S(2)}, u32[]{:S(2)}) collective-permute-start(bf16[144,256]{1,0:T(8,128)(2,1)S(1)} %shard_map.67), channel_id=1, source_target_pairs={{0,9},{1,4},{2,7},{3,10},{4,1},{5,12},{6,15},{7,2},{8,13},{9,0},{1... | collective-permute-start | bytes 221192 | tf_op jit(solution)/shard_map/ppermute | solution.py:51
  5.1 4.4 %collective-permute-start.1 = (bf16[144,256]{1,0:T(8,128)(2,1)S(1)}, bf16[144,256]{1,0:T(8,128)(2,1)S(1)}, u32[]{:S(2)}, u32[]{:S(2)}) collective-permute-start(bf16[144,256]{1,0:T(8,128)(2,1)S(1)} %shard_map.67), channel_id=1, source_target_pairs={{0,3},{1,2},{2,1},{3,0},{4,7},{5,6},{6,5},{7,4},{8,11},{9,10},{10,... | collective-permute-start | bytes 221192 | tf_op jit(solution)/shard_map/ppermute | solution.py:51
  9.6 5.8 %collective-permute-start.4 = (bf16[1024,256]{1,0:T(8,128)(2,1)S(1)}, bf16[1024,256]{1,0:T(8,128)(2,1)S(1)}, u32[]{:S(2)}, u32[]{:S(2)}) collective-permute-start(bf16[1024,256]{1,0:T(8,128)(2,1)S(1)} %fusion.2.own_ref), channel_id=1, source_target_pairs={{0,1},{1,0},{2,3},{3,2},{4,5},{5,4},{6,7},{7,6},{8,9},{9,8},{10,11... | collective-permute-start | bytes 1572872 | tf_op jit(solution)/shard_map/ppermute | solution.py:56
  9.6 5.7 %collective-permute-start.2 = (bf16[288,256]{1,0:T(8,128)(2,1)S(1)}, bf16[288,256]{1,0:T(8,128)(2,1)S(1)}, u32[]{:S(2)}, u32[]{:S(2)}) collective-permute-start(bf16[288,256]{1,0:T(8,128)(2,1)S(1)} %pad_maximum_fusion.1), channel_id=1, source_target_pairs={{0,5},{1,8},{2,11},{3,6},{4,13},{5,0},{6,3},{7,14},{8,1},{9,12},{1... | collective-permute-start | bytes 442376 | tf_op jit(solution)/shard_map/ppermute | solution.py:51
  10.9 4.4 %collective-permute-start.3 = (bf16[144,256]{1,0:T(8,128)(2,1)S(1)}, bf16[144,256]{1,0:T(8,128)(2,1)S(1)}, u32[]{:S(2)}, u32[]{:S(2)}) collective-permute-start(bf16[144,256]{1,0:T(8,128)(2,1)S(1)} %collective-permute-done), channel_id=1, source_target_pairs={{0,3},{1,2},{2,1},{3,0},{4,7},{5,6},{6,5},{7,4},{8,11},{9,10},{10,... | collective-permute-start | bytes 221192 | tf_op jit(solution)/shard_map/ppermute | solution.py:51
  11.8 1.5 %collective-permute-start.5 = (s32[8,128]{1,0:T(8,128)S(1)}, s32[8,128]{1,0:T(8,128)S(1)}, u32[]{:S(2)}, u32[]{:S(2)}) collective-permute-start(s32[8,128]{1,0:T(8,128)S(1)} %bitcast.5), channel_id=1, source_target_pairs={{0,1},{1,0},{2,3},{3,2},{4,5},{5,4},{6,7},{7,6},{8,9},{9,8},{10,11... | collective-permute-start | bytes 12296 | tf_op jit(solution)/shard_map/ppermute | solution.py:56
  15.3 5.7 %collective-permute-start.6 = (bf16[288,256]{1,0:T(8,128)(2,1)S(1)}, bf16[288,256]{1,0:T(8,128)(2,1)S(1)}, u32[]{:S(2)}, u32[]{:S(2)}) collective-permute-start(bf16[288,256]{1,0:T(8,128)(2,1)S(1)} %collective-permute-done.2), channel_id=1, source_target_pairs={{0,3},{1,2},{2,1},{3,0},{4,7},{5,6},{6,5},{7,4},{8,11},{9,10},{10,... | collective-permute-start | bytes 442376 | tf_op jit(solution)/shard_map/ppermute | solution.py:51
  22.0 1.7 %collective-permute-start.7 = (f32[24,128]{1,0:T(8,128)S(1)}, f32[24,128]{1,0:T(8,128)S(1)}, u32[]{:S(2)}, u32[]{:S(2)}) collective-permute-start(f32[24,128]{1,0:T(8,128)S(1)} %shard_map.71.mine_ref), channel_id=1, source_target_pairs={{0,1},{1,0},{2,3},{3,2},{4,5},{5,4},{6,7},{7,6},{8,9},{9,8},{10,11... | collective-permute-start | bytes 36872 | tf_op jit(solution)/shard_map/ppermute | solution.py:56
  24.6 5.0 %collective-permute-start.8 = (bf16[8,32,128]{2,1,0:T(8,128)(2,1)S(1)}, bf16[8,32,128]{2,1,0:T(8,128)(2,1)S(1)}, u32[]{:S(2)}, u32[]{:S(2)}) collective-permute-start(bf16[8,32,128]{2,1,0:T(8,128)(2,1)S(1)} %get-tuple-element.115), channel_id=1, source_target_pairs={{0,5},{1,2},{2,1},{3,6},{4,7},{5,0},{6,3},{7,4},{8,11},{9,12},{10,... | collective-permute-start | bytes 196616 | tf_op jit(solution)/shard_map/ppermute | solution.py:51
  26.3 5.3 %collective-permute-start.9 = (bf16[8,32,128]{2,1,0:T(8,128)(2,1)S(1)}, bf16[8,32,128]{2,1,0:T(8,128)(2,1)S(1)}, u32[]{:S(2)}, u32[]{:S(2)}) collective-permute-start(bf16[8,32,128]{2,1,0:T(8,128)(2,1)S(1)} %get-tuple-element.115), channel_id=1, source_target_pairs={{0,9},{1,4},{2,7},{3,10},{4,1},{5,12},{6,15},{7,2},{8,13},{9,0},{1... | collective-permute-start | bytes 196616 | tf_op jit(solution)/shard_map/ppermute | solution.py:51
  26.7 6.2 %collective-permute-start.10 = (bf16[8,32,128]{2,1,0:T(8,128)(2,1)S(1)}, bf16[8,32,128]{2,1,0:T(8,128)(2,1)S(1)}, u32[]{:S(2)}, u32[]{:S(2)}) collective-permute-start(bf16[8,32,128]{2,1,0:T(8,128)(2,1)S(1)} %get-tuple-element.115), channel_id=1, source_target_pairs={{0,12},{1,7},{2,4},{3,15},{4,2},{5,9},{6,10},{7,1},{8,14},{9,5},{1... | collective-permute-start | bytes 196616 | tf_op jit(solution)/shard_map/ppermute | solution.py:51
  32.9 3.8 %collective-permute-start.11 = (bf16[8,32,128]{2,1,0:T(8,128)(2,1)S(1)}, bf16[8,32,128]{2,1,0:T(8,128)(2,1)S(1)}, u32[]{:S(2)}, u32[]{:S(2)}) collective-permute-start(bf16[8,32,128]{2,1,0:T(8,128)(2,1)S(1)} %get-tuple-element.120), channel_id=1, source_target_pairs={{0,3},{1,8},{2,11},{3,0},{4,13},{5,6},{6,5},{7,14},{8,1},{9,10},{1... | collective-permute-start | bytes 196616 | tf_op jit(solution)/shard_map/ppermute | solution.py:51
  37.2 1.6 %collective-permute-start.13 = (bf16[32,1024]{1,0:T(8,128)(2,1)S(1)}, bf16[32,1024]{1,0:T(8,128)(2,1)S(1)}, u32[]{:S(2)}, u32[]{:S(2)}) collective-permute-start(bf16[32,1024]{1,0:T(8,128)(2,1)S(1)} %get-tuple-element.133), channel_id=1, source_target_pairs={{0,1},{1,0},{2,3},{3,2},{4,5},{5,4},{6,7},{7,6},{8,9},{9,8},{10,11... | collective-permute-start | bytes 196616 | tf_op jit(solution)/shard_map/ppermute | solution.py:56
  38.3 1.3 %collective-permute-start.12 = (bf16[32,1024]{1,0:T(8,128)(2,1)S(1)}, bf16[32,1024]{1,0:T(8,128)(2,1)S(1)}, u32[]{:S(2)}, u32[]{:S(2)}) collective-permute-start(bf16[32,1024]{1,0:T(8,128)(2,1)S(1)} %get-tuple-element.130), channel_id=1, source_target_pairs={{0,1},{1,0},{2,3},{3,2},{4,5},{5,4},{6,7},{7,6},{8,9},{9,8},{10,11... | collective-permute-start | bytes 196616 | tf_op jit(solution)/shard_map/ppermute | solution.py:56
  40.0 4.2 %collective-permute-start.14 = (bf16[8,32,128]{2,1,0:T(8,128)(2,1)S(1)}, bf16[8,32,128]{2,1,0:T(8,128)(2,1)S(1)}, u32[]{:S(2)}, u32[]{:S(2)}) collective-permute-start(bf16[8,32,128]{2,1,0:T(8,128)(2,1)S(1)} %get-tuple-element.136), channel_id=1, source_target_pairs={{0,5},{1,2},{2,1},{3,6},{4,7},{5,0},{6,3},{7,4},{8,11},{9,12},{10,... | collective-permute-start | bytes 196616 | tf_op jit(solution)/shard_map/ppermute | solution.py:51
  41.6 4.7 %collective-permute-start.15 = (bf16[8,32,128]{2,1,0:T(8,128)(2,1)S(1)}, bf16[8,32,128]{2,1,0:T(8,128)(2,1)S(1)}, u32[]{:S(2)}, u32[]{:S(2)}) collective-permute-start(bf16[8,32,128]{2,1,0:T(8,128)(2,1)S(1)} %get-tuple-element.136), channel_id=1, source_target_pairs={{0,9},{1,4},{2,7},{3,10},{4,1},{5,12},{6,15},{7,2},{8,13},{9,0},{1... | collective-permute-start | bytes 196616 | tf_op jit(solution)/shard_map/ppermute | solution.py:51
  42.8 6.1 %collective-permute-start.16 = (bf16[8,32,128]{2,1,0:T(8,128)(2,1)S(1)}, bf16[8,32,128]{2,1,0:T(8,128)(2,1)S(1)}, u32[]{:S(2)}, u32[]{:S(2)}) collective-permute-start(bf16[8,32,128]{2,1,0:T(8,128)(2,1)S(1)} %get-tuple-element.136), channel_id=1, source_target_pairs={{0,12},{1,7},{2,4},{3,15},{4,2},{5,9},{6,10},{7,1},{8,14},{9,5},{1... | collective-permute-start | bytes 196616 | tf_op jit(solution)/shard_map/ppermute | solution.py:51
  48.9 3.8 %collective-permute-start.17 = (bf16[8,32,128]{2,1,0:T(8,128)(2,1)S(1)}, bf16[8,32,128]{2,1,0:T(8,128)(2,1)S(1)}, u32[]{:S(2)}, u32[]{:S(2)}) collective-permute-start(bf16[8,32,128]{2,1,0:T(8,128)(2,1)S(1)} %get-tuple-element.138), channel_id=1, source_target_pairs={{0,3},{1,8},{2,11},{3,0},{4,13},{5,6},{6,5},{7,14},{8,1},{9,10},{1... | collective-permute-start | bytes 196616 | tf_op jit(solution)/shard_map/ppermute | solution.py:51
  53.7 1.4 %collective-permute-start.18 = (bf16[32,1024]{1,0:T(8,128)(2,1)S(1)}, bf16[32,1024]{1,0:T(8,128)(2,1)S(1)}, u32[]{:S(2)}, u32[]{:S(2)}) collective-permute-start(bf16[32,1024]{1,0:T(8,128)(2,1)S(1)} %get-tuple-element.140), channel_id=1, source_target_pairs={{0,1},{1,0},{2,3},{3,2},{4,5},{5,4},{6,7},{7,6},{8,9},{9,8},{10,11... | collective-permute-start | bytes 196616 | tf_op jit(solution)/shard_map/ppermute | solution.py:56
  55.6 4.2 %collective-permute-start.20 = (bf16[8,32,128]{2,1,0:T(8,128)(2,1)S(1)}, bf16[8,32,128]{2,1,0:T(8,128)(2,1)S(1)}, u32[]{:S(2)}, u32[]{:S(2)}) collective-permute-start(bf16[8,32,128]{2,1,0:T(8,128)(2,1)S(1)} %get-tuple-element.145), channel_id=1, source_target_pairs={{0,5},{1,2},{2,1},{3,6},{4,7},{5,0},{6,3},{7,4},{8,11},{9,12},{10,... | collective-permute-start | bytes 196616 | tf_op jit(solution)/shard_map/ppermute | solution.py:51
  56.7 4.6 %collective-permute-start.21 = (bf16[8,32,128]{2,1,0:T(8,128)(2,1)S(1)}, bf16[8,32,128]{2,1,0:T(8,128)(2,1)S(1)}, u32[]{:S(2)}, u32[]{:S(2)}) collective-permute-start(bf16[8,32,128]{2,1,0:T(8,128)(2,1)S(1)} %get-tuple-element.145), channel_id=1, source_target_pairs={{0,9},{1,4},{2,7},{3,10},{4,1},{5,12},{6,15},{7,2},{8,13},{9,0},{1... | collective-permute-start | bytes 196616 | tf_op jit(solution)/shard_map/ppermute | solution.py:51
  57.3 6.2 %collective-permute-start.22 = (bf16[8,32,128]{2,1,0:T(8,128)(2,1)S(1)}, bf16[8,32,128]{2,1,0:T(8,128)(2,1)S(1)}, u32[]{:S(2)}, u32[]{:S(2)}) collective-permute-start(bf16[8,32,128]{2,1,0:T(8,128)(2,1)S(1)} %get-tuple-element.145), channel_id=1, source_target_pairs={{0,12},{1,7},{2,4},{3,15},{4,2},{5,9},{6,10},{7,1},{8,14},{9,5},{1... | collective-permute-start | bytes 196616 | tf_op jit(solution)/shard_map/ppermute | solution.py:51
  63.6 3.8 %collective-permute-start.23 = (bf16[8,32,128]{2,1,0:T(8,128)(2,1)S(1)}, bf16[8,32,128]{2,1,0:T(8,128)(2,1)S(1)}, u32[]{:S(2)}, u32[]{:S(2)}) collective-permute-start(bf16[8,32,128]{2,1,0:T(8,128)(2,1)S(1)} %get-tuple-element.146), channel_id=1, source_target_pairs={{0,3},{1,8},{2,11},{3,0},{4,13},{5,6},{6,5},{7,14},{8,1},{9,10},{1... | collective-permute-start | bytes 196616 | tf_op jit(solution)/shard_map/ppermute | solution.py:51
  68.5 2.1 %collective-permute-start.24 = (bf16[32,1024]{1,0:T(8,128)(2,1)S(1)}, bf16[32,1024]{1,0:T(8,128)(2,1)S(1)}, u32[]{:S(2)}, u32[]{:S(2)}) collective-permute-start(bf16[32,1024]{1,0:T(8,128)(2,1)S(1)} %get-tuple-element.153), channel_id=1, source_target_pairs={{0,1},{1,0},{2,3},{3,2},{4,5},{5,4},{6,7},{7,6},{8,9},{9,8},{10,11... | collective-permute-start | bytes 196616 | tf_op jit(solution)/shard_map/ppermute | solution.py:56
  (3 other events, 9.6 us)

commit v22 on v20

--- a/solution.py
+++ b/solution.py
@@ -30,7 +30,7 @@
 
 def rounds(kind, top):
     bits = list(range(1, top))
-    bits = bits[1 - kind :] + bits[: 1 - kind]
+    bits = bits[kind:] + bits[:kind]
     return [bits[low : low + 2] for low in range(0, len(bits), 2)]
 
 

time: 70.8 us -> 70.9 us (level)
  waiting for transfers between devices: 25.8 us -> 30.1 us
  starting transfers between devices: 29.4 us -> 25.1 us
    ppermute x17, waiting for transfers between devices: 22.2 us -> 26.1 us  [exchange(): return lax.ppermute(block, 'row', pairs)]
    ppermute x17, starting transfers between devices: 25.6 us -> 22.4 us  [exchange(): return lax.ppermute(block, 'row', pairs)]
    ppermute x8, starting transfers between devices: 3.79 us -> 2.76 us  [swap(): return lax.ppermute(block, 'row', [(d, d ^ 1) for d in range(devices)])]
  transfers between devices with their start and end apart: 25 -> 25, of which waited for: 19 -> 21; matrix products, arithmetic and copies ran while one was open for 3% -> 3% of each run, Pallas kernels for 8% -> 8%
where the time goes in v22:
time: 70.9 us; the launch traced here: 70.7 us
  waiting for transfers between devices  30.1 us (42%)
  starting transfers between devices  25.1 us (35%)
  Pallas kernels  11.9 us (17%)
  other arithmetic  2.21 us (3%)
  between operations  0.85 us (1%)
    ppermute x17, waiting for transfers between devices, exchange(): return lax.ppermute(block, 'row', pairs)  26.1 us
    ppermute x17, starting transfers between devices, exchange(): return lax.ppermute(block, 'row', pairs)  22.4 us
    pallas_call x25, Pallas kernels, call(): pl.pallas_call(body, out_shape=[pltpu.VMEM(shape, dtype) for shape, dtype...  10.2 us
    ppermute x8, waiting for transfers between devices, swap(): return lax.ppermute(block, 'row', [(d, d ^ 1) for d in range(devices)])  3.97 us
    ppermute x8, starting transfers between devices, swap(): return lax.ppermute(block, 'row', [(d, d ^ 1) for d in range(devices)])  2.76 us
  transfers between devices with their start and end apart: 25, of which 21 were waited for; matrix products, arithmetic and copies ran while one was open for 3% of the time, Pallas kernels for 8%

profile of v22, /device:TPU:0, one launch (start us, length us, event | category | flops | bytes accessed | tf_op | source)
XLA Modules:
  0.0 70.7 jit_solution(8741198057739944471)
XLA Ops:
  1.6 3.5 %collective-permute-start = (bf16[144,256]{1,0:T(8,128)(2,1)S(1)}, bf16[144,256]{1,0:T(8,128)(2,1)S(1)}, u32[]{:S(2)}, u32[]{:S(2)}) collective-permute-start(bf16[144,256]{1,0:T(8,128)(2,1)S(1)} %shard_map.67), channel_id=1, source_target_pairs={{0,9},{1,4},{2,7},{3,10},{4,1},{5,12},{6,15},{7,2},{8,13},{9,0},{1... | collective-permute-start | bytes 221192 | tf_op jit(solution)/shard_map/ppermute | solution.py:51
  5.1 1.8 %collective-permute-start.1 = (bf16[144,256]{1,0:T(8,128)(2,1)S(1)}, bf16[144,256]{1,0:T(8,128)(2,1)S(1)}, u32[]{:S(2)}, u32[]{:S(2)}) collective-permute-start(bf16[144,256]{1,0:T(8,128)(2,1)S(1)} %shard_map.67), channel_id=1, source_target_pairs={{0,3},{1,2},{2,1},{3,0},{4,7},{5,6},{6,5},{7,4},{8,11},{9,10},{10,... | collective-permute-start | bytes 221192 | tf_op jit(solution)/shard_map/ppermute | solution.py:51
  6.9 1.3 %fusion = f32[1024]{0:T(1024)S(1)} fusion(bf16[1024,256]{1,0:T(8,128)(2,1)} %param.4), kind=kLoop, calls=%fused_computation.2 | loop fusion | flops 785408 | bytes 528384 | tf_op jit(solution)/shard_map/reduce_sum | solution.py:74
  9.6 1.3 %collective-permute-start.2 = (bf16[288,256]{1,0:T(8,128)(2,1)S(1)}, bf16[288,256]{1,0:T(8,128)(2,1)S(1)}, u32[]{:S(2)}, u32[]{:S(2)}) collective-permute-start(bf16[288,256]{1,0:T(8,128)(2,1)S(1)} %pad_maximum_fusion.1), channel_id=1, source_target_pairs={{0,5},{1,8},{2,11},{3,6},{4,13},{5,0},{6,3},{7,14},{8,1},{9,12},{1... | collective-permute-start | bytes 442376 | tf_op jit(solution)/shard_map/ppermute | solution.py:51
  13.3 2.0 %collective-permute-done.3 = bf16[144,256]{1,0:T(8,128)(2,1)S(1)} collective-permute-done((bf16[144,256]{1,0:T(8,128)(2,1)S(1)}, bf16[144,256]{1,0:T(8,128)(2,1)S(1)}, u32[]{:S(2)}, u32[]{:S(2)}) %collective-permute-start.3) | collective-permute-done | bytes 73760 | tf_op jit(solution)/shard_map/ppermute | solution.py:51
  15.3 1.7 %collective-permute-start.6 = (bf16[288,256]{1,0:T(8,128)(2,1)S(1)}, bf16[288,256]{1,0:T(8,128)(2,1)S(1)}, u32[]{:S(2)}, u32[]{:S(2)}) collective-permute-start(bf16[288,256]{1,0:T(8,128)(2,1)S(1)} %collective-permute-done.2), channel_id=1, source_target_pairs={{0,3},{1,2},{2,1},{3,0},{4,7},{5,6},{6,5},{7,4},{8,11},{9,10},{10,... | collective-permute-start | bytes 442376 | tf_op jit(solution)/shard_map/ppermute | solution.py:51
  17.7 1.0 %shard_map.68 = (bf16[1024,512]{1,0:T(8,128)(2,1)S(1)}, bf16[1024,512]{1,0:T(8,128)(2,1)S(1)}, f32[1024,128]{1,0:T(8,128)S(1)}, f32[1024,128]{1,0:T(8,128)S(1)}) custom-call(bf16[1024,256]{1,0:T(8,128)(2,1)S(1)} %fusion.2.own_ref, bf16[1024,256]{1,0:T(8,128)(2,1)S(1)} %collective-permute-done.4.other_ref, ...), custom_call_target="tpu_custom_call" | custom-call | flops 1073741824 | bytes 1343488 | tf_op jit(solution)/shard_map/pallas_call | solution.py:62
  18.7 2.3 %collective-permute-done.6.held_ref.refs_8_.refs_2_ = bf16[288,256]{1,0:T(8,128)(2,1)S(1)} collective-permute-done((bf16[288,256]{1,0:T(8,128)(2,1)S(1)}, bf16[288,256]{1,0:T(8,128)(2,1)S(1)}, u32[]{:S(2)}, u32[]{:S(2)}) %collective-permute-start.6) | collective-permute-done | bytes 147488 | tf_op jit(solution)/shard_map/ppermute | solution.py:51
  24.6 1.5 %collective-permute-start.8 = (bf16[8,32,128]{2,1,0:T(8,128)(2,1)S(1)}, bf16[8,32,128]{2,1,0:T(8,128)(2,1)S(1)}, u32[]{:S(2)}, u32[]{:S(2)}) collective-permute-start(bf16[8,32,128]{2,1,0:T(8,128)(2,1)S(1)} %get-tuple-element.105), channel_id=1, source_target_pairs={{0,3},{1,4},{2,7},{3,0},{4,1},{5,6},{6,5},{7,2},{8,13},{9,10},{10,... | collective-permute-start | bytes 196616 | tf_op jit(solution)/shard_map/ppermute | solution.py:51
  26.4 1.5 %collective-permute-start.10 = (bf16[8,32,128]{2,1,0:T(8,128)(2,1)S(1)}, bf16[8,32,128]{2,1,0:T(8,128)(2,1)S(1)}, u32[]{:S(2)}, u32[]{:S(2)}) collective-permute-start(bf16[8,32,128]{2,1,0:T(8,128)(2,1)S(1)} %get-tuple-element.105), channel_id=1, source_target_pairs={{0,6},{1,13},{2,14},{3,5},{4,8},{5,3},{6,0},{7,11},{8,4},{9,15},{1... | collective-permute-start | bytes 196616 | tf_op jit(solution)/shard_map/ppermute | solution.py:51
  28.7 1.2 %collective-permute-done.9.refs_1_ = bf16[8,32,128]{2,1,0:T(8,128)(2,1)S(1)} collective-permute-done((bf16[8,32,128]{2,1,0:T(8,128)(2,1)S(1)}, bf16[8,32,128]{2,1,0:T(8,128)(2,1)S(1)}, u32[]{:S(2)}, u32[]{:S(2)}) %collective-permute-start.9) | collective-permute-done | bytes 65568 | tf_op jit(solution)/shard_map/ppermute | solution.py:51
  29.8 1.8 %collective-permute-done.10.refs_2_ = bf16[8,32,128]{2,1,0:T(8,128)(2,1)S(1)} collective-permute-done((bf16[8,32,128]{2,1,0:T(8,128)(2,1)S(1)}, bf16[8,32,128]{2,1,0:T(8,128)(2,1)S(1)}, u32[]{:S(2)}, u32[]{:S(2)}) %collective-permute-start.10) | collective-permute-done | bytes 65568 | tf_op jit(solution)/shard_map/ppermute | solution.py:51
  31.7 1.5 %collective-permute-start.11 = (bf16[8,32,128]{2,1,0:T(8,128)(2,1)S(1)}, bf16[8,32,128]{2,1,0:T(8,128)(2,1)S(1)}, u32[]{:S(2)}, u32[]{:S(2)}) collective-permute-start(bf16[8,32,128]{2,1,0:T(8,128)(2,1)S(1)} %get-tuple-element.110), channel_id=1, source_target_pairs={{0,9},{1,2},{2,1},{3,10},{4,7},{5,12},{6,15},{7,4},{8,11},{9,0},{1... | collective-permute-start | bytes 196616 | tf_op jit(solution)/shard_map/ppermute | solution.py:51
  34.4 2.6 %collective-permute-done.11.refs_0_ = bf16[8,32,128]{2,1,0:T(8,128)(2,1)S(1)} collective-permute-done((bf16[8,32,128]{2,1,0:T(8,128)(2,1)S(1)}, bf16[8,32,128]{2,1,0:T(8,128)(2,1)S(1)}, u32[]{:S(2)}, u32[]{:S(2)}) %collective-permute-start.11) | collective-permute-done | bytes 65568 | tf_op jit(solution)/shard_map/ppermute | solution.py:51
  40.4 1.8 %collective-permute-start.14 = (bf16[8,32,128]{2,1,0:T(8,128)(2,1)S(1)}, bf16[8,32,128]{2,1,0:T(8,128)(2,1)S(1)}, u32[]{:S(2)}, u32[]{:S(2)}) collective-permute-start(bf16[8,32,128]{2,1,0:T(8,128)(2,1)S(1)} %get-tuple-element.122), channel_id=1, source_target_pairs={{0,3},{1,4},{2,7},{3,0},{4,1},{5,6},{6,5},{7,2},{8,13},{9,10},{10,... | collective-permute-start | bytes 196616 | tf_op jit(solution)/shard_map/ppermute | solution.py:51
  42.2 1.5 %collective-permute-start.16 = (bf16[8,32,128]{2,1,0:T(8,128)(2,1)S(1)}, bf16[8,32,128]{2,1,0:T(8,128)(2,1)S(1)}, u32[]{:S(2)}, u32[]{:S(2)}) collective-permute-start(bf16[8,32,128]{2,1,0:T(8,128)(2,1)S(1)} %get-tuple-element.122), channel_id=1, source_target_pairs={{0,6},{1,13},{2,14},{3,5},{4,8},{5,3},{6,0},{7,11},{8,4},{9,15},{1... | collective-permute-start | bytes 196616 | tf_op jit(solution)/shard_map/ppermute | solution.py:51
  44.1 2.0 %collective-permute-done.15.refs_1_ = bf16[8,32,128]{2,1,0:T(8,128)(2,1)S(1)} collective-permute-done((bf16[8,32,128]{2,1,0:T(8,128)(2,1)S(1)}, bf16[8,32,128]{2,1,0:T(8,128)(2,1)S(1)}, u32[]{:S(2)}, u32[]{:S(2)}) %collective-permute-start.15) | collective-permute-done | bytes 65568 | tf_op jit(solution)/shard_map/ppermute | solution.py:51
  46.2 1.3 %collective-permute-done.16.refs_2_ = bf16[8,32,128]{2,1,0:T(8,128)(2,1)S(1)} collective-permute-done((bf16[8,32,128]{2,1,0:T(8,128)(2,1)S(1)}, bf16[8,32,128]{2,1,0:T(8,128)(2,1)S(1)}, u32[]{:S(2)}, u32[]{:S(2)}) %collective-permute-start.16) | collective-permute-done | bytes 65568 | tf_op jit(solution)/shard_map/ppermute | solution.py:51
  48.4 4.4 %collective-permute-done.17.refs_0_ = bf16[8,32,128]{2,1,0:T(8,128)(2,1)S(1)} collective-permute-done((bf16[8,32,128]{2,1,0:T(8,128)(2,1)S(1)}, bf16[8,32,128]{2,1,0:T(8,128)(2,1)S(1)}, u32[]{:S(2)}, u32[]{:S(2)}) %collective-permute-start.17) | collective-permute-done | bytes 65568 | tf_op jit(solution)/shard_map/ppermute | solution.py:51
  55.8 1.1 %collective-permute-start.20 = (bf16[8,32,128]{2,1,0:T(8,128)(2,1)S(1)}, bf16[8,32,128]{2,1,0:T(8,128)(2,1)S(1)}, u32[]{:S(2)}, u32[]{:S(2)}) collective-permute-start(bf16[8,32,128]{2,1,0:T(8,128)(2,1)S(1)} %get-tuple-element.127), channel_id=1, source_target_pairs={{0,3},{1,4},{2,7},{3,0},{4,1},{5,6},{6,5},{7,2},{8,13},{9,10},{10,... | collective-permute-start | bytes 196616 | tf_op jit(solution)/shard_map/ppermute | solution.py:51
  57.6 1.5 %collective-permute-start.22 = (bf16[8,32,128]{2,1,0:T(8,128)(2,1)S(1)}, bf16[8,32,128]{2,1,0:T(8,128)(2,1)S(1)}, u32[]{:S(2)}, u32[]{:S(2)}) collective-permute-start(bf16[8,32,128]{2,1,0:T(8,128)(2,1)S(1)} %get-tuple-element.127), channel_id=1, source_target_pairs={{0,6},{1,13},{2,14},{3,5},{4,8},{5,3},{6,0},{7,11},{8,4},{9,15},{1... | collective-permute-start | bytes 196616 | tf_op jit(solution)/shard_map/ppermute | solution.py:51
  59.5 1.9 %collective-permute-done.21.refs_1_ = bf16[8,32,128]{2,1,0:T(8,128)(2,1)S(1)} collective-permute-done((bf16[8,32,128]{2,1,0:T(8,128)(2,1)S(1)}, bf16[8,32,128]{2,1,0:T(8,128)(2,1)S(1)}, u32[]{:S(2)}, u32[]{:S(2)}) %collective-permute-start.21) | collective-permute-done | bytes 65568 | tf_op jit(solution)/shard_map/ppermute | solution.py:51
  61.5 1.2 %collective-permute-done.22.refs_2_ = bf16[8,32,128]{2,1,0:T(8,128)(2,1)S(1)} collective-permute-done((bf16[8,32,128]{2,1,0:T(8,128)(2,1)S(1)}, bf16[8,32,128]{2,1,0:T(8,128)(2,1)S(1)}, u32[]{:S(2)}, u32[]{:S(2)}) %collective-permute-start.22) | collective-permute-done | bytes 65568 | tf_op jit(solution)/shard_map/ppermute | solution.py:51
  64.2 3.9 %collective-permute-done.23.refs_0_ = bf16[8,32,128]{2,1,0:T(8,128)(2,1)S(1)} collective-permute-done((bf16[8,32,128]{2,1,0:T(8,128)(2,1)S(1)}, bf16[8,32,128]{2,1,0:T(8,128)(2,1)S(1)}, u32[]{:S(2)}, u32[]{:S(2)}) %collective-permute-start.23) | collective-permute-done | bytes 65568 | tf_op jit(solution)/shard_map/ppermute | solution.py:51
  (67 shorter events, 24.1 us)
Async XLA Ops:
  1.6 7.3 %collective-permute-start = (bf16[144,256]{1,0:T(8,128)(2,1)S(1)}, bf16[144,256]{1,0:T(8,128)(2,1)S(1)}, u32[]{:S(2)}, u32[]{:S(2)}) collective-permute-start(bf16[144,256]{1,0:T(8,128)(2,1)S(1)} %shard_map.67), channel_id=1, source_target_pairs={{0,9},{1,4},{2,7},{3,10},{4,1},{5,12},{6,15},{7,2},{8,13},{9,0},{1... | collective-permute-start | bytes 221192 | tf_op jit(solution)/shard_map/ppermute | solution.py:51
  5.1 4.4 %collective-permute-start.1 = (bf16[144,256]{1,0:T(8,128)(2,1)S(1)}, bf16[144,256]{1,0:T(8,128)(2,1)S(1)}, u32[]{:S(2)}, u32[]{:S(2)}) collective-permute-start(bf16[144,256]{1,0:T(8,128)(2,1)S(1)} %shard_map.67), channel_id=1, source_target_pairs={{0,3},{1,2},{2,1},{3,0},{4,7},{5,6},{6,5},{7,4},{8,11},{9,10},{10,... | collective-permute-start | bytes 221192 | tf_op jit(solution)/shard_map/ppermute | solution.py:51
  9.6 5.8 %collective-permute-start.4 = (bf16[1024,256]{1,0:T(8,128)(2,1)S(1)}, bf16[1024,256]{1,0:T(8,128)(2,1)S(1)}, u32[]{:S(2)}, u32[]{:S(2)}) collective-permute-start(bf16[1024,256]{1,0:T(8,128)(2,1)S(1)} %fusion.2.own_ref), channel_id=1, source_target_pairs={{0,1},{1,0},{2,3},{3,2},{4,5},{5,4},{6,7},{7,6},{8,9},{9,8},{10,11... | collective-permute-start | bytes 1572872 | tf_op jit(solution)/shard_map/ppermute | solution.py:56
  9.6 5.7 %collective-permute-start.2 = (bf16[288,256]{1,0:T(8,128)(2,1)S(1)}, bf16[288,256]{1,0:T(8,128)(2,1)S(1)}, u32[]{:S(2)}, u32[]{:S(2)}) collective-permute-start(bf16[288,256]{1,0:T(8,128)(2,1)S(1)} %pad_maximum_fusion.1), channel_id=1, source_target_pairs={{0,5},{1,8},{2,11},{3,6},{4,13},{5,0},{6,3},{7,14},{8,1},{9,12},{1... | collective-permute-start | bytes 442376 | tf_op jit(solution)/shard_map/ppermute | solution.py:51
  10.9 4.4 %collective-permute-start.3 = (bf16[144,256]{1,0:T(8,128)(2,1)S(1)}, bf16[144,256]{1,0:T(8,128)(2,1)S(1)}, u32[]{:S(2)}, u32[]{:S(2)}) collective-permute-start(bf16[144,256]{1,0:T(8,128)(2,1)S(1)} %collective-permute-done), channel_id=1, source_target_pairs={{0,3},{1,2},{2,1},{3,0},{4,7},{5,6},{6,5},{7,4},{8,11},{9,10},{10,... | collective-permute-start | bytes 221192 | tf_op jit(solution)/shard_map/ppermute | solution.py:51
  11.8 1.5 %collective-permute-start.5 = (s32[8,128]{1,0:T(8,128)S(1)}, s32[8,128]{1,0:T(8,128)S(1)}, u32[]{:S(2)}, u32[]{:S(2)}) collective-permute-start(s32[8,128]{1,0:T(8,128)S(1)} %bitcast.5), channel_id=1, source_target_pairs={{0,1},{1,0},{2,3},{3,2},{4,5},{5,4},{6,7},{7,6},{8,9},{9,8},{10,11... | collective-permute-start | bytes 12296 | tf_op jit(solution)/shard_map/ppermute | solution.py:56
  15.3 5.7 %collective-permute-start.6 = (bf16[288,256]{1,0:T(8,128)(2,1)S(1)}, bf16[288,256]{1,0:T(8,128)(2,1)S(1)}, u32[]{:S(2)}, u32[]{:S(2)}) collective-permute-start(bf16[288,256]{1,0:T(8,128)(2,1)S(1)} %collective-permute-done.2), channel_id=1, source_target_pairs={{0,3},{1,2},{2,1},{3,0},{4,7},{5,6},{6,5},{7,4},{8,11},{9,10},{10,... | collective-permute-start | bytes 442376 | tf_op jit(solution)/shard_map/ppermute | solution.py:51
  22.0 1.7 %collective-permute-start.7 = (f32[24,128]{1,0:T(8,128)S(1)}, f32[24,128]{1,0:T(8,128)S(1)}, u32[]{:S(2)}, u32[]{:S(2)}) collective-permute-start(f32[24,128]{1,0:T(8,128)S(1)} %shard_map.71.mine_ref), channel_id=1, source_target_pairs={{0,1},{1,0},{2,3},{3,2},{4,5},{5,4},{6,7},{7,6},{8,9},{9,8},{10,11... | collective-permute-start | bytes 36872 | tf_op jit(solution)/shard_map/ppermute | solution.py:56
  24.6 4.1 %collective-permute-start.8 = (bf16[8,32,128]{2,1,0:T(8,128)(2,1)S(1)}, bf16[8,32,128]{2,1,0:T(8,128)(2,1)S(1)}, u32[]{:S(2)}, u32[]{:S(2)}) collective-permute-start(bf16[8,32,128]{2,1,0:T(8,128)(2,1)S(1)} %get-tuple-element.105), channel_id=1, source_target_pairs={{0,3},{1,4},{2,7},{3,0},{4,1},{5,6},{6,5},{7,2},{8,13},{9,10},{10,... | collective-permute-start | bytes 196616 | tf_op jit(solution)/shard_map/ppermute | solution.py:51
  26.2 3.7 %collective-permute-start.9 = (bf16[8,32,128]{2,1,0:T(8,128)(2,1)S(1)}, bf16[8,32,128]{2,1,0:T(8,128)(2,1)S(1)}, u32[]{:S(2)}, u32[]{:S(2)}) collective-permute-start(bf16[8,32,128]{2,1,0:T(8,128)(2,1)S(1)} %get-tuple-element.105), channel_id=1, source_target_pairs={{0,5},{1,8},{2,11},{3,6},{4,13},{5,0},{6,3},{7,14},{8,1},{9,12},{1... | collective-permute-start | bytes 196616 | tf_op jit(solution)/shard_map/ppermute | solution.py:51
  26.4 5.3 %collective-permute-start.10 = (bf16[8,32,128]{2,1,0:T(8,128)(2,1)S(1)}, bf16[8,32,128]{2,1,0:T(8,128)(2,1)S(1)}, u32[]{:S(2)}, u32[]{:S(2)}) collective-permute-start(bf16[8,32,128]{2,1,0:T(8,128)(2,1)S(1)} %get-tuple-element.105), channel_id=1, source_target_pairs={{0,6},{1,13},{2,14},{3,5},{4,8},{5,3},{6,0},{7,11},{8,4},{9,15},{1... | collective-permute-start | bytes 196616 | tf_op jit(solution)/shard_map/ppermute | solution.py:51
  31.7 5.4 %collective-permute-start.11 = (bf16[8,32,128]{2,1,0:T(8,128)(2,1)S(1)}, bf16[8,32,128]{2,1,0:T(8,128)(2,1)S(1)}, u32[]{:S(2)}, u32[]{:S(2)}) collective-permute-start(bf16[8,32,128]{2,1,0:T(8,128)(2,1)S(1)} %get-tuple-element.110), channel_id=1, source_target_pairs={{0,9},{1,2},{2,1},{3,10},{4,7},{5,12},{6,15},{7,4},{8,11},{9,0},{1... | collective-permute-start | bytes 196616 | tf_op jit(solution)/shard_map/ppermute | solution.py:51
  37.5 1.5 %collective-permute-start.13 = (f32[32,1024]{1,0:T(8,128)S(1)}, f32[32,1024]{1,0:T(8,128)S(1)}, u32[]{:S(2)}, u32[]{:S(2)}) collective-permute-start(f32[32,1024]{1,0:T(8,128)S(1)} %shard_map.79.image_ref), channel_id=1, source_target_pairs={{0,1},{1,0},{2,3},{3,2},{4,5},{5,4},{6,7},{7,6},{8,9},{9,8},{10,11... | collective-permute-start | bytes 393224 | tf_op jit(solution)/shard_map/ppermute | solution.py:56
  40.4 3.7 %collective-permute-start.14 = (bf16[8,32,128]{2,1,0:T(8,128)(2,1)S(1)}, bf16[8,32,128]{2,1,0:T(8,128)(2,1)S(1)}, u32[]{:S(2)}, u32[]{:S(2)}) collective-permute-start(bf16[8,32,128]{2,1,0:T(8,128)(2,1)S(1)} %get-tuple-element.122), channel_id=1, source_target_pairs={{0,3},{1,4},{2,7},{3,0},{4,1},{5,6},{6,5},{7,2},{8,13},{9,10},{10,... | collective-permute-start | bytes 196616 | tf_op jit(solution)/shard_map/ppermute | solution.py:51
  42.2 4.0 %collective-permute-start.15 = (bf16[8,32,128]{2,1,0:T(8,128)(2,1)S(1)}, bf16[8,32,128]{2,1,0:T(8,128)(2,1)S(1)}, u32[]{:S(2)}, u32[]{:S(2)}) collective-permute-start(bf16[8,32,128]{2,1,0:T(8,128)(2,1)S(1)} %get-tuple-element.122), channel_id=1, source_target_pairs={{0,5},{1,8},{2,11},{3,6},{4,13},{5,0},{6,3},{7,14},{8,1},{9,12},{1... | collective-permute-start | bytes 196616 | tf_op jit(solution)/shard_map/ppermute | solution.py:51
  42.2 5.3 %collective-permute-start.16 = (bf16[8,32,128]{2,1,0:T(8,128)(2,1)S(1)}, bf16[8,32,128]{2,1,0:T(8,128)(2,1)S(1)}, u32[]{:S(2)}, u32[]{:S(2)}) collective-permute-start(bf16[8,32,128]{2,1,0:T(8,128)(2,1)S(1)} %get-tuple-element.122), channel_id=1, source_target_pairs={{0,6},{1,13},{2,14},{3,5},{4,8},{5,3},{6,0},{7,11},{8,4},{9,15},{1... | collective-permute-start | bytes 196616 | tf_op jit(solution)/shard_map/ppermute | solution.py:51
  47.5 5.4 %collective-permute-start.17 = (bf16[8,32,128]{2,1,0:T(8,128)(2,1)S(1)}, bf16[8,32,128]{2,1,0:T(8,128)(2,1)S(1)}, u32[]{:S(2)}, u32[]{:S(2)}) collective-permute-start(bf16[8,32,128]{2,1,0:T(8,128)(2,1)S(1)} %get-tuple-element.124), channel_id=1, source_target_pairs={{0,9},{1,2},{2,1},{3,10},{4,7},{5,12},{6,15},{7,4},{8,11},{9,0},{1... | collective-permute-start | bytes 196616 | tf_op jit(solution)/shard_map/ppermute | solution.py:51
  53.3 1.4 %collective-permute-start.19 = (f32[32,1024]{1,0:T(8,128)S(1)}, f32[32,1024]{1,0:T(8,128)S(1)}, u32[]{:S(2)}, u32[]{:S(2)}) collective-permute-start(f32[32,1024]{1,0:T(8,128)S(1)} %shard_map.85.image_ref), channel_id=1, source_target_pairs={{0,1},{1,0},{2,3},{3,2},{4,5},{5,4},{6,7},{7,6},{8,9},{9,8},{10,11... | collective-permute-start | bytes 393224 | tf_op jit(solution)/shard_map/ppermute | solution.py:56
  53.8 1.5 %collective-permute-start.18 = (f32[32,1024]{1,0:T(8,128)S(1)}, f32[32,1024]{1,0:T(8,128)S(1)}, u32[]{:S(2)}, u32[]{:S(2)}) collective-permute-start(f32[32,1024]{1,0:T(8,128)S(1)} %shard_map.86.image_ref), channel_id=1, source_target_pairs={{0,1},{1,0},{2,3},{3,2},{4,5},{5,4},{6,7},{7,6},{8,9},{9,8},{10,11... | collective-permute-start | bytes 393224 | tf_op jit(solution)/shard_map/ppermute | solution.py:56
  55.8 3.7 %collective-permute-start.20 = (bf16[8,32,128]{2,1,0:T(8,128)(2,1)S(1)}, bf16[8,32,128]{2,1,0:T(8,128)(2,1)S(1)}, u32[]{:S(2)}, u32[]{:S(2)}) collective-permute-start(bf16[8,32,128]{2,1,0:T(8,128)(2,1)S(1)} %get-tuple-element.127), channel_id=1, source_target_pairs={{0,3},{1,4},{2,7},{3,0},{4,1},{5,6},{6,5},{7,2},{8,13},{9,10},{10,... | collective-permute-start | bytes 196616 | tf_op jit(solution)/shard_map/ppermute | solution.py:51
  56.9 4.6 %collective-permute-start.21 = (bf16[8,32,128]{2,1,0:T(8,128)(2,1)S(1)}, bf16[8,32,128]{2,1,0:T(8,128)(2,1)S(1)}, u32[]{:S(2)}, u32[]{:S(2)}) collective-permute-start(bf16[8,32,128]{2,1,0:T(8,128)(2,1)S(1)} %get-tuple-element.127), channel_id=1, source_target_pairs={{0,5},{1,8},{2,11},{3,6},{4,13},{5,0},{6,3},{7,14},{8,1},{9,12},{1... | collective-permute-start | bytes 196616 | tf_op jit(solution)/shard_map/ppermute | solution.py:51
  57.6 5.2 %collective-permute-start.22 = (bf16[8,32,128]{2,1,0:T(8,128)(2,1)S(1)}, bf16[8,32,128]{2,1,0:T(8,128)(2,1)S(1)}, u32[]{:S(2)}, u32[]{:S(2)}) collective-permute-start(bf16[8,32,128]{2,1,0:T(8,128)(2,1)S(1)} %get-tuple-element.127), channel_id=1, source_target_pairs={{0,6},{1,13},{2,14},{3,5},{4,8},{5,3},{6,0},{7,11},{8,4},{9,15},{1... | collective-permute-start | bytes 196616 | tf_op jit(solution)/shard_map/ppermute | solution.py:51
  62.8 5.4 %collective-permute-start.23 = (bf16[8,32,128]{2,1,0:T(8,128)(2,1)S(1)}, bf16[8,32,128]{2,1,0:T(8,128)(2,1)S(1)}, u32[]{:S(2)}, u32[]{:S(2)}) collective-permute-start(bf16[8,32,128]{2,1,0:T(8,128)(2,1)S(1)} %get-tuple-element.128), channel_id=1, source_target_pairs={{0,9},{1,2},{2,1},{3,10},{4,7},{5,12},{6,15},{7,4},{8,11},{9,0},{1... | collective-permute-start | bytes 196616 | tf_op jit(solution)/shard_map/ppermute | solution.py:51
  68.6 1.4 %collective-permute-start.24 = (f32[32,1024]{1,0:T(8,128)S(1)}, f32[32,1024]{1,0:T(8,128)S(1)}, u32[]{:S(2)}, u32[]{:S(2)}) collective-permute-start(f32[32,1024]{1,0:T(8,128)S(1)} %shard_map.92), channel_id=1, source_target_pairs={{0,1},{1,0},{2,3},{3,2},{4,5},{5,4},{6,7},{7,6},{8,9},{9,8},{10,11... | collective-permute-start | bytes 393224 | tf_op jit(solution)/shard_map/ppermute | solution.py:56
  (3 other events, 9.7 us)
